TPU v7x, 32 devices: a whole 2x2x4 slice. The times are simulated.
32 devices in a mesh: req: 8 (over z, core), mp: 4 (over y, x).
Axes of the slice: x: 2, y: 2, z: 4, core: 2. Of those that a mesh axis runs over, the one named last changes fastest.
Arguments:
- tokens: bfloat16 [784, 7168], P('req', 'mp'), may hold values from -6 to 6
- layernorm_scale: float32 [7168], replicated, may hold values from 0.5 to 1.5
- layernorm_bias: float32 [7168], replicated, may hold values from -3 to 3
- query_key_value_weight: bfloat16 [3, 7168, 6144], P(None, 'req', 'mp'), may hold values from -0.0625 to 0.0625
- query_key_value_bias: float32 [3, 6144], P(None, 'mp'), may hold values from -3 to 3
- adapter_down_weight: bfloat16 [64, 7168, 32], P('req', 'mp'), may hold values from -0.0625 to 0.0625
- adapter_up_weight: bfloat16 [64, 2, 16, 6144], P('req', None, None, 'mp'), may hold values from -1.5 to 1.5
- adapter_index_table: int32 [8, 5], P('req'), may hold values from 0 to 63
- prompt_length_list: int32 [24], P('req'), may hold values from 1 to 32, 480 in all
- cache: bfloat16 [16, 2048, 2, 6144], P('req', None, None, 'mp'), may hold values from -320 to 320, as said below
- cache_length_list: int32 [16], P('req'), may hold values from 1 to 2048, 10240 in all
- output_weight: bfloat16 [6144, 7168], P('mp', 'req'), may hold values from -0.078125 to 0.078125
- output_bias: float32 [7168], P('mp'), may hold values from -3 to 3
Outputs:
- layer_out: bfloat16 [784, 7168], P('req', 'mp')
Inputs may be any that keep to these rules, and one draw needn't show every extreme that they name: Each prompt fills the first prompt_length_list rows of its slot of 32 rows. Live cache positions are the first cache_length_list of each slot. `cache`: entries mostly of order one, though rare keys may be larger.
All inputs are finite; a program needn't handle non-finite values. No bound on the sum of `prompt_length_list` or of `cache_length_list` on one device may be relied on, other than what follows from the above.
Results may differ from a plain program's by a relative error of at most 0.015.
Values may be sent and summed in bfloat16 or wider, within the bound.
No kernel may reach another device: no remote copies, remote signals or barrier semaphores. Data moves between devices by JAX's collectives and lax.ppermute only.
A program may use at most 256 MiB of HBM per device.

v0:
```python
import jax
import jax.numpy as jnp
from jax import lax
from jax.sharding import PartitionSpec as P

HEAD_DIM = 128
ADAPTER_RANK = 16


def layer_norm(row_data, gain_vec, shift_vec):
    values = row_data.astype(jnp.float32)
    average = jnp.mean(values, axis=-1, keepdims=True)
    centred = values - average
    variance = jnp.mean(centred * centred, axis=-1, keepdims=True)
    scaled = centred * lax.rsqrt(variance + 1e-05)
    return (scaled * gain_vec + shift_vec).astype(jnp.bfloat16)


def on_device(
    tokens,
    layernorm_scale,
    layernorm_bias,
    query_key_value_weight,
    query_key_value_bias,
    adapter_down_weight,
    adapter_up_weight,
    adapter_index_table,
    prompt_length_list,
    cache,
    cache_length_list,
    output_weight,
    output_bias,
):
    rows_dev = tokens.shape[0]
    part_cols = tokens.shape[1]
    decode_count = cache.shape[0]
    slot_count = prompt_length_list.shape[0]
    prompt_rows = rows_dev - decode_count
    slot_len = prompt_rows // slot_count
    rank_size = ADAPTER_RANK
    head_count = query_key_value_weight.shape[2] // HEAD_DIM
    score_scale = HEAD_DIM ** (-0.5)
    gathered = lax.all_gather(tokens, "mp", axis=1, tiled=True)
    normed = layer_norm(gathered, layernorm_scale, layernorm_bias)
    column = lax.axis_index("mp")
    slice_m = lax.dynamic_slice_in_dim(normed, column * part_cols, part_cols, 1)
    spread = lax.all_to_all(normed, "req", split_axis=1, concat_axis=0, tiled=True)
    projected = lax.psum_scatter(
        jnp.einsum(
            "rd,cde->rce", spread, query_key_value_weight, preferred_element_type=jnp.float32
        ),
        "req",
        scatter_dimension=0,
        tiled=True,
    )
    projected = projected + query_key_value_bias[None]
    positions = jnp.arange(rows_dev)
    request_slot = jnp.where(
        positions < prompt_rows, positions // slot_len, slot_count + positions - prompt_rows
    )
    slot_match = request_slot[:, None] == jnp.arange(slot_count + decode_count)[None, :]
    row_adapter = jnp.sum(jnp.where(slot_match, adapter_index_table[0][None, :], 0), axis=1)
    adapter_on_device = adapter_down_weight.shape[0]
    owners = lax.axis_size("req")
    owner_row = row_adapter // adapter_on_device
    to_owner = owner_row[None, :] == jnp.arange(owners)[:, None]
    outgoing = jnp.where(to_owner[:, :, None], slice_m[None], jnp.zeros((), jnp.bfloat16))
    labels = jnp.where(to_owner, (row_adapter - owner_row * adapter_on_device)[None, :], -1)
    received_rows = lax.all_to_all(outgoing, "req", split_axis=0, concat_axis=0, tiled=True)
    arrived_labels = lax.all_to_all(labels, "req", split_axis=0, concat_axis=0, tiled=True)
    sources, items = arrived_labels.shape
    selection_mask = (
        arrived_labels[:, :, None] == jnp.arange(adapter_on_device)[None, None, :]
    ).astype(jnp.float32)
    adapter_wise_sums = jnp.einsum(
        "yju,ouv->yjov", received_rows, adapter_down_weight, preferred_element_type=jnp.float32
    )
    reduced_rank_rows = jnp.einsum("ogf,ogft->ogt", selection_mask, adapter_wise_sums)
    reduced_rank_rows = lax.psum(reduced_rank_rows, "mp").astype(jnp.bfloat16)
    broadcast_rank_rows = selection_mask.astype(jnp.bfloat16)[
        :, :, :, None, None
    ] * reduced_rank_rows.reshape(sources, items, 1, 2, rank_size)
    corrections = jnp.einsum(
        "pqwgd,wgdx->pqgx",
        broadcast_rank_rows,
        adapter_up_weight,
        preferred_element_type=jnp.float32,
    ).astype(jnp.bfloat16)
    returned = lax.all_to_all(corrections, "req", split_axis=0, concat_axis=0, tiled=True)
    adapter_delta = jnp.sum(returned.astype(jnp.float32), axis=0)
    queries = (projected[:, 0] + adapter_delta[:, 0]).astype(jnp.bfloat16)
    keys_new = projected[:, 1].astype(jnp.bfloat16)
    values_new = (projected[:, 2] + adapter_delta[:, 1]).astype(jnp.bfloat16)
    prompt_q = queries[:prompt_rows].reshape(slot_count, slot_len, head_count, HEAD_DIM)
    prompt_k = keys_new[:prompt_rows].reshape(slot_count, slot_len, head_count, HEAD_DIM)
    prompt_v = values_new[:prompt_rows].reshape(slot_count, slot_len, head_count, HEAD_DIM)
    scores = (
        jnp.einsum("sihd,sjhd->shij", prompt_q, prompt_k, preferred_element_type=jnp.float32)
        * score_scale
    )
    causal = jnp.arange(slot_len)[None, :] <= jnp.arange(slot_len)[:, None]
    scores = jnp.where(causal[None, None], scores, -1e30)
    highest = jnp.max(scores, axis=3, keepdims=True)
    weights = jnp.where(causal[None, None], jnp.exp(scores - highest), 0.0)
    weights = (weights / jnp.sum(weights, axis=3, keepdims=True)).astype(jnp.bfloat16)
    prompt_out = jnp.einsum(
        "shij,sjhd->sihd", weights, prompt_v, preferred_element_type=jnp.float32
    )
    active = jnp.arange(slot_len)[None, :] < prompt_length_list[:, None]
    prompt_out = (
        jnp.where(active[:, :, None, None], prompt_out, 0.0)
        .astype(jnp.bfloat16)
        .reshape(prompt_rows, -1)
    )
    cache_len = cache.shape[1]
    decode_q = queries[prompt_rows:].reshape(decode_count, head_count, HEAD_DIM)
    decode_k = keys_new[prompt_rows:].reshape(decode_count, head_count, HEAD_DIM)
    decode_v = values_new[prompt_rows:].reshape(decode_count, head_count, HEAD_DIM)
    keys_old = cache[:, :, 0].reshape(decode_count, cache_len, head_count, HEAD_DIM)
    values_old = cache[:, :, 1].reshape(decode_count, cache_len, head_count, HEAD_DIM)
    cache_scores = (
        jnp.einsum("dhe,dthe->dht", decode_q, keys_old, preferred_element_type=jnp.float32)
        * score_scale
    )
    live_cache = jnp.arange(cache_len)[None, None, :] < cache_length_list[:, None, None]
    cache_scores = jnp.where(live_cache, cache_scores, -1e30)
    self_score = (
        jnp.einsum("dhe,dhe->dh", decode_q, decode_k, preferred_element_type=jnp.float32)
        * score_scale
    )
    row_top = jnp.maximum(jnp.max(cache_scores, axis=2), self_score)
    cache_weights = jnp.where(live_cache, jnp.exp(cache_scores - row_top[:, :, None]), 0.0)
    self_weight = jnp.exp(self_score - row_top)
    totals = jnp.sum(cache_weights, axis=2) + self_weight
    cache_weights = (cache_weights / totals[:, :, None]).astype(jnp.bfloat16)
    self_weight = (self_weight / totals).astype(jnp.bfloat16)
    decode_out = jnp.einsum(
        "dht,dthe->dhe", cache_weights, values_old, preferred_element_type=jnp.float32
    )
    decode_out = decode_out + self_weight.astype(jnp.float32)[:, :, None] * decode_v.astype(
        jnp.float32
    )
    decode_out = decode_out.astype(jnp.bfloat16).reshape(decode_count, -1)
    attended = jnp.concatenate([prompt_out, decode_out], axis=0)
    mixed = jnp.dot(
        attended,
        lax.all_gather(output_weight, "req", axis=1, tiled=True),
        preferred_element_type=jnp.float32,
    )
    summed = lax.psum_scatter(
        mixed.astype(jnp.bfloat16), "mp", scatter_dimension=1, tiled=True
    ).astype(jnp.float32)
    return (tokens.astype(jnp.float32) + summed + output_bias[None]).astype(jnp.bfloat16)


def solution(mesh):
    placed = (
        P("req", "mp"),
        P(),
        P(),
        P(None, "req", "mp"),
        P(None, "mp"),
        P("req", "mp", None),
        P("req", None, None, "mp"),
        P("req", None),
        P("req"),
        P("req", None, None, "mp"),
        P("req"),
        P("mp", "req"),
        P("mp"),
    )
    return jax.shard_map(
        on_device, mesh=mesh, in_specs=placed, out_specs=P("req", "mp"), check_vma=False
    )
```

profile of v0, /device:TPU:0, one launch (start us, length us, event | category | flops | bytes accessed | tf_op | source)
XLA Modules:
  0.0 803.4 jit_solution(10173468510459794882)
XLA Ops:
  6.5 0.7 all-gather.3.cloned.1.call-update
  7.3 34.9 %all-gather.3.cloned.1.call-done = bf16[98,7168]{1,0:T(8,128)(2,1)} async-done(((bf16[98,1792]{1,0:T(8,128)(2,1)}), bf16[98,7168]{1,0:T(8,128)(2,1)}) %all-gather.3.cloned.1.call-update) | async-done | bytes 1404944 | tf_op jit(solution)/shard_map/all_gather | solution.py:43
  42.3 1.8 convert_reduce_fusion.1
  44.1 1.9 fusion.4
  46.0 0.6 fusion.7
  46.7 0.2 copy.91
  47.2 40.6 %all_to_all.35 = bf16[98,8,896]{2,0,1:T(8,128)(2,1)} all-to-all(bf16[98,8,896]{2,0,1:T(8,128)(2,1)S(1)} %copy.53), channel_id=1, replica_groups=mesh['req'=8,'mp'=4] {'req'}, dimensions={1} | all-to-all | bytes 2809856 | tf_op jit(solution)/shard_map/all_to_all | solution.py:47
  87.8 2.4 reshape.246
  90.2 13.4 %fusion.59 = f32[784,3,1536]{2,0,1:T(8,128)} fusion(bf16[784,896,1]{1,0,2:T(8,128)(2,1)} %reshape.246, bf16[3,896,1536]{2,1,0:T(8,128)(2,1)} %param.16), kind=kOutput, calls=%fused_computation.107 | convolution fusion | flops 6473908224 | bytes 24113152 | tf_op jit(solution)/shard_map/rd,cde->rce/dot_general | solution.py:49
  103.8 0.7 all-gather.5.cloned.1.call-update
  104.6 0.6 compare_select_fusion
  105.2 3.3 all-to-all-start.1
  108.6 2.0 broadcast_select_fusion
  110.5 3.4 all-to-all-done.1
  113.9 4.4 all-to-all-start.2
  118.4 99.5 %all-to-all-done.2 = bf16[8,98,1792]{2,1,0:T(8,128)(2,1)} async-done(((bf16[8,98,1792]{2,1,0:T(8,128)(2,1)}), bf16[8,98,1792]{2,1,0:T(8,128)(2,1)}, u32[]{:S(2)}, u32[]{:S(2)}) %all-to-all-start.2) | async-done | bytes 2809888 | tf_op jit(solution)/shard_map/all_to_all | solution.py:69
  217.9 3.2 fusion.16
  221.2 17.9 %psum.7 = bf16[8,98,32]{1,2,0:T(8,128)(2,1)S(1)} all-reduce(f32[8,98,32]{1,2,0:T(8,128)S(1)} %fusion.16), channel_id=1, replica_groups=mesh['req'=8,'mp'=4] {'mp'}, use_global_device_ids=true, to_apply=%region_4.5 | all-reduce | flops 25088 | bytes 150528 | tf_op jit(solution)/shard_map/psum | solution.py:79
  239.0 3.8 fusion.1
  242.9 9.5 %copy.57 = bf16[8,98,2,1536]{3,2,1,0:T(2,128)(2,1)} copy(bf16[8,98,2,1536]{3,1,0,2:T(8,128)(2,1)} %fusion.1) | data formatting | bytes 9633792 | tf_op jit(solution)/shard_map/convert_element_type | solution.py:88
  252.4 4.6 all-to-all-start.3
  257.0 0.3 reduce-scatter.3.cloned.1.call-start
  257.3 48.3 %fusion.57 = (bf16[2,2048,1,1536]{3,2,1,0:T(2,128)(2,1)}, bf16[2,2048,1,1536]{3,2,1,0:T(2,128)(2,1)}) fusion(bf16[2,2048,2,1536]{3,2,1,0:T(2,128)(2,1)} %param.22), kind=kLoop, calls=%fused_computation.105 | loop fusion | bytes 50331648 | tf_op jit(solution)/shard_map/slice | solution.py:119
  305.6 58.0 %copy.88 = bf16[2,2048,1,1536]{1,3,0,2:T(8,128)(2,1)} copy(bf16[2,2048,1,1536]{3,2,1,0:T(2,128)(2,1)} %get-tuple-element.9) | data formatting | bytes 25165824
  363.6 58.0 %copy.89 = bf16[2,2048,1,1536]{1,3,0,2:T(8,128)(2,1)} copy(bf16[2,2048,1,1536]{3,2,1,0:T(2,128)(2,1)} %get-tuple-element.10) | data formatting | bytes 25165824
  421.7 0.6 dynamic-slice
  423.1 134.0 %all-reduce.3.cloned.1.call-done = f32[784,3,1536]{2,0,1:T(8,128)} async-done(((f32[784,3,1536]{2,0,1:T(8,128)}), f32[784,3,1536]{2,0,1:T(8,128)}) %all-reduce.3.cloned.1.call-update) | async-done | bytes 14450704
  557.1 1.8 constant_dynamic-slice_fusion
  558.9 1.6 fusion.55
  560.5 1.0 copy-done.3
  561.5 1.8 slice_reduce_fusion
  563.3 0.9 reshape.240
  564.2 0.8 slice_reduce_fusion.3
  565.0 8.8 %convert_reduce_fusion = f32[98,2,1536]{2,1,0:T(2,128)} fusion(bf16[8,98,2,1536]{3,2,1,0:T(2,128)(2,1)} %all-to-all-done.3), kind=kLoop, calls=%fused_computation.2 | loop fusion | flops 4515840 | bytes 6021120 | tf_op jit(solution)/shard_map/reduce_sum | solution.py:90
  573.9 3.4 fusion.24
  577.3 0.8 copy-done.4
  578.1 2.5 slice_reduce_fusion.1
  581.1 0.3 fusion.19
  581.6 0.4 fusion.21
  582.4 6.4 fusion.45
  588.8 0.3 fusion.40
  589.2 0.4 fusion.56
  589.7 0.8 fusion.44
  590.6 6.6 fusion.37
  597.3 155.6 %all-gather.5.cloned.1.call-done = bf16[1536,7168]{1,0:T(8,128)(2,1)} async-done(((bf16[1536,896]{1,0:T(8,128)(2,1)}), bf16[1536,7168]{1,0:T(8,128)(2,1)}) %all-gather.5.cloned.1.call-update) | async-done | bytes 22020112 | tf_op jit(solution)/shard_map/all_gather | solution.py:147
  752.9 11.9 %convolution_convert_fusion = bf16[98,7168]{1,0:T(8,128)(2,1)} fusion(bf16[1536,7168]{1,0:T(8,128)(2,1)} %all-gather.5.cloned.1.call-done, bf16[2,1536]{1,0:T(2,128)(2,1)S(1)} %bitcast.82, bf16[96,1536]{1,0:T(8,128)(2,1)S(1)} %bitcast.80), kind=kOutput, calls=%fused_computation.3 | convolution fusion | flops 2159273984 | bytes 23726080 | tf_op jit(solution)/shard_map/dot_general | solution.py:145
  764.8 29.8 %reduce-scatter.3.cloned.1.call-done = bf16[98,1792]{1,0:T(8,128)(2,1)} async-done(((bf16[98,7168]{1,0:T(8,128)(2,1)}), bf16[98,1792]{1,0:T(8,128)(2,1)}) %reduce-scatter.3.cloned.1.call-update) | async-done | bytes 351248 | tf_op jit(solution)/shard_map/reduce_scatter | solution.py:150
  794.6 1.8 add_convert_fusion
  (66 shorter events, 2.2 us)
Async XLA Ops:
  6.5 211.4 %copy-start = (bf16[8,1792,32]{1,2,0:T(8,128)(2,1)S(1)}, bf16[8,1792,32]{1,2,0:T(8,128)(2,1)}, u32[]{:S(2)}) copy-start(bf16[8,1792,32]{1,2,0:T(8,128)(2,1)} %param.18) | copy-start | bytes 2752516
  6.5 39.5 %copy-start.9 = (f32[7168]{0:T(1024)S(1)}, f32[7168]{0:T(1024)}, u32[]{:S(2)}) copy-start(f32[7168]{0:T(1024)} %param.14) | copy-start | bytes 86020
  6.5 39.5 %copy-start.8 = (f32[7168]{0:T(1024)S(1)}, f32[7168]{0:T(1024)}, u32[]{:S(2)}) copy-start(f32[7168]{0:T(1024)} %param.15) | copy-start | bytes 86020
  6.5 35.7 %all-gather.3.cloned.1.call-start = ((), (), s32[]{:S(2)}) async-start(), calls=%async_computation.5 | async-start | bytes 1863680 | tf_op jit(solution)/shard_map/all_gather | solution.py:43
  7.3 549.8 %all-reduce.3.cloned.1.call-start = ((), (), s32[]{:S(2)}) async-start(), calls=%async_computation.8 | async-start | bytes 28901376
  42.3 3.8 copy-start.2
  103.7 0.8 copy-start.13
  103.7 649.2 %all-gather.5.cloned.1.call-start = ((), (), s32[]{:S(2)}) async-start(), calls=%async_computation.6 | async-start | bytes 24772608 | tf_op jit(solution)/shard_map/all_gather | solution.py:147
  105.2 8.8 %all-to-all-start.1 = ((s32[8,1,98]{2,1,0:T(1,128)}), s32[8,1,98]{2,1,0:T(1,128)S(1)}, u32[]{:S(2)}, u32[]{:S(2)}) async-start(s32[8,1,98]{2,1,0:T(1,128)} %compare_select_fusion), calls=%async_computation.1 | async-start | bytes 8192 | tf_op jit(solution)/shard_map/all_to_all | solution.py:70
  113.9 104.0 %all-to-all-start.2 = ((bf16[8,98,1792]{2,1,0:T(8,128)(2,1)}), bf16[8,98,1792]{2,1,0:T(8,128)(2,1)}, u32[]{:S(2)}, u32[]{:S(2)}) async-start(bf16[8,98,1792]{2,1,0:T(8,128)(2,1)} %broadcast_select_fusion), calls=%async_computation.2 | async-start | bytes 5963776 | tf_op jit(solution)/shard_map/all_to_all | solution.py:69
  217.9 21.1 %copy-start.6 = (bf16[8,2,16,1536]{3,2,1,0:T(8,128)(2,1)S(1)}, bf16[8,2,16,1536]{3,2,1,0:T(8,128)(2,1)}, u32[]{:S(2)}) copy-start(bf16[8,2,16,1536]{3,2,1,0:T(8,128)(2,1)} %param.19) | copy-start | bytes 2359300
  252.4 312.7 %all-to-all-start.3 = ((bf16[8,98,2,1536]{3,2,1,0:T(2,128)(2,1)}), bf16[8,98,2,1536]{3,2,1,0:T(2,128)(2,1)}, u32[]{:S(2)}, u32[]{:S(2)}) async-start(bf16[8,98,2,1536]{3,2,1,0:T(2,128)(2,1)} %copy.57), calls=%async_computation.3 | async-start | bytes 9633792 | tf_op jit(solution)/shard_map/all_to_all | solution.py:89
  257.0 537.5 %reduce-scatter.3.cloned.1.call-start = ((), (), s32[]{:S(2)}) async-start(), calls=%async_computation.7 | async-start | bytes 1863680 | tf_op jit(solution)/shard_map/reduce_scatter | solution.py:150
  363.6 58.0 %copy-start.15 = (u32[32]{0:T(128)S(1)}, u32[32]{0:T(128)}, u32[]{:S(2)}) copy-start(u32[32]{0:T(128)} %constant.74) | copy-start | bytes 388
  363.6 59.3 %copy-start.14 = (s32[3]{0:T(128)S(1)}, s32[3]{0:T(128)}, u32[]{:S(2)}) copy-start(s32[3]{0:T(128)} %param.21) | copy-start | bytes 40
  363.6 59.4 %copy-start.12 = (s32[2]{0:T(128)S(1)}, s32[2]{0:T(128)}, u32[]{:S(2)}) copy-start(s32[2]{0:T(128)} %param.23) | copy-start | bytes 28
  421.7 137.2 %copy-start.10 = (f32[3,1536]{1,0:T(4,128)S(1)}, f32[3,1536]{1,0:T(4,128)}, u32[]{:S(2)}) copy-start(f32[3,1536]{1,0:T(4,128)} %param.17) | copy-start | bytes 55300
  560.5 1.0 copy-start.3
  577.3 0.8 copy-start.4
  577.3 3.7 copy-start.7
  752.9 41.7 %copy-start.5 = (bf16[98,1792]{1,0:T(8,128)(2,1)S(1)}, bf16[98,1792]{1,0:T(8,128)(2,1)}, u32[]{:S(2)}) copy-start(bf16[98,1792]{1,0:T(8,128)(2,1)} %param.13) | copy-start | bytes 1053700
  752.9 41.7 %copy-start.11 = (f32[1792]{0:T(1024)S(1)}, f32[1792]{0:T(1024)}, u32[]{:S(2)}) copy-start(f32[1792]{0:T(1024)} %param.25) | copy-start | bytes 21508
  752.9 43.5 %copy-start.1 = (bf16[8,1792,32]{1,2,0:T(8,128)(2,1)S(1)}, bf16[8,1792,32]{1,2,0:T(8,128)(2,1)}, u32[]{:S(2)}) copy-start(bf16[8,1792,32]{1,2,0:T(8,128)(2,1)} %param.18) | copy-start | bytes 2752516
Sparse Core Ops, SparseCore 0:
  9.2 32.9 all-gather.2
  103.8 453.2 all-reduce.2
  558.8 194.0 all-gather.4
  764.9 29.6 reduce-scatter.2
where the time goes:
time: 812 us; the launch traced here: 803 us
  waiting for transfers between devices  459 us (57%)
  local copies, waits for them, and re-layouts  188 us (23%)
  blocking collectives  58.5 us (7%)
  matrix products  46 us (6%)
  other arithmetic  24.9 us (3%)
  between operations  14.6 us (2%)
  starting transfers between devices  12.7 us (2%)
    all_gather x1, waiting for transfers between devices, on_device(): lax.all_gather(output_weight, 'req', axis=1, tiled=True)  156 us
    unnamed x5, waiting for transfers between devices  135 us
    unnamed x39, local copies, waits for them, and re-layouts  121 us
    all_to_all x1, waiting for transfers between devices, on_device(): lax.all_to_all(outgoing, 'req', split_axis=0, concat_axis=0, tiled=True)  99.5 us
    slice x1, local copies, waits for them, and re-layouts, on_device(): cache[:, :, 0].reshape(decode_count, cache_len, head_count, HEAD_DIM)  48.3 us
    all_to_all x1, blocking collectives, on_device(): lax.all_to_all(normed, 'req', split_axis=1, concat_axis=0, tiled=True)  40.6 us
    all_gather x1, waiting for transfers between devices, on_device(): gathered = lax.all_gather(tokens, 'mp', axis=1, tiled=True)  34.9 us
    reduce_scatter x1, waiting for transfers between devices, on_device(): lax.psum_scatter(mixed.astype(jnp.bfloat16), 'mp', scatter_dimension=1, t...  29.8 us
  transfers between devices with their start and end apart: 7, of which 6 were waited for; matrix products, arithmetic and copies ran while one was open for 28% of the time, Pallas kernels for 0%

commit v1 on v0

--- a/solution.py
+++ b/solution.py
@@ -1,10 +1,517 @@
+import functools
+
 import jax
 import jax.numpy as jnp
 from jax import lax
+from jax.experimental import pallas as pl
+from jax.experimental.pallas import tpu as pltpu
 from jax.sharding import PartitionSpec as P
 
 HEAD_DIM = 128
 ADAPTER_RANK = 16
+BF = jnp.bfloat16
+F32 = jnp.float32
+MIB = 1 << 20
+
+NZ, NM = 4, 4
+SLOTS, PLEN, DEC = 3, 32, 2
+QROWS = 24
+BLK = 32
+CHUNK = 128
+DCH = 16
+
+
+def swap_req(x, bits):
+    return lax.ppermute(x, "req", [(i, i ^ bits) for i in range(2 * NZ)])
+
+
+def swap_mp(x, bits):
+    return lax.ppermute(x, "mp", [(i, i ^ bits) for i in range(NM)])
+
+
+def move_z(x, hops):
+    return lax.ppermute(x, "req", [(a * 2 + c, b * 2 + c) for a, b in hops for c in range(2)])
+
+
+RIGHT = [[(0, 1), (1, 2), (2, 3)], [(1, 2), (2, 3)], [(2, 3)]]
+LEFT = [[(3, 2), (2, 1), (1, 0)], [(2, 1), (1, 0)], [(1, 0)]]
+
+
+def gather_z(x):
+    right, left = [x], [x]
+    for s in range(NZ - 1):
+        right.append(move_z(right[-1], RIGHT[s]))
+        left.append(move_z(left[-1], LEFT[s]))
+    return [x] + [right[s] + left[NZ - s] for s in range(1, NZ)]
+
+
+def norm_kernel(place_ref, own_ref, r1_ref, r2_ref, r3_ref, gain_ref, shift_ref, table_ref, o0, o1, o2, o3, held):
+    z, m = place_ref[0], place_ref[1]
+    for k, ref in enumerate((own_ref, r1_ref, r2_ref, r3_ref)):
+        held[k] = ref[...].astype(F32)
+    width = NM * held.shape[2]
+    mean = sum(jnp.sum(held[k], axis=1, keepdims=True) for k in range(NM)) / width
+    var = sum(jnp.sum((held[k] - mean) ** 2, axis=1, keepdims=True) for k in range(NM)) / width
+    rstd = lax.rsqrt(var + 1e-05)
+    last = lax.broadcasted_iota(jnp.int32, held.shape[1:], 0) == BLK - 1
+    for k, out in enumerate((o0, o1, o2, o3)):
+        block = jnp.bitwise_xor(z, k)
+        x = held[jnp.bitwise_xor(block, m)]
+        y = (x - mean) * rstd * gain_ref[block] + shift_ref[block]
+        out[...] = jnp.where(last, table_ref[...], y).astype(BF)
+
+
+def norm_rows(place, blocks, gain, shift, table):
+    cols = blocks[0].shape[1]
+    out = jax.ShapeDtypeStruct((BLK, cols), BF)
+    vmem = pl.BlockSpec(memory_space=pltpu.VMEM)
+    return pl.pallas_call(
+        norm_kernel,
+        out_shape=[out] * 4,
+        in_specs=[pl.BlockSpec(memory_space=pltpu.SMEM)] + [vmem] * 7,
+        out_specs=[vmem] * 4,
+        scratch_shapes=[pltpu.VMEM((NM, BLK, cols), F32)],
+        compiler_params=pltpu.CompilerParams(vmem_limit_bytes=24 * MIB),
+        name="norm_rows",
+    )(place, *blocks, gain, shift, table)
+
+
+def prompt_kernel(q_ref, ka_ref, kb_ref, va_ref, vb_ref, cr_ref, cc_ref, o_ref):
+    rows = cr_ref[...]
+    cols = cc_ref[...]
+    allowed = ((rows >> 5) == (cols >> 5)) & (cols <= rows)
+    keys = jnp.concatenate([ka_ref[...], kb_ref[...]], axis=0)
+    values = jnp.concatenate([va_ref[...], vb_ref[...]], axis=0)
+    for h in range(q_ref.shape[1] // HEAD_DIM):
+        at = slice(h * HEAD_DIM, (h + 1) * HEAD_DIM)
+        s = lax.dot_general(q_ref[:, at], keys[:, at], (((1,), (1,)), ((), ())), preferred_element_type=F32)
+        s = jnp.where(allowed, s * HEAD_DIM**-0.5, -1e30)
+        top = jnp.max(s, axis=1, keepdims=True)
+        w = jnp.where(allowed, jnp.exp(s - top), 0.0)
+        w = (w / jnp.sum(w, axis=1, keepdims=True)).astype(BF)
+        o_ref[:, at] = jnp.dot(w, values[:, at], preferred_element_type=F32).astype(BF)
+
+
+def prompt_attention(q, ka, kb, va, vb, code_rows, code_cols):
+    vmem = pl.BlockSpec(memory_space=pltpu.VMEM)
+    return pl.pallas_call(
+        prompt_kernel,
+        out_shape=jax.ShapeDtypeStruct(q.shape, BF),
+        in_specs=[vmem] * 7,
+        out_specs=vmem,
+        compiler_params=pltpu.CompilerParams(vmem_limit_bytes=32 * MIB),
+        name="prompt_attention",
+    )(q, ka, kb, va, vb, code_rows, code_cols)
+
+
+def decode_kernel(len_ref, q_ref, k_ref, v_ref, c_ref, o_ref, qbd, top, total, acc):
+    d, t = pl.program_id(0), pl.program_id(1)
+    span = c_ref.shape[1]
+    live = len_ref[d]
+    heads, feats = qbd.shape
+    diag = lax.broadcasted_iota(jnp.int32, (heads, feats), 1) // HEAD_DIM == lax.broadcasted_iota(
+        jnp.int32, (heads, feats), 0
+    )
+
+    @pl.when(t == 0)
+    def _():
+        q = jnp.where(diag, q_ref[0].astype(F32), 0.0)
+        qbd[...] = q.astype(BF)
+        own = jnp.sum(q * k_ref[0].astype(F32), axis=1, keepdims=True) * HEAD_DIM**-0.5
+        top[...] = jnp.broadcast_to(own, top.shape)
+        total[...] = jnp.ones_like(total)
+        acc[...] = jnp.broadcast_to(v_ref[0].astype(F32), acc.shape)
+
+    @pl.when(t * span < live)
+    def _():
+        x = c_ref[0].reshape(2 * span, feats)
+        s = lax.dot_general(qbd[...], x, (((1,), (1,)), ((), ())), preferred_element_type=F32)
+        column = lax.broadcasted_iota(jnp.int32, s.shape, 1)
+        valid = (column % 2 == 0) & (t * span + column // 2 < live)
+        s = jnp.where(valid, s * HEAD_DIM**-0.5, -1e30)
+        before = top[:, :1]
+        now = jnp.maximum(before, jnp.max(s, axis=1, keepdims=True))
+        fade = jnp.exp(before - now)
+        w = jnp.where(valid, jnp.exp(s - now), 0.0)
+        total[...] = total[...] * fade + jnp.sum(w, axis=1, keepdims=True)
+        top[...] = jnp.broadcast_to(now, top.shape)
+        w = pltpu.roll(w, 1, 1).astype(BF)
+        acc[...] = acc[...] * fade + jnp.dot(w, x, preferred_element_type=F32)
+
+    @pl.when(t == pl.num_programs(1) - 1)
+    def _():
+        o = acc[...] / total[:, :1]
+        o_ref[0] = jnp.sum(jnp.where(diag, o, 0.0), axis=0, keepdims=True).astype(BF)
+
+
+def decode_attention(lengths, q, k, v, cache, span=256):
+    count, positions, _, feats = cache.shape
+    steps = positions // span
+    row = pl.BlockSpec((1, 1, feats), lambda d, t, n: (d, 0, 0))
+    heads = 16
+    return pl.pallas_call(
+        decode_kernel,
+        grid_spec=pltpu.PrefetchScalarGridSpec(
+            num_scalar_prefetch=1,
+            grid=(count, steps),
+            in_specs=[row, row, row]
+            + [
+                pl.BlockSpec(
+                    (1, span, 2, feats),
+                    lambda d, t, n: (d, jnp.minimum(t, (n[d] - 1) // span), 0, 0),
+                )
+            ],
+            out_specs=row,
+            scratch_shapes=[
+                pltpu.VMEM((heads, feats), BF),
+                pltpu.VMEM((heads, 128), F32),
+                pltpu.VMEM((heads, 128), F32),
+                pltpu.VMEM((heads, feats), F32),
+            ],
+        ),
+        out_shape=jax.ShapeDtypeStruct((count, 1, feats), BF),
+        compiler_params=pltpu.CompilerParams(vmem_limit_bytes=32 * MIB),
+        cost_estimate=pl.CostEstimate(
+            flops=4 * 256 * count * positions * feats, bytes_accessed=4 * count * positions * feats, transcendentals=0
+        ),
+        name="decode_attention",
+    )(lengths, q, k, v, cache)
+
+
+def out_kernel(place_ref, *refs):
+    own, other, dec_ref, w_ref, pos_ref, o_ref, mixed = refs[:4], refs[4:8], *refs[8:]
+    z = place_ref[0]
+    half, width = own[0].shape
+    for base, parts in ((0, own), (half, other)):
+        total = None
+        for s in range(NZ):
+            block = jnp.bitwise_and(z - s, NZ - 1)
+            w = w_ref[pl.ds(pl.multiple_of(block * width, width), width), :]
+            term = jnp.dot(parts[s][...], w, preferred_element_type=F32)
+            total = term if total is None else total + term
+        mixed[pl.ds(base, half), :] = total.astype(BF)
+    mixed[pl.ds(2 * half, dec_ref.shape[0]), :] = jnp.dot(
+        dec_ref[...], w_ref[...], preferred_element_type=F32
+    ).astype(BF)
+    pos = pos_ref[...]
+    pick = (pos == lax.broadcasted_iota(jnp.int32, (pos.shape[0], mixed.shape[0]), 1)).astype(BF)
+    o_ref[...] = jnp.dot(pick, mixed[...], preferred_element_type=F32).astype(BF)
+
+
+def out_project(place, own, other, dec, weight, pos):
+    vmem = pl.BlockSpec(memory_space=pltpu.VMEM)
+    rows = 2 * own[0].shape[0] + dec.shape[0]
+    return pl.pallas_call(
+        out_kernel,
+        out_shape=jax.ShapeDtypeStruct((pos.shape[0], weight.shape[1]), BF),
+        in_specs=[pl.BlockSpec(memory_space=pltpu.SMEM)] + [vmem] * 11,
+        out_specs=vmem,
+        scratch_shapes=[pltpu.VMEM((rows, weight.shape[1]), BF)],
+        compiler_params=pltpu.CompilerParams(vmem_limit_bytes=40 * MIB),
+        name="out_project",
+    )(place, *own, *other, dec, weight, pos)
+
+
+def quarter_of(index, size):
+    return sum((index >= j * size).astype(jnp.int32) for j in range(1, NM))
+
+
+def packed_device(
+    tokens,
+    layernorm_scale,
+    layernorm_bias,
+    query_key_value_weight,
+    query_key_value_bias,
+    adapter_down_weight,
+    adapter_up_weight,
+    adapter_index_table,
+    prompt_length_list,
+    cache,
+    cache_length_list,
+    output_weight,
+    output_bias,
+):
+    i32 = jnp.int32
+    r = lax.axis_index("req").astype(i32)
+    m = lax.axis_index("mp").astype(i32)
+    z, c = r >> 1, r & 1
+    place = jnp.stack([z, m])
+    rows_dev, cols = tokens.shape
+    prompt_rows = SLOTS * PLEN
+    feats = query_key_value_weight.shape[2]
+    depth = query_key_value_weight.shape[1]
+    per_z = feats // NZ
+    own_adapters = adapter_down_weight.shape[0]
+
+    down = jnp.transpose(adapter_down_weight, (0, 2, 1)).reshape(own_adapters * 2 * ADAPTER_RANK, cols)
+    down_chip = jnp.concatenate([down, swap_req(down, 1)], axis=0)
+
+    with jax.named_scope("deal"):
+        lens = prompt_length_list
+        starts = jnp.concatenate([jnp.zeros((1,), i32), jnp.cumsum(lens)[:-1].astype(i32)])
+        size = (jnp.sum(lens) + 3) >> 2
+        at = jnp.arange(PLEN, dtype=i32)[None, :]
+        index = starts[:, None] + at
+        quarter = quarter_of(index, size)
+        target = jnp.where(at < lens[:, None], quarter * BLK + index - quarter * size, -1).reshape(-1)
+        target = jnp.concatenate([target, z * BLK + QROWS + jnp.arange(DEC, dtype=i32)])
+        pick = (jnp.arange(NM * BLK, dtype=i32)[:, None] == target[None, :]).astype(BF)
+        dealt = jnp.dot(pick, tokens, preferred_element_type=F32).astype(BF).reshape(NM, BLK, cols)
+
+        def block(k):
+            return lax.dynamic_index_in_dim(dealt, m ^ k, 0, keepdims=False)
+
+        blocks = [block(0)] + [swap_mp(block(k), k) for k in range(1, NM)]
+    with jax.named_scope("norm_rows"):
+        table = jnp.concatenate([lens, adapter_index_table[0]]).astype(F32)
+        table = jnp.pad(table, (0, depth - table.shape[0]))
+        table = jnp.tile(table, 2)[None, :]
+        gain = layernorm_scale.reshape(NM, 1, cols)
+        shift = layernorm_bias.reshape(NM, 1, cols)
+        normed = norm_rows(place, blocks, gain, shift, table)
+    with jax.named_scope("spread_z"):
+        rows = jnp.concatenate([normed[0]] + [swap_req(normed[k], 2 * k) for k in range(1, NZ)], axis=0)
+        mine = lax.dynamic_slice_in_dim(rows, c * depth, depth, 1)
+        theirs = swap_req(lax.dynamic_slice_in_dim(rows, (1 - c) * depth, depth, 1), 1)
+        both = jnp.concatenate([mine, theirs], axis=0)
+
+    with jax.named_scope("tables"):
+        tables = both.reshape(2 * NZ, BLK, depth)[:, BLK - 1, : SLOTS + SLOTS + DEC].astype(i32)
+        order = jnp.arange(2 * NZ, dtype=i32)
+        source = ((z ^ (order & 3)) << 1) + (c ^ (order >> 2))
+        tables = jnp.sum(
+            jnp.where(source[None, :, None] == order[:, None, None], tables[None], 0), axis=1
+        )
+        all_lens, all_adapters = tables[:, :SLOTS], tables[:, SLOTS:]
+        live_count = jnp.sum(all_lens, axis=1)
+        sizes = (live_count + 3) >> 2
+        offsets = jnp.sum(jnp.where(order[None, :] < order[:, None], sizes[None, :], 0), axis=1)
+
+        def by_source(values, src):
+            return jnp.sum(jnp.where(src[:, None] == order[None, :], values[None, :], 0), axis=1)
+
+    with jax.named_scope("pack"):
+        src_size = by_source(sizes, source)
+        src_live = by_source(live_count, source)
+        src_off = by_source(offsets, source)
+        t = jnp.arange(BLK, dtype=i32)[None, :]
+        have = jnp.clip(src_live - m * src_size, 0, src_size)
+        prompt_to = jnp.where(t < have[:, None], src_off[:, None] + t, -1)
+        decode_to = jnp.where(
+            (t >= QROWS) & (t < QROWS + DEC) & ((source >> 1) == m)[:, None],
+            CHUNK + (source & 1)[:, None] * DEC + t - QROWS,
+            -1,
+        )
+        to = jnp.where(t < QROWS, prompt_to, decode_to).reshape(-1)
+        pick = (jnp.arange(CHUNK + DCH, dtype=i32)[:, None] == to[None, :]).astype(BF)
+        chunk = jnp.dot(pick, both, preferred_element_type=F32).astype(BF)
+    with jax.named_scope("gather_chunks"):
+        chunks = [chunk] + [swap_mp(chunk, k) for k in range(1, NM)]
+        low = jnp.concatenate([chunks[0][:CHUNK], chunks[1][:CHUNK]], axis=0)
+        high = jnp.concatenate([chunks[2][:CHUNK], chunks[3][:CHUNK]], axis=0)
+        x_own = jnp.where(c == 0, low, high)
+        x_other = jnp.where(c == 0, high, low)
+        dec_one = 2 * DEC
+        x_dec = jnp.concatenate([v[CHUNK : CHUNK + dec_one] for v in chunks], axis=0)
+
+    with jax.named_scope("places"):
+        all_starts = jnp.concatenate(
+            [jnp.zeros((2 * NZ, 1), i32), all_lens[:, :1], all_lens[:, :1] + all_lens[:, 1:2]], axis=1
+        )
+        index = (all_starts[:, :, None] + at[None]).reshape(2 * NZ, prompt_rows)
+        alive = (at[None] < all_lens[:, :, None]).reshape(2 * NZ, prompt_rows)
+        quarter = quarter_of(index, sizes[:, None])
+        spot = (quarter ^ m) * CHUNK + offsets[:, None] + index - quarter * sizes[:, None]
+        spot = jnp.where(alive, spot, -1)
+        spot = jnp.where(alive, ((spot >> 8) ^ c) * 2 * CHUNK + (spot & (2 * CHUNK - 1)), -1)
+        dec_ids = jnp.arange(DEC, dtype=i32)[None, :]
+        dec_spot = 4 * CHUNK + ((order >> 1) ^ m)[:, None] * dec_one + (order & 1)[:, None] * DEC + dec_ids
+        home_spot = jnp.concatenate([spot, dec_spot], axis=1)
+        home_adapter = jnp.concatenate(
+            [jnp.repeat(all_adapters[:, :SLOTS], PLEN, axis=1), all_adapters[:, SLOTS:]], axis=1
+        )
+        packed = NM * (CHUNK + dec_one)
+        flat_spot = home_spot.reshape(-1)
+        hit = jnp.arange(packed, dtype=i32)[:, None] == flat_spot[None, :]
+        row_adapter = jnp.sum(jnp.where(hit, home_adapter.reshape(-1)[None, :] + 1, 0), axis=1) - 1
+        prompt_id = order[:, None] * SLOTS + jnp.arange(rows_dev, dtype=i32)[None, :] // PLEN
+        code = prompt_id * PLEN + jnp.arange(rows_dev, dtype=i32)[None, :] % PLEN
+        row_code = jnp.sum(jnp.where(hit, code.reshape(-1)[None, :] + 1, 0), axis=1) - 1
+        unused = jnp.arange(packed, dtype=i32) * PLEN + (1 << 16)
+        row_code = jnp.where(row_code < 0, unused, row_code)[: 4 * CHUNK]
+
+    with jax.named_scope("home_norm"):
+        home = tokens.astype(F32)
+        mean = jnp.mean(home, axis=1)
+        spread = jnp.sum((home - mean[:, None]) ** 2, axis=1)
+        stats = jnp.stack([mean, spread])
+        stats = jnp.stack([stats] + [swap_mp(stats, k) for k in range(1, NM)])
+        mean_all = jnp.mean(stats[:, 0], axis=0)
+        var = (jnp.sum(stats[:, 1], axis=0) + cols * jnp.sum((stats[:, 0] - mean_all) ** 2, axis=0)) / (NM * cols)
+        my_gain = lax.dynamic_slice_in_dim(layernorm_scale, m * cols, cols, 0)
+        my_shift = lax.dynamic_slice_in_dim(layernorm_bias, m * cols, cols, 0)
+        home = (home - mean_all[:, None]) * lax.rsqrt(var + 1e-05)[:, None]
+        home = (home * my_gain + my_shift).astype(BF)
+    with jax.named_scope("low_rank"):
+        pieces = gather_z(home)
+        piece_source = [(((z - s) & 3) << 1) + c for s in range(NZ)]
+        chip_ids = jnp.concatenate(
+            [r * own_adapters + jnp.arange(own_adapters, dtype=i32), (r ^ 1) * own_adapters + jnp.arange(own_adapters, dtype=i32)]
+        )
+        rank_parts = []
+        for s in range(NZ):
+            y = lax.dot_general(down_chip, pieces[s], (((1,), (1,)), ((), ())), preferred_element_type=F32)
+            y = y.reshape(2 * own_adapters, 2 * ADAPTER_RANK, rows_dev)
+            adapters = jnp.sum(jnp.where((order == piece_source[s])[:, None], home_adapter, 0), axis=0)
+            rank_parts.append(jnp.sum(jnp.where((chip_ids[:, None] == adapters[None, :])[:, None, :], y, 0.0), axis=0))
+        part = jnp.concatenate(rank_parts, axis=1)
+        low_rank = part + sum(swap_mp(part, k) for k in range(1, NM))
+        low_rank = low_rank.astype(BF)
+        low_rank = jnp.concatenate([low_rank, swap_req(low_rank, 1)], axis=1)
+        src = jnp.stack(piece_source + [s ^ 1 for s in piece_source])
+        spots = jnp.sum(jnp.where((src[:, None] == order[None, :])[:, :, None], home_spot[None], 0), axis=1).reshape(-1)
+        hit2 = (jnp.arange(packed, dtype=i32)[:, None] == spots[None, :]).astype(BF)
+        packed_rank = lax.dot_general(
+            hit2, low_rank, (((1,), (1,)), ((), ())), preferred_element_type=F32
+        )
+        mine_ids = r * own_adapters + jnp.arange(own_adapters, dtype=i32)
+        owned = row_adapter[:, None] == mine_ids[None, :]
+
+        def expand(v):
+            return jnp.where(owned[:, :, None], v[:, None, :], 0.0).astype(BF).reshape(packed, own_adapters * ADAPTER_RANK)
+
+        expanded = [expand(packed_rank[:, :ADAPTER_RANK]), None, expand(packed_rank[:, ADAPTER_RANK:])]
+        ups = [adapter_up_weight[:, 0].reshape(-1, feats), None, adapter_up_weight[:, 1].reshape(-1, feats)]
+
+    half = 2 * CHUNK
+
+    def partial_sums(x, part, rows_at):
+        y = jnp.dot(x, query_key_value_weight[part], preferred_element_type=F32)
+        if expanded[part] is not None:
+            y = y + jnp.dot(expanded[part][rows_at], ups[part], preferred_element_type=F32)
+        return y
+
+    def reduce_z(total):
+        def piece(i):
+            return lax.dynamic_slice_in_dim(total, jnp.clip(i, 0, NZ - 1) * per_z, per_z, 1)
+
+        def add(own, got, when=None):
+            got = got.astype(F32)
+            return own + (got if when is None else jnp.where(when, got, 0.0))
+
+        first = move_z(piece(jnp.where(z == 0, 3, 0)).astype(BF), [(0, 1), (3, 2)])
+        right = move_z(add(piece(2 + z), first, z == 1).astype(BF), [(0, 1), (1, 2)])
+        left = move_z(add(piece(z - 2), first, z == 2).astype(BF), [(3, 2), (2, 1)])
+        right = move_z(add(piece(1 + z), right).astype(BF), [(0, 1), (1, 2), (2, 3)])
+        left = move_z(add(piece(z - 1), left).astype(BF), [(3, 2), (2, 1), (1, 0)])
+        return add(add(piece(z), right), left)
+
+    def finish(total, part):
+        bias = lax.dynamic_slice_in_dim(query_key_value_bias[part], z * per_z, per_z, 0)
+        return (total + bias[None]).astype(BF)
+
+    def project(part):
+        sent = swap_req(partial_sums(x_other, part, slice(half, 2 * half)).astype(BF), 1)
+        total = partial_sums(x_own, part, slice(0, half)) + sent.astype(F32)
+        return finish(reduce_z(total), part)
+
+    with jax.named_scope("decode_rows"):
+        dec = jnp.stack([partial_sums(x_dec, part, slice(4 * CHUNK, None)) for part in range(3)], axis=1)
+        dec = dec.reshape(NZ, 2, DEC, 3, feats)
+        dec = jnp.stack([lax.dynamic_index_in_dim(dec, zz ^ m, 0, keepdims=False) for zz in range(NZ)])
+        dec = lax.dynamic_index_in_dim(dec, c, 1, keepdims=False) + swap_req(
+            lax.dynamic_index_in_dim(dec, 1 - c, 1, keepdims=False), 1
+        )
+        hi = z >> 1
+        dec = lax.dynamic_slice_in_dim(dec, 2 * hi, 2, 0) + swap_req(
+            lax.dynamic_slice_in_dim(dec, 2 * (1 - hi), 2, 0), 4
+        )
+        lo = z & 1
+        dec = lax.dynamic_index_in_dim(dec, lo, 0, keepdims=False) + swap_req(
+            lax.dynamic_index_in_dim(dec, 1 - lo, 0, keepdims=False), 2
+        )
+        dec = (dec + query_key_value_bias[None]).astype(BF)
+    with jax.named_scope("decode_attention"):
+        dec_out = decode_attention(cache_length_list, dec[:, 0:1], dec[:, 1:2], dec[:, 2:3], cache)
+        dec_all = dec_out.reshape(DEC, feats)
+        for bits in (1, 2, 4):
+            dec_all = jnp.concatenate([dec_all, swap_req(dec_all, bits)], axis=0)
+
+    with jax.named_scope("keys"):
+        keys = project(1)
+    with jax.named_scope("values"):
+        values = project(2)
+    with jax.named_scope("queries"):
+        queries = project(0)
+    with jax.named_scope("prompt_attention"):
+        attended = prompt_attention(
+            queries,
+            keys,
+            swap_req(keys, 1),
+            values,
+            swap_req(values, 1),
+            row_code[:half, None],
+            row_code[None, :],
+        )
+    with jax.named_scope("gather_attended"):
+        own = gather_z(attended)
+        other = [swap_req(v, 1) for v in own]
+    with jax.named_scope("out_project"):
+        where_to = home_spot[:, :prompt_rows].reshape(NZ, 2, 2, prompt_rows // 2)
+        where_to = where_to.transpose(1, 2, 0, 3).reshape(NM, NZ * prompt_rows // 2)
+        dec_to = 4 * CHUNK + (order[:, None] ^ r) * DEC + dec_ids
+        dec_to = dec_to.reshape(NZ, 2, DEC).transpose(1, 2, 0).reshape(NM, NZ)
+        tail = jnp.full((NM, 4), -1, i32)
+        pos = jnp.concatenate([where_to, dec_to, tail], axis=1)
+        quarter_rows = pos.shape[1]
+        mixed = out_project(place, own, other, dec_all, output_weight, pos.reshape(-1, 1))
+        mixed = mixed.reshape(NM, quarter_rows, -1)
+    with jax.named_scope("sum_mp"):
+
+        def share(k):
+            return lax.dynamic_index_in_dim(mixed, m ^ k, 0, keepdims=False)
+
+        total = share(0).astype(F32)
+        for k in range(1, NM):
+            total = total + swap_mp(share(k), k).astype(F32)
+        total = total.astype(BF)
+    with jax.named_scope("return_z"):
+        n = prompt_rows // 2
+        grid = jnp.concatenate(
+            [
+                total[: NZ * n].reshape(NZ, n, -1),
+                jnp.pad(total[NZ * n : NZ * n + NZ].reshape(NZ, 1, -1), ((0, 0), (0, 7), (0, 0))),
+            ],
+            axis=1,
+        )
+
+        def for_z(k):
+            return lax.dynamic_index_in_dim(grid, z ^ k, 0, keepdims=False)
+
+        got = jnp.stack([for_z(0)] + [swap_req(for_z(k), 2 * k) for k in range(1, NZ)])
+    with jax.named_scope("return_plane"):
+        corner = 2 * c + (m & 1)
+        parts = []
+        for k in range(NM):
+            hops = []
+            for zz in range(NZ):
+                for cc in range(2):
+                    for mm in range(NM):
+                        h, l = mm >> 1, mm & 1
+                        hops.append(((zz * 2 + cc) * NM + mm, (zz * 2 + h) * NM + ((2 * cc + l) ^ k)))
+            piece = lax.dynamic_index_in_dim(got, corner ^ k ^ z, 0, keepdims=False)
+            parts.append(lax.ppermute(piece, ("req", "mp"), hops))
+        parts = jnp.stack(parts)
+
+        def corner_part(cc, l):
+            return lax.dynamic_index_in_dim(parts, (2 * cc + l) ^ m, 0, keepdims=False)
+
+        columns = []
+        for cc in range(2):
+            a, b = corner_part(cc, 0), corner_part(cc, 1)
+            columns.append(jnp.concatenate([a[:n], b[:n], a[n : n + 1], b[n : n + 1]], axis=0))
+        summed = jnp.concatenate(columns, axis=1).astype(F32)
+        return (tokens.astype(F32) + summed + output_bias[None]).astype(BF)
 
 
 def layer_norm(row_data, gain_vec, shift_vec):
@@ -169,6 +676,7 @@
         P("mp", "req"),
         P("mp"),
     )
+    quick = mesh.shape["req"] == 2 * NZ and mesh.shape["mp"] == NM
     return jax.shard_map(
-        on_device, mesh=mesh, in_specs=placed, out_specs=P("req", "mp"), check_vma=False
-    )
+        packed_device if quick else on_device, mesh=mesh, in_specs=placed, out_specs=P("req", "mp"), check_vma=False
+    )

time: 812 us -> 275 us (0.34)
  waiting for transfers between devices: 459 us -> 86.6 us
  local copies, waits for them, and re-layouts: 188 us -> 12.6 us
  starting transfers between devices: 12.7 us -> 104 us
  blocking collectives: 58.5 us -> 0 us
  Pallas kernels: 0 us -> 21.8 us
  matrix products: 46 us -> 31.2 us
  between operations: 14.6 us -> 2.46 us
  other arithmetic: 24.9 us -> 13.7 us
    all_gather x2 -> x0, waiting for transfers between devices: 191 us -> none  [the longest x1 156 us: on_device(): lax.all_gather(output_weight, 'req', axis=1, tiled=True)]
    unnamed x5 -> x0, waiting for transfers between devices: 135 us -> none
    unnamed x39 -> x65, local copies, waits for them, and re-layouts: 121 us -> 2.15 us
    ppermute x0 -> x70, starting transfers between devices: none -> 104 us  [the longest x27 57.9 us: move_z(): lax.ppermute(x, 'req', [(a * 2 + c, b * 2 + c) for a, b in hops for c in...]
    all_to_all x3 -> x0, waiting for transfers between devices: 103 us -> none  [the longest x1 99.5 us: on_device(): lax.all_to_all(outgoing, 'req', split_axis=0, concat_axis=0, tiled=True)]
    ppermute x0 -> x70, waiting for transfers between devices: none -> 86.6 us  [the longest x27 32.3 us: move_z(): lax.ppermute(x, 'req', [(a * 2 + c, b * 2 + c) for a, b in hops for c in...]
    slice x5 -> x24, local copies, waits for them, and re-layouts: 53.4 us -> 1.68 us  [the longest x4 1.28 us: partial_sums(): expanded[part][rows_at]]
    all_to_all x1 -> x0, blocking collectives: 40.6 us -> none  [on_device(): lax.all_to_all(normed, 'req', split_axis=1, concat_axis=0, tiled=True)]
  transfers between devices with their start and end apart: 7 -> 70, of which waited for: 6 -> 27; matrix products, arithmetic and copies ran while one was open for 28% -> 17% of each run, Pallas kernels for 0% -> 6%
where the time goes in v1:
time: 275 us; the launch traced here: 273 us
  starting transfers between devices  104 us (38%)
  waiting for transfers between devices  86.6 us (31%)
  matrix products  31.2 us (11%)
  Pallas kernels  21.8 us (8%)
  other arithmetic  13.7 us (5%)
  local copies, waits for them, and re-layouts  12.6 us (5%)
    ppermute x27, starting transfers between devices, move_z(): lax.ppermute(x, 'req', [(a * 2 + c, b * 2 + c) for a, b in hops for c in...  57.9 us
    ppermute x27, waiting for transfers between devices, move_z(): lax.ppermute(x, 'req', [(a * 2 + c, b * 2 + c) for a, b in hops for c in...  32.3 us
    ppermute x24, waiting for transfers between devices, swap_req(): return lax.ppermute(x, 'req', [(i, i ^ bits) for i in range(2 * NZ)])  26.1 us
    ppermute x15, waiting for transfers between devices, swap_mp(): return lax.ppermute(x, 'mp', [(i, i ^ bits) for i in range(NM)])  23.1 us
    ppermute x15, starting transfers between devices, swap_mp(): return lax.ppermute(x, 'mp', [(i, i ^ bits) for i in range(NM)])  21 us
    dot_general x9, matrix products, partial_sums(): y = jnp.dot(x, query_key_value_weight[part], preferred_element_type=F32)  19.8 us
    ppermute x24, starting transfers between devices, swap_req(): return lax.ppermute(x, 'req', [(i, i ^ bits) for i in range(2 * NZ)])  19.6 us
    pallas_call x1, Pallas kernels, decode_attention(): pl.pallas_call(decode_kernel, grid_spec=pltpu.PrefetchScalarGridSpec(num_...  14.9 us
  transfers between devices with their start and end apart: 70, of which 27 were waited for; matrix products, arithmetic and copies ran while one was open for 17% of the time, Pallas kernels for 6%

profile of v1, /device:TPU:0, one launch (start us, length us, event | category | flops | bytes accessed | tf_op | source)
XLA Modules:
  0.0 272.5 jit_solution(5071628020401421221)
XLA Ops:
  2.5 3.0 %collective-permute-start.11 = (f32[2,98]{1,0:T(2,128)S(1)}, f32[2,98]{1,0:T(2,128)S(1)}, u32[]{:S(2)}, u32[]{:S(2)}) collective-permute-start(f32[2,98]{1,0:T(2,128)S(1)} %get-tuple-element.100), channel_id=1, source_target_pairs={{0,1},{1,0},{2,3},{3,2},{4,5},{5,4},{6,7},{7,6},{8,9},{9,8},{10,11... | collective-permute-start | bytes 2360 | tf_op jit(solution)/shard_map/home_norm/ppermute | solution.py:29
  12.5 2.0 collective-permute-start
  18.7 5.3 %collective-permute-start.14 = (bf16[98,1792]{1,0:T(8,128)(2,1)S(1)}, bf16[98,1792]{1,0:T(8,128)(2,1)}, u32[]{:S(2)}, u32[]{:S(2)}) collective-permute-start(bf16[98,1792]{1,0:T(8,128)(2,1)S(1)} %fusion.50), channel_id=1, source_target_pairs={{0,8},{4,12},{8,16},{12,20},{16,24},{20,28},{1,9},{5,13},{9,17},{1... | collective-permute-start | bytes 1053704 | tf_op jit(solution)/shard_map/low_rank/ppermute | solution.py:33
  27.9 7.6 %collective-permute-done.3 = bf16[32,1792]{1,0:T(8,128)(2,1)S(1)} collective-permute-done((bf16[32,1792]{1,0:T(8,128)(2,1)S(1)}, bf16[32,1792]{1,0:T(8,128)(2,1)S(1)}, u32[]{:S(2)}, u32[]{:S(2)}) %collective-permute-start.3) | collective-permute-done | bytes 114720 | tf_op jit(solution)/shard_map/spread_z/ppermute | solution.py:25
  35.5 5.7 %collective-permute-start.5 = (bf16[32,1792]{1,0:T(8,128)(2,1)S(1)}, bf16[32,1792]{1,0:T(8,128)(2,1)S(1)}, u32[]{:S(2)}, u32[]{:S(2)}) collective-permute-start(bf16[32,1792]{1,0:T(8,128)(2,1)S(1)} %get-tuple-element.12), channel_id=1, source_target_pairs={{0,24},{4,28},{8,16},{12,20},{16,8},{20,12},{24,0},{28,4},{1,25},{... | collective-permute-start | bytes 344072 | tf_op jit(solution)/shard_map/spread_z/ppermute | solution.py:25
  41.2 2.8 %collective-permute-done.5 = bf16[32,1792]{1,0:T(8,128)(2,1)S(1)} collective-permute-done((bf16[32,1792]{1,0:T(8,128)(2,1)S(1)}, bf16[32,1792]{1,0:T(8,128)(2,1)S(1)}, u32[]{:S(2)}, u32[]{:S(2)}) %collective-permute-start.5) | collective-permute-done | bytes 114720 | tf_op jit(solution)/shard_map/spread_z/ppermute | solution.py:25
  57.9 3.4 %collective-permute-done.16 = bf16[98,1792]{1,0:T(8,128)(2,1)} collective-permute-done((bf16[98,1792]{1,0:T(8,128)(2,1)S(1)}, bf16[98,1792]{1,0:T(8,128)(2,1)}, u32[]{:S(2)}, u32[]{:S(2)}) %collective-permute-start.16) | collective-permute-done | bytes 351264 | tf_op jit(solution)/shard_map/low_rank/ppermute | solution.py:33
  61.3 2.6 collective-permute-start.9
  67.5 2.5 collective-permute-done.9
  70.3 2.9 %fusion.21 = bf16[256,1536]{1,0:T(8,128)(2,1)S(1)} fusion(bf16[256,896]{1,0:T(8,128)(2,1)S(1)} %get-tuple-element.43, bf16[3,896,1536]{2,1,0:T(8,128)(2,1)} %param.16), kind=kOutput, calls=%fused_computation.22 | convolution fusion | flops 705036288 | bytes 3997696 | tf_op jit(solution)/shard_map/keys/dot_general | solution.py:389
  73.2 1.8 fusion.98
  75.1 2.0 fusion.71
  77.4 1.9 fusion.73
  79.3 1.8 fusion.69
  87.7 1.9 collective-permute-done.22
  89.7 2.3 fusion.30
  94.6 2.3 fusion.24
  97.2 2.3 fusion.27
  101.0 3.0 %fusion.18 = bf16[256,1536]{1,0:T(8,128)(2,1)S(1)} fusion(f32[256,1536]{1,0:T(8,128)S(1)} %fusion.110, bf16[256,896]{1,0:T(8,128)(2,1)S(1)} %copy-done.7, bf16[3,896,1536]{2,1,0:T(8,128)(2,1)} %param.16), kind=kOutput, calls=%fused_computation.21 | convolution fusion | flops 705429504 | bytes 5570560 | tf_op jit(solution)/shard_map/values/dot_general | solution.py:389
  104.8 3.0 %fusion.15 = bf16[256,1536]{1,0:T(8,128)(2,1)S(1)} fusion(f32[256,1536]{1,0:T(8,128)S(1)} %fusion.108, bf16[256,896]{1,0:T(8,128)(2,1)S(1)} %copy-done.7, bf16[3,896,1536]{2,1,0:T(8,128)(2,1)} %param.16), kind=kOutput, calls=%fused_computation.20 | convolution fusion | flops 705429504 | bytes 5570560 | tf_op jit(solution)/shard_map/queries/dot_general | solution.py:389
  109.5 5.2 %collective-permute-done.55 = f32[2,2,3,1536]{3,0,2,1:T(2,128)S(1)} collective-permute-done((f32[2,2,3,1536]{3,0,2,1:T(2,128)S(1)}, f32[2,2,3,1536]{3,0,2,1:T(2,128)S(1)}, u32[]{:S(2)}, u32[]{:S(2)}) %collective-permute-start.55) | collective-permute-done | bytes 73760 | tf_op jit(solution)/shard_map/decode_rows/ppermute | solution.py:25
  115.5 3.6 %collective-permute-done.56 = f32[2,3,1536]{2,1,0:T(4,128)S(1)} collective-permute-done((f32[2,3,1536]{2,1,0:T(4,128)S(1)}, f32[2,3,1536]{2,1,0:T(4,128)S(1)}, u32[]{:S(2)}, u32[]{:S(2)}) %collective-permute-start.56) | collective-permute-done | bytes 36896 | tf_op jit(solution)/shard_map/decode_rows/ppermute | solution.py:25
  119.2 2.1 convolution_add_fusion.2
  121.4 2.0 collective-permute-start.31
  123.4 14.9 %decode_attention.1 = bf16[2,1,1536]{2,1,0:T(2,128)(2,1)S(1)} custom-call(s32[2]{0:T(128)S(1)} %copy-done.3, bf16[2,1,1536]{2,1,0:T(2,128)(2,1)S(1)} %get-tuple-element.85.q_ref, bf16[2,1,1536]{2,1,0:T(2,128)(2,1)S(1)} %get-tuple-element.84.k_ref, bf16[2,1,1536]{2,1,0:T(2,128)(2,1)S(1)} %get-tuple-element.83.v_ref, bf16[2,2048,2,1536]{3,2,1,0:T(2,128)(2,1)} %c_ref.1), custom_call_target="tpu_custom_call" | custom-call | flops 6442450944 | bytes 25165824 | tf_op jit(solution)/shard_map/decode_attention/decode_attention/pallas_call | solution.py:152
  140.6 4.4 %collective-permute-done.32 = bf16[256,384]{1,0:T(8,128)(2,1)S(1)} collective-permute-done((bf16[256,384]{1,0:T(8,128)(2,1)S(1)}, bf16[256,384]{1,0:T(8,128)(2,1)S(1)}, u32[]{:S(2)}, u32[]{:S(2)}) %collective-permute-start.32) | collective-permute-done | bytes 196640 | tf_op jit(solution)/shard_map/keys/ppermute | solution.py:33
  145.1 4.4 %collective-permute-start.33 = (bf16[256,384]{1,0:T(8,128)(2,1)S(1)}, bf16[256,384]{1,0:T(8,128)(2,1)S(1)}, u32[]{:S(2)}, u32[]{:S(2)}) collective-permute-start(bf16[256,384]{1,0:T(8,128)(2,1)S(1)} %get-tuple-element.36), channel_id=1, source_target_pairs={{0,8},{4,12},{8,16},{12,20},{16,24},{20,28},{1,9},{5,13},{9,17},{1... | collective-permute-start | bytes 589832 | tf_op jit(solution)/shard_map/keys/ppermute | solution.py:33
  151.9 4.8 %collective-permute-start.38 = (bf16[256,384]{1,0:T(8,128)(2,1)S(1)}, bf16[256,384]{1,0:T(8,128)(2,1)S(1)}, u32[]{:S(2)}, u32[]{:S(2)}) collective-permute-start(bf16[256,384]{1,0:T(8,128)(2,1)S(1)} %dynamic-slice_convert_fusion), channel_id=1, source_target_pairs={{0,8},{4,12},{24,16},{28,20},{1,9},{5,13},{25,17},{29,21},{2,10},{... | collective-permute-start | bytes 589832 | tf_op jit(solution)/shard_map/values/ppermute | solution.py:33
  159.3 2.4 collective-permute-done.38
  161.7 4.4 %collective-permute-start.39 = (bf16[256,384]{1,0:T(8,128)(2,1)S(1)}, bf16[256,384]{1,0:T(8,128)(2,1)S(1)}, u32[]{:S(2)}, u32[]{:S(2)}) collective-permute-start(bf16[256,384]{1,0:T(8,128)(2,1)S(1)} %get-tuple-element.28), channel_id=1, source_target_pairs={{0,8},{4,12},{8,16},{12,20},{1,9},{5,13},{9,17},{13,21},{2,10},{6,... | collective-permute-start | bytes 589832 | tf_op jit(solution)/shard_map/values/ppermute | solution.py:33
  167.0 3.0 %collective-permute-start.26 = (bf16[256,384]{1,0:T(8,128)(2,1)S(1)}, bf16[256,384]{1,0:T(8,128)(2,1)S(1)}, u32[]{:S(2)}, u32[]{:S(2)}) collective-permute-start(bf16[256,384]{1,0:T(8,128)(2,1)S(1)} %get-tuple-element.32), channel_id=1, source_target_pairs={{0,8},{4,12},{8,16},{12,20},{1,9},{5,13},{9,17},{13,21},{2,10},{6,... | collective-permute-start | bytes 589832 | tf_op jit(solution)/shard_map/queries/ppermute | solution.py:33
  172.3 5.0 %collective-permute-start.40 = (bf16[256,384]{1,0:T(8,128)(2,1)S(1)}, bf16[256,384]{1,0:T(8,128)(2,1)S(1)}, u32[]{:S(2)}, u32[]{:S(2)}) collective-permute-start(bf16[256,384]{1,0:T(8,128)(2,1)S(1)} %get-tuple-element.34), channel_id=1, source_target_pairs={{0,8},{4,12},{8,16},{12,20},{16,24},{20,28},{1,9},{5,13},{9,17},{1... | collective-permute-start | bytes 589832 | tf_op jit(solution)/shard_map/values/ppermute | solution.py:33
  178.8 6.1 %collective-permute-start.27 = (bf16[256,384]{1,0:T(8,128)(2,1)S(1)}, bf16[256,384]{1,0:T(8,128)(2,1)S(1)}, u32[]{:S(2)}, u32[]{:S(2)}) collective-permute-start(bf16[256,384]{1,0:T(8,128)(2,1)S(1)} %get-tuple-element.38), channel_id=1, source_target_pairs={{0,8},{4,12},{8,16},{12,20},{16,24},{20,28},{1,9},{5,13},{9,17},{1... | collective-permute-start | bytes 589832 | tf_op jit(solution)/shard_map/queries/ppermute | solution.py:33
  188.2 4.4 %collective-permute-done.29 = bf16[256,384]{1,0:T(8,128)(2,1)S(1)} collective-permute-done((bf16[256,384]{1,0:T(8,128)(2,1)S(1)}, bf16[256,384]{1,0:T(8,128)(2,1)S(1)}, u32[]{:S(2)}, u32[]{:S(2)}) %collective-permute-start.29) | collective-permute-done | bytes 196640 | tf_op jit(solution)/shard_map/queries/ppermute | solution.py:33
  194.2 3.0 %collective-permute-start.44 = (bf16[256,384]{1,0:T(8,128)(2,1)S(1)}, bf16[256,384]{1,0:T(8,128)(2,1)S(1)}, u32[]{:S(2)}, u32[]{:S(2)}) collective-permute-start(bf16[256,384]{1,0:T(8,128)(2,1)S(1)} %prompt_attention.1.refs_0_), channel_id=1, source_target_pairs={{0,8},{4,12},{8,16},{12,20},{16,24},{20,28},{1,9},{5,13},{9,17},{1... | collective-permute-start | bytes 589832 | tf_op jit(solution)/shard_map/gather_attended/ppermute | solution.py:33
  201.0 3.7 %collective-permute-done.45 = bf16[256,384]{1,0:T(8,128)(2,1)S(1)} collective-permute-done((bf16[256,384]{1,0:T(8,128)(2,1)S(1)}, bf16[256,384]{1,0:T(8,128)(2,1)S(1)}, u32[]{:S(2)}, u32[]{:S(2)}) %collective-permute-start.45) | collective-permute-done | bytes 196640 | tf_op jit(solution)/shard_map/gather_attended/ppermute | solution.py:33
  206.1 2.9 %collective-permute-start.59 = (bf16[8,1536]{1,0:T(8,128)(2,1)S(1)}, bf16[8,1536]{1,0:T(8,128)(2,1)S(1)}, u32[]{:S(2)}, u32[]{:S(2)}) collective-permute-start(bf16[8,1536]{1,0:T(8,128)(2,1)S(1)} %pad_maximum_fusion.11), channel_id=1, source_target_pairs={{0,16},{4,20},{8,24},{12,28},{16,0},{20,4},{24,8},{28,12},{1,17},{... | collective-permute-start | bytes 73736 | tf_op jit(solution)/shard_map/decode_attention/ppermute | solution.py:25
  209.6 4.1 %collective-permute-done.46 = bf16[256,384]{1,0:T(8,128)(2,1)S(1)} collective-permute-done((bf16[256,384]{1,0:T(8,128)(2,1)S(1)}, bf16[256,384]{1,0:T(8,128)(2,1)S(1)}, u32[]{:S(2)}, u32[]{:S(2)}) %collective-permute-start.46) | collective-permute-done | bytes 196640 | tf_op jit(solution)/shard_map/gather_attended/ppermute | solution.py:33
  216.1 5.1 %collective-permute-done.47 = bf16[256,384]{1,0:T(8,128)(2,1)S(1)} collective-permute-done((bf16[256,384]{1,0:T(8,128)(2,1)S(1)}, bf16[256,384]{1,0:T(8,128)(2,1)S(1)}, u32[]{:S(2)}, u32[]{:S(2)}) %collective-permute-start.47) | collective-permute-done | bytes 196640 | tf_op jit(solution)/shard_map/gather_attended/ppermute | solution.py:33
  222.8 1.8 copy-done
  224.6 4.3 %out_project.1 = bf16[800,896]{1,0:T(8,128)(2,1)S(1)} custom-call(s32[2]{0:T(128)S(1)} %pad_add_fusion.3.place_ref, bf16[256,384]{1,0:T(8,128)(2,1)S(1)} %prompt_attention.1.refs_0_, bf16[256,384]{1,0:T(8,128)(2,1)S(1)} %add.811.refs_1_, bf16[256,384]{1,0:T(8,128)(2,1)S(1)} %add.812.refs_2_, bf16[256,384]{1,0:T(8,128)(2,1)S(1)} %add.813.refs_3_, ...), custom_call_target="tpu_custom_call" | custom-call | tf_op jit(solution)/shard_map/out_project/out_project/pallas_call | solution.py:204
  233.4 7.9 %collective-permute-done.60 = bf16[200,896]{1,0:T(8,128)(2,1)S(1)} collective-permute-done((bf16[200,896]{1,0:T(8,128)(2,1)}, bf16[200,896]{1,0:T(8,128)(2,1)S(1)}, u32[]{:S(2)}, u32[]{:S(2)}) %collective-permute-start.60) | collective-permute-done | bytes 358432 | tf_op jit(solution)/shard_map/sum_mp/ppermute | solution.py:29
  241.3 8.0 %collective-permute-done.61 = bf16[200,896]{1,0:T(8,128)(2,1)S(1)} collective-permute-done((bf16[200,896]{1,0:T(8,128)(2,1)}, bf16[200,896]{1,0:T(8,128)(2,1)S(1)}, u32[]{:S(2)}, u32[]{:S(2)}) %collective-permute-start.61) | collective-permute-done | bytes 358432 | tf_op jit(solution)/shard_map/sum_mp/ppermute | solution.py:29
  250.8 4.3 %collective-permute-start.65 = (bf16[56,896]{1,0:T(8,128)(2,1)S(1)}, bf16[56,896]{1,0:T(8,128)(2,1)S(1)}, u32[]{:S(2)}, u32[]{:S(2)}) collective-permute-start(bf16[56,896]{1,0:T(8,128)(2,1)S(1)} %get-tuple-element.66), channel_id=1, source_target_pairs={{0,24},{4,28},{8,16},{12,20},{16,8},{20,12},{24,0},{28,4},{1,25},{... | collective-permute-start | bytes 301064 | tf_op jit(solution)/shard_map/return_z/ppermute | solution.py:25
  255.4 5.3 %collective-permute-done.64 = bf16[56,896]{1,0:T(8,128)(2,1)S(1)} collective-permute-done((bf16[56,896]{1,0:T(8,128)(2,1)S(1)}, bf16[56,896]{1,0:T(8,128)(2,1)S(1)}, u32[]{:S(2)}, u32[]{:S(2)}) %collective-permute-start.64) | collective-permute-done | bytes 100384 | tf_op jit(solution)/shard_map/return_z/ppermute | solution.py:25
  262.4 3.9 %collective-permute-start.68 = (bf16[56,896]{1,0:T(8,128)(2,1)S(1)}, bf16[56,896]{1,0:T(8,128)(2,1)S(1)}, u32[]{:S(2)}, u32[]{:S(2)}) collective-permute-start(bf16[56,896]{1,0:T(8,128)(2,1)S(1)} %get-tuple-element.63), channel_id=1, source_target_pairs={{0,2},{1,3},{2,6},{3,7},{4,0},{5,1},{6,4},{7,5},{8,10},{9,11},{10,... | collective-permute-start | bytes 301064 | tf_op jit(solution)/shard_map/return_plane/ppermute | solution.py:503
  266.5 2.1 collective-permute-done.68
  268.6 2.9 %collective-permute-done.69 = bf16[56,896]{1,0:T(8,128)(2,1)S(1)} collective-permute-done((bf16[56,896]{1,0:T(8,128)(2,1)S(1)}, bf16[56,896]{1,0:T(8,128)(2,1)S(1)}, u32[]{:S(2)}, u32[]{:S(2)}) %collective-permute-start.69) | collective-permute-done | bytes 100384 | tf_op jit(solution)/shard_map/return_plane/ppermute | solution.py:503
  (362 shorter events, 84.1 us)
Async XLA Ops:
  2.5 14.3 %collective-permute-start.11 = (f32[2,98]{1,0:T(2,128)S(1)}, f32[2,98]{1,0:T(2,128)S(1)}, u32[]{:S(2)}, u32[]{:S(2)}) collective-permute-start(f32[2,98]{1,0:T(2,128)S(1)} %get-tuple-element.100), channel_id=1, source_target_pairs={{0,1},{1,0},{2,3},{3,2},{4,5},{5,4},{6,7},{7,6},{8,9},{9,8},{10,11... | collective-permute-start | bytes 2360 | tf_op jit(solution)/shard_map/home_norm/ppermute | solution.py:29
  5.6 11.4 %collective-permute-start.12 = (f32[2,98]{1,0:T(2,128)S(1)}, f32[2,98]{1,0:T(2,128)S(1)}, u32[]{:S(2)}, u32[]{:S(2)}) collective-permute-start(f32[2,98]{1,0:T(2,128)S(1)} %get-tuple-element.100), channel_id=1, source_target_pairs={{0,2},{1,3},{2,0},{3,1},{4,6},{5,7},{6,4},{7,5},{8,10},{9,11},{10,... | collective-permute-start | bytes 2360 | tf_op jit(solution)/shard_map/home_norm/ppermute | solution.py:29
  7.1 9.9 %collective-permute-start.13 = (f32[2,98]{1,0:T(2,128)S(1)}, f32[2,98]{1,0:T(2,128)S(1)}, u32[]{:S(2)}, u32[]{:S(2)}) collective-permute-start(f32[2,98]{1,0:T(2,128)S(1)} %get-tuple-element.100), channel_id=1, source_target_pairs={{0,3},{1,2},{2,1},{3,0},{4,7},{5,6},{6,5},{7,4},{8,11},{9,10},{10,... | collective-permute-start | bytes 2360 | tf_op jit(solution)/shard_map/home_norm/ppermute | solution.py:29
  14.5 9.5 %collective-permute-start.1 = (bf16[32,1792]{1,0:T(8,128)(2,1)S(1)}, bf16[32,1792]{1,0:T(8,128)(2,1)S(1)}, u32[]{:S(2)}, u32[]{:S(2)}) collective-permute-start(bf16[32,1792]{1,0:T(8,128)(2,1)S(1)} %get-tuple-element.50), channel_id=1, source_target_pairs={{0,2},{1,3},{2,0},{3,1},{4,6},{5,7},{6,4},{7,5},{8,10},{9,11},{10,... | collective-permute-start | bytes 344072 | tf_op jit(solution)/shard_map/deal/ppermute | solution.py:29
  16.9 7.1 %collective-permute-start.2 = (bf16[32,1792]{1,0:T(8,128)(2,1)S(1)}, bf16[32,1792]{1,0:T(8,128)(2,1)S(1)}, u32[]{:S(2)}, u32[]{:S(2)}) collective-permute-start(bf16[32,1792]{1,0:T(8,128)(2,1)S(1)} %get-tuple-element.49), channel_id=1, source_target_pairs={{0,3},{1,2},{2,1},{3,0},{4,7},{5,6},{6,5},{7,4},{8,11},{9,10},{10,... | collective-permute-start | bytes 344072 | tf_op jit(solution)/shard_map/deal/ppermute | solution.py:29
  16.9 56.3 %collective-permute-start.10 = (bf16[256,1792]{1,0:T(8,128)(2,1)}, bf16[256,1792]{1,0:T(8,128)(2,1)}, u32[]{:S(2)}, u32[]{:S(2)}) collective-permute-start(bf16[256,1792]{1,0:T(8,128)(2,1)} %bitcast.237), channel_id=1, source_target_pairs={{0,4},{4,0},{8,12},{12,8},{16,20},{20,16},{24,28},{28,24},{1,5},{5... | collective-permute-start | bytes 2752520 | tf_op jit(solution)/shard_map/ppermute | solution.py:25
  17.4 30.8 %collective-permute-start.15 = (bf16[98,1792]{1,0:T(8,128)(2,1)S(1)}, bf16[98,1792]{1,0:T(8,128)(2,1)S(1)}, u32[]{:S(2)}, u32[]{:S(2)}) collective-permute-start(bf16[98,1792]{1,0:T(8,128)(2,1)S(1)} %fusion.50), channel_id=1, source_target_pairs={{24,16},{28,20},{16,8},{20,12},{8,0},{12,4},{25,17},{29,21},{17,9}... | collective-permute-start | bytes 1053704 | tf_op jit(solution)/shard_map/low_rank/ppermute | solution.py:33
  18.7 30.8 %collective-permute-start.14 = (bf16[98,1792]{1,0:T(8,128)(2,1)S(1)}, bf16[98,1792]{1,0:T(8,128)(2,1)}, u32[]{:S(2)}, u32[]{:S(2)}) collective-permute-start(bf16[98,1792]{1,0:T(8,128)(2,1)S(1)} %fusion.50), channel_id=1, source_target_pairs={{0,8},{4,12},{8,16},{12,20},{16,24},{20,28},{1,9},{5,13},{9,17},{1... | collective-permute-start | bytes 1053704 | tf_op jit(solution)/shard_map/low_rank/ppermute | solution.py:33
  25.1 10.4 %collective-permute-start.3 = (bf16[32,1792]{1,0:T(8,128)(2,1)S(1)}, bf16[32,1792]{1,0:T(8,128)(2,1)S(1)}, u32[]{:S(2)}, u32[]{:S(2)}) collective-permute-start(bf16[32,1792]{1,0:T(8,128)(2,1)S(1)} %get-tuple-element.10), channel_id=1, source_target_pairs={{0,8},{4,12},{8,0},{12,4},{16,24},{20,28},{24,16},{28,20},{1,9},{5... | collective-permute-start | bytes 344072 | tf_op jit(solution)/shard_map/spread_z/ppermute | solution.py:25
  26.4 14.8 %collective-permute-start.4 = (bf16[32,1792]{1,0:T(8,128)(2,1)S(1)}, bf16[32,1792]{1,0:T(8,128)(2,1)S(1)}, u32[]{:S(2)}, u32[]{:S(2)}) collective-permute-start(bf16[32,1792]{1,0:T(8,128)(2,1)S(1)} %get-tuple-element.11), channel_id=1, source_target_pairs={{0,16},{4,20},{8,24},{12,28},{16,0},{20,4},{24,8},{28,12},{1,17},{... | collective-permute-start | bytes 344072 | tf_op jit(solution)/shard_map/spread_z/ppermute | solution.py:25
  35.5 8.5 %collective-permute-start.5 = (bf16[32,1792]{1,0:T(8,128)(2,1)S(1)}, bf16[32,1792]{1,0:T(8,128)(2,1)S(1)}, u32[]{:S(2)}, u32[]{:S(2)}) collective-permute-start(bf16[32,1792]{1,0:T(8,128)(2,1)S(1)} %get-tuple-element.12), channel_id=1, source_target_pairs={{0,24},{4,28},{8,16},{12,20},{16,8},{20,12},{24,0},{28,4},{1,25},{... | collective-permute-start | bytes 344072 | tf_op jit(solution)/shard_map/spread_z/ppermute | solution.py:25
  48.2 13.1 %collective-permute-start.16 = (bf16[98,1792]{1,0:T(8,128)(2,1)S(1)}, bf16[98,1792]{1,0:T(8,128)(2,1)}, u32[]{:S(2)}, u32[]{:S(2)}) collective-permute-start(bf16[98,1792]{1,0:T(8,128)(2,1)S(1)} %collective-permute-done.15), channel_id=1, source_target_pairs={{16,8},{20,12},{8,0},{12,4},{17,9},{21,13},{9,1},{13,5},{18,10},{2... | collective-permute-start | bytes 1053704 | tf_op jit(solution)/shard_map/low_rank/ppermute | solution.py:33
  49.5 15.7 %collective-permute-start.18 = (bf16[98,1792]{1,0:T(8,128)(2,1)}, bf16[98,1792]{1,0:T(8,128)(2,1)}, u32[]{:S(2)}, u32[]{:S(2)}) collective-permute-start(bf16[98,1792]{1,0:T(8,128)(2,1)} %collective-permute-done.14), channel_id=1, source_target_pairs={{8,16},{12,20},{16,24},{20,28},{9,17},{13,21},{17,25},{21,29},{10,... | collective-permute-start | bytes 1053704 | tf_op jit(solution)/shard_map/low_rank/ppermute | solution.py:33
  52.0 14.5 %collective-permute-start.7 = (bf16[144,896]{1,0:T(8,128)(2,1)S(1)}, bf16[144,896]{1,0:T(8,128)(2,1)S(1)}, u32[]{:S(2)}, u32[]{:S(2)}) collective-permute-start(bf16[144,896]{1,0:T(8,128)(2,1)S(1)} %convolution_convert_fusion.1), channel_id=1, source_target_pairs={{0,1},{1,0},{2,3},{3,2},{4,5},{5,4},{6,7},{7,6},{8,9},{9,8},{10,11... | collective-permute-start | bytes 774152 | tf_op jit(solution)/shard_map/gather_chunks/ppermute | solution.py:29
  53.8 13.7 %collective-permute-start.8 = (bf16[144,896]{1,0:T(8,128)(2,1)S(1)}, bf16[144,896]{1,0:T(8,128)(2,1)S(1)}, u32[]{:S(2)}, u32[]{:S(2)}) collective-permute-start(bf16[144,896]{1,0:T(8,128)(2,1)S(1)} %convolution_convert_fusion.1), channel_id=1, source_target_pairs={{0,2},{1,3},{2,0},{3,1},{4,6},{5,7},{6,4},{7,5},{8,10},{9,11},{10,... | collective-permute-start | bytes 774152 | tf_op jit(solution)/shard_map/gather_chunks/ppermute | solution.py:29
  61.3 8.7 %collective-permute-start.9 = (bf16[144,896]{1,0:T(8,128)(2,1)S(1)}, bf16[144,896]{1,0:T(8,128)(2,1)S(1)}, u32[]{:S(2)}, u32[]{:S(2)}) collective-permute-start(bf16[144,896]{1,0:T(8,128)(2,1)S(1)} %convolution_convert_fusion.1), channel_id=1, source_target_pairs={{0,3},{1,2},{2,1},{3,0},{4,7},{5,6},{6,5},{7,4},{8,11},{9,10},{10,... | collective-permute-start | bytes 774152 | tf_op jit(solution)/shard_map/gather_chunks/ppermute | solution.py:29
  65.2 12.1 %collective-permute-start.17 = (bf16[98,1792]{1,0:T(8,128)(2,1)}, bf16[98,1792]{1,0:T(8,128)(2,1)S(1)}, u32[]{:S(2)}, u32[]{:S(2)}) collective-permute-start(bf16[98,1792]{1,0:T(8,128)(2,1)} %collective-permute-done.16), channel_id=1, source_target_pairs={{8,0},{12,4},{9,1},{13,5},{10,2},{14,6},{11,3},{15,7}} | collective-permute-start | bytes 1053704 | tf_op jit(solution)/shard_map/low_rank/ppermute | solution.py:33
  66.5 12.8 %collective-permute-start.19 = (bf16[98,1792]{1,0:T(8,128)(2,1)}, bf16[98,1792]{1,0:T(8,128)(2,1)S(1)}, u32[]{:S(2)}, u32[]{:S(2)}) collective-permute-start(bf16[98,1792]{1,0:T(8,128)(2,1)} %collective-permute-done.18), channel_id=1, source_target_pairs={{16,24},{20,28},{17,25},{21,29},{18,26},{22,30},{19,27},{23,31}} | collective-permute-start | bytes 1053704 | tf_op jit(solution)/shard_map/low_rank/ppermute | solution.py:33
  92.0 27.1 %collective-permute-start.30 = (bf16[256,1536]{1,0:T(8,128)(2,1)S(1)}, bf16[256,1536]{1,0:T(8,128)(2,1)}, u32[]{:S(2)}, u32[]{:S(2)}) collective-permute-start(bf16[256,1536]{1,0:T(8,128)(2,1)S(1)} %fusion.21), channel_id=1, source_target_pairs={{0,4},{4,0},{8,12},{12,8},{16,20},{20,16},{24,28},{28,24},{1,5},{5... | collective-permute-start | bytes 2359304 | tf_op jit(solution)/shard_map/keys/ppermute | solution.py:25
  100.3 7.4 %collective-permute-start.54 = (f32[4,2,3,1536]{3,0,2,1:T(4,128)S(1)}, f32[4,2,3,1536]{3,0,2,1:T(4,128)S(1)}, u32[]{:S(2)}, u32[]{:S(2)}) collective-permute-start(f32[4,2,3,1536]{3,0,2,1:T(4,128)S(1)} %bitcast.213), channel_id=1, source_target_pairs={{0,4},{4,0},{8,12},{12,8},{16,20},{20,16},{24,28},{28,24},{1,5},{5... | collective-permute-start | bytes 442376 | tf_op jit(solution)/shard_map/decode_rows/ppermute | solution.py:25
  103.9 46.9 %collective-permute-start.37 = (bf16[256,1536]{1,0:T(8,128)(2,1)S(1)}, bf16[256,1536]{1,0:T(8,128)(2,1)S(1)}, u32[]{:S(2)}, u32[]{:S(2)}) collective-permute-start(bf16[256,1536]{1,0:T(8,128)(2,1)S(1)} %fusion.18), channel_id=1, source_target_pairs={{0,4},{4,0},{8,12},{12,8},{16,20},{20,16},{24,28},{28,24},{1,5},{5... | collective-permute-start | bytes 2359304 | tf_op jit(solution)/shard_map/values/ppermute | solution.py:25
  107.8 6.9 %collective-permute-start.55 = (f32[2,2,3,1536]{3,0,2,1:T(2,128)S(1)}, f32[2,2,3,1536]{3,0,2,1:T(2,128)S(1)}, u32[]{:S(2)}, u32[]{:S(2)}) collective-permute-start(f32[2,2,3,1536]{3,0,2,1:T(2,128)S(1)} %constant_dynamic-slice_fusion.7), channel_id=1, source_target_pairs={{0,16},{4,20},{8,24},{12,28},{16,0},{20,4},{24,8},{28,12},{1,17},{... | collective-permute-start | bytes 221192 | tf_op jit(solution)/shard_map/decode_rows/ppermute | solution.py:25
  109.4 47.2 %collective-permute-start.24 = (bf16[256,1536]{1,0:T(8,128)(2,1)S(1)}, bf16[256,1536]{1,0:T(8,128)(2,1)S(1)}, u32[]{:S(2)}, u32[]{:S(2)}) collective-permute-start(bf16[256,1536]{1,0:T(8,128)(2,1)S(1)} %fusion.15), channel_id=1, source_target_pairs={{0,4},{4,0},{8,12},{12,8},{16,20},{20,16},{24,28},{28,24},{1,5},{5... | collective-permute-start | bytes 2359304 | tf_op jit(solution)/shard_map/queries/ppermute | solution.py:25
  121.4 17.0 %collective-permute-start.31 = (bf16[256,384]{1,0:T(8,128)(2,1)S(1)}, bf16[256,384]{1,0:T(8,128)(2,1)S(1)}, u32[]{:S(2)}, u32[]{:S(2)}) collective-permute-start(bf16[256,384]{1,0:T(8,128)(2,1)S(1)} %dynamic-slice_convert_fusion.1), channel_id=1, source_target_pairs={{0,8},{4,12},{24,16},{28,20},{1,9},{5,13},{25,17},{29,21},{2,10},{... | collective-permute-start | bytes 589832 | tf_op jit(solution)/shard_map/keys/ppermute | solution.py:33
  140.5 65.5 %collective-permute-start.58 = (bf16[4,1536]{1,0:T(4,128)(2,1)S(1)}, bf16[4,1536]{1,0:T(4,128)(2,1)S(1)}, u32[]{:S(2)}, u32[]{:S(2)}) collective-permute-start(bf16[4,1536]{1,0:T(4,128)(2,1)S(1)} %pad_maximum_fusion.12), channel_id=1, source_target_pairs={{0,8},{4,12},{8,0},{12,4},{16,24},{20,28},{24,16},{28,20},{1,9},{5... | collective-permute-start | bytes 36872 | tf_op jit(solution)/shard_map/decode_attention/ppermute | solution.py:25
  145.1 13.9 %collective-permute-start.33 = (bf16[256,384]{1,0:T(8,128)(2,1)S(1)}, bf16[256,384]{1,0:T(8,128)(2,1)S(1)}, u32[]{:S(2)}, u32[]{:S(2)}) collective-permute-start(bf16[256,384]{1,0:T(8,128)(2,1)S(1)} %get-tuple-element.36), channel_id=1, source_target_pairs={{0,8},{4,12},{8,16},{12,20},{16,24},{20,28},{1,9},{5,13},{9,17},{1... | collective-permute-start | bytes 589832 | tf_op jit(solution)/shard_map/keys/ppermute | solution.py:33
  149.5 9.5 %collective-permute-start.35 = (bf16[256,384]{1,0:T(8,128)(2,1)S(1)}, bf16[256,384]{1,0:T(8,128)(2,1)S(1)}, u32[]{:S(2)}, u32[]{:S(2)}) collective-permute-start(bf16[256,384]{1,0:T(8,128)(2,1)S(1)} %get-tuple-element.37), channel_id=1, source_target_pairs={{24,16},{28,20},{16,8},{20,12},{8,0},{12,4},{25,17},{29,21},{17,9}... | collective-permute-start | bytes 589832 | tf_op jit(solution)/shard_map/keys/ppermute | solution.py:33
  151.9 9.7 %collective-permute-start.38 = (bf16[256,384]{1,0:T(8,128)(2,1)S(1)}, bf16[256,384]{1,0:T(8,128)(2,1)S(1)}, u32[]{:S(2)}, u32[]{:S(2)}) collective-permute-start(bf16[256,384]{1,0:T(8,128)(2,1)S(1)} %dynamic-slice_convert_fusion), channel_id=1, source_target_pairs={{0,8},{4,12},{24,16},{28,20},{1,9},{5,13},{25,17},{29,21},{2,10},{... | collective-permute-start | bytes 589832 | tf_op jit(solution)/shard_map/values/ppermute | solution.py:33
  157.8 9.1 %collective-permute-start.25 = (bf16[256,384]{1,0:T(8,128)(2,1)S(1)}, bf16[256,384]{1,0:T(8,128)(2,1)S(1)}, u32[]{:S(2)}, u32[]{:S(2)}) collective-permute-start(bf16[256,384]{1,0:T(8,128)(2,1)S(1)} %dynamic-slice_convert_fusion.2), channel_id=1, source_target_pairs={{0,8},{4,12},{24,16},{28,20},{1,9},{5,13},{25,17},{29,21},{2,10},{... | collective-permute-start | bytes 589832 | tf_op jit(solution)/shard_map/queries/ppermute | solution.py:33
  159.2 33.5 %collective-permute-start.36 = (bf16[256,384]{1,0:T(8,128)(2,1)S(1)}, bf16[256,384]{1,0:T(8,128)(2,1)S(1)}, u32[]{:S(2)}, u32[]{:S(2)}) collective-permute-start(bf16[256,384]{1,0:T(8,128)(2,1)S(1)} %add_convert_fusion.3.ka_ref), channel_id=1, source_target_pairs={{0,4},{4,0},{8,12},{12,8},{16,20},{20,16},{24,28},{28,24},{1,5},{5... | collective-permute-start | bytes 589832 | tf_op jit(solution)/shard_map/prompt_attention/ppermute | solution.py:25
  161.7 9.6 %collective-permute-start.39 = (bf16[256,384]{1,0:T(8,128)(2,1)S(1)}, bf16[256,384]{1,0:T(8,128)(2,1)S(1)}, u32[]{:S(2)}, u32[]{:S(2)}) collective-permute-start(bf16[256,384]{1,0:T(8,128)(2,1)S(1)} %get-tuple-element.28), channel_id=1, source_target_pairs={{0,8},{4,12},{8,16},{12,20},{1,9},{5,13},{9,17},{13,21},{2,10},{6,... | collective-permute-start | bytes 589832 | tf_op jit(solution)/shard_map/values/ppermute | solution.py:33
  167.0 10.3 %collective-permute-start.26 = (bf16[256,384]{1,0:T(8,128)(2,1)S(1)}, bf16[256,384]{1,0:T(8,128)(2,1)S(1)}, u32[]{:S(2)}, u32[]{:S(2)}) collective-permute-start(bf16[256,384]{1,0:T(8,128)(2,1)S(1)} %get-tuple-element.32), channel_id=1, source_target_pairs={{0,8},{4,12},{8,16},{12,20},{1,9},{5,13},{9,17},{13,21},{2,10},{6,... | collective-permute-start | bytes 589832 | tf_op jit(solution)/shard_map/queries/ppermute | solution.py:33
  171.4 7.3 %collective-permute-start.28 = (bf16[256,384]{1,0:T(8,128)(2,1)S(1)}, bf16[256,384]{1,0:T(8,128)(2,1)S(1)}, u32[]{:S(2)}, u32[]{:S(2)}) collective-permute-start(bf16[256,384]{1,0:T(8,128)(2,1)S(1)} %get-tuple-element.33), channel_id=1, source_target_pairs={{24,16},{28,20},{16,8},{20,12},{25,17},{29,21},{17,9},{21,13},{26,... | collective-permute-start | bytes 589832 | tf_op jit(solution)/shard_map/queries/ppermute | solution.py:33
  172.3 12.7 %collective-permute-start.40 = (bf16[256,384]{1,0:T(8,128)(2,1)S(1)}, bf16[256,384]{1,0:T(8,128)(2,1)S(1)}, u32[]{:S(2)}, u32[]{:S(2)}) collective-permute-start(bf16[256,384]{1,0:T(8,128)(2,1)S(1)} %get-tuple-element.34), channel_id=1, source_target_pairs={{0,8},{4,12},{8,16},{12,20},{16,24},{20,28},{1,9},{5,13},{9,17},{1... | collective-permute-start | bytes 589832 | tf_op jit(solution)/shard_map/values/ppermute | solution.py:33
  177.3 9.3 %collective-permute-start.42 = (bf16[256,384]{1,0:T(8,128)(2,1)S(1)}, bf16[256,384]{1,0:T(8,128)(2,1)S(1)}, u32[]{:S(2)}, u32[]{:S(2)}) collective-permute-start(bf16[256,384]{1,0:T(8,128)(2,1)S(1)} %get-tuple-element.35), channel_id=1, source_target_pairs={{24,16},{28,20},{16,8},{20,12},{8,0},{12,4},{25,17},{29,21},{17,9}... | collective-permute-start | bytes 589832 | tf_op jit(solution)/shard_map/values/ppermute | solution.py:33
  178.8 9.3 %collective-permute-start.27 = (bf16[256,384]{1,0:T(8,128)(2,1)S(1)}, bf16[256,384]{1,0:T(8,128)(2,1)S(1)}, u32[]{:S(2)}, u32[]{:S(2)}) collective-permute-start(bf16[256,384]{1,0:T(8,128)(2,1)S(1)} %get-tuple-element.38), channel_id=1, source_target_pairs={{0,8},{4,12},{8,16},{12,20},{16,24},{20,28},{1,9},{5,13},{9,17},{1... | collective-permute-start | bytes 589832 | tf_op jit(solution)/shard_map/queries/ppermute | solution.py:33
  185.0 7.6 %collective-permute-start.29 = (bf16[256,384]{1,0:T(8,128)(2,1)S(1)}, bf16[256,384]{1,0:T(8,128)(2,1)S(1)}, u32[]{:S(2)}, u32[]{:S(2)}) collective-permute-start(bf16[256,384]{1,0:T(8,128)(2,1)S(1)} %get-tuple-element.39), channel_id=1, source_target_pairs={{24,16},{28,20},{16,8},{20,12},{8,0},{12,4},{25,17},{29,21},{17,9}... | collective-permute-start | bytes 589832 | tf_op jit(solution)/shard_map/queries/ppermute | solution.py:33
  197.2 7.6 %collective-permute-start.45 = (bf16[256,384]{1,0:T(8,128)(2,1)S(1)}, bf16[256,384]{1,0:T(8,128)(2,1)S(1)}, u32[]{:S(2)}, u32[]{:S(2)}) collective-permute-start(bf16[256,384]{1,0:T(8,128)(2,1)S(1)} %prompt_attention.1.refs_0_), channel_id=1, source_target_pairs={{24,16},{28,20},{16,8},{20,12},{8,0},{12,4},{25,17},{29,21},{17,9}... | collective-permute-start | bytes 589832 | tf_op jit(solution)/shard_map/gather_attended/ppermute | solution.py:33
  200.3 8.6 %collective-permute-start.48 = (bf16[256,384]{1,0:T(8,128)(2,1)S(1)}, bf16[256,384]{1,0:T(8,128)(2,1)S(1)}, u32[]{:S(2)}, u32[]{:S(2)}) collective-permute-start(bf16[256,384]{1,0:T(8,128)(2,1)S(1)} %collective-permute-done.44), channel_id=1, source_target_pairs={{8,16},{12,20},{16,24},{20,28},{9,17},{13,21},{17,25},{21,29},{10,... | collective-permute-start | bytes 589832 | tf_op jit(solution)/shard_map/gather_attended/ppermute | solution.py:33
  204.7 8.9 %collective-permute-start.46 = (bf16[256,384]{1,0:T(8,128)(2,1)S(1)}, bf16[256,384]{1,0:T(8,128)(2,1)S(1)}, u32[]{:S(2)}, u32[]{:S(2)}) collective-permute-start(bf16[256,384]{1,0:T(8,128)(2,1)S(1)} %collective-permute-done.45), channel_id=1, source_target_pairs={{16,8},{20,12},{8,0},{12,4},{17,9},{21,13},{9,1},{13,5},{18,10},{2... | collective-permute-start | bytes 589832 | tf_op jit(solution)/shard_map/gather_attended/ppermute | solution.py:33
  206.1 15.3 %collective-permute-start.59 = (bf16[8,1536]{1,0:T(8,128)(2,1)S(1)}, bf16[8,1536]{1,0:T(8,128)(2,1)S(1)}, u32[]{:S(2)}, u32[]{:S(2)}) collective-permute-start(bf16[8,1536]{1,0:T(8,128)(2,1)S(1)} %pad_maximum_fusion.11), channel_id=1, source_target_pairs={{0,16},{4,20},{8,24},{12,28},{16,0},{20,4},{24,8},{28,12},{1,17},{... | collective-permute-start | bytes 73736 | tf_op jit(solution)/shard_map/decode_attention/ppermute | solution.py:25
  208.9 7.0 %collective-permute-start.49 = (bf16[256,384]{1,0:T(8,128)(2,1)S(1)}, bf16[256,384]{1,0:T(8,128)(2,1)S(1)}, u32[]{:S(2)}, u32[]{:S(2)}) collective-permute-start(bf16[256,384]{1,0:T(8,128)(2,1)S(1)} %collective-permute-done.48), channel_id=1, source_target_pairs={{16,24},{20,28},{17,25},{21,29},{18,26},{22,30},{19,27},{23,31}} | collective-permute-start | bytes 589832 | tf_op jit(solution)/shard_map/gather_attended/ppermute | solution.py:33
  213.7 7.6 %collective-permute-start.47 = (bf16[256,384]{1,0:T(8,128)(2,1)S(1)}, bf16[256,384]{1,0:T(8,128)(2,1)S(1)}, u32[]{:S(2)}, u32[]{:S(2)}) collective-permute-start(bf16[256,384]{1,0:T(8,128)(2,1)S(1)} %collective-permute-done.46), channel_id=1, source_target_pairs={{8,0},{12,4},{9,1},{13,5},{10,2},{14,6},{11,3},{15,7}} | collective-permute-start | bytes 589832 | tf_op jit(solution)/shard_map/gather_attended/ppermute | solution.py:33
  229.9 11.4 %collective-permute-start.60 = (bf16[200,896]{1,0:T(8,128)(2,1)}, bf16[200,896]{1,0:T(8,128)(2,1)S(1)}, u32[]{:S(2)}, u32[]{:S(2)}) collective-permute-start(bf16[200,896]{1,0:T(8,128)(2,1)} %get-tuple-element.40), channel_id=1, source_target_pairs={{0,1},{1,0},{2,3},{3,2},{4,5},{5,4},{6,7},{7,6},{8,9},{9,8},{10,11... | collective-permute-start | bytes 1075208 | tf_op jit(solution)/shard_map/sum_mp/ppermute | solution.py:29
  231.3 18.0 %collective-permute-start.61 = (bf16[200,896]{1,0:T(8,128)(2,1)}, bf16[200,896]{1,0:T(8,128)(2,1)S(1)}, u32[]{:S(2)}, u32[]{:S(2)}) collective-permute-start(bf16[200,896]{1,0:T(8,128)(2,1)} %get-tuple-element.42), channel_id=1, source_target_pairs={{0,2},{1,3},{2,0},{3,1},{4,6},{5,7},{6,4},{7,5},{8,10},{9,11},{10,... | collective-permute-start | bytes 1075208 | tf_op jit(solution)/shard_map/sum_mp/ppermute | solution.py:29
  231.8 17.5 %collective-permute-start.62 = (bf16[200,896]{1,0:T(8,128)(2,1)S(1)}, bf16[200,896]{1,0:T(8,128)(2,1)}, u32[]{:S(2)}, u32[]{:S(2)}) collective-permute-start(bf16[200,896]{1,0:T(8,128)(2,1)S(1)} %get-tuple-element.41), channel_id=1, source_target_pairs={{0,3},{1,2},{2,1},{3,0},{4,7},{5,6},{6,5},{7,4},{8,11},{9,10},{10,... | collective-permute-start | bytes 1075208 | tf_op jit(solution)/shard_map/sum_mp/ppermute | solution.py:29
  250.8 9.9 %collective-permute-start.64 = (bf16[56,896]{1,0:T(8,128)(2,1)S(1)}, bf16[56,896]{1,0:T(8,128)(2,1)S(1)}, u32[]{:S(2)}, u32[]{:S(2)}) collective-permute-start(bf16[56,896]{1,0:T(8,128)(2,1)S(1)} %get-tuple-element.67), channel_id=1, source_target_pairs={{0,16},{4,20},{8,24},{12,28},{16,0},{20,4},{24,8},{28,12},{1,17},{... | collective-permute-start | bytes 301064 | tf_op jit(solution)/shard_map/return_z/ppermute | solution.py:25
  250.8 9.9 %collective-permute-start.65 = (bf16[56,896]{1,0:T(8,128)(2,1)S(1)}, bf16[56,896]{1,0:T(8,128)(2,1)S(1)}, u32[]{:S(2)}, u32[]{:S(2)}) collective-permute-start(bf16[56,896]{1,0:T(8,128)(2,1)S(1)} %get-tuple-element.66), channel_id=1, source_target_pairs={{0,24},{4,28},{8,16},{12,20},{16,8},{20,12},{24,0},{28,4},{1,25},{... | collective-permute-start | bytes 301064 | tf_op jit(solution)/shard_map/return_z/ppermute | solution.py:25
  (51 other events, 531.4 us)

commit v2 on v0

--- a/solution.py
+++ b/solution.py
@@ -1,10 +1,884 @@
+import functools
+
 import jax
 import jax.numpy as jnp
 from jax import lax
+from jax.experimental import pallas as pl
+from jax.experimental.pallas import tpu as pltpu
 from jax.sharding import PartitionSpec as P
 
 HEAD_DIM = 128
 ADAPTER_RANK = 16
+BF = jnp.bfloat16
+F32 = jnp.float32
+MIB = 1 << 20
+
+NZ, NM = 4, 4
+SLOTS, PLEN, DEC = 3, 32, 2
+QROWS = 24
+STAT_ROW = 26
+BLK = 32
+CHUNK = 128
+DCH = 16
+PACKED = NM * CHUNK + 2 * NZ * DEC
+LANES = 128
+DECODE_ROWS = 16
+SMALL = pl.CostEstimate(flops=1, bytes_accessed=1, transcendentals=0)
+VMEM = pl.BlockSpec(memory_space=pltpu.VMEM)
+SMEM = pl.BlockSpec(memory_space=pltpu.SMEM)
+ANY = pl.BlockSpec(memory_space=pl.ANY)
+
+
+def swap_req(x, bits):
+    return lax.ppermute(x, "req", [(i, i ^ bits) for i in range(2 * NZ)])
+
+
+def swap_mp(x, bits):
+    return lax.ppermute(x, "mp", [(i, i ^ bits) for i in range(NM)])
+
+
+def gather_z(x):
+    far, near = swap_req(x, 4), swap_req(x, 2)
+    return [x, near, far, swap_req(far, 2)]
+
+
+def gather_mp(x):
+    one, two = swap_mp(x, 1), swap_mp(x, 2)
+    return [x, one, two, swap_mp(one, 2)]
+
+
+def limit(mib):
+    return pltpu.CompilerParams(vmem_limit_bytes=mib * MIB)
+
+
+def iota(shape, axis):
+    return lax.broadcasted_iota(jnp.int32, shape, axis)
+
+
+def three(x):
+    a = x.astype(BF)
+    rest = x - a.astype(F32)
+    b = rest.astype(BF)
+    return [a.astype(F32), b.astype(F32), (rest - b.astype(F32)).astype(BF).astype(F32)]
+
+
+class Source:
+    def __init__(self, s_ref, t_ref, j):
+        z, core = s_ref[3], s_ref[6]
+        self.z = jnp.bitwise_xor(z, j % NZ)
+        self.core = jnp.bitwise_xor(core, j // NZ)
+        self.index = self.z * 2 + self.core
+        self.lens = [t_ref[j, i] for i in range(SLOTS)]
+        self.adapters = [t_ref[j, SLOTS + i] for i in range(SLOTS + DEC)]
+        self.live = self.lens[0] + self.lens[1] + self.lens[2]
+        self.size = (self.live + 3) >> 2
+
+
+def sources(s_ref, t_ref):
+    found = [Source(s_ref, t_ref, j) for j in range(2 * NZ)]
+    for a in found:
+        a.offset = sum(jnp.where(b.index < a.index, b.size, 0) for b in found)
+    return found
+
+
+def by_slot(h, values):
+    out = jnp.full_like(h, -1)
+    for j in range(SLOTS):
+        out = jnp.where((h >> 5) == j, values[j], out)
+    return out
+
+
+def chunk_places(found, other, t, seg, m):
+    out = jnp.full_like(t, -1)
+    for k in range(NZ):
+        a = found[other * NZ + k]
+        have = jnp.clip(a.live - m * a.size, 0, a.size)
+        prompt = jnp.where(t < have, a.offset + t, -1)
+        decode = jnp.where((t < QROWS + DEC) & (a.z == m), CHUNK + a.core * DEC + t - QROWS, -1)
+        out = jnp.where(seg == k, jnp.where(t < QROWS, prompt, decode), out)
+    return out
+
+
+def packed_places(a, j, h, m, core):
+    i = h & (PLEN - 1)
+    starts = [0, a.lens[0], a.lens[0] + a.lens[1]]
+    index = by_slot(h, starts) + i
+    quarter = sum((index >= q * a.size).astype(jnp.int32) for q in range(1, NM))
+    spot = jnp.bitwise_xor(quarter, m) * CHUNK + a.offset + index - quarter * a.size
+    half = 2 * CHUNK
+    spot = jnp.bitwise_xor(spot >> 8, core) * half + (spot & (half - 1))
+    prompt = jnp.where(i < by_slot(h, a.lens), spot, -1)
+    first = SLOTS * PLEN
+    decode = jnp.where(h < first + DEC, NM * CHUNK + j * DEC + h - first, -1)
+    return jnp.where(h < first, prompt, decode)
+
+
+def home_adapters(a, h):
+    out = by_slot(h, a.adapters)
+    for j in range(DEC):
+        out = jnp.where(h == SLOTS * PLEN + j, a.adapters[SLOTS + j], out)
+    return out
+
+
+def deal_kernel(s_ref, x_ref, *outs):
+    len0, len1, len2, z, m = [s_ref[i] for i in range(5)]
+    size = (len0 + len1 + len2 + 3) >> 2
+    rows, cols = x_ref.shape
+    prompt_rows = SLOTS * PLEN
+    t, h = iota((BLK, rows), 0), iota((BLK, rows), 1)
+    slot, i = h >> 5, h & (PLEN - 1)
+    start = jnp.where(slot == 0, 0, jnp.where(slot == 1, len0, len0 + len1))
+    length = jnp.where(slot == 0, len0, jnp.where(slot == 1, len1, len2))
+    live = (i < length) & (h < prompt_rows) & (t < size)
+    x = x_ref[...]
+    wide = x.astype(F32)
+    mean = jnp.sum(wide, axis=1, keepdims=True) / cols
+    spread = jnp.sum((wide - mean) ** 2, axis=1, keepdims=True)
+    lane = iota((rows, LANES), 1)
+    stats = jnp.zeros((rows, LANES), F32)
+    for j, term in enumerate(three(mean) + three(spread)):
+        stats = jnp.where(lane == 2 + j, term, stats)
+    same = (iota((rows, LANES), 0) == lane).astype(BF)
+    turned = lax.dot_general(stats.astype(BF), same, (((0,), (0,)), ((), ())), preferred_element_type=F32)
+    turned = jnp.concatenate([jnp.zeros((8, LANES), F32), turned[:8]], axis=0)
+    for k, out in enumerate(outs):
+        q = jnp.bitwise_xor(m, k)
+        mine = live & (start + i - q * size == t)
+        decode = (h >= prompt_rows) & (t == QROWS + h - prompt_rows) & (q == z)
+        y = jnp.dot((mine | decode).astype(BF), x, preferred_element_type=F32)
+        out[...] = y.astype(BF)
+        out[16:32, :LANES] = (y[16:32, :LANES] + turned).astype(BF)
+
+
+def deal(scalars, tokens):
+    return pl.pallas_call(
+        deal_kernel,
+        out_shape=[jax.ShapeDtypeStruct((BLK, tokens.shape[1]), BF)] * NM,
+        in_specs=[SMEM, VMEM],
+        out_specs=[VMEM] * NM,
+        compiler_params=limit(24),
+        cost_estimate=SMALL,
+        name="deal_rows",
+    )(scalars, tokens)
+
+
+def norm_kernel(s_ref, b0, b1, b2, b3, gain_ref, shift_ref, table_ref, _, __, o0, o1, o2, o3, held):
+    z, m = s_ref[3], s_ref[4]
+    cols = b0.shape[1]
+    for k, ref in enumerate((b0, b1, b2, b3)):
+        held[k] = ref[...].astype(F32)
+    width = NM * cols
+    means, spreads = [], []
+    for k in range(NM):
+        part = held[k, 24:32, :LANES]
+        means.append(part[2:3] + part[3:4] + part[4:5])
+        spreads.append(part[5:6] + part[6:7] + part[7:8])
+    mean = sum(means) / NM
+    var = (sum(spreads) + cols * sum((v - mean) ** 2 for v in means)) / width
+    row = iota((BLK, LANES), 0)
+    extra = []
+    for value in (mean, lax.rsqrt(var + 1e-05)):
+        block = jnp.zeros((BLK, LANES), F32)
+        for j, term in enumerate(three(value)):
+            block = jnp.where(row == STAT_ROW + j, term, block)
+        extra.append(block)
+    extra = jnp.concatenate(extra, axis=1)
+    extra = jnp.where(iota(extra.shape, 0) == BLK - 1, table_ref[:, : 2 * LANES], extra)
+    mean = sum(jnp.sum(held[k], axis=1, keepdims=True) for k in range(NM)) / width
+    var = sum(jnp.sum((held[k] - mean) ** 2, axis=1, keepdims=True) for k in range(NM)) / width
+    rstd = lax.rsqrt(var + 1e-05)
+    last = iota((BLK, cols), 0) == BLK - 1
+    stats = iota((BLK, 2 * LANES), 0) >= STAT_ROW
+    for k, out in enumerate((o0, o1, o2, o3)):
+        block = jnp.bitwise_xor(z, k)
+        x = held[jnp.bitwise_xor(block, m)]
+        y = (x - mean) * rstd * gain_ref[block] + shift_ref[block]
+        y = jnp.where(last, table_ref[...], y)
+        out[...] = y.astype(BF)
+        out[:, : 2 * LANES] = jnp.where(stats, extra, y[:, : 2 * LANES]).astype(BF)
+
+
+def norm_rows(scalars, blocks, gain, shift, table, near, far):
+    return pl.pallas_call(
+        norm_kernel,
+        out_shape=[jax.ShapeDtypeStruct(blocks[0].shape, BF)] * NZ,
+        in_specs=[SMEM] + [VMEM] * 7 + [ANY] * 2,
+        out_specs=[VMEM] * NZ,
+        scratch_shapes=[pltpu.VMEM((NM,) + blocks[0].shape, F32)],
+        compiler_params=limit(32),
+        cost_estimate=SMALL,
+        name="norm_rows",
+    )(scalars, *blocks, gain, shift, table, near, far)
+
+
+def pack_kernel(s_ref, t_ref, a_ref, b_ref, o_ref):
+    found = sources(s_ref, t_ref)
+    half = a_ref.shape[0]
+    lane = iota((1, half), 1)
+    total = None
+    for other, ref in enumerate((a_ref, b_ref)):
+        to = chunk_places(found, other, lane & (BLK - 1), lane // BLK, s_ref[4])
+        pick = (iota((o_ref.shape[0], half), 0) == to).astype(BF)
+        term = jnp.dot(pick, ref[...], preferred_element_type=F32)
+        total = term if total is None else total + term
+    o_ref[...] = total.astype(BF)
+
+
+def pack_rows(scalars, tables, mine, theirs):
+    return pl.pallas_call(
+        pack_kernel,
+        out_shape=jax.ShapeDtypeStruct((CHUNK + DCH, mine.shape[1]), BF),
+        in_specs=[SMEM] * 2 + [VMEM] * 2,
+        out_specs=VMEM,
+        compiler_params=limit(16),
+        cost_estimate=SMALL,
+        name="pack_rows",
+    )(scalars, tables, mine, theirs)
+
+
+def code_kernel(s_ref, t_ref, col_ref, row_ref):
+    found = sources(s_ref, t_ref)
+    m, core = s_ref[4], s_ref[6]
+    n = NM * CHUNK
+    lane, sub = iota((1, LANES), 1), iota((LANES, 1), 0)
+    down, across = iota((n, LANES), 0), iota((LANES, n), 1)
+    cols, rows = jnp.zeros((n, 1), jnp.int32), jnp.zeros((1, n), jnp.int32)
+    for j, a in enumerate(found):
+        first = a.index * SLOTS * PLEN + 1
+        hit = down == packed_places(a, j, lane, m, core)
+        cols = cols + jnp.sum(jnp.where(hit, first + lane, 0), axis=1, keepdims=True)
+        hit = across == packed_places(a, j, sub, m, core)
+        rows = rows + jnp.sum(jnp.where(hit, first + sub, 0), axis=0, keepdims=True)
+    unused = (1 << 16) + PLEN * iota((n, 1), 0)
+    col_ref[...] = jnp.where(cols > 0, cols - 1, unused)
+    unused = (1 << 16) + PLEN * iota((1, n), 1)
+    row_ref[...] = jnp.where(rows > 0, rows - 1, unused)
+
+
+def packed_codes(scalars, tables):
+    n = NM * CHUNK
+    return pl.pallas_call(
+        code_kernel,
+        out_shape=[jax.ShapeDtypeStruct((n, 1), jnp.int32), jax.ShapeDtypeStruct((1, n), jnp.int32)],
+        in_specs=[SMEM] * 2,
+        out_specs=[VMEM] * 2,
+        compiler_params=limit(16),
+        cost_estimate=SMALL,
+        name="packed_codes",
+    )(scalars, tables)
+
+
+def rank_kernel(s_ref, table_ref, da_ref, db_ref, x0, x1, x2, x3, t0, t1, t2, t3, gain_ref, shift_ref, o_ref):
+    m, r = s_ref[4], s_ref[5]
+    width = 2 * ADAPTER_RANK
+    count = da_ref.shape[0] // width
+    rows = x0.shape[0]
+    same = (iota((rows, LANES), 0) == iota((rows, LANES), 1)).astype(BF)
+    o_ref[...] = jnp.zeros_like(o_ref)
+    for k, (x, stats) in enumerate(zip((x0, x1, x2, x3), (t0, t1, t2, t3))):
+
+        def column(at):
+            turned = lax.dot_general(
+                same, stats[16:32, at], (((1,), (1,)), ((), ())), preferred_element_type=F32
+            )
+            j = STAT_ROW - 16
+            return turned[:, j : j + 1] + turned[:, j + 1 : j + 2] + turned[:, j + 2 : j + 3]
+
+        mean, rstd = column(slice(0, LANES)), column(slice(LANES, 2 * LANES))
+        normed = ((x[...].astype(F32) - mean) * rstd * gain_ref[m] + shift_ref[m]).astype(BF)
+        ids = home_adapters(Source(s_ref, table_ref, k), iota((1, rows), 1))
+        total = jnp.zeros((width, rows), F32)
+        for core, d in enumerate((da_ref, db_ref)):
+            y = lax.dot_general(d[...], normed, (((1,), (1,)), ((), ())), preferred_element_type=F32)
+            first = jnp.bitwise_xor(r, core) * count
+            for a in range(count):
+                total = total + jnp.where(ids == first + a, y[a * width : (a + 1) * width], 0.0)
+        o_ref[:, k * LANES : k * LANES + rows] = total
+
+
+def low_rank_rows(scalars, tables, down, down_other, pieces, stats, gain, shift):
+    return pl.pallas_call(
+        rank_kernel,
+        out_shape=jax.ShapeDtypeStruct((2 * ADAPTER_RANK, NZ * LANES), F32),
+        in_specs=[SMEM] * 2 + [VMEM] * 12,
+        out_specs=VMEM,
+        compiler_params=limit(32),
+        cost_estimate=SMALL,
+        name="low_rank_rows",
+    )(scalars, tables, down, down_other, *pieces, *stats, gain, shift)
+
+
+def expand_kernel(s_ref, t_ref, low_ref, low_other_ref, _, o_ref, *, count):
+    m, r, core = s_ref[4], s_ref[5], s_ref[6]
+    found = sources(s_ref, t_ref)
+    width = count * ADAPTER_RANK
+    repeat = []
+    for t in range(2):
+        shape = (width, 2 * ADAPTER_RANK)
+        repeat.append((iota(shape, 1) == t * ADAPTER_RANK + iota(shape, 0) % ADAPTER_RANK).astype(BF))
+    repeat = jnp.concatenate(repeat, axis=0)
+    adapter = r * count + (iota((2 * width, LANES), 0) % width) // ADAPTER_RANK
+    lane = iota((1, LANES), 1)
+    total = jnp.zeros((PACKED, 2 * width), F32)
+    for j, a in enumerate(found):
+        ref = low_other_ref if j >= NZ else low_ref
+        k = j % NZ
+        low = jnp.dot(repeat, ref[:, k * LANES : (k + 1) * LANES], preferred_element_type=F32)
+        low = jnp.where(adapter == home_adapters(a, lane), low, 0.0).astype(BF)
+        hit = (iota((PACKED, LANES), 0) == packed_places(a, j, lane, m, core)).astype(BF)
+        total = total + lax.dot_general(hit, low, (((1,), (1,)), ((), ())), preferred_element_type=F32)
+    o_ref[0] = total[:, :width].astype(BF)
+    o_ref[1] = total[:, width:].astype(BF)
+
+
+def expand_rows(scalars, tables, low, low_other, count, after):
+    return pl.pallas_call(
+        functools.partial(expand_kernel, count=count),
+        out_shape=jax.ShapeDtypeStruct((2, PACKED, count * ADAPTER_RANK), BF),
+        in_specs=[SMEM] * 2 + [VMEM] * 2 + [ANY],
+        out_specs=VMEM,
+        compiler_params=limit(32),
+        cost_estimate=SMALL,
+        name="expand_rows",
+    )(scalars, tables, low, low_other, after)
+
+
+def emit_sums(y, own_ref, other_ref, dec_ref):
+    half = 2 * CHUNK
+    own_ref[...] = y[:half]
+    other_ref[...] = y[half : 2 * half].astype(BF)
+    dec_ref[...] = y[2 * half :]
+
+
+def first_project_kernel(s_ref, c0, c1, c2, c3, w_ref, _, own_ref, other_ref, dec_ref, x):
+    z, m, core = s_ref[3], s_ref[4], s_ref[6]
+
+    @pl.when(pl.program_id(0) == 0)
+    def _():
+        chunks = (c0, c1, c2, c3)
+        for k, chunk in enumerate(chunks):
+            base = jnp.bitwise_xor(core, k >> 1) * 2 * CHUNK + (k & 1) * CHUNK
+            x[pl.ds(pl.multiple_of(base, CHUNK), CHUNK), :] = chunk[:CHUNK, :]
+        n, at = iota((2 * NZ * DEC, NM * DCH), 0), iota((2 * NZ * DEC, NM * DCH), 1)
+        chip = jnp.bitwise_xor(z, (n >> 1) & 3)
+        want = jnp.bitwise_xor(chip, m) * DCH + jnp.bitwise_xor(core, n >> 3) * DEC + (n & 1)
+        rows = jnp.concatenate([chunk[CHUNK:, :] for chunk in chunks], axis=0)
+        x[NM * CHUNK :, :] = jnp.dot((want == at).astype(BF), rows, preferred_element_type=F32).astype(BF)
+
+    emit_sums(jnp.dot(x[...], w_ref[0], preferred_element_type=F32), own_ref, other_ref, dec_ref)
+
+
+def project_rows(scalars, chunks, weight, part, after):
+    _, depth, feats = weight.shape
+    tile = feats // 2
+    half = 2 * CHUNK
+    whole = [pl.BlockSpec(v.shape, lambda j: (0, 0)) for v in chunks]
+    out_shape = [
+        jax.ShapeDtypeStruct((half, feats), F32),
+        jax.ShapeDtypeStruct((half, feats), BF),
+        jax.ShapeDtypeStruct((PACKED - 2 * half, feats), F32),
+        jax.ShapeDtypeStruct((PACKED, depth), BF),
+    ]
+    out_specs = [pl.BlockSpec((v.shape[0], tile), lambda j: (0, j)) for v in out_shape[:3]]
+    out_specs.append(pl.BlockSpec((PACKED, depth), lambda j: (0, 0)))
+    return pl.pallas_call(
+        first_project_kernel,
+        grid=(feats // tile,),
+        out_shape=out_shape,
+        in_specs=[SMEM] + whole + [pl.BlockSpec((1, depth, tile), lambda j: (part, 0, j)), ANY],
+        out_specs=out_specs,
+        compiler_params=limit(56),
+        cost_estimate=SMALL,
+        name="project_keys",
+    )(scalars, *chunks, weight, after)
+
+
+def adapted_kernel(x_ref, w_ref, e_ref, u_ref, _, *outs):
+    y = jnp.dot(x_ref[...], w_ref[0], preferred_element_type=F32)
+    up = u_ref[...].reshape(-1, u_ref.shape[-1])
+    y = y + jnp.dot(e_ref[0], up, preferred_element_type=F32)
+    emit_sums(y, *outs)
+
+
+def project_adapted(rows, weight, part, expanded, up, after):
+    _, depth, feats = weight.shape
+    tile = feats // 2
+    half = 2 * CHUNK
+    which = part // 2
+    out_shape = [
+        jax.ShapeDtypeStruct((half, feats), F32),
+        jax.ShapeDtypeStruct((half, feats), BF),
+        jax.ShapeDtypeStruct((PACKED - 2 * half, feats), F32),
+    ]
+    return pl.pallas_call(
+        adapted_kernel,
+        grid=(2,),
+        out_shape=out_shape,
+        in_specs=[
+            pl.BlockSpec(rows.shape, lambda j: (0, 0)),
+            pl.BlockSpec((1, depth, tile), lambda j: (part, 0, j)),
+            pl.BlockSpec((1,) + expanded.shape[1:], lambda j: (which, 0, 0)),
+            pl.BlockSpec((up.shape[0], 1, up.shape[2], tile), lambda j: (0, which, 0, j)),
+            ANY,
+        ],
+        out_specs=[pl.BlockSpec((v.shape[0], tile), lambda j: (0, j)) for v in out_shape],
+        compiler_params=limit(56),
+        cost_estimate=SMALL,
+        name="project_adapted",
+    )(rows, weight, expanded, up, after)
+
+
+def split_kernel(q_ref, k_ref, v_ref, _, keep_ref, send_ref):
+    half = keep_ref.shape[0]
+    feats = q_ref.shape[1]
+    for j, ref in enumerate((q_ref, k_ref, v_ref)):
+        at = slice(j * feats, (j + 1) * feats)
+        keep_ref[:, at] = ref[:half, :]
+        send_ref[:, at] = ref[half:, :]
+
+
+def split_decode(parts, after):
+    rows, feats = parts[0].shape
+    out = jax.ShapeDtypeStruct((rows // 2, 3 * feats), F32)
+    return pl.pallas_call(
+        split_kernel,
+        out_shape=[out, out],
+        in_specs=[VMEM] * 3 + [ANY],
+        out_specs=[VMEM] * 2,
+        compiler_params=limit(16),
+        cost_estimate=SMALL,
+        name="split_decode",
+    )(*parts, after)
+
+
+def halve_kernel(s_ref, *refs, bit, groups):
+    *ins, _, send_ref, keep_ref = refs
+    count = len(ins) // 2
+    side = (s_ref[3] >> bit) & 1
+    to = 0
+    for total_ref, got_ref in zip(ins[:count], ins[count:]):
+        width = total_ref.shape[1] // groups // 2
+
+        for g in range(groups):
+
+            def part(which):
+                at = pl.ds(pl.multiple_of((2 * g + which) * width, LANES), width)
+                return total_ref[:, at] + got_ref[:, at].astype(F32)
+
+            send_ref[:, to : to + width] = part(1 - side).astype(BF)
+            keep_ref[:, to : to + width] = part(side)
+            to += width
+
+
+def halve(scalars, totals, gots, bit, after, groups=1):
+    rows = totals[0].shape[0]
+    feats = sum(v.shape[1] for v in totals) // 2
+    return pl.pallas_call(
+        functools.partial(halve_kernel, bit=bit, groups=groups),
+        out_shape=[jax.ShapeDtypeStruct((rows, feats), BF), jax.ShapeDtypeStruct((rows, feats), F32)],
+        in_specs=[SMEM] + [VMEM] * (2 * len(totals)) + [ANY],
+        out_specs=[VMEM, VMEM],
+        compiler_params=limit(16),
+        cost_estimate=SMALL,
+        name="halve_sums",
+    )(scalars, *totals, *gots, after)
+
+
+def finish_kernel(s_ref, total_ref, got_ref, bias_ref, _, *outs, parts):
+    for j, (part, out) in enumerate(zip(parts, outs)):
+        width = out.shape[1]
+        at = pl.ds(pl.multiple_of(place_of(s_ref[3]) * width, LANES), width)
+        mine = slice(j * width, (j + 1) * width)
+        total = total_ref[:, mine] + got_ref[:, mine].astype(F32) + bias_ref[part : part + 1, at]
+        out[...] = total.astype(BF)
+
+
+def finish(scalars, total, got, bias, parts, after):
+    rows, feats = total.shape
+    return pl.pallas_call(
+        functools.partial(finish_kernel, parts=parts),
+        out_shape=[jax.ShapeDtypeStruct((rows, feats // len(parts)), BF)] * len(parts),
+        in_specs=[SMEM, VMEM, VMEM, VMEM, ANY],
+        out_specs=[VMEM] * len(parts),
+        compiler_params=limit(16),
+        cost_estimate=SMALL,
+        name="finish_sums",
+    )(scalars, total, got, bias, after)
+
+
+def prompt_kernel(q_ref, ka_ref, kb_ref, va_ref, vb_ref, cr_ref, cc_ref, d0_ref, d1_ref, o_ref):
+    rows = cr_ref[...]
+    cols = cc_ref[...]
+    allowed = ((rows >> 5) == (cols >> 5)) & (cols <= rows)
+    keys = jnp.concatenate([ka_ref[...], kb_ref[...]], axis=0)
+    values = jnp.concatenate([va_ref[...], vb_ref[...]], axis=0)
+    for h in range(q_ref.shape[1] // HEAD_DIM):
+        at = slice(h * HEAD_DIM, (h + 1) * HEAD_DIM)
+        s = lax.dot_general(q_ref[:, at], keys[:, at], (((1,), (1,)), ((), ())), preferred_element_type=F32)
+        s = jnp.where(allowed, s * HEAD_DIM**-0.5, -1e30)
+        top = jnp.max(s, axis=1, keepdims=True)
+        w = jnp.where(allowed, jnp.exp(s - top), 0.0)
+        w = (w / jnp.sum(w, axis=1, keepdims=True)).astype(BF)
+        o_ref[: q_ref.shape[0], at] = jnp.dot(w, values[:, at], preferred_element_type=F32).astype(BF)
+    width = q_ref.shape[1]
+    n = iota((DECODE_ROWS, width), 0)
+    tail = jnp.zeros((DECODE_ROWS, width), F32)
+    for b in range(NZ):
+        for j, ref in enumerate((d0_ref, d1_ref)):
+            tail = jnp.where(n == b * DEC + j, ref[:, b * width : (b + 1) * width].astype(F32), tail)
+    o_ref[q_ref.shape[0] :, :] = tail.astype(BF)
+
+
+def prompt_attention(q, ka, kb, va, vb, code_rows, code_cols, dec):
+    return pl.pallas_call(
+        prompt_kernel,
+        out_shape=jax.ShapeDtypeStruct((q.shape[0] + DECODE_ROWS, q.shape[1]), BF),
+        in_specs=[VMEM] * 9,
+        out_specs=VMEM,
+        compiler_params=limit(32),
+        cost_estimate=SMALL,
+        name="prompt_attention",
+    )(q, ka, kb, va, vb, code_rows, code_cols, *dec)
+
+
+def decode_kernel(len_ref, q_ref, k_ref, v_ref, c_ref, _, o_ref, qbd, top, total, acc):
+    t = pl.program_id(0)
+    span = c_ref.shape[1]
+    live = len_ref[0]
+    heads, feats = qbd.shape
+    diag = lax.broadcasted_iota(jnp.int32, (heads, feats), 1) // HEAD_DIM == lax.broadcasted_iota(
+        jnp.int32, (heads, feats), 0
+    )
+
+    @pl.when(t == 0)
+    def _():
+        q = jnp.where(diag, q_ref[0].astype(F32), 0.0)
+        qbd[...] = q.astype(BF)
+        own = jnp.sum(q * k_ref[0].astype(F32), axis=1, keepdims=True) * HEAD_DIM**-0.5
+        top[...] = jnp.broadcast_to(own, top.shape)
+        total[...] = jnp.ones_like(total)
+        acc[...] = jnp.broadcast_to(v_ref[0].astype(F32), acc.shape)
+
+    @pl.when(t * span < live)
+    def _():
+        x = c_ref[0].reshape(2 * span, feats)
+        s = lax.dot_general(qbd[...], x, (((1,), (1,)), ((), ())), preferred_element_type=F32)
+        column = lax.broadcasted_iota(jnp.int32, s.shape, 1)
+        valid = (column % 2 == 0) & (t * span + column // 2 < live)
+        s = jnp.where(valid, s * HEAD_DIM**-0.5, -1e30)
+        before = top[:, :1]
+        now = jnp.maximum(before, jnp.max(s, axis=1, keepdims=True))
+        fade = jnp.exp(before - now)
+        w = jnp.where(valid, jnp.exp(s - now), 0.0)
+        total[...] = total[...] * fade + jnp.sum(w, axis=1, keepdims=True)
+        top[...] = jnp.broadcast_to(now, top.shape)
+        w = pltpu.roll(w, 1, 1).astype(BF)
+        acc[...] = acc[...] * fade + jnp.dot(w, x, preferred_element_type=F32)
+
+    @pl.when(t == pl.num_programs(0) - 1)
+    def _():
+        o = acc[...] / total[:, :1]
+        o_ref[0] = jnp.sum(jnp.where(diag, o, 0.0), axis=0, keepdims=True).astype(BF)
+
+
+def decode_attention(length, q, k, v, cache, which, after, span=256):
+    _, positions, _, feats = cache.shape
+    row = pl.BlockSpec((1, 1, feats), lambda t, n: (0, 0, 0))
+    heads = 16
+    return pl.pallas_call(
+        decode_kernel,
+        grid_spec=pltpu.PrefetchScalarGridSpec(
+            num_scalar_prefetch=1,
+            grid=(positions // span,),
+            in_specs=[row, row, row]
+            + [pl.BlockSpec((1, span, 2, feats), lambda t, n: (which, jnp.minimum(t, (n[0] - 1) // span), 0, 0)), ANY],
+            out_specs=row,
+            scratch_shapes=[
+                pltpu.VMEM((heads, feats), BF),
+                pltpu.VMEM((heads, LANES), F32),
+                pltpu.VMEM((heads, LANES), F32),
+                pltpu.VMEM((heads, feats), F32),
+            ],
+        ),
+        out_shape=jax.ShapeDtypeStruct((1, 1, feats), BF),
+        compiler_params=limit(32),
+        cost_estimate=SMALL,
+        name="decode_attention",
+    )(length, q, k, v, cache, after)
+
+
+def out_kernel(place_ref, *refs):
+    own, other, w_ref, outs, mixed = refs[:4], refs[4:8], refs[8], refs[9:13], refs[13]
+    z, m, core = place_ref[3], place_ref[4], place_ref[6]
+    width = own[0].shape[1]
+    half = own[0].shape[0] - DECODE_ROWS
+    total = None
+    for k in range(NZ):
+        block = place_of(jnp.bitwise_xor(z, k))
+        w = w_ref[pl.ds(pl.multiple_of(block * width, width), width), :]
+        rows = jnp.concatenate([own[k][:half, :], other[k][:half, :]], axis=0)
+        term = jnp.dot(rows, w, preferred_element_type=F32)
+        total = term if total is None else total + term
+    mixed[...] = total.astype(BF)
+    tails = jnp.concatenate([v[half:, :] for v in own + other], axis=0)
+    count = 2 * NZ * DEC
+    n, at = iota((count, tails.shape[0]), 0), iota((count, tails.shape[0]), 1)
+    total = None
+    for b in range(NZ):
+        pick = (at == (n // DEC) * DECODE_ROWS + b * DEC + n % DEC).astype(BF)
+        rows = jnp.dot(pick, tails, preferred_element_type=F32).astype(BF)
+        term = jnp.dot(rows, w_ref[b * width : (b + 1) * width, :], preferred_element_type=F32)
+        total = term if total is None else total + term
+    decode = total.astype(BF)
+    n, at = iota((DCH, count), 0), iota((DCH, count), 1)
+    for k, out in enumerate(outs):
+        base = jnp.bitwise_xor(core, k >> 1) * 2 * CHUNK + (k & 1) * CHUNK
+        out[:CHUNK, :] = mixed[pl.ds(pl.multiple_of(base, CHUNK), CHUNK), :]
+        far = jnp.bitwise_xor(jnp.bitwise_xor(m, k), z)
+        want = (jnp.bitwise_xor(core, n >> 1) * NZ + far) * DEC + (n & 1)
+        pick = ((at == want) & (n < 2 * DEC)).astype(BF)
+        out[CHUNK:, :] = jnp.dot(pick, decode, preferred_element_type=F32).astype(BF)
+
+
+def out_project(scalars, own, other, weight):
+    feats = weight.shape[1]
+    return pl.pallas_call(
+        out_kernel,
+        out_shape=[jax.ShapeDtypeStruct((CHUNK + DCH, feats), BF)] * NM,
+        in_specs=[SMEM] + [VMEM] * 9,
+        out_specs=[VMEM] * NM,
+        scratch_shapes=[pltpu.VMEM((NM * CHUNK, feats), BF)],
+        compiler_params=limit(40),
+        cost_estimate=SMALL,
+        name="out_project",
+    )(scalars, *own, *other, weight)
+
+
+def unpack_kernel(s_ref, t_ref, c0, c1, c2, c3, *outs):
+    total = sum(c[...].astype(F32) for c in (c0, c1, c2, c3)).astype(BF)
+    found = sources(s_ref, t_ref)
+    n = iota((NZ * BLK, 1), 0)
+    for other in range(2):
+        to = chunk_places(found, other, n & (BLK - 1), n // BLK, s_ref[4])
+        pick = (iota((NZ * BLK, total.shape[0]), 1) == to).astype(BF)
+        rows = jnp.dot(pick, total, preferred_element_type=F32).astype(BF)
+        for k, out in enumerate(outs):
+            out[other * BLK : (other + 1) * BLK, :] = rows[k * BLK : (k + 1) * BLK]
+
+
+def unpack_rows(scalars, tables, chunks):
+    feats = chunks[0].shape[1]
+    return pl.pallas_call(
+        unpack_kernel,
+        out_shape=[jax.ShapeDtypeStruct((2 * BLK, feats), BF)] * NZ,
+        in_specs=[SMEM] * 2 + [VMEM] * 4,
+        out_specs=[VMEM] * NZ,
+        compiler_params=limit(16),
+        cost_estimate=SMALL,
+        name="unpack_rows",
+    )(scalars, tables, *chunks)
+
+
+def join_kernel(s_ref, a0, a1, a2, a3, other_ref, o0, o1, o2, o3, held):
+    z, m, core = s_ref[3], s_ref[4], s_ref[6]
+    width = a0.shape[1]
+    mine = pl.ds(pl.multiple_of(core * width, LANES), width)
+    theirs = pl.ds(pl.multiple_of((1 - core) * width, LANES), width)
+    for k, ref in enumerate((a0, a1, a2, a3)):
+        held[k, :, mine] = ref[:BLK, :]
+        held[k, :, theirs] = other_ref[k * BLK : (k + 1) * BLK, :]
+    for k, out in enumerate((o0, o1, o2, o3)):
+        out[...] = held[jnp.bitwise_xor(jnp.bitwise_xor(z, m), k)]
+
+
+def join_halves(scalars, parts, other):
+    shape = (BLK, 2 * parts[0].shape[1])
+    return pl.pallas_call(
+        join_kernel,
+        out_shape=[jax.ShapeDtypeStruct(shape, BF)] * NM,
+        in_specs=[SMEM] + [VMEM] * 5,
+        out_specs=[VMEM] * NM,
+        scratch_shapes=[pltpu.VMEM((NZ,) + shape, BF)],
+        compiler_params=limit(16),
+        cost_estimate=SMALL,
+        name="join_halves",
+    )(scalars, *parts, other)
+
+
+def home_kernel(s_ref, x_ref, bias_ref, b0, b1, b2, b3, o_ref):
+    len0, len1, len2, z, m = [s_ref[i] for i in range(5)]
+    size = (len0 + len1 + len2 + 3) >> 2
+    rows = x_ref.shape[0]
+    prompt_rows = SLOTS * PLEN
+    t, h = iota((rows, BLK), 1), iota((rows, BLK), 0)
+    slot, i = h >> 5, h & (PLEN - 1)
+    start = jnp.where(slot == 0, 0, jnp.where(slot == 1, len0, len0 + len1))
+    length = jnp.where(slot == 0, len0, jnp.where(slot == 1, len1, len2))
+    live = (i < length) & (h < prompt_rows) & (t < size)
+    total = x_ref[...].astype(F32) + bias_ref[...]
+    for k, ref in enumerate((b0, b1, b2, b3)):
+        q = jnp.bitwise_xor(m, k)
+        mine = live & (start + i - q * size == t)
+        decode = (h >= prompt_rows) & (t == QROWS + h - prompt_rows) & (q == z)
+        total = total + jnp.dot((mine | decode).astype(BF), ref[...], preferred_element_type=F32)
+    o_ref[...] = total.astype(BF)
+
+
+def add_home(scalars, tokens, bias, blocks):
+    return pl.pallas_call(
+        home_kernel,
+        out_shape=jax.ShapeDtypeStruct(tokens.shape, BF),
+        in_specs=[SMEM] + [VMEM] * 6,
+        out_specs=VMEM,
+        compiler_params=limit(24),
+        cost_estimate=SMALL,
+        name="add_home",
+    )(scalars, tokens, bias, *blocks)
+
+
+def place_of(z):
+    return (z & 1) * 2 + (z >> 1)
+
+
+def packed_device(
+    tokens,
+    layernorm_scale,
+    layernorm_bias,
+    query_key_value_weight,
+    query_key_value_bias,
+    adapter_down_weight,
+    adapter_up_weight,
+    adapter_index_table,
+    prompt_length_list,
+    cache,
+    cache_length_list,
+    output_weight,
+    output_bias,
+):
+    i32 = jnp.int32
+    r = lax.axis_index("req").astype(i32)
+    m = lax.axis_index("mp").astype(i32)
+    z, c = r >> 1, r & 1
+    rows_dev, cols = tokens.shape
+    prompt_rows = SLOTS * PLEN
+    feats = query_key_value_weight.shape[2]
+    depth = query_key_value_weight.shape[1]
+    per_z = feats // NZ
+    own_adapters = adapter_down_weight.shape[0]
+    half = 2 * CHUNK
+    order = jnp.arange(2 * NZ, dtype=i32)
+    source = ((z ^ (order & 3)) << 1) + (c ^ (order >> 2))
+    lens = prompt_length_list
+    scalars = jnp.concatenate([lens, jnp.stack([z, m, r, c])])
+
+    down = jnp.transpose(adapter_down_weight, (0, 2, 1)).reshape(own_adapters * 2 * ADAPTER_RANK, cols)
+    down_other = swap_req(down, 1)
+
+    with jax.named_scope("gather_home"):
+        pieces = gather_z(tokens)
+
+    with jax.named_scope("deal"):
+        dealt = deal(scalars, tokens)
+        blocks = [dealt[0]] + [swap_mp(dealt[k], k) for k in range(1, NM)]
+    with jax.named_scope("norm_rows"):
+        table = jnp.concatenate([lens, adapter_index_table[0]]).astype(F32)
+        table = jnp.pad(table, (0, depth - table.shape[0]))
+        table = jnp.tile(table, 2)[None, :]
+        gain = layernorm_scale.reshape(NM, 1, cols)
+        shift = layernorm_bias.reshape(NM, 1, cols)
+        normed = norm_rows(scalars, blocks, gain, shift, table, pieces[1], pieces[2])
+    with jax.named_scope("spread_z"):
+        spread = [normed[0]] + [swap_req(normed[k], 2 * k) for k in range(1, NZ)]
+        rows = jnp.concatenate(spread, axis=0)
+        mine = lax.dynamic_slice_in_dim(rows, c * depth, depth, 1)
+        theirs = swap_req(lax.dynamic_slice_in_dim(rows, (1 - c) * depth, depth, 1), 1)
+
+    with jax.named_scope("tables"):
+        tables = jnp.concatenate(
+            [v.reshape(NZ, BLK, depth)[:, BLK - 1, : SLOTS + SLOTS + DEC] for v in (mine, theirs)], axis=0
+        ).astype(i32)
+    with jax.named_scope("pack"):
+        chunk = pack_rows(scalars, tables, mine, theirs)
+    with jax.named_scope("gather_chunks"):
+        chunks = gather_mp(chunk)
+
+    with jax.named_scope("codes"):
+        code_col, code_row = packed_codes(scalars, tables)
+
+    with jax.named_scope("low_rank"):
+        part = low_rank_rows(scalars, tables, down, down_other, pieces, spread, gain, shift)
+        two = part + swap_mp(part, 1)
+        low_rank = (two + swap_mp(two, 2)).astype(BF)
+    with jax.named_scope("keys"):
+        own_k, other_k, dec_k, x_rows = project_rows(scalars, chunks, query_key_value_weight, 1, part)
+        send_k, keep_k = halve(scalars, [own_k], [swap_req(other_k, 1)], 0, other_k)
+        got_k = swap_req(send_k, 2)
+    with jax.named_scope("low_rank"):
+        expanded = expand_rows(scalars, tables, low_rank, swap_req(low_rank, 1), own_adapters, send_k)
+    with jax.named_scope("values"):
+        own_v, other_v, dec_v = project_adapted(x_rows, query_key_value_weight, 2, expanded, adapter_up_weight, send_k)
+        core_v = swap_req(other_v, 1)
+    with jax.named_scope("keys"):
+        send_k, keep_k = halve(scalars, [keep_k], [got_k], 1, other_v)
+        got_k = swap_req(send_k, 4)
+    with jax.named_scope("queries"):
+        own_q, other_q, dec_q = project_adapted(x_rows, query_key_value_weight, 0, expanded, adapter_up_weight, send_k)
+        core_q = swap_req(other_q, 1)
+    with jax.named_scope("keys"):
+        (keys,) = finish(scalars, keep_k, got_k, query_key_value_bias, (1,), keep_k)
+        keys_other = swap_req(keys, 1)
+    with jax.named_scope("values_queries"):
+        send, keep = halve(scalars, [own_v, own_q], [core_v, core_q], 0, keys)
+        got = swap_req(send, 2)
+    with jax.named_scope("decode_rows"):
+        dec, dec_sent = split_decode((dec_q, dec_k, dec_v), send)
+        dec = dec + swap_req(dec_sent, 1)
+        for bits in (4, 2):
+            count = dec.shape[0] // 2
+            dec = dec[:count] + swap_req(dec[count:], bits)
+        dec = (dec.reshape(DEC, 3, feats) + query_key_value_bias[None]).astype(BF)
+
+    def decode_one(j, after):
+        return decode_attention(
+            cache_length_list[j : j + 1], dec[j : j + 1, 0:1], dec[j : j + 1, 1:2], dec[j : j + 1, 2:3], cache, j, after
+        ).reshape(1, feats)
+
+    with jax.named_scope("decode_attention"):
+        dec_first = decode_one(0, send)
+    with jax.named_scope("values_queries"):
+        send, keep = halve(scalars, [keep], [got], 1, dec_first, groups=2)
+        got = swap_req(send, 4)
+    with jax.named_scope("decode_attention"):
+        dec_second = decode_one(1, send)
+    with jax.named_scope("values_queries"):
+        values, queries = finish(scalars, keep, got, query_key_value_bias, (2, 0), dec_second)
+        values_other = swap_req(values, 1)
+    with jax.named_scope("prompt_attention"):
+        attended = prompt_attention(
+            queries,
+            keys,
+            keys_other,
+            values,
+            values_other,
+            code_col[: 2 * CHUNK],
+            code_row,
+            (dec_first, dec_second),
+        )
+    with jax.named_scope("gather_attended"):
+        own = gather_z(attended)
+        other = [swap_req(v, 1) for v in own]
+    with jax.named_scope("out_project"):
+        mixed = out_project(scalars, own, other, output_weight)
+    with jax.named_scope("sum_mp"):
+        shares = [mixed[0]] + [swap_mp(mixed[k], k) for k in range(1, NM)]
+    with jax.named_scope("return_z"):
+        back = unpack_rows(scalars, tables, shares)
+        back = [back[0]] + [swap_req(back[k], 2 * k) for k in range(1, NZ)]
+        back_other = swap_req(jnp.concatenate([v[BLK:] for v in back], axis=0), 1)
+    with jax.named_scope("return_plane"):
+        joined = join_halves(scalars, back, back_other)
+        joined = [joined[0]] + [swap_mp(joined[k], k) for k in range(1, NM)]
+        return add_home(scalars, tokens, output_bias[None], joined)
 
 
 def layer_norm(row_data, gain_vec, shift_vec):
@@ -169,6 +1043,7 @@
         P("mp", "req"),
         P("mp"),
     )
+    quick = mesh.shape["req"] == 2 * NZ and mesh.shape["mp"] == NM
     return jax.shard_map(
-        on_device, mesh=mesh, in_specs=placed, out_specs=P("req", "mp"), check_vma=False
-    )
+        packed_device if quick else on_device, mesh=mesh, in_specs=placed, out_specs=P("req", "mp"), check_vma=False
+    )

time: 812 us -> 230 us (0.28)
  waiting for transfers between devices: 459 us -> 121 us
  local copies, waits for them, and re-layouts: 188 us -> 12.8 us
  blocking collectives: 58.5 us -> 0 us
  Pallas kernels: 0 us -> 51.6 us
  matrix products: 46 us -> 0 us
  starting transfers between devices: 12.7 us -> 42.8 us
  other arithmetic: 24.9 us -> 0.88 us
  between operations: 14.6 us -> 0.53 us
    all_gather x2 -> x0, waiting for transfers between devices: 191 us -> none  [the longest x1 156 us: on_device(): lax.all_gather(output_weight, 'req', axis=1, tiled=True)]
    unnamed x5 -> x0, waiting for transfers between devices: 135 us -> none
    ppermute x0 -> x46, waiting for transfers between devices: none -> 121 us  [the longest x32 90.6 us: swap_req(): return lax.ppermute(x, 'req', [(i, i ^ bits) for i in range(2 * NZ)])]
    unnamed x39 -> x65, local copies, waits for them, and re-layouts: 121 us -> 11.2 us
    all_to_all x3 -> x0, waiting for transfers between devices: 103 us -> none  [the longest x1 99.5 us: on_device(): lax.all_to_all(outgoing, 'req', split_axis=0, concat_axis=0, tiled=True)]
    slice x5 -> x11, local copies, waits for them, and re-layouts: 53.4 us -> 0.7 us  [the longest x1 0.58 us: decode_one(): cache_length_list[j:j + 1]]
    pallas_call x0 -> x23, Pallas kernels: none -> 51.6 us  [the longest x2 10.7 us: decode_attention(): pl.pallas_call(decode_kernel, grid_spec=pltpu.PrefetchScalarGridSpec(num_...]
    dot_general x8 -> x0, matrix products: 46 us -> none  [the longest x1 13.4 us: on_device(): jnp.einsum('rd,cde->rce', spread, query_key_value_weight, preferred_eleme...]
  transfers between devices with their start and end apart: 7 -> 46, of which waited for: 6 -> 32; matrix products, arithmetic and copies ran while one was open for 28% -> 1% of each run, Pallas kernels for 0% -> 15%
where the time goes in v2:
time: 230 us; the launch traced here: 229 us
  waiting for transfers between devices  121 us (53%)
  Pallas kernels  51.6 us (22%)
  starting transfers between devices  42.8 us (19%)
  local copies, waits for them, and re-layouts  12.8 us (6%)
    ppermute x32, waiting for transfers between devices, swap_req(): return lax.ppermute(x, 'req', [(i, i ^ bits) for i in range(2 * NZ)])  90.6 us
    ppermute x14, waiting for transfers between devices, swap_mp(): return lax.ppermute(x, 'mp', [(i, i ^ bits) for i in range(NM)])  30.2 us
    ppermute x32, starting transfers between devices, swap_req(): return lax.ppermute(x, 'req', [(i, i ^ bits) for i in range(2 * NZ)])  25.4 us
    ppermute x14, starting transfers between devices, swap_mp(): return lax.ppermute(x, 'mp', [(i, i ^ bits) for i in range(NM)])  17.4 us
    unnamed x65, local copies, waits for them, and re-layouts  11.2 us
    pallas_call x2, Pallas kernels, decode_attention(): pl.pallas_call(decode_kernel, grid_spec=pltpu.PrefetchScalarGridSpec(num_...  10.7 us
    pallas_call x2, Pallas kernels, project_adapted(): pl.pallas_call(adapted_kernel, grid=(2,), out_shape=out_shape, in_specs=[...  10.5 us
    pallas_call x1, Pallas kernels, project_rows(): pl.pallas_call(first_project_kernel, grid=(feats // tile,), out_shape=out...  4.81 us
  transfers between devices with their start and end apart: 46, of which 32 were waited for; matrix products, arithmetic and copies ran while one was open for 1% of the time, Pallas kernels for 15%

profile of v2, /device:TPU:0, one launch (start us, length us, event | category | flops | bytes accessed | tf_op | source)
XLA Modules:
  0.0 229.4 jit_solution(4314575043213029989)
XLA Ops:
  0.0 4.0 %collective-permute-start.4 = (bf16[98,1792]{1,0:T(8,128)(2,1)}, bf16[98,1792]{1,0:T(8,128)(2,1)S(1)}, u32[]{:S(2)}, u32[]{:S(2)}) collective-permute-start(bf16[98,1792]{1,0:T(8,128)(2,1)} %x_ref.3), channel_id=1, source_target_pairs={{0,16},{4,20},{8,24},{12,28},{16,0},{20,4},{24,8},{28,12},{1,17},{... | collective-permute-start | bytes 1053704 | tf_op jit(solution)/shard_map/gather_home/ppermute | solution.py:33
  4.0 1.6 collective-permute-start.3
  8.5 1.6 collective-permute-start
  10.1 1.5 collective-permute-start.1
  14.0 2.5 %collective-permute-done.1.b2 = bf16[32,1792]{1,0:T(8,128)(2,1)S(1)} collective-permute-done((bf16[32,1792]{1,0:T(8,128)(2,1)S(1)}, bf16[32,1792]{1,0:T(8,128)(2,1)S(1)}, u32[]{:S(2)}, u32[]{:S(2)}) %collective-permute-start.1) | collective-permute-done | bytes 114720 | tf_op jit(solution)/shard_map/deal/ppermute | solution.py:37
  17.3 3.7 %collective-permute-done.4.__.x2 = bf16[98,1792]{1,0:T(8,128)(2,1)S(1)} collective-permute-done((bf16[98,1792]{1,0:T(8,128)(2,1)}, bf16[98,1792]{1,0:T(8,128)(2,1)S(1)}, u32[]{:S(2)}, u32[]{:S(2)}) %collective-permute-start.4) | collective-permute-done | bytes 351264 | tf_op jit(solution)/shard_map/gather_home/ppermute | solution.py:33
  23.8 1.6 collective-permute-start.5
  25.3 2.3 %collective-permute-start.6 = (bf16[32,1792]{1,0:T(8,128)(2,1)S(1)}, bf16[32,1792]{1,0:T(8,128)(2,1)S(1)}, u32[]{:S(2)}, u32[]{:S(2)}) collective-permute-start(bf16[32,1792]{1,0:T(8,128)(2,1)S(1)} %get-tuple-element.55), channel_id=1, source_target_pairs={{0,16},{4,20},{8,24},{12,28},{16,0},{20,4},{24,8},{28,12},{1,17},{... | collective-permute-start | bytes 344072 | tf_op jit(solution)/shard_map/spread_z/ppermute | solution.py:33
  28.3 1.6 collective-permute-done.5.t1
  29.9 7.0 %collective-permute-done.6.t2 = bf16[32,1792]{1,0:T(8,128)(2,1)S(1)} collective-permute-done((bf16[32,1792]{1,0:T(8,128)(2,1)S(1)}, bf16[32,1792]{1,0:T(8,128)(2,1)S(1)}, u32[]{:S(2)}, u32[]{:S(2)}) %collective-permute-start.6) | collective-permute-done | bytes 114720 | tf_op jit(solution)/shard_map/spread_z/ppermute | solution.py:33
  39.6 1.6 collective-permute-start.9
  41.2 1.8 collective-permute-start.13
  42.9 1.5 collective-permute-start.10
  44.5 3.5 %collective-permute-done.9.c1 = bf16[144,896]{1,0:T(8,128)(2,1)S(1)} collective-permute-done((bf16[144,896]{1,0:T(8,128)(2,1)S(1)}, bf16[144,896]{1,0:T(8,128)(2,1)S(1)}, u32[]{:S(2)}, u32[]{:S(2)}) %collective-permute-start.9) | collective-permute-done | bytes 258080 | tf_op jit(solution)/shard_map/gather_chunks/ppermute | solution.py:37
  48.0 1.5 collective-permute-start.11
  49.5 2.2 collective-permute-done.13.x3
  51.7 4.0 %low_rank_rows.1._ = f32[32,512]{1,0:T(8,128)S(1)} custom-call(s32[7]{0:T(128)S(1)} %concatenate.15.s_ref.place_ref, s32[8,8]{1,0:T(8,128)S(1)} %maximum_convert_fusion.t_ref.table_ref, bf16[256,1792]{1,0:T(8,128)(2,1)S(1)} %bitcast.26, bf16[256,1792]{1,0:T(8,128)(2,1)S(1)} %collective-permute-done.12.db_ref, bf16[98,1792]{1,0:T(8,128)(2,1)S(1)} %copy-done.1, ...), custom_call_target="tpu_custom_call" | custom-call | flops 1 | bytes 1 | tf_op jit(solution)/shard_map/low_rank/low_rank_rows/pallas_call | solution.py:300
  57.7 4.8 %project_keys.1 = (f32[256,1536]{1,0:T(8,128)}, bf16[256,1536]{1,0:T(8,128)(2,1)}, f32[16,1536]{1,0:T(8,128)}, bf16[528,896]{1,0:T(8,128)(2,1)}) custom-call(s32[7]{0:T(128)} %copy-done.17, bf16[144,896]{1,0:T(8,128)(2,1)} %copy-done.8, bf16[144,896]{1,0:T(8,128)(2,1)} %copy-done.24, bf16[144,896]{1,0:T(8,128)(2,1)} %copy-done.25, ...), custom_call_target="tpu_custom_call" | custom-call | flops 1 | bytes 1 | tf_op jit(solution)/shard_map/keys/project_keys/pallas_call | solution.py:384
  62.5 2.5 %collective-permute-done.17.refs_1_ = bf16[256,1536]{1,0:T(8,128)(2,1)S(1)} collective-permute-done((bf16[256,1536]{1,0:T(8,128)(2,1)}, bf16[256,1536]{1,0:T(8,128)(2,1)S(1)}, u32[]{:S(2)}, u32[]{:S(2)}) %collective-permute-start.17) | collective-permute-done | bytes 786464 | tf_op jit(solution)/shard_map/keys/ppermute | solution.py:33
  68.3 1.8 collective-permute-start.18
  70.6 3.7 %collective-permute-done.14 = f32[32,512]{1,0:T(8,128)S(1)} collective-permute-done((f32[32,512]{1,0:T(8,128)S(1)}, f32[32,512]{1,0:T(8,128)S(1)}, u32[]{:S(2)}, u32[]{:S(2)}) %collective-permute-start.14) | collective-permute-done | bytes 65568 | tf_op jit(solution)/shard_map/low_rank/ppermute | solution.py:37
  74.4 1.6 collective-permute-start.15
  76.0 2.8 %collective-permute-done.15 = f32[32,512]{1,0:T(8,128)S(1)} collective-permute-done((f32[32,512]{1,0:T(8,128)S(1)}, f32[32,512]{1,0:T(8,128)S(1)}, u32[]{:S(2)}, u32[]{:S(2)}) %collective-permute-start.15) | collective-permute-done | bytes 65568 | tf_op jit(solution)/shard_map/low_rank/ppermute | solution.py:37
  80.0 2.4 %expand_rows.1.e_ref = bf16[2,528,128]{2,1,0:T(8,128)(2,1)S(1)} custom-call(s32[7]{0:T(128)S(1)} %copy-done.18, s32[8,8]{1,0:T(8,128)S(1)} %maximum_convert_fusion.t_ref.table_ref, bf16[32,512]{1,0:T(8,128)(2,1)S(1)} %add_convert_fusion.low_ref, bf16[32,512]{1,0:T(8,128)(2,1)S(1)} %collective-permute-done.16.low_other_ref, ...), custom_call_target="tpu_custom_call" | custom-call | flops 1 | bytes 1 | tf_op jit(solution)/shard_map/low_rank/expand_rows/pallas_call | solution.py:335
  83.1 5.2 %project_adapted.2 = (f32[256,1536]{1,0:T(8,128)}, bf16[256,1536]{1,0:T(8,128)(2,1)}, f32[16,1536]{1,0:T(8,128)}) custom-call(bf16[528,896]{1,0:T(8,128)(2,1)} %get-tuple-element.57.x_ref, bf16[3,896,1536]{2,1,0:T(8,128)(2,1)} %w_ref.5, bf16[2,528,128]{2,1,0:T(8,128)(2,1)} %copy-done.3, bf16[8,2,16,1536]{3,2,1,0:T(8,128)(2,1)} %u_ref.3, ...), custom_call_target="tpu_custom_call" | custom-call | flops 1 | bytes 1 | tf_op jit(solution)/shard_map/values/project_adapted/pallas_call | solution.py:413
  91.0 5.3 %project_adapted.3 = (f32[256,1536]{1,0:T(8,128)}, bf16[256,1536]{1,0:T(8,128)(2,1)}, f32[16,1536]{1,0:T(8,128)}) custom-call(bf16[528,896]{1,0:T(8,128)(2,1)} %get-tuple-element.57.x_ref, bf16[3,896,1536]{2,1,0:T(8,128)(2,1)} %w_ref.5, bf16[2,528,128]{2,1,0:T(8,128)(2,1)} %copy-done.3, bf16[8,2,16,1536]{3,2,1,0:T(8,128)(2,1)} %u_ref.3, ...), custom_call_target="tpu_custom_call" | custom-call | flops 1 | bytes 1 | tf_op jit(solution)/shard_map/queries/project_adapted/pallas_call | solution.py:413
  97.9 10.6 %collective-permute-done.21.got_ref = bf16[256,384]{1,0:T(8,128)(2,1)S(1)} collective-permute-done((bf16[256,384]{1,0:T(8,128)(2,1)S(1)}, bf16[256,384]{1,0:T(8,128)(2,1)S(1)}, u32[]{:S(2)}, u32[]{:S(2)}) %collective-permute-start.21) | collective-permute-done | bytes 196640 | tf_op jit(solution)/shard_map/keys/ppermute | solution.py:33
  113.1 6.5 %collective-permute-done.24 = f32[4,4608]{1,0:T(4,128)S(1)} collective-permute-done((f32[4,4608]{1,0:T(4,128)S(1)}, f32[4,4608]{1,0:T(4,128)S(1)}, u32[]{:S(2)}, u32[]{:S(2)}) %collective-permute-start.24) | collective-permute-done | bytes 73760 | tf_op jit(solution)/shard_map/decode_rows/ppermute | solution.py:33
  120.4 2.0 collective-permute-start.22
  122.4 1.7 collective-permute-done.25
  124.3 4.5 %decode_attention.2 = bf16[1,1,1536]{2,1,0:T(2,128)(2,1)S(1)} custom-call(s32[1]{0:T(128)} %get-tuple-element.102.len_ref, bf16[1,1,1536]{2,1,0:T(2,128)(2,1)S(1)} %get-tuple-element.100.q_ref, bf16[1,1,1536]{2,1,0:T(2,128)(2,1)S(1)} %get-tuple-element.99.k_ref, bf16[1,1,1536]{2,1,0:T(2,128)(2,1)S(1)} %get-tuple-element.98.v_ref, ...), custom_call_target="tpu_custom_call" | custom-call | flops 1 | bytes 1 | tf_op jit(solution)/shard_map/decode_attention/decode_attention/pallas_call | solution.py:588
  128.8 11.6 %collective-permute-done.22.refs_1_ = bf16[256,1536]{1,0:T(8,128)(2,1)} collective-permute-done((bf16[256,1536]{1,0:T(8,128)(2,1)S(1)}, bf16[256,1536]{1,0:T(8,128)(2,1)}, u32[]{:S(2)}, u32[]{:S(2)}) %collective-permute-start.22) | collective-permute-done | bytes 786464 | tf_op jit(solution)/shard_map/values_queries/ppermute | solution.py:33
  142.7 6.2 %decode_attention.3 = bf16[1,1,1536]{2,1,0:T(2,128)(2,1)S(1)} custom-call(s32[1]{0:T(128)} %get-tuple-element.101.len_ref, bf16[1,1,1536]{2,1,0:T(2,128)(2,1)S(1)} %get-tuple-element.97.q_ref, bf16[1,1,1536]{2,1,0:T(2,128)(2,1)S(1)} %get-tuple-element.96.k_ref, bf16[1,1,1536]{2,1,0:T(2,128)(2,1)S(1)} %get-tuple-element.95.v_ref, ...), custom_call_target="tpu_custom_call" | custom-call | flops 1 | bytes 1 | tf_op jit(solution)/shard_map/decode_attention/decode_attention/pallas_call | solution.py:588
  148.9 12.6 %collective-permute-done.26.got_ref = bf16[256,768]{1,0:T(8,128)(2,1)S(1)} collective-permute-done((bf16[256,768]{1,0:T(8,128)(2,1)S(1)}, bf16[256,768]{1,0:T(8,128)(2,1)S(1)}, u32[]{:S(2)}, u32[]{:S(2)}) %collective-permute-start.26) | collective-permute-done | bytes 393248 | tf_op jit(solution)/shard_map/values_queries/ppermute | solution.py:33
  162.2 2.5 %packed_codes.1 = (s32[512,1]{1,0:T(8,128)S(1)}, s32[1,512]{1,0:T(1,128)S(1)}) custom-call(s32[7]{0:T(128)S(1)} %copy-done.18, s32[8,8]{1,0:T(8,128)S(1)} %maximum_convert_fusion.t_ref.table_ref), custom_call_target="tpu_custom_call" | custom-call | flops 1 | bytes 1 | tf_op jit(solution)/shard_map/codes/packed_codes/pallas_call | solution.py:260
  164.7 1.5 prompt_attention.1.refs_0_
  167.7 9.8 %collective-permute-done.30.refs_2_ = bf16[272,384]{1,0:T(8,128)(2,1)S(1)} collective-permute-done((bf16[272,384]{1,0:T(8,128)(2,1)S(1)}, bf16[272,384]{1,0:T(8,128)(2,1)S(1)}, u32[]{:S(2)}, u32[]{:S(2)}) %collective-permute-start.30) | collective-permute-done | bytes 208928 | tf_op jit(solution)/shard_map/gather_attended/ppermute | solution.py:33
  178.4 6.2 %collective-permute-done.31.refs_3_ = bf16[272,384]{1,0:T(8,128)(2,1)S(1)} collective-permute-done((bf16[272,384]{1,0:T(8,128)(2,1)S(1)}, bf16[272,384]{1,0:T(8,128)(2,1)S(1)}, u32[]{:S(2)}, u32[]{:S(2)}) %collective-permute-start.31) | collective-permute-done | bytes 208928 | tf_op jit(solution)/shard_map/gather_attended/ppermute | solution.py:33
  186.1 3.7 %out_project.1 = (bf16[144,896]{1,0:T(8,128)(2,1)S(1)}, bf16[144,896]{1,0:T(8,128)(2,1)S(1)}, bf16[144,896]{1,0:T(8,128)(2,1)S(1)}, bf16[144,896]{1,0:T(8,128)(2,1)S(1)}) custom-call(s32[7]{0:T(128)S(1)} %copy-done.18, bf16[272,384]{1,0:T(8,128)(2,1)S(1)} %prompt_attention.1.refs_0_, bf16[272,384]{1,0:T(8,128)(2,1)S(1)} %collective-permute-done.29.refs_1_, ...), custom_call_target="tpu_custom_call" | custom-call | flops 1 | bytes 1 | tf_op jit(solution)/shard_map/out_project/out_project/pallas_call | solution.py:645
  190.5 1.5 collective-permute-start.37
  193.4 5.6 %collective-permute-done.36.c1 = bf16[144,896]{1,0:T(8,128)(2,1)S(1)} collective-permute-done((bf16[144,896]{1,0:T(8,128)(2,1)S(1)}, bf16[144,896]{1,0:T(8,128)(2,1)S(1)}, u32[]{:S(2)}, u32[]{:S(2)}) %collective-permute-start.36) | collective-permute-done | bytes 258080 | tf_op jit(solution)/shard_map/sum_mp/ppermute | solution.py:37
  199.0 4.1 %collective-permute-done.37.c2 = bf16[144,896]{1,0:T(8,128)(2,1)S(1)} collective-permute-done((bf16[144,896]{1,0:T(8,128)(2,1)S(1)}, bf16[144,896]{1,0:T(8,128)(2,1)S(1)}, u32[]{:S(2)}, u32[]{:S(2)}) %collective-permute-start.37) | collective-permute-done | bytes 258080 | tf_op jit(solution)/shard_map/sum_mp/ppermute | solution.py:37
  203.1 1.6 collective-permute-done.38.c3
  206.0 2.6 %collective-permute-start.40 = (bf16[64,896]{1,0:T(8,128)(2,1)S(1)}, bf16[64,896]{1,0:T(8,128)(2,1)S(1)}, u32[]{:S(2)}, u32[]{:S(2)}) collective-permute-start(bf16[64,896]{1,0:T(8,128)(2,1)S(1)} %get-tuple-element.87), channel_id=1, source_target_pairs={{0,16},{4,20},{8,24},{12,28},{16,0},{20,4},{24,8},{28,12},{1,17},{... | collective-permute-start | bytes 344072 | tf_op jit(solution)/shard_map/return_z/ppermute | solution.py:33
  211.5 5.7 %collective-permute-done.40.a2 = bf16[64,896]{1,0:T(8,128)(2,1)S(1)} collective-permute-done((bf16[64,896]{1,0:T(8,128)(2,1)S(1)}, bf16[64,896]{1,0:T(8,128)(2,1)S(1)}, u32[]{:S(2)}, u32[]{:S(2)}) %collective-permute-start.40) | collective-permute-done | bytes 114720 | tf_op jit(solution)/shard_map/return_z/ppermute | solution.py:33
  223.0 2.5 %collective-permute-done.43.b1 = bf16[32,1792]{1,0:T(8,128)(2,1)S(1)} collective-permute-done((bf16[32,1792]{1,0:T(8,128)(2,1)S(1)}, bf16[32,1792]{1,0:T(8,128)(2,1)S(1)}, u32[]{:S(2)}, u32[]{:S(2)}) %collective-permute-start.43) | collective-permute-done | bytes 114720 | tf_op jit(solution)/shard_map/return_plane/ppermute | solution.py:37
  225.5 2.0 collective-permute-done.44.b2
  227.5 1.8 add_home.1
  (158 shorter events, 48.5 us)
Async XLA Ops:
  0.0 21.0 %collective-permute-start.4 = (bf16[98,1792]{1,0:T(8,128)(2,1)}, bf16[98,1792]{1,0:T(8,128)(2,1)S(1)}, u32[]{:S(2)}, u32[]{:S(2)}) collective-permute-start(bf16[98,1792]{1,0:T(8,128)(2,1)} %x_ref.3), channel_id=1, source_target_pairs={{0,16},{4,20},{8,24},{12,28},{16,0},{20,4},{24,8},{28,12},{1,17},{... | collective-permute-start | bytes 1053704 | tf_op jit(solution)/shard_map/gather_home/ppermute | solution.py:33
  4.0 17.2 %collective-permute-start.3 = (bf16[98,1792]{1,0:T(8,128)(2,1)}, bf16[98,1792]{1,0:T(8,128)(2,1)S(1)}, u32[]{:S(2)}, u32[]{:S(2)}) collective-permute-start(bf16[98,1792]{1,0:T(8,128)(2,1)} %x_ref.3), channel_id=1, source_target_pairs={{0,8},{4,12},{8,0},{12,4},{16,24},{20,28},{24,16},{28,20},{1,9},{5... | collective-permute-start | bytes 1053704 | tf_op jit(solution)/shard_map/gather_home/ppermute | solution.py:33
  7.3 44.3 %copy-start.17 = (s32[7]{0:T(128)}, s32[7]{0:T(128)S(1)}, u32[]{:S(2)}) copy-start(s32[7]{0:T(128)S(1)} %concatenate.15.s_ref.place_ref) | copy-start | bytes 88
  8.5 5.4 %collective-permute-start = (bf16[32,1792]{1,0:T(8,128)(2,1)S(1)}, bf16[32,1792]{1,0:T(8,128)(2,1)S(1)}, u32[]{:S(2)}, u32[]{:S(2)}) collective-permute-start(bf16[32,1792]{1,0:T(8,128)(2,1)S(1)} %get-tuple-element.50), channel_id=1, source_target_pairs={{0,1},{1,0},{2,3},{3,2},{4,5},{5,4},{6,7},{7,6},{8,9},{9,8},{10,11... | collective-permute-start | bytes 344072 | tf_op jit(solution)/shard_map/deal/ppermute | solution.py:37
  10.1 6.4 %collective-permute-start.1 = (bf16[32,1792]{1,0:T(8,128)(2,1)S(1)}, bf16[32,1792]{1,0:T(8,128)(2,1)S(1)}, u32[]{:S(2)}, u32[]{:S(2)}) collective-permute-start(bf16[32,1792]{1,0:T(8,128)(2,1)S(1)} %get-tuple-element.51), channel_id=1, source_target_pairs={{0,2},{1,3},{2,0},{3,1},{4,6},{5,7},{6,4},{7,5},{8,10},{9,11},{10,... | collective-permute-start | bytes 344072 | tf_op jit(solution)/shard_map/deal/ppermute | solution.py:37
  11.6 5.7 %collective-permute-start.2 = (bf16[32,1792]{1,0:T(8,128)(2,1)S(1)}, bf16[32,1792]{1,0:T(8,128)(2,1)S(1)}, u32[]{:S(2)}, u32[]{:S(2)}) collective-permute-start(bf16[32,1792]{1,0:T(8,128)(2,1)S(1)} %get-tuple-element.52), channel_id=1, source_target_pairs={{0,3},{1,2},{2,1},{3,0},{4,7},{5,6},{6,5},{7,4},{8,11},{9,10},{10,... | collective-permute-start | bytes 344072 | tf_op jit(solution)/shard_map/deal/ppermute | solution.py:37
  14.0 37.7 %collective-permute-start.12 = (bf16[256,1792]{1,0:T(8,128)(2,1)}, bf16[256,1792]{1,0:T(8,128)(2,1)S(1)}, u32[]{:S(2)}, u32[]{:S(2)}) collective-permute-start(bf16[256,1792]{1,0:T(8,128)(2,1)} %bitcast.25), channel_id=1, source_target_pairs={{0,4},{4,0},{8,12},{12,8},{16,20},{20,16},{24,28},{28,24},{1,5},{5... | collective-permute-start | bytes 2752520 | tf_op jit(solution)/shard_map/ppermute | solution.py:33
  23.8 6.1 %collective-permute-start.5 = (bf16[32,1792]{1,0:T(8,128)(2,1)S(1)}, bf16[32,1792]{1,0:T(8,128)(2,1)S(1)}, u32[]{:S(2)}, u32[]{:S(2)}) collective-permute-start(bf16[32,1792]{1,0:T(8,128)(2,1)S(1)} %get-tuple-element.54), channel_id=1, source_target_pairs={{0,8},{4,12},{8,0},{12,4},{16,24},{20,28},{24,16},{28,20},{1,9},{5... | collective-permute-start | bytes 344072 | tf_op jit(solution)/shard_map/spread_z/ppermute | solution.py:33
  25.3 11.6 %collective-permute-start.6 = (bf16[32,1792]{1,0:T(8,128)(2,1)S(1)}, bf16[32,1792]{1,0:T(8,128)(2,1)S(1)}, u32[]{:S(2)}, u32[]{:S(2)}) collective-permute-start(bf16[32,1792]{1,0:T(8,128)(2,1)S(1)} %get-tuple-element.55), channel_id=1, source_target_pairs={{0,16},{4,20},{8,24},{12,28},{16,0},{20,4},{24,8},{28,12},{1,17},{... | collective-permute-start | bytes 344072 | tf_op jit(solution)/shard_map/spread_z/ppermute | solution.py:33
  27.7 9.2 %collective-permute-start.7 = (bf16[32,1792]{1,0:T(8,128)(2,1)S(1)}, bf16[32,1792]{1,0:T(8,128)(2,1)S(1)}, u32[]{:S(2)}, u32[]{:S(2)}) collective-permute-start(bf16[32,1792]{1,0:T(8,128)(2,1)S(1)} %get-tuple-element.56), channel_id=1, source_target_pairs={{0,24},{4,28},{8,16},{12,20},{16,8},{20,12},{24,0},{28,4},{1,25},{... | collective-permute-start | bytes 344072 | tf_op jit(solution)/shard_map/spread_z/ppermute | solution.py:33
  37.0 1.6 collective-permute-start.8
  39.6 8.3 %collective-permute-start.9 = (bf16[144,896]{1,0:T(8,128)(2,1)S(1)}, bf16[144,896]{1,0:T(8,128)(2,1)S(1)}, u32[]{:S(2)}, u32[]{:S(2)}) collective-permute-start(bf16[144,896]{1,0:T(8,128)(2,1)S(1)} %pack_rows.1.c0), channel_id=1, source_target_pairs={{0,1},{1,0},{2,3},{3,2},{4,5},{5,4},{6,7},{7,6},{8,9},{9,8},{10,11... | collective-permute-start | bytes 774152 | tf_op jit(solution)/shard_map/gather_chunks/ppermute | solution.py:37
  41.2 10.5 %collective-permute-start.13 = (bf16[98,1792]{1,0:T(8,128)(2,1)S(1)}, bf16[98,1792]{1,0:T(8,128)(2,1)S(1)}, u32[]{:S(2)}, u32[]{:S(2)}) collective-permute-start(bf16[98,1792]{1,0:T(8,128)(2,1)S(1)} %collective-permute-done.4.__.x2), channel_id=1, source_target_pairs={{0,8},{4,12},{8,0},{12,4},{16,24},{20,28},{24,16},{28,20},{1,9},{5... | collective-permute-start | bytes 1053704 | tf_op jit(solution)/shard_map/gather_home/ppermute | solution.py:33
  42.9 13.4 %collective-permute-start.10 = (bf16[144,896]{1,0:T(8,128)(2,1)S(1)}, bf16[144,896]{1,0:T(8,128)(2,1)S(1)}, u32[]{:S(2)}, u32[]{:S(2)}) collective-permute-start(bf16[144,896]{1,0:T(8,128)(2,1)S(1)} %pack_rows.1.c0), channel_id=1, source_target_pairs={{0,2},{1,3},{2,0},{3,1},{4,6},{5,7},{6,4},{7,5},{8,10},{9,11},{10,... | collective-permute-start | bytes 774152 | tf_op jit(solution)/shard_map/gather_chunks/ppermute | solution.py:37
  48.0 8.4 %collective-permute-start.11 = (bf16[144,896]{1,0:T(8,128)(2,1)S(1)}, bf16[144,896]{1,0:T(8,128)(2,1)S(1)}, u32[]{:S(2)}, u32[]{:S(2)}) collective-permute-start(bf16[144,896]{1,0:T(8,128)(2,1)S(1)} %collective-permute-done.9.c1), channel_id=1, source_target_pairs={{0,2},{1,3},{2,0},{3,1},{4,6},{5,7},{6,4},{7,5},{8,10},{9,11},{10,... | collective-permute-start | bytes 774152 | tf_op jit(solution)/shard_map/gather_chunks/ppermute | solution.py:37
  62.5 2.5 %collective-permute-start.17 = (bf16[256,1536]{1,0:T(8,128)(2,1)}, bf16[256,1536]{1,0:T(8,128)(2,1)S(1)}, u32[]{:S(2)}, u32[]{:S(2)}) collective-permute-start(bf16[256,1536]{1,0:T(8,128)(2,1)} %get-tuple-element.59.refs_2_), channel_id=1, source_target_pairs={{0,4},{4,0},{8,12},{12,8},{16,20},{20,16},{24,28},{28,24},{1,5},{5... | collective-permute-start | bytes 2359304 | tf_op jit(solution)/shard_map/keys/ppermute | solution.py:33
  68.3 20.2 %collective-permute-start.18 = (bf16[256,768]{1,0:T(8,128)(2,1)S(1)}, bf16[256,768]{1,0:T(8,128)(2,1)S(1)}, u32[]{:S(2)}, u32[]{:S(2)}) collective-permute-start(bf16[256,768]{1,0:T(8,128)(2,1)S(1)} %get-tuple-element.60._), channel_id=1, source_target_pairs={{0,8},{4,12},{8,0},{12,4},{16,24},{20,28},{24,16},{28,20},{1,9},{5... | collective-permute-start | bytes 1179656 | tf_op jit(solution)/shard_map/keys/ppermute | solution.py:33
  70.1 4.3 %collective-permute-start.14 = (f32[32,512]{1,0:T(8,128)S(1)}, f32[32,512]{1,0:T(8,128)S(1)}, u32[]{:S(2)}, u32[]{:S(2)}) collective-permute-start(f32[32,512]{1,0:T(8,128)S(1)} %copy-done.13), channel_id=1, source_target_pairs={{0,1},{1,0},{2,3},{3,2},{4,5},{5,4},{6,7},{7,6},{8,9},{9,8},{10,11... | collective-permute-start | bytes 196616 | tf_op jit(solution)/shard_map/low_rank/ppermute | solution.py:37
  74.4 4.3 %collective-permute-start.15 = (f32[32,512]{1,0:T(8,128)S(1)}, f32[32,512]{1,0:T(8,128)S(1)}, u32[]{:S(2)}, u32[]{:S(2)}) collective-permute-start(f32[32,512]{1,0:T(8,128)S(1)} %add.33), channel_id=1, source_target_pairs={{0,2},{1,3},{2,0},{3,1},{4,6},{5,7},{6,4},{7,5},{8,10},{9,11},{10,... | collective-permute-start | bytes 196616 | tf_op jit(solution)/shard_map/low_rank/ppermute | solution.py:37
  78.7 1.3 collective-permute-start.16
  88.3 20.8 %collective-permute-start.19 = (bf16[256,1536]{1,0:T(8,128)(2,1)}, bf16[256,1536]{1,0:T(8,128)(2,1)S(1)}, u32[]{:S(2)}, u32[]{:S(2)}) collective-permute-start(bf16[256,1536]{1,0:T(8,128)(2,1)} %get-tuple-element.63.refs_2_), channel_id=1, source_target_pairs={{0,4},{4,0},{8,12},{12,8},{16,20},{20,16},{24,28},{28,24},{1,5},{5... | collective-permute-start | bytes 2359304 | tf_op jit(solution)/shard_map/values/ppermute | solution.py:33
  96.3 12.8 %collective-permute-start.20 = (bf16[256,1536]{1,0:T(8,128)(2,1)}, bf16[256,1536]{1,0:T(8,128)(2,1)S(1)}, u32[]{:S(2)}, u32[]{:S(2)}) collective-permute-start(bf16[256,1536]{1,0:T(8,128)(2,1)} %get-tuple-element.66), channel_id=1, source_target_pairs={{0,4},{4,0},{8,12},{12,8},{16,20},{20,16},{24,28},{28,24},{1,5},{5... | collective-permute-start | bytes 2359304 | tf_op jit(solution)/shard_map/queries/ppermute | solution.py:33
  96.6 11.9 %collective-permute-start.21 = (bf16[256,384]{1,0:T(8,128)(2,1)S(1)}, bf16[256,384]{1,0:T(8,128)(2,1)S(1)}, u32[]{:S(2)}, u32[]{:S(2)}) collective-permute-start(bf16[256,384]{1,0:T(8,128)(2,1)S(1)} %copy-done.16), channel_id=1, source_target_pairs={{0,16},{4,20},{8,24},{12,28},{16,0},{20,4},{24,8},{28,12},{1,17},{... | collective-permute-start | bytes 589832 | tf_op jit(solution)/shard_map/keys/ppermute | solution.py:33
  111.6 1.4 collective-permute-start.23
  113.0 6.6 %collective-permute-start.24 = (f32[4,4608]{1,0:T(4,128)S(1)}, f32[4,4608]{1,0:T(4,128)S(1)}, u32[]{:S(2)}, u32[]{:S(2)}) collective-permute-start(f32[4,4608]{1,0:T(4,128)S(1)} %slice.79), channel_id=1, source_target_pairs={{0,16},{4,20},{8,24},{12,28},{16,0},{20,4},{24,8},{28,12},{1,17},{... | collective-permute-start | bytes 221192 | tf_op jit(solution)/shard_map/decode_rows/ppermute | solution.py:33
  119.7 4.4 %collective-permute-start.25 = (f32[2,4608]{1,0:T(2,128)S(1)}, f32[2,4608]{1,0:T(2,128)S(1)}, u32[]{:S(2)}, u32[]{:S(2)}) collective-permute-start(f32[2,4608]{1,0:T(2,128)S(1)} %slice.81), channel_id=1, source_target_pairs={{0,8},{4,12},{8,0},{12,4},{16,24},{20,28},{24,16},{28,20},{1,9},{5... | collective-permute-start | bytes 110600 | tf_op jit(solution)/shard_map/decode_rows/ppermute | solution.py:33
  120.4 20.0 %collective-permute-start.22 = (bf16[256,1536]{1,0:T(8,128)(2,1)S(1)}, bf16[256,1536]{1,0:T(8,128)(2,1)}, u32[]{:S(2)}, u32[]{:S(2)}) collective-permute-start(bf16[256,1536]{1,0:T(8,128)(2,1)S(1)} %get-tuple-element.69._), channel_id=1, source_target_pairs={{0,8},{4,12},{8,0},{12,4},{16,24},{20,28},{24,16},{28,20},{1,9},{5... | collective-permute-start | bytes 2359304 | tf_op jit(solution)/shard_map/values_queries/ppermute | solution.py:33
  141.7 19.8 %collective-permute-start.26 = (bf16[256,768]{1,0:T(8,128)(2,1)S(1)}, bf16[256,768]{1,0:T(8,128)(2,1)S(1)}, u32[]{:S(2)}, u32[]{:S(2)}) collective-permute-start(bf16[256,768]{1,0:T(8,128)(2,1)S(1)} %get-tuple-element.76._), channel_id=1, source_target_pairs={{0,16},{4,20},{8,24},{12,28},{16,0},{20,4},{24,8},{28,12},{1,17},{... | collective-permute-start | bytes 1179656 | tf_op jit(solution)/shard_map/values_queries/ppermute | solution.py:33
  142.7 22.0 %collective-permute-start.27 = (bf16[256,384]{1,0:T(8,128)(2,1)S(1)}, bf16[256,384]{1,0:T(8,128)(2,1)S(1)}, u32[]{:S(2)}, u32[]{:S(2)}) collective-permute-start(bf16[256,384]{1,0:T(8,128)(2,1)S(1)} %finish_sums.2.refs_4_.ka_ref), channel_id=1, source_target_pairs={{0,4},{4,0},{8,12},{12,8},{16,20},{20,16},{24,28},{28,24},{1,5},{5... | collective-permute-start | bytes 589832 | tf_op jit(solution)/shard_map/keys/ppermute | solution.py:33
  148.9 37.2 %copy-start.2 = (bf16[1536,896]{1,0:T(8,128)(2,1)S(1)}, bf16[1536,896]{1,0:T(8,128)(2,1)}, u32[]{:S(2)}) copy-start(bf16[1536,896]{1,0:T(8,128)(2,1)} %refs_8_.1) | copy-start | bytes 8257540
  162.1 2.6 %collective-permute-start.28 = (bf16[256,384]{1,0:T(8,128)(2,1)S(1)}, bf16[256,384]{1,0:T(8,128)(2,1)S(1)}, u32[]{:S(2)}, u32[]{:S(2)}) collective-permute-start(bf16[256,384]{1,0:T(8,128)(2,1)S(1)} %get-tuple-element.78.va_ref), channel_id=1, source_target_pairs={{0,4},{4,0},{8,12},{12,8},{16,20},{20,16},{24,28},{28,24},{1,5},{5... | collective-permute-start | bytes 589832 | tf_op jit(solution)/shard_map/values_queries/ppermute | solution.py:33
  166.2 11.3 %collective-permute-start.30 = (bf16[272,384]{1,0:T(8,128)(2,1)S(1)}, bf16[272,384]{1,0:T(8,128)(2,1)S(1)}, u32[]{:S(2)}, u32[]{:S(2)}) collective-permute-start(bf16[272,384]{1,0:T(8,128)(2,1)S(1)} %prompt_attention.1.refs_0_), channel_id=1, source_target_pairs={{0,16},{4,20},{8,24},{12,28},{16,0},{20,4},{24,8},{28,12},{1,17},{... | collective-permute-start | bytes 626696 | tf_op jit(solution)/shard_map/gather_attended/ppermute | solution.py:33
  166.3 12.1 %collective-permute-start.29 = (bf16[272,384]{1,0:T(8,128)(2,1)S(1)}, bf16[272,384]{1,0:T(8,128)(2,1)S(1)}, u32[]{:S(2)}, u32[]{:S(2)}) collective-permute-start(bf16[272,384]{1,0:T(8,128)(2,1)S(1)} %prompt_attention.1.refs_0_), channel_id=1, source_target_pairs={{0,8},{4,12},{8,0},{12,4},{16,24},{20,28},{24,16},{28,20},{1,9},{5... | collective-permute-start | bytes 626696 | tf_op jit(solution)/shard_map/gather_attended/ppermute | solution.py:33
  177.6 7.1 %collective-permute-start.31 = (bf16[272,384]{1,0:T(8,128)(2,1)S(1)}, bf16[272,384]{1,0:T(8,128)(2,1)S(1)}, u32[]{:S(2)}, u32[]{:S(2)}) collective-permute-start(bf16[272,384]{1,0:T(8,128)(2,1)S(1)} %collective-permute-done.30.refs_2_), channel_id=1, source_target_pairs={{0,8},{4,12},{8,0},{12,4},{16,24},{20,28},{24,16},{28,20},{1,9},{5... | collective-permute-start | bytes 626696 | tf_op jit(solution)/shard_map/gather_attended/ppermute | solution.py:33
  177.6 7.1 %collective-permute-start.32 = (bf16[272,384]{1,0:T(8,128)(2,1)S(1)}, bf16[272,384]{1,0:T(8,128)(2,1)S(1)}, u32[]{:S(2)}, u32[]{:S(2)}) collective-permute-start(bf16[272,384]{1,0:T(8,128)(2,1)S(1)} %prompt_attention.1.refs_0_), channel_id=1, source_target_pairs={{0,4},{4,0},{8,12},{12,8},{16,20},{20,16},{24,28},{28,24},{1,5},{5... | collective-permute-start | bytes 626696 | tf_op jit(solution)/shard_map/gather_attended/ppermute | solution.py:33
  177.6 7.1 %collective-permute-start.34 = (bf16[272,384]{1,0:T(8,128)(2,1)S(1)}, bf16[272,384]{1,0:T(8,128)(2,1)S(1)}, u32[]{:S(2)}, u32[]{:S(2)}) collective-permute-start(bf16[272,384]{1,0:T(8,128)(2,1)S(1)} %collective-permute-done.30.refs_2_), channel_id=1, source_target_pairs={{0,4},{4,0},{8,12},{12,8},{16,20},{20,16},{24,28},{28,24},{1,5},{5... | collective-permute-start | bytes 626696 | tf_op jit(solution)/shard_map/gather_attended/ppermute | solution.py:33
  178.4 6.2 %collective-permute-start.33 = (bf16[272,384]{1,0:T(8,128)(2,1)S(1)}, bf16[272,384]{1,0:T(8,128)(2,1)S(1)}, u32[]{:S(2)}, u32[]{:S(2)}) collective-permute-start(bf16[272,384]{1,0:T(8,128)(2,1)S(1)} %collective-permute-done.29.refs_1_), channel_id=1, source_target_pairs={{0,4},{4,0},{8,12},{12,8},{16,20},{20,16},{24,28},{28,24},{1,5},{5... | collective-permute-start | bytes 626696 | tf_op jit(solution)/shard_map/gather_attended/ppermute | solution.py:33
  184.6 1.5 collective-permute-start.35
  189.8 9.1 %collective-permute-start.36 = (bf16[144,896]{1,0:T(8,128)(2,1)S(1)}, bf16[144,896]{1,0:T(8,128)(2,1)S(1)}, u32[]{:S(2)}, u32[]{:S(2)}) collective-permute-start(bf16[144,896]{1,0:T(8,128)(2,1)S(1)} %get-tuple-element.82), channel_id=1, source_target_pairs={{0,1},{1,0},{2,3},{3,2},{4,5},{5,4},{6,7},{7,6},{8,9},{9,8},{10,11... | collective-permute-start | bytes 774152 | tf_op jit(solution)/shard_map/sum_mp/ppermute | solution.py:37
  190.5 12.6 %collective-permute-start.37 = (bf16[144,896]{1,0:T(8,128)(2,1)S(1)}, bf16[144,896]{1,0:T(8,128)(2,1)S(1)}, u32[]{:S(2)}, u32[]{:S(2)}) collective-permute-start(bf16[144,896]{1,0:T(8,128)(2,1)S(1)} %get-tuple-element.83), channel_id=1, source_target_pairs={{0,2},{1,3},{2,0},{3,1},{4,6},{5,7},{6,4},{7,5},{8,10},{9,11},{10,... | collective-permute-start | bytes 774152 | tf_op jit(solution)/shard_map/sum_mp/ppermute | solution.py:37
  192.0 12.7 %collective-permute-start.38 = (bf16[144,896]{1,0:T(8,128)(2,1)S(1)}, bf16[144,896]{1,0:T(8,128)(2,1)S(1)}, u32[]{:S(2)}, u32[]{:S(2)}) collective-permute-start(bf16[144,896]{1,0:T(8,128)(2,1)S(1)} %get-tuple-element.84), channel_id=1, source_target_pairs={{0,3},{1,2},{2,1},{3,0},{4,7},{5,6},{6,5},{7,4},{8,11},{9,10},{10,... | collective-permute-start | bytes 774152 | tf_op jit(solution)/shard_map/sum_mp/ppermute | solution.py:37
  205.6 5.9 %collective-permute-start.39 = (bf16[64,896]{1,0:T(8,128)(2,1)S(1)}, bf16[64,896]{1,0:T(8,128)(2,1)S(1)}, u32[]{:S(2)}, u32[]{:S(2)}) collective-permute-start(bf16[64,896]{1,0:T(8,128)(2,1)S(1)} %get-tuple-element.86), channel_id=1, source_target_pairs={{0,8},{4,12},{8,0},{12,4},{16,24},{20,28},{24,16},{28,20},{1,9},{5... | collective-permute-start | bytes 344072 | tf_op jit(solution)/shard_map/return_z/ppermute | solution.py:33
  206.0 11.2 %collective-permute-start.40 = (bf16[64,896]{1,0:T(8,128)(2,1)S(1)}, bf16[64,896]{1,0:T(8,128)(2,1)S(1)}, u32[]{:S(2)}, u32[]{:S(2)}) collective-permute-start(bf16[64,896]{1,0:T(8,128)(2,1)S(1)} %get-tuple-element.87), channel_id=1, source_target_pairs={{0,16},{4,20},{8,24},{12,28},{16,0},{20,4},{24,8},{28,12},{1,17},{... | collective-permute-start | bytes 344072 | tf_op jit(solution)/shard_map/return_z/ppermute | solution.py:33
  208.6 8.6 %collective-permute-start.41 = (bf16[64,896]{1,0:T(8,128)(2,1)S(1)}, bf16[64,896]{1,0:T(8,128)(2,1)S(1)}, u32[]{:S(2)}, u32[]{:S(2)}) collective-permute-start(bf16[64,896]{1,0:T(8,128)(2,1)S(1)} %get-tuple-element.88), channel_id=1, source_target_pairs={{0,24},{4,28},{8,16},{12,20},{16,8},{20,12},{24,0},{28,4},{1,25},{... | collective-permute-start | bytes 344072 | tf_op jit(solution)/shard_map/return_z/ppermute | solution.py:33
  217.3 1.6 collective-permute-start.42
  219.5 6.1 %collective-permute-start.43 = (bf16[32,1792]{1,0:T(8,128)(2,1)S(1)}, bf16[32,1792]{1,0:T(8,128)(2,1)S(1)}, u32[]{:S(2)}, u32[]{:S(2)}) collective-permute-start(bf16[32,1792]{1,0:T(8,128)(2,1)S(1)} %get-tuple-element.90), channel_id=1, source_target_pairs={{0,1},{1,0},{2,3},{3,2},{4,5},{5,4},{6,7},{7,6},{8,9},{9,8},{10,11... | collective-permute-start | bytes 344072 | tf_op jit(solution)/shard_map/return_plane/ppermute | solution.py:37
  220.2 7.4 %collective-permute-start.44 = (bf16[32,1792]{1,0:T(8,128)(2,1)S(1)}, bf16[32,1792]{1,0:T(8,128)(2,1)S(1)}, u32[]{:S(2)}, u32[]{:S(2)}) collective-permute-start(bf16[32,1792]{1,0:T(8,128)(2,1)S(1)} %get-tuple-element.91), channel_id=1, source_target_pairs={{0,2},{1,3},{2,0},{3,1},{4,6},{5,7},{6,4},{7,5},{8,10},{9,11},{10,... | collective-permute-start | bytes 344072 | tf_op jit(solution)/shard_map/return_plane/ppermute | solution.py:37
  221.5 6.0 %collective-permute-start.45 = (bf16[32,1792]{1,0:T(8,128)(2,1)S(1)}, bf16[32,1792]{1,0:T(8,128)(2,1)S(1)}, u32[]{:S(2)}, u32[]{:S(2)}) collective-permute-start(bf16[32,1792]{1,0:T(8,128)(2,1)S(1)} %get-tuple-element.92), channel_id=1, source_target_pairs={{0,3},{1,2},{2,1},{3,0},{4,7},{5,6},{6,5},{7,4},{8,11},{9,10},{10,... | collective-permute-start | bytes 344072 | tf_op jit(solution)/shard_map/return_plane/ppermute | solution.py:37
  (27 other events, 202.5 us)

commit v3 on v2

--- a/solution.py
+++ b/solution.py
@@ -109,7 +109,8 @@
     spot = jnp.bitwise_xor(spot >> 8, core) * half + (spot & (half - 1))
     prompt = jnp.where(i < by_slot(h, a.lens), spot, -1)
     first = SLOTS * PLEN
-    decode = jnp.where(h < first + DEC, NM * CHUNK + j * DEC + h - first, -1)
+    base = NM * CHUNK + (j // NZ * NZ + turned_bits(j % NZ)) * DEC - first
+    decode = jnp.where(h < first + DEC, base + h, -1)
     return jnp.where(h < first, prompt, decode)
 
 
@@ -162,7 +163,7 @@
     )(scalars, tokens)
 
 
-def norm_kernel(s_ref, b0, b1, b2, b3, gain_ref, shift_ref, table_ref, _, __, o0, o1, o2, o3, held):
+def norm_kernel(s_ref, b0, b1, b2, b3, affine_ref, table_ref, _, __, o0, o1, o2, o3, held):
     z, m = s_ref[3], s_ref[4]
     cols = b0.shape[1]
     for k, ref in enumerate((b0, b1, b2, b3)):
@@ -192,23 +193,45 @@
     for k, out in enumerate((o0, o1, o2, o3)):
         block = jnp.bitwise_xor(z, k)
         x = held[jnp.bitwise_xor(block, m)]
-        y = (x - mean) * rstd * gain_ref[block] + shift_ref[block]
+        y = (x - mean) * rstd * affine_ref[block] + affine_ref[NM + block]
         y = jnp.where(last, table_ref[...], y)
         out[...] = y.astype(BF)
         out[:, : 2 * LANES] = jnp.where(stats, extra, y[:, : 2 * LANES]).astype(BF)
 
 
-def norm_rows(scalars, blocks, gain, shift, table, near, far):
+def norm_rows(scalars, blocks, affine, table, near, far):
     return pl.pallas_call(
         norm_kernel,
         out_shape=[jax.ShapeDtypeStruct(blocks[0].shape, BF)] * NZ,
-        in_specs=[SMEM] + [VMEM] * 7 + [ANY] * 2,
+        in_specs=[SMEM] + [VMEM] * 6 + [ANY] * 2,
         out_specs=[VMEM] * NZ,
         scratch_shapes=[pltpu.VMEM((NM,) + blocks[0].shape, F32)],
         compiler_params=limit(32),
         cost_estimate=SMALL,
         name="norm_rows",
-    )(scalars, *blocks, gain, shift, table, near, far)
+    )(scalars, *blocks, affine, table, near, far)
+
+
+def cores_kernel(s_ref, b0, b1, b2, b3, mine_ref, theirs_ref):
+    core = s_ref[6]
+    width = mine_ref.shape[1]
+    for k, ref in enumerate((b0, b1, b2, b3)):
+        rows = slice(k * BLK, (k + 1) * BLK)
+        mine_ref[rows, :] = ref[:, pl.ds(pl.multiple_of(core * width, LANES), width)]
+        theirs_ref[rows, :] = ref[:, pl.ds(pl.multiple_of((1 - core) * width, LANES), width)]
+
+
+def split_cores(scalars, blocks):
+    out = jax.ShapeDtypeStruct((NZ * BLK, blocks[0].shape[1] // 2), BF)
+    return pl.pallas_call(
+        cores_kernel,
+        out_shape=[out, out],
+        in_specs=[SMEM] + [VMEM] * NZ,
+        out_specs=[VMEM] * 2,
+        compiler_params=limit(16),
+        cost_estimate=SMALL,
+        name="split_cores",
+    )(scalars, *blocks)
 
 
 def pack_kernel(s_ref, t_ref, a_ref, b_ref, o_ref):
@@ -236,7 +259,23 @@
     )(scalars, tables, mine, theirs)
 
 
-def code_kernel(s_ref, t_ref, col_ref, row_ref):
+def copy_kernel(x_ref, _, o_ref):
+    o_ref[...] = x_ref[...]
+
+
+def copy_rows(x, after):
+    return pl.pallas_call(
+        copy_kernel,
+        out_shape=jax.ShapeDtypeStruct(x.shape, x.dtype),
+        in_specs=[VMEM, ANY],
+        out_specs=VMEM,
+        compiler_params=limit(16),
+        cost_estimate=SMALL,
+        name="copy_rows",
+    )(x, after)
+
+
+def code_kernel(s_ref, t_ref, _, col_ref, row_ref):
     found = sources(s_ref, t_ref)
     m, core = s_ref[4], s_ref[6]
     n = NM * CHUNK
@@ -255,20 +294,20 @@
     row_ref[...] = jnp.where(rows > 0, rows - 1, unused)
 
 
-def packed_codes(scalars, tables):
+def packed_codes(scalars, tables, after):
     n = NM * CHUNK
     return pl.pallas_call(
         code_kernel,
         out_shape=[jax.ShapeDtypeStruct((n, 1), jnp.int32), jax.ShapeDtypeStruct((1, n), jnp.int32)],
-        in_specs=[SMEM] * 2,
+        in_specs=[SMEM] * 2 + [ANY],
         out_specs=[VMEM] * 2,
         compiler_params=limit(16),
         cost_estimate=SMALL,
         name="packed_codes",
-    )(scalars, tables)
-
-
-def rank_kernel(s_ref, table_ref, da_ref, db_ref, x0, x1, x2, x3, t0, t1, t2, t3, gain_ref, shift_ref, o_ref):
+    )(scalars, tables, after)
+
+
+def rank_kernel(s_ref, table_ref, da_ref, db_ref, x0, x1, x2, x3, t0, t1, t2, t3, affine_ref, o_ref):
     m, r = s_ref[4], s_ref[5]
     width = 2 * ADAPTER_RANK
     count = da_ref.shape[0] // width
@@ -285,7 +324,7 @@
             return turned[:, j : j + 1] + turned[:, j + 1 : j + 2] + turned[:, j + 2 : j + 3]
 
         mean, rstd = column(slice(0, LANES)), column(slice(LANES, 2 * LANES))
-        normed = ((x[...].astype(F32) - mean) * rstd * gain_ref[m] + shift_ref[m]).astype(BF)
+        normed = ((x[...].astype(F32) - mean) * rstd * affine_ref[m] + affine_ref[NM + m]).astype(BF)
         ids = home_adapters(Source(s_ref, table_ref, k), iota((1, rows), 1))
         total = jnp.zeros((width, rows), F32)
         for core, d in enumerate((da_ref, db_ref)):
@@ -296,19 +335,19 @@
         o_ref[:, k * LANES : k * LANES + rows] = total
 
 
-def low_rank_rows(scalars, tables, down, down_other, pieces, stats, gain, shift):
+def low_rank_rows(scalars, tables, down, down_other, pieces, stats, affine):
     return pl.pallas_call(
         rank_kernel,
         out_shape=jax.ShapeDtypeStruct((2 * ADAPTER_RANK, NZ * LANES), F32),
-        in_specs=[SMEM] * 2 + [VMEM] * 12,
+        in_specs=[SMEM] * 2 + [VMEM] * 11,
         out_specs=VMEM,
         compiler_params=limit(32),
         cost_estimate=SMALL,
         name="low_rank_rows",
-    )(scalars, tables, down, down_other, *pieces, *stats, gain, shift)
-
-
-def expand_kernel(s_ref, t_ref, low_ref, low_other_ref, _, o_ref, *, count):
+    )(scalars, tables, down, down_other, *pieces, *stats, affine)
+
+
+def expand_kernel(s_ref, t_ref, low_ref, low_other_ref, base_ref, up_ref, _, o_ref, keep_ref, send_ref, *, count):
     m, r, core = s_ref[4], s_ref[5], s_ref[6]
     found = sources(s_ref, t_ref)
     width = count * ADAPTER_RANK
@@ -327,30 +366,39 @@
         low = jnp.where(adapter == home_adapters(a, lane), low, 0.0).astype(BF)
         hit = (iota((PACKED, LANES), 0) == packed_places(a, j, lane, m, core)).astype(BF)
         total = total + lax.dot_general(hit, low, (((1,), (1,)), ((), ())), preferred_element_type=F32)
-    o_ref[0] = total[:, :width].astype(BF)
-    o_ref[1] = total[:, width:].astype(BF)
-
-
-def expand_rows(scalars, tables, low, low_other, count, after):
+    feats = up_ref.shape[3]
+    half = keep_ref.shape[0]
+    keep_ref[...] = base_ref[:half, :]
+    send_ref[...] = base_ref[half:, :]
+    for t, first in ((0, 0), (1, 2 * feats)):
+        rows = total[:, t * width : (t + 1) * width].astype(BF)
+        o_ref[t] = rows
+        up = up_ref[:, t].reshape(-1, feats)
+        term = jnp.dot(rows[NM * CHUNK :, :], up, preferred_element_type=F32)
+        keep_ref[:, first : first + feats] += term[:half]
+        send_ref[:, first : first + feats] += term[half:]
+
+
+def expand_rows(scalars, tables, low, low_other, base, up, count, after):
+    half = jax.ShapeDtypeStruct((base.shape[0] // 2, base.shape[1]), F32)
     return pl.pallas_call(
         functools.partial(expand_kernel, count=count),
-        out_shape=jax.ShapeDtypeStruct((2, PACKED, count * ADAPTER_RANK), BF),
-        in_specs=[SMEM] * 2 + [VMEM] * 2 + [ANY],
-        out_specs=VMEM,
+        out_shape=[jax.ShapeDtypeStruct((2, PACKED, count * ADAPTER_RANK), BF), half, half],
+        in_specs=[SMEM] * 2 + [VMEM] * 4 + [ANY],
+        out_specs=[VMEM] * 3,
         compiler_params=limit(32),
         cost_estimate=SMALL,
         name="expand_rows",
-    )(scalars, tables, low, low_other, after)
-
-
-def emit_sums(y, own_ref, other_ref, dec_ref):
+    )(scalars, tables, low, low_other, base, up, after)
+
+
+def emit_sums(y, own_ref, other_ref):
     half = 2 * CHUNK
-    own_ref[...] = y[:half]
+    own_ref[...] = y[:half].astype(BF)
     other_ref[...] = y[half : 2 * half].astype(BF)
-    dec_ref[...] = y[2 * half :]
-
-
-def first_project_kernel(s_ref, c0, c1, c2, c3, w_ref, _, own_ref, other_ref, dec_ref, x):
+
+
+def first_project_kernel(s_ref, c0, c1, c2, c3, w_ref, _, own_ref, other_ref, x):
     z, m, core = s_ref[3], s_ref[4], s_ref[6]
 
     @pl.when(pl.program_id(0) == 0)
@@ -360,12 +408,12 @@
             base = jnp.bitwise_xor(core, k >> 1) * 2 * CHUNK + (k & 1) * CHUNK
             x[pl.ds(pl.multiple_of(base, CHUNK), CHUNK), :] = chunk[:CHUNK, :]
         n, at = iota((2 * NZ * DEC, NM * DCH), 0), iota((2 * NZ * DEC, NM * DCH), 1)
-        chip = jnp.bitwise_xor(z, (n >> 1) & 3)
+        chip = jnp.bitwise_xor(z, turned_bits((n >> 1) & 3))
         want = jnp.bitwise_xor(chip, m) * DCH + jnp.bitwise_xor(core, n >> 3) * DEC + (n & 1)
         rows = jnp.concatenate([chunk[CHUNK:, :] for chunk in chunks], axis=0)
         x[NM * CHUNK :, :] = jnp.dot((want == at).astype(BF), rows, preferred_element_type=F32).astype(BF)
 
-    emit_sums(jnp.dot(x[...], w_ref[0], preferred_element_type=F32), own_ref, other_ref, dec_ref)
+    emit_sums(jnp.dot(x[: NM * CHUNK, :], w_ref[0], preferred_element_type=F32), own_ref, other_ref)
 
 
 def project_rows(scalars, chunks, weight, part, after):
@@ -374,12 +422,11 @@
     half = 2 * CHUNK
     whole = [pl.BlockSpec(v.shape, lambda j: (0, 0)) for v in chunks]
     out_shape = [
-        jax.ShapeDtypeStruct((half, feats), F32),
         jax.ShapeDtypeStruct((half, feats), BF),
-        jax.ShapeDtypeStruct((PACKED - 2 * half, feats), F32),
+        jax.ShapeDtypeStruct((half, feats), BF),
         jax.ShapeDtypeStruct((PACKED, depth), BF),
     ]
-    out_specs = [pl.BlockSpec((v.shape[0], tile), lambda j: (0, j)) for v in out_shape[:3]]
+    out_specs = [pl.BlockSpec((v.shape[0], tile), lambda j: (0, j)) for v in out_shape[:2]]
     out_specs.append(pl.BlockSpec((PACKED, depth), lambda j: (0, 0)))
     return pl.pallas_call(
         first_project_kernel,
@@ -394,9 +441,9 @@
 
 
 def adapted_kernel(x_ref, w_ref, e_ref, u_ref, _, *outs):
-    y = jnp.dot(x_ref[...], w_ref[0], preferred_element_type=F32)
+    y = jnp.dot(x_ref[: NM * CHUNK, :], w_ref[0], preferred_element_type=F32)
     up = u_ref[...].reshape(-1, u_ref.shape[-1])
-    y = y + jnp.dot(e_ref[0], up, preferred_element_type=F32)
+    y = y + jnp.dot(e_ref[0, : NM * CHUNK, :], up, preferred_element_type=F32)
     emit_sums(y, *outs)
 
 
@@ -406,9 +453,8 @@
     half = 2 * CHUNK
     which = part // 2
     out_shape = [
-        jax.ShapeDtypeStruct((half, feats), F32),
         jax.ShapeDtypeStruct((half, feats), BF),
-        jax.ShapeDtypeStruct((PACKED - 2 * half, feats), F32),
+        jax.ShapeDtypeStruct((half, feats), BF),
     ]
     return pl.pallas_call(
         adapted_kernel,
@@ -428,27 +474,65 @@
     )(rows, weight, expanded, up, after)
 
 
-def split_kernel(q_ref, k_ref, v_ref, _, keep_ref, send_ref):
-    half = keep_ref.shape[0]
-    feats = q_ref.shape[1]
-    for j, ref in enumerate((q_ref, k_ref, v_ref)):
-        at = slice(j * feats, (j + 1) * feats)
-        keep_ref[:, at] = ref[:half, :]
-        send_ref[:, at] = ref[half:, :]
-
-
-def split_decode(parts, after):
-    rows, feats = parts[0].shape
-    out = jax.ShapeDtypeStruct((rows // 2, 3 * feats), F32)
-    return pl.pallas_call(
-        split_kernel,
-        out_shape=[out, out],
+def add_kernel(a_ref, b_ref, _, o_ref):
+    o_ref[...] = (a_ref[: b_ref.shape[0], :] + b_ref[...]).astype(o_ref.dtype)
+
+
+def add_rows(a, b, after, dtype=F32):
+    return pl.pallas_call(
+        add_kernel,
+        out_shape=jax.ShapeDtypeStruct(b.shape, dtype),
+        in_specs=[VMEM] * 2 + [ANY],
+        out_specs=VMEM,
+        compiler_params=limit(16),
+        cost_estimate=SMALL,
+        name="add_rows",
+    )(a, b, after)
+
+
+def decode_finish_kernel(a_ref, b_ref, bias_ref, _, q_ref, k_ref, v_ref):
+    total = a_ref[: b_ref.shape[0], :] + b_ref[...]
+    feats = bias_ref.shape[1]
+    for j, out in enumerate((q_ref, k_ref, v_ref)):
+        part = total[:, j * feats : (j + 1) * feats] + bias_ref[j : j + 1, :]
+        for i in range(out.shape[0]):
+            out[i] = part[i : i + 1].astype(BF)
+
+
+def decode_finish(a, b, bias, after):
+    out = jax.ShapeDtypeStruct((b.shape[0], 1, bias.shape[1]), BF)
+    return pl.pallas_call(
+        decode_finish_kernel,
+        out_shape=[out] * 3,
         in_specs=[VMEM] * 3 + [ANY],
-        out_specs=[VMEM] * 2,
+        out_specs=[VMEM] * 3,
         compiler_params=limit(16),
         cost_estimate=SMALL,
-        name="split_decode",
-    )(*parts, after)
+        name="decode_finish",
+    )(a, b, bias, after)
+
+
+def decode_base_kernel(x_ref, w_ref, _, o_ref):
+    o_ref[...] = jnp.dot(x_ref[...], w_ref[0], preferred_element_type=F32)
+
+
+def decode_base(rows, weight, after):
+    parts, depth, feats = weight.shape
+    count = PACKED - NM * CHUNK
+    return pl.pallas_call(
+        decode_base_kernel,
+        grid=(parts,),
+        out_shape=jax.ShapeDtypeStruct((count, parts * feats), F32),
+        in_specs=[
+            pl.BlockSpec((count, depth), lambda p: (NM * CHUNK // count, 0)),
+            pl.BlockSpec((1, depth, feats), lambda p: (p, 0, 0)),
+            ANY,
+        ],
+        out_specs=pl.BlockSpec((count, feats), lambda p: (0, p)),
+        compiler_params=limit(56),
+        cost_estimate=SMALL,
+        name="decode_base",
+    )(rows, weight, after)
 
 
 def halve_kernel(s_ref, *refs, bit, groups):
@@ -463,7 +547,7 @@
 
             def part(which):
                 at = pl.ds(pl.multiple_of((2 * g + which) * width, LANES), width)
-                return total_ref[:, at] + got_ref[:, at].astype(F32)
+                return total_ref[:, at].astype(F32) + got_ref[:, at].astype(F32)
 
             send_ref[:, to : to + width] = part(1 - side).astype(BF)
             keep_ref[:, to : to + width] = part(side)
@@ -478,7 +562,7 @@
         out_shape=[jax.ShapeDtypeStruct((rows, feats), BF), jax.ShapeDtypeStruct((rows, feats), F32)],
         in_specs=[SMEM] + [VMEM] * (2 * len(totals)) + [ANY],
         out_specs=[VMEM, VMEM],
-        compiler_params=limit(16),
+        compiler_params=limit(24),
         cost_estimate=SMALL,
         name="halve_sums",
     )(scalars, *totals, *gots, after)
@@ -506,7 +590,7 @@
     )(scalars, total, got, bias, after)
 
 
-def prompt_kernel(q_ref, ka_ref, kb_ref, va_ref, vb_ref, cr_ref, cc_ref, d0_ref, d1_ref, o_ref):
+def prompt_kernel(q_ref, ka_ref, kb_ref, va_ref, vb_ref, cr_ref, cc_ref, d_ref, o_ref):
     rows = cr_ref[...]
     cols = cc_ref[...]
     allowed = ((rows >> 5) == (cols >> 5)) & (cols <= rows)
@@ -524,8 +608,8 @@
     n = iota((DECODE_ROWS, width), 0)
     tail = jnp.zeros((DECODE_ROWS, width), F32)
     for b in range(NZ):
-        for j, ref in enumerate((d0_ref, d1_ref)):
-            tail = jnp.where(n == b * DEC + j, ref[:, b * width : (b + 1) * width].astype(F32), tail)
+        for j in range(DEC):
+            tail = jnp.where(n == b * DEC + j, d_ref[j : j + 1, b * width : (b + 1) * width].astype(F32), tail)
     o_ref[q_ref.shape[0] :, :] = tail.astype(BF)
 
 
@@ -533,18 +617,18 @@
     return pl.pallas_call(
         prompt_kernel,
         out_shape=jax.ShapeDtypeStruct((q.shape[0] + DECODE_ROWS, q.shape[1]), BF),
-        in_specs=[VMEM] * 9,
+        in_specs=[VMEM] * 8,
         out_specs=VMEM,
         compiler_params=limit(32),
         cost_estimate=SMALL,
         name="prompt_attention",
-    )(q, ka, kb, va, vb, code_rows, code_cols, *dec)
+    )(q, ka, kb, va, vb, code_rows, code_cols, dec)
 
 
 def decode_kernel(len_ref, q_ref, k_ref, v_ref, c_ref, _, o_ref, qbd, top, total, acc):
-    t = pl.program_id(0)
+    d, t = pl.program_id(0), pl.program_id(1)
     span = c_ref.shape[1]
-    live = len_ref[0]
+    live = len_ref[d]
     heads, feats = qbd.shape
     diag = lax.broadcasted_iota(jnp.int32, (heads, feats), 1) // HEAD_DIM == lax.broadcasted_iota(
         jnp.int32, (heads, feats), 0
@@ -575,23 +659,23 @@
         w = pltpu.roll(w, 1, 1).astype(BF)
         acc[...] = acc[...] * fade + jnp.dot(w, x, preferred_element_type=F32)
 
-    @pl.when(t == pl.num_programs(0) - 1)
+    @pl.when(t == pl.num_programs(1) - 1)
     def _():
         o = acc[...] / total[:, :1]
         o_ref[0] = jnp.sum(jnp.where(diag, o, 0.0), axis=0, keepdims=True).astype(BF)
 
 
-def decode_attention(length, q, k, v, cache, which, after, span=256):
-    _, positions, _, feats = cache.shape
-    row = pl.BlockSpec((1, 1, feats), lambda t, n: (0, 0, 0))
+def decode_attention(lengths, q, k, v, cache, after, span=256):
+    count, positions, _, feats = cache.shape
+    row = pl.BlockSpec((1, 1, feats), lambda d, t, n: (d, 0, 0))
     heads = 16
     return pl.pallas_call(
         decode_kernel,
         grid_spec=pltpu.PrefetchScalarGridSpec(
             num_scalar_prefetch=1,
-            grid=(positions // span,),
+            grid=(count, positions // span),
             in_specs=[row, row, row]
-            + [pl.BlockSpec((1, span, 2, feats), lambda t, n: (which, jnp.minimum(t, (n[0] - 1) // span), 0, 0)), ANY],
+            + [pl.BlockSpec((1, span, 2, feats), lambda d, t, n: (d, jnp.minimum(t, (n[d] - 1) // span), 0, 0)), ANY],
             out_specs=row,
             scratch_shapes=[
                 pltpu.VMEM((heads, feats), BF),
@@ -600,11 +684,11 @@
                 pltpu.VMEM((heads, feats), F32),
             ],
         ),
-        out_shape=jax.ShapeDtypeStruct((1, 1, feats), BF),
+        out_shape=jax.ShapeDtypeStruct((count, 1, feats), BF),
         compiler_params=limit(32),
         cost_estimate=SMALL,
         name="decode_attention",
-    )(length, q, k, v, cache, after)
+    )(lengths, q, k, v, cache, after)
 
 
 def out_kernel(place_ref, *refs):
@@ -736,8 +820,12 @@
     )(scalars, tokens, bias, *blocks)
 
 
+def turned_bits(k):
+    return (k & 1) * 2 + (k >> 1)
+
+
 def place_of(z):
-    return (z & 1) * 2 + (z >> 1)
+    return turned_bits(z)
 
 
 def packed_device(
@@ -772,26 +860,23 @@
     scalars = jnp.concatenate([lens, jnp.stack([z, m, r, c])])
 
     down = jnp.transpose(adapter_down_weight, (0, 2, 1)).reshape(own_adapters * 2 * ADAPTER_RANK, cols)
-    down_other = swap_req(down, 1)
-
+
+    with jax.named_scope("deal"):
+        dealt = deal(scalars, tokens)
     with jax.named_scope("gather_home"):
         pieces = gather_z(tokens)
-
     with jax.named_scope("deal"):
-        dealt = deal(scalars, tokens)
         blocks = [dealt[0]] + [swap_mp(dealt[k], k) for k in range(1, NM)]
     with jax.named_scope("norm_rows"):
         table = jnp.concatenate([lens, adapter_index_table[0]]).astype(F32)
         table = jnp.pad(table, (0, depth - table.shape[0]))
         table = jnp.tile(table, 2)[None, :]
-        gain = layernorm_scale.reshape(NM, 1, cols)
-        shift = layernorm_bias.reshape(NM, 1, cols)
-        normed = norm_rows(scalars, blocks, gain, shift, table, pieces[1], pieces[2])
+        affine = jnp.stack([layernorm_scale, layernorm_bias]).reshape(2 * NM, 1, cols)
+        normed = norm_rows(scalars, blocks, affine, table, pieces[1], pieces[2])
     with jax.named_scope("spread_z"):
         spread = [normed[0]] + [swap_req(normed[k], 2 * k) for k in range(1, NZ)]
-        rows = jnp.concatenate(spread, axis=0)
-        mine = lax.dynamic_slice_in_dim(rows, c * depth, depth, 1)
-        theirs = swap_req(lax.dynamic_slice_in_dim(rows, (1 - c) * depth, depth, 1), 1)
+        mine, theirs = split_cores(scalars, spread)
+        theirs = swap_req(theirs, 1)
 
     with jax.named_scope("tables"):
         tables = jnp.concatenate(
@@ -802,56 +887,54 @@
     with jax.named_scope("gather_chunks"):
         chunks = gather_mp(chunk)
 
-    with jax.named_scope("codes"):
-        code_col, code_row = packed_codes(scalars, tables)
-
     with jax.named_scope("low_rank"):
-        part = low_rank_rows(scalars, tables, down, down_other, pieces, spread, gain, shift)
-        two = part + swap_mp(part, 1)
-        low_rank = (two + swap_mp(two, 2)).astype(BF)
+        down_other = swap_req(copy_rows(down, chunk), 1)
+        part = low_rank_rows(scalars, tables, down, down_other, pieces, spread, affine)
     with jax.named_scope("keys"):
-        own_k, other_k, dec_k, x_rows = project_rows(scalars, chunks, query_key_value_weight, 1, part)
-        send_k, keep_k = halve(scalars, [own_k], [swap_req(other_k, 1)], 0, other_k)
+        own_k, other_k, x_rows = project_rows(scalars, chunks, query_key_value_weight, 1, part)
+        core_k = swap_req(other_k, 1)
+    with jax.named_scope("decode_rows"):
+        base = decode_base(x_rows, query_key_value_weight, other_k)
+    with jax.named_scope("low_rank"):
+        two = add_rows(part, swap_mp(part, 1), base)
+    with jax.named_scope("keys"):
+        send_k, keep_k = halve(scalars, [own_k], [core_k], 0, two)
         got_k = swap_req(send_k, 2)
     with jax.named_scope("low_rank"):
-        expanded = expand_rows(scalars, tables, low_rank, swap_req(low_rank, 1), own_adapters, send_k)
+        code_col, code_row = packed_codes(scalars, tables, send_k)
+        low_rank = add_rows(two, swap_mp(two, 2), code_row, BF)
+        expanded, dec, dec_sent = expand_rows(
+            scalars, tables, low_rank, swap_req(low_rank, 1), base, adapter_up_weight, own_adapters, base
+        )
+    with jax.named_scope("decode_rows"):
+        dec_chip = add_rows(dec, swap_req(dec_sent, 1), expanded)
+    with jax.named_scope("keys"):
+        send_k, keep_k = halve(scalars, [keep_k], [got_k], 1, dec_chip)
+        got_k = swap_req(send_k, 4)
     with jax.named_scope("values"):
-        own_v, other_v, dec_v = project_adapted(x_rows, query_key_value_weight, 2, expanded, adapter_up_weight, send_k)
+        own_v, other_v = project_adapted(x_rows, query_key_value_weight, 2, expanded, adapter_up_weight, send_k)
         core_v = swap_req(other_v, 1)
+    with jax.named_scope("decode_rows"):
+        dec_pair = add_rows(dec_chip, swap_req(dec_chip[4:], 2), own_v)
     with jax.named_scope("keys"):
-        send_k, keep_k = halve(scalars, [keep_k], [got_k], 1, other_v)
-        got_k = swap_req(send_k, 4)
+        (keys,) = finish(scalars, keep_k, got_k, query_key_value_bias, (1,), dec_pair)
+        keys_other = swap_req(keys, 1)
     with jax.named_scope("queries"):
-        own_q, other_q, dec_q = project_adapted(x_rows, query_key_value_weight, 0, expanded, adapter_up_weight, send_k)
+        own_q, other_q = project_adapted(x_rows, query_key_value_weight, 0, expanded, adapter_up_weight, keys)
         core_q = swap_req(other_q, 1)
-    with jax.named_scope("keys"):
-        (keys,) = finish(scalars, keep_k, got_k, query_key_value_bias, (1,), keep_k)
-        keys_other = swap_req(keys, 1)
-    with jax.named_scope("values_queries"):
-        send, keep = halve(scalars, [own_v, own_q], [core_v, core_q], 0, keys)
+    with jax.named_scope("decode_rows"):
+        dec = decode_finish(dec_pair, swap_req(dec_pair[2:], 4), query_key_value_bias, own_q)
+    with jax.named_scope("reduce_z"):
+        send, keep = halve(scalars, [own_v, own_q], [core_v, core_q], 0, dec[0])
         got = swap_req(send, 2)
-    with jax.named_scope("decode_rows"):
-        dec, dec_sent = split_decode((dec_q, dec_k, dec_v), send)
-        dec = dec + swap_req(dec_sent, 1)
-        for bits in (4, 2):
-            count = dec.shape[0] // 2
-            dec = dec[:count] + swap_req(dec[count:], bits)
-        dec = (dec.reshape(DEC, 3, feats) + query_key_value_bias[None]).astype(BF)
-
-    def decode_one(j, after):
-        return decode_attention(
-            cache_length_list[j : j + 1], dec[j : j + 1, 0:1], dec[j : j + 1, 1:2], dec[j : j + 1, 2:3], cache, j, after
-        ).reshape(1, feats)
-
-    with jax.named_scope("decode_attention"):
-        dec_first = decode_one(0, send)
-    with jax.named_scope("values_queries"):
-        send, keep = halve(scalars, [keep], [got], 1, dec_first, groups=2)
+    with jax.named_scope("reduce_z"):
+        send, keep = halve(scalars, [keep], [got], 1, send, groups=2)
         got = swap_req(send, 4)
     with jax.named_scope("decode_attention"):
-        dec_second = decode_one(1, send)
-    with jax.named_scope("values_queries"):
-        values, queries = finish(scalars, keep, got, query_key_value_bias, (2, 0), dec_second)
+        dec_out = decode_attention(cache_length_list, *dec, cache, send)
+        dec_out = dec_out.reshape(DEC, feats)
+    with jax.named_scope("reduce_z"):
+        values, queries = finish(scalars, keep, got, query_key_value_bias, (2, 0), dec_out)
         values_other = swap_req(values, 1)
     with jax.named_scope("prompt_attention"):
         attended = prompt_attention(
@@ -862,7 +945,7 @@
             values_other,
             code_col[: 2 * CHUNK],
             code_row,
-            (dec_first, dec_second),
+            dec_out,
         )
     with jax.named_scope("gather_attended"):
         own = gather_z(attended)

time: 230 us -> 220 us (0.957)
  waiting for transfers between devices: 121 us -> 105 us
  Pallas kernels: 51.6 us -> 56.4 us
    ppermute x32, waiting for transfers between devices: 90.6 us -> 80.7 us  [swap_req(): return lax.ppermute(x, 'req', [(i, i ^ bits) for i in range(2 * NZ)])]
    pallas_call x2 -> x9, Pallas kernels: 2.45 us -> 8.62 us  [the longest x1 5.27 us: decode_base(): pl.pallas_call(decode_base_kernel, grid=(parts,), out_shape=jax.ShapeDtyp...]
    ppermute x14, waiting for transfers between devices: 30.2 us -> 24.4 us  [swap_mp(): return lax.ppermute(x, 'mp', [(i, i ^ bits) for i in range(NM)])]
    unnamed x65 -> x63, local copies, waits for them, and re-layouts: 11.2 us -> 12.5 us
    pallas_call x2 -> x1, Pallas kernels: 10.7 us -> 10.4 us  [decode_attention(): pl.pallas_call(decode_kernel, grid_spec=pltpu.PrefetchScalarGridSpec(num_...]
  transfers between devices with their start and end apart: 46 -> 46, of which waited for: 32 -> 29; matrix products, arithmetic and copies ran while one was open for 1% -> 1% of each run, Pallas kernels for 15% -> 17%
where the time goes in v3:
time: 220 us
  waiting for transfers between devices  105 us (48%)
  Pallas kernels  56.4 us (26%)
  starting transfers between devices  42.4 us (19%)
  local copies, waits for them, and re-layouts  13.5 us (6%)
    ppermute x32, waiting for transfers between devices, swap_req(): return lax.ppermute(x, 'req', [(i, i ^ bits) for i in range(2 * NZ)])  80.7 us
    ppermute x32, starting transfers between devices, swap_req(): return lax.ppermute(x, 'req', [(i, i ^ bits) for i in range(2 * NZ)])  25.1 us
    ppermute x14, waiting for transfers between devices, swap_mp(): return lax.ppermute(x, 'mp', [(i, i ^ bits) for i in range(NM)])  24.4 us
    ppermute x14, starting transfers between devices, swap_mp(): return lax.ppermute(x, 'mp', [(i, i ^ bits) for i in range(NM)])  17.3 us
    unnamed x63, local copies, waits for them, and re-layouts  12.5 us
    pallas_call x1, Pallas kernels, decode_attention(): pl.pallas_call(decode_kernel, grid_spec=pltpu.PrefetchScalarGridSpec(num_...  10.4 us
    pallas_call x2, Pallas kernels, project_adapted(): pl.pallas_call(adapted_kernel, grid=(2,), out_shape=out_shape, in_specs=[...  9.96 us
    pallas_call x1, Pallas kernels, decode_base(): pl.pallas_call(decode_base_kernel, grid=(parts,), out_shape=jax.ShapeDtyp...  5.27 us
  transfers between devices with their start and end apart: 46, of which 29 were waited for; matrix products, arithmetic and copies ran while one was open for 1% of the time, Pallas kernels for 17%

profile of v3, /device:TPU:0, one launch (start us, length us, event | category | flops | bytes accessed | tf_op | source)
XLA Modules:
  0.0 219.5 jit_solution(2711971535283888613)
XLA Ops:
  0.0 4.0 %collective-permute-start.4 = (bf16[98,1792]{1,0:T(8,128)(2,1)}, bf16[98,1792]{1,0:T(8,128)(2,1)S(1)}, u32[]{:S(2)}, u32[]{:S(2)}) collective-permute-start(bf16[98,1792]{1,0:T(8,128)(2,1)} %x_ref.3), channel_id=1, source_target_pairs={{0,16},{4,20},{8,24},{12,28},{16,0},{20,4},{24,8},{28,12},{1,17},{... | collective-permute-start | bytes 1053704 | tf_op jit(solution)/shard_map/gather_home/ppermute | solution.py:33
  4.8 1.6 collective-permute-start.3
  8.6 1.6 collective-permute-start
  10.1 1.5 collective-permute-start.1
  14.0 2.5 %collective-permute-done.1.b2 = bf16[32,1792]{1,0:T(8,128)(2,1)S(1)} collective-permute-done((bf16[32,1792]{1,0:T(8,128)(2,1)S(1)}, bf16[32,1792]{1,0:T(8,128)(2,1)S(1)}, u32[]{:S(2)}, u32[]{:S(2)}) %collective-permute-start.1) | collective-permute-done | bytes 114720 | tf_op jit(solution)/shard_map/deal/ppermute | solution.py:37
  17.4 3.6 %collective-permute-done.4.__.x2 = bf16[98,1792]{1,0:T(8,128)(2,1)S(1)} collective-permute-done((bf16[98,1792]{1,0:T(8,128)(2,1)}, bf16[98,1792]{1,0:T(8,128)(2,1)S(1)}, u32[]{:S(2)}, u32[]{:S(2)}) %collective-permute-start.4) | collective-permute-done | bytes 351264 | tf_op jit(solution)/shard_map/gather_home/ppermute | solution.py:33
  23.8 2.3 %collective-permute-start.6 = (bf16[32,1792]{1,0:T(8,128)(2,1)S(1)}, bf16[32,1792]{1,0:T(8,128)(2,1)S(1)}, u32[]{:S(2)}, u32[]{:S(2)}) collective-permute-start(bf16[32,1792]{1,0:T(8,128)(2,1)S(1)} %get-tuple-element.58), channel_id=1, source_target_pairs={{0,16},{4,20},{8,24},{12,28},{16,0},{20,4},{24,8},{28,12},{1,17},{... | collective-permute-start | bytes 344072 | tf_op jit(solution)/shard_map/spread_z/ppermute | solution.py:33
  27.5 1.9 collective-permute-done.5.b1.t1
  29.3 6.1 %collective-permute-done.6.b2.t2 = bf16[32,1792]{1,0:T(8,128)(2,1)S(1)} collective-permute-done((bf16[32,1792]{1,0:T(8,128)(2,1)S(1)}, bf16[32,1792]{1,0:T(8,128)(2,1)S(1)}, u32[]{:S(2)}, u32[]{:S(2)}) %collective-permute-start.6) | collective-permute-done | bytes 114720 | tf_op jit(solution)/shard_map/spread_z/ppermute | solution.py:33
  40.1 1.5 collective-permute-start.9
  41.6 1.8 collective-permute-start.13
  43.4 1.5 collective-permute-start.10
  44.9 3.7 %collective-permute-done.9.c1 = bf16[144,896]{1,0:T(8,128)(2,1)S(1)} collective-permute-done((bf16[144,896]{1,0:T(8,128)(2,1)S(1)}, bf16[144,896]{1,0:T(8,128)(2,1)S(1)}, u32[]{:S(2)}, u32[]{:S(2)}) %collective-permute-start.9) | collective-permute-done | bytes 258080 | tf_op jit(solution)/shard_map/gather_chunks/ppermute | solution.py:37
  48.6 1.5 collective-permute-start.11
  50.1 2.2 collective-permute-done.13.x3
  54.5 4.0 %low_rank_rows.1._.a_ref = f32[32,512]{1,0:T(8,128)S(1)} custom-call(s32[7]{0:T(128)S(1)} %concatenate.12.s_ref.place_ref, s32[8,8]{1,0:T(8,128)S(1)} %maximum_convert_fusion.t_ref.table_ref, bf16[256,1792]{1,0:T(8,128)(2,1)S(1)} %bitcast.26, bf16[256,1792]{1,0:T(8,128)(2,1)S(1)} %collective-permute-done.12.db_ref, bf16[98,1792]{1,0:T(8,128)(2,1)S(1)} %copy-done.6, ...), custom_call_target="tpu_custom_call" | custom-call | flops 1 | bytes 1 | tf_op jit(solution)/shard_map/low_rank/low_rank_rows/pallas_call | solution.py:339
  60.6 4.9 %project_keys.1 = (bf16[256,1536]{1,0:T(8,128)(2,1)}, bf16[256,1536]{1,0:T(8,128)(2,1)}, bf16[528,896]{1,0:T(8,128)(2,1)}) custom-call(s32[7]{0:T(128)} %copy-done.22, bf16[144,896]{1,0:T(8,128)(2,1)} %copy-done.14, bf16[144,896]{1,0:T(8,128)(2,1)} %copy-done.25, bf16[144,896]{1,0:T(8,128)(2,1)} %copy-done.26, bf16[144,896]{1,0:T(8,128)(2,1)} %copy-done.27, ...), custom_call_target="tpu_custom_call" | custom-call | flops 1 | bytes 1 | tf_op jit(solution)/shard_map/keys/project_keys/pallas_call | solution.py:431
  66.2 5.3 %decode_base.1._.base_ref = f32[16,4608]{1,0:T(8,128)} custom-call(bf16[528,896]{1,0:T(8,128)(2,1)} %get-tuple-element.62.x_ref, bf16[3,896,1536]{2,1,0:T(8,128)(2,1)} %w_ref.7, bf16[256,1536]{1,0:T(8,128)(2,1)} %get-tuple-element.63._), custom_call_target="tpu_custom_call" | custom-call | flops 1 | bytes 1 | tf_op jit(solution)/shard_map/decode_rows/decode_base/pallas_call | solution.py:522
  73.2 1.8 collective-permute-start.18
  75.0 1.5 collective-permute-start.15
  76.5 2.4 %packed_codes.1 = (s32[512,1]{1,0:T(8,128)S(1)}, s32[1,512]{1,0:T(1,128)S(1)}) custom-call(s32[7]{0:T(128)S(1)} %copy-done.23, s32[8,8]{1,0:T(8,128)S(1)} %maximum_convert_fusion.t_ref.table_ref, bf16[256,768]{1,0:T(8,128)(2,1)S(1)} %get-tuple-element.65._), custom_call_target="tpu_custom_call" | custom-call | flops 1 | bytes 1 | tf_op jit(solution)/shard_map/low_rank/packed_codes/pallas_call | solution.py:299
  81.5 2.6 %expand_rows.1 = (bf16[2,528,128]{2,1,0:T(8,128)(2,1)S(1)}, f32[8,4608]{1,0:T(8,128)S(1)}, f32[8,4608]{1,0:T(8,128)S(1)}) custom-call(s32[7]{0:T(128)S(1)} %copy-done.23, s32[8,8]{1,0:T(8,128)S(1)} %maximum_convert_fusion.t_ref.table_ref, bf16[32,512]{1,0:T(8,128)(2,1)S(1)} %add_rows.5.low_ref, bf16[32,512]{1,0:T(8,128)(2,1)S(1)} %collective-permute-done.17.low_other_ref, ...), custom_call_target="tpu_custom_call" | custom-call | flops 1 | bytes 1 | tf_op jit(solution)/shard_map/low_rank/expand_rows/pallas_call | solution.py:384
  86.3 1.6 collective-permute-start.20
  87.9 1.5 collective-permute-start.21
  89.4 5.0 %project_adapted.2 = (bf16[256,1536]{1,0:T(8,128)(2,1)}, bf16[256,1536]{1,0:T(8,128)(2,1)}) custom-call(bf16[528,896]{1,0:T(8,128)(2,1)} %get-tuple-element.62.x_ref, bf16[3,896,1536]{2,1,0:T(8,128)(2,1)} %w_ref.7, bf16[2,528,128]{2,1,0:T(8,128)(2,1)} %copy-done.13, bf16[8,2,16,1536]{3,2,1,0:T(8,128)(2,1)} %u_ref.3, bf16[256,384]{1,0:T(8,128)(2,1)} %copy-done.21), custom_call_target="tpu_custom_call" | custom-call | flops 1 | bytes 1 | tf_op jit(solution)/shard_map/values/project_adapted/pallas_call | solution.py:459
  95.5 2.7 %collective-permute-done.20.got_ref = bf16[256,384]{1,0:T(8,128)(2,1)S(1)} collective-permute-done((bf16[256,384]{1,0:T(8,128)(2,1)S(1)}, bf16[256,384]{1,0:T(8,128)(2,1)S(1)}, u32[]{:S(2)}, u32[]{:S(2)}) %collective-permute-start.20) | collective-permute-done | bytes 196640 | tf_op jit(solution)/shard_map/keys/ppermute | solution.py:33
  99.5 5.0 %project_adapted.3 = (bf16[256,1536]{1,0:T(8,128)(2,1)}, bf16[256,1536]{1,0:T(8,128)(2,1)}) custom-call(bf16[528,896]{1,0:T(8,128)(2,1)} %get-tuple-element.62.x_ref, bf16[3,896,1536]{2,1,0:T(8,128)(2,1)} %w_ref.7, bf16[2,528,128]{2,1,0:T(8,128)(2,1)} %copy-done.13, bf16[8,2,16,1536]{3,2,1,0:T(8,128)(2,1)} %u_ref.3, bf16[256,384]{1,0:T(8,128)(2,1)} %copy-done.15), custom_call_target="tpu_custom_call" | custom-call | flops 1 | bytes 1 | tf_op jit(solution)/shard_map/queries/project_adapted/pallas_call | solution.py:459
  105.1 4.9 %collective-permute-done.24.b_ref = f32[2,4608]{1,0:T(2,128)S(1)} collective-permute-done((f32[2,4608]{1,0:T(2,128)S(1)}, f32[2,4608]{1,0:T(2,128)S(1)}, u32[]{:S(2)}, u32[]{:S(2)}) %collective-permute-start.24) | collective-permute-done | bytes 36896 | tf_op jit(solution)/shard_map/decode_rows/ppermute | solution.py:33
  113.3 19.2 %collective-permute-done.25.refs_1_ = bf16[256,1536]{1,0:T(8,128)(2,1)S(1)} collective-permute-done((bf16[256,1536]{1,0:T(8,128)(2,1)S(1)}, bf16[256,1536]{1,0:T(8,128)(2,1)S(1)}, u32[]{:S(2)}, u32[]{:S(2)}) %collective-permute-start.25) | collective-permute-done | bytes 786464 | tf_op jit(solution)/shard_map/reduce_z/ppermute | solution.py:33
  133.6 10.4 %decode_attention.1 = bf16[2,1,1536]{2,1,0:T(2,128)(2,1)S(1)} custom-call(s32[2]{0:T(128)S(1)} %copy-done.24, bf16[2,1,1536]{2,1,0:T(2,128)(2,1)S(1)} %get-tuple-element.77.refs_4_.q_ref, bf16[2,1,1536]{2,1,0:T(2,128)(2,1)S(1)} %get-tuple-element.82.k_ref, bf16[2,1,1536]{2,1,0:T(2,128)(2,1)S(1)} %get-tuple-element.83.v_ref, ...), custom_call_target="tpu_custom_call" | custom-call | flops 1 | bytes 1 | tf_op jit(solution)/shard_map/decode_attention/decode_attention/pallas_call | solution.py:672
  144.0 8.5 %collective-permute-done.26.got_ref = bf16[256,768]{1,0:T(8,128)(2,1)S(1)} collective-permute-done((bf16[256,768]{1,0:T(8,128)(2,1)S(1)}, bf16[256,768]{1,0:T(8,128)(2,1)S(1)}, u32[]{:S(2)}, u32[]{:S(2)}) %collective-permute-start.26) | collective-permute-done | bytes 393248 | tf_op jit(solution)/shard_map/reduce_z/ppermute | solution.py:33
  154.6 1.5 prompt_attention.1.refs_0_
  156.2 1.6 collective-permute-start.30
  157.7 9.2 %collective-permute-done.30.refs_2_ = bf16[272,384]{1,0:T(8,128)(2,1)S(1)} collective-permute-done((bf16[272,384]{1,0:T(8,128)(2,1)S(1)}, bf16[272,384]{1,0:T(8,128)(2,1)S(1)}, u32[]{:S(2)}, u32[]{:S(2)}) %collective-permute-start.30) | collective-permute-done | bytes 208928 | tf_op jit(solution)/shard_map/gather_attended/ppermute | solution.py:33
  167.4 1.7 collective-permute-done.29.refs_1_
  169.1 4.8 %collective-permute-done.31.refs_3_ = bf16[272,384]{1,0:T(8,128)(2,1)S(1)} collective-permute-done((bf16[272,384]{1,0:T(8,128)(2,1)S(1)}, bf16[272,384]{1,0:T(8,128)(2,1)S(1)}, u32[]{:S(2)}, u32[]{:S(2)}) %collective-permute-start.31) | collective-permute-done | bytes 208928 | tf_op jit(solution)/shard_map/gather_attended/ppermute | solution.py:33
  175.4 3.7 %out_project.1 = (bf16[144,896]{1,0:T(8,128)(2,1)S(1)}, bf16[144,896]{1,0:T(8,128)(2,1)S(1)}, bf16[144,896]{1,0:T(8,128)(2,1)S(1)}, bf16[144,896]{1,0:T(8,128)(2,1)S(1)}) custom-call(s32[7]{0:T(128)S(1)} %copy-done.23, bf16[272,384]{1,0:T(8,128)(2,1)S(1)} %prompt_attention.1.refs_0_, bf16[272,384]{1,0:T(8,128)(2,1)S(1)} %collective-permute-done.29.refs_1_, ...), custom_call_target="tpu_custom_call" | custom-call | flops 1 | bytes 1 | tf_op jit(solution)/shard_map/out_project/out_project/pallas_call | solution.py:729
  179.1 1.5 collective-permute-start.36
  180.7 1.5 collective-permute-start.37
  182.7 5.6 %collective-permute-done.36.c1 = bf16[144,896]{1,0:T(8,128)(2,1)S(1)} collective-permute-done((bf16[144,896]{1,0:T(8,128)(2,1)S(1)}, bf16[144,896]{1,0:T(8,128)(2,1)S(1)}, u32[]{:S(2)}, u32[]{:S(2)}) %collective-permute-start.36) | collective-permute-done | bytes 258080 | tf_op jit(solution)/shard_map/sum_mp/ppermute | solution.py:37
  188.2 5.9 %collective-permute-done.37.c2 = bf16[144,896]{1,0:T(8,128)(2,1)S(1)} collective-permute-done((bf16[144,896]{1,0:T(8,128)(2,1)S(1)}, bf16[144,896]{1,0:T(8,128)(2,1)S(1)}, u32[]{:S(2)}, u32[]{:S(2)}) %collective-permute-start.37) | collective-permute-done | bytes 258080 | tf_op jit(solution)/shard_map/sum_mp/ppermute | solution.py:37
  195.5 2.2 collective-permute-start.40
  197.7 2.0 collective-permute-start.41
  200.8 5.8 %collective-permute-done.40.a2 = bf16[64,896]{1,0:T(8,128)(2,1)S(1)} collective-permute-done((bf16[64,896]{1,0:T(8,128)(2,1)S(1)}, bf16[64,896]{1,0:T(8,128)(2,1)S(1)}, u32[]{:S(2)}, u32[]{:S(2)}) %collective-permute-start.40) | collective-permute-done | bytes 114720 | tf_op jit(solution)/shard_map/return_z/ppermute | solution.py:33
  208.8 1.5 collective-permute-start.43
  212.3 1.7 collective-permute-done.43.b1
  214.1 3.6 %collective-permute-done.44.b2 = bf16[32,1792]{1,0:T(8,128)(2,1)S(1)} collective-permute-done((bf16[32,1792]{1,0:T(8,128)(2,1)S(1)}, bf16[32,1792]{1,0:T(8,128)(2,1)S(1)}, u32[]{:S(2)}, u32[]{:S(2)}) %collective-permute-start.44) | collective-permute-done | bytes 114720 | tf_op jit(solution)/shard_map/return_plane/ppermute | solution.py:37
  217.7 1.8 add_home.1
  (153 shorter events, 44.8 us)
Async XLA Ops:
  0.0 21.0 %collective-permute-start.4 = (bf16[98,1792]{1,0:T(8,128)(2,1)}, bf16[98,1792]{1,0:T(8,128)(2,1)S(1)}, u32[]{:S(2)}, u32[]{:S(2)}) collective-permute-start(bf16[98,1792]{1,0:T(8,128)(2,1)} %x_ref.3), channel_id=1, source_target_pairs={{0,16},{4,20},{8,24},{12,28},{16,0},{20,4},{24,8},{28,12},{1,17},{... | collective-permute-start | bytes 1053704 | tf_op jit(solution)/shard_map/gather_home/ppermute | solution.py:33
  4.8 17.2 %collective-permute-start.3 = (bf16[98,1792]{1,0:T(8,128)(2,1)}, bf16[98,1792]{1,0:T(8,128)(2,1)S(1)}, u32[]{:S(2)}, u32[]{:S(2)}) collective-permute-start(bf16[98,1792]{1,0:T(8,128)(2,1)} %x_ref.3), channel_id=1, source_target_pairs={{0,8},{4,12},{8,0},{12,4},{16,24},{20,28},{24,16},{28,20},{1,9},{5... | collective-permute-start | bytes 1053704 | tf_op jit(solution)/shard_map/gather_home/ppermute | solution.py:33
  8.6 5.4 %collective-permute-start = (bf16[32,1792]{1,0:T(8,128)(2,1)S(1)}, bf16[32,1792]{1,0:T(8,128)(2,1)S(1)}, u32[]{:S(2)}, u32[]{:S(2)}) collective-permute-start(bf16[32,1792]{1,0:T(8,128)(2,1)S(1)} %get-tuple-element.53), channel_id=1, source_target_pairs={{0,1},{1,0},{2,3},{3,2},{4,5},{5,4},{6,7},{7,6},{8,9},{9,8},{10,11... | collective-permute-start | bytes 344072 | tf_op jit(solution)/shard_map/deal/ppermute | solution.py:37
  10.1 6.4 %collective-permute-start.1 = (bf16[32,1792]{1,0:T(8,128)(2,1)S(1)}, bf16[32,1792]{1,0:T(8,128)(2,1)S(1)}, u32[]{:S(2)}, u32[]{:S(2)}) collective-permute-start(bf16[32,1792]{1,0:T(8,128)(2,1)S(1)} %get-tuple-element.54), channel_id=1, source_target_pairs={{0,2},{1,3},{2,0},{3,1},{4,6},{5,7},{6,4},{7,5},{8,10},{9,11},{10,... | collective-permute-start | bytes 344072 | tf_op jit(solution)/shard_map/deal/ppermute | solution.py:37
  11.7 5.7 %collective-permute-start.2 = (bf16[32,1792]{1,0:T(8,128)(2,1)S(1)}, bf16[32,1792]{1,0:T(8,128)(2,1)S(1)}, u32[]{:S(2)}, u32[]{:S(2)}) collective-permute-start(bf16[32,1792]{1,0:T(8,128)(2,1)S(1)} %get-tuple-element.55), channel_id=1, source_target_pairs={{0,3},{1,2},{2,1},{3,0},{4,7},{5,6},{6,5},{7,4},{8,11},{9,10},{10,... | collective-permute-start | bytes 344072 | tf_op jit(solution)/shard_map/deal/ppermute | solution.py:37
  23.0 6.3 %collective-permute-start.5 = (bf16[32,1792]{1,0:T(8,128)(2,1)S(1)}, bf16[32,1792]{1,0:T(8,128)(2,1)S(1)}, u32[]{:S(2)}, u32[]{:S(2)}) collective-permute-start(bf16[32,1792]{1,0:T(8,128)(2,1)S(1)} %get-tuple-element.57), channel_id=1, source_target_pairs={{0,8},{4,12},{8,0},{12,4},{16,24},{20,28},{24,16},{28,20},{1,9},{5... | collective-permute-start | bytes 344072 | tf_op jit(solution)/shard_map/spread_z/ppermute | solution.py:33
  23.8 11.6 %collective-permute-start.6 = (bf16[32,1792]{1,0:T(8,128)(2,1)S(1)}, bf16[32,1792]{1,0:T(8,128)(2,1)S(1)}, u32[]{:S(2)}, u32[]{:S(2)}) collective-permute-start(bf16[32,1792]{1,0:T(8,128)(2,1)S(1)} %get-tuple-element.58), channel_id=1, source_target_pairs={{0,16},{4,20},{8,24},{12,28},{16,0},{20,4},{24,8},{28,12},{1,17},{... | collective-permute-start | bytes 344072 | tf_op jit(solution)/shard_map/spread_z/ppermute | solution.py:33
  26.2 9.2 %collective-permute-start.7 = (bf16[32,1792]{1,0:T(8,128)(2,1)S(1)}, bf16[32,1792]{1,0:T(8,128)(2,1)S(1)}, u32[]{:S(2)}, u32[]{:S(2)}) collective-permute-start(bf16[32,1792]{1,0:T(8,128)(2,1)S(1)} %get-tuple-element.59), channel_id=1, source_target_pairs={{0,24},{4,28},{8,16},{12,20},{16,8},{20,12},{24,0},{28,4},{1,25},{... | collective-permute-start | bytes 344072 | tf_op jit(solution)/shard_map/spread_z/ppermute | solution.py:33
  36.0 1.6 collective-permute-start.8
  39.9 12.4 %collective-permute-start.12 = (bf16[256,1792]{1,0:T(8,128)(2,1)S(1)}, bf16[256,1792]{1,0:T(8,128)(2,1)S(1)}, u32[]{:S(2)}, u32[]{:S(2)}) collective-permute-start(bf16[256,1792]{1,0:T(8,128)(2,1)S(1)} %copy_rows.1), channel_id=1, source_target_pairs={{0,4},{4,0},{8,12},{12,8},{16,20},{20,16},{24,28},{28,24},{1,5},{5... | collective-permute-start | bytes 2752520 | tf_op jit(solution)/shard_map/low_rank/ppermute | solution.py:33
  40.1 8.5 %collective-permute-start.9 = (bf16[144,896]{1,0:T(8,128)(2,1)S(1)}, bf16[144,896]{1,0:T(8,128)(2,1)S(1)}, u32[]{:S(2)}, u32[]{:S(2)}) collective-permute-start(bf16[144,896]{1,0:T(8,128)(2,1)S(1)} %pack_rows.1._.c0), channel_id=1, source_target_pairs={{0,1},{1,0},{2,3},{3,2},{4,5},{5,4},{6,7},{7,6},{8,9},{9,8},{10,11... | collective-permute-start | bytes 774152 | tf_op jit(solution)/shard_map/gather_chunks/ppermute | solution.py:37
  41.6 10.7 %collective-permute-start.13 = (bf16[98,1792]{1,0:T(8,128)(2,1)S(1)}, bf16[98,1792]{1,0:T(8,128)(2,1)S(1)}, u32[]{:S(2)}, u32[]{:S(2)}) collective-permute-start(bf16[98,1792]{1,0:T(8,128)(2,1)S(1)} %collective-permute-done.4.__.x2), channel_id=1, source_target_pairs={{0,8},{4,12},{8,0},{12,4},{16,24},{20,28},{24,16},{28,20},{1,9},{5... | collective-permute-start | bytes 1053704 | tf_op jit(solution)/shard_map/gather_home/ppermute | solution.py:33
  43.4 15.7 %collective-permute-start.10 = (bf16[144,896]{1,0:T(8,128)(2,1)S(1)}, bf16[144,896]{1,0:T(8,128)(2,1)S(1)}, u32[]{:S(2)}, u32[]{:S(2)}) collective-permute-start(bf16[144,896]{1,0:T(8,128)(2,1)S(1)} %pack_rows.1._.c0), channel_id=1, source_target_pairs={{0,2},{1,3},{2,0},{3,1},{4,6},{5,7},{6,4},{7,5},{8,10},{9,11},{10,... | collective-permute-start | bytes 774152 | tf_op jit(solution)/shard_map/gather_chunks/ppermute | solution.py:37
  48.6 10.5 %collective-permute-start.11 = (bf16[144,896]{1,0:T(8,128)(2,1)S(1)}, bf16[144,896]{1,0:T(8,128)(2,1)S(1)}, u32[]{:S(2)}, u32[]{:S(2)}) collective-permute-start(bf16[144,896]{1,0:T(8,128)(2,1)S(1)} %collective-permute-done.9.c1), channel_id=1, source_target_pairs={{0,2},{1,3},{2,0},{3,1},{4,6},{5,7},{6,4},{7,5},{8,10},{9,11},{10,... | collective-permute-start | bytes 774152 | tf_op jit(solution)/shard_map/gather_chunks/ppermute | solution.py:37
  65.5 6.9 %collective-permute-start.16 = (bf16[256,1536]{1,0:T(8,128)(2,1)}, bf16[256,1536]{1,0:T(8,128)(2,1)S(1)}, u32[]{:S(2)}, u32[]{:S(2)}) collective-permute-start(bf16[256,1536]{1,0:T(8,128)(2,1)} %get-tuple-element.63._), channel_id=1, source_target_pairs={{0,4},{4,0},{8,12},{12,8},{16,20},{20,16},{24,28},{28,24},{1,5},{5... | collective-permute-start | bytes 2359304 | tf_op jit(solution)/shard_map/keys/ppermute | solution.py:33
  65.6 5.9 %collective-permute-start.14 = (f32[32,512]{1,0:T(8,128)S(1)}, f32[32,512]{1,0:T(8,128)S(1)}, u32[]{:S(2)}, u32[]{:S(2)}) collective-permute-start(f32[32,512]{1,0:T(8,128)S(1)} %copy-done.19), channel_id=1, source_target_pairs={{0,1},{1,0},{2,3},{3,2},{4,5},{5,4},{6,7},{7,6},{8,9},{9,8},{10,11... | collective-permute-start | bytes 196616 | tf_op jit(solution)/shard_map/low_rank/ppermute | solution.py:37
  73.2 12.4 %collective-permute-start.18 = (bf16[256,768]{1,0:T(8,128)(2,1)S(1)}, bf16[256,768]{1,0:T(8,128)(2,1)S(1)}, u32[]{:S(2)}, u32[]{:S(2)}) collective-permute-start(bf16[256,768]{1,0:T(8,128)(2,1)S(1)} %get-tuple-element.65._), channel_id=1, source_target_pairs={{0,8},{4,12},{8,0},{12,4},{16,24},{20,28},{24,16},{28,20},{1,9},{5... | collective-permute-start | bytes 1179656 | tf_op jit(solution)/shard_map/keys/ppermute | solution.py:33
  75.0 4.3 %collective-permute-start.15 = (f32[32,512]{1,0:T(8,128)S(1)}, f32[32,512]{1,0:T(8,128)S(1)}, u32[]{:S(2)}, u32[]{:S(2)}) collective-permute-start(f32[32,512]{1,0:T(8,128)S(1)} %add_rows.4.refs_2_.a_ref), channel_id=1, source_target_pairs={{0,2},{1,3},{2,0},{3,1},{4,6},{5,7},{6,4},{7,5},{8,10},{9,11},{10,... | collective-permute-start | bytes 196616 | tf_op jit(solution)/shard_map/low_rank/ppermute | solution.py:37
  79.3 1.3 collective-permute-start.17
  84.1 1.4 collective-permute-start.19
  86.3 11.9 %collective-permute-start.20 = (bf16[256,384]{1,0:T(8,128)(2,1)S(1)}, bf16[256,384]{1,0:T(8,128)(2,1)S(1)}, u32[]{:S(2)}, u32[]{:S(2)}) collective-permute-start(bf16[256,384]{1,0:T(8,128)(2,1)S(1)} %get-tuple-element.71._), channel_id=1, source_target_pairs={{0,16},{4,20},{8,24},{12,28},{16,0},{20,4},{24,8},{28,12},{1,17},{... | collective-permute-start | bytes 589832 | tf_op jit(solution)/shard_map/keys/ppermute | solution.py:33
  87.9 6.5 %collective-permute-start.21 = (f32[4,4608]{1,0:T(4,128)S(1)}, f32[4,4608]{1,0:T(4,128)S(1)}, u32[]{:S(2)}, u32[]{:S(2)}) collective-permute-start(f32[4,4608]{1,0:T(4,128)S(1)} %slice.38), channel_id=1, source_target_pairs={{0,8},{4,12},{8,0},{12,4},{16,24},{20,28},{24,16},{28,20},{1,9},{5... | collective-permute-start | bytes 221192 | tf_op jit(solution)/shard_map/decode_rows/ppermute | solution.py:33
  99.5 11.6 %collective-permute-start.22 = (bf16[256,1536]{1,0:T(8,128)(2,1)}, bf16[256,1536]{1,0:T(8,128)(2,1)S(1)}, u32[]{:S(2)}, u32[]{:S(2)}) collective-permute-start(bf16[256,1536]{1,0:T(8,128)(2,1)} %get-tuple-element.75), channel_id=1, source_target_pairs={{0,4},{4,0},{8,12},{12,8},{16,20},{20,16},{24,28},{28,24},{1,5},{5... | collective-permute-start | bytes 2359304 | tf_op jit(solution)/shard_map/values/ppermute | solution.py:33
  104.5 6.6 %collective-permute-start.23 = (bf16[256,1536]{1,0:T(8,128)(2,1)}, bf16[256,1536]{1,0:T(8,128)(2,1)S(1)}, u32[]{:S(2)}, u32[]{:S(2)}) collective-permute-start(bf16[256,1536]{1,0:T(8,128)(2,1)} %get-tuple-element.76), channel_id=1, source_target_pairs={{0,4},{4,0},{8,12},{12,8},{16,20},{20,16},{24,28},{28,24},{1,5},{5... | collective-permute-start | bytes 2359304 | tf_op jit(solution)/shard_map/queries/ppermute | solution.py:33
  105.0 5.0 %collective-permute-start.24 = (f32[2,4608]{1,0:T(2,128)S(1)}, f32[2,4608]{1,0:T(2,128)S(1)}, u32[]{:S(2)}, u32[]{:S(2)}) collective-permute-start(f32[2,4608]{1,0:T(2,128)S(1)} %slice.39), channel_id=1, source_target_pairs={{0,16},{4,20},{8,24},{12,28},{16,0},{20,4},{24,8},{28,12},{1,17},{... | collective-permute-start | bytes 110600 | tf_op jit(solution)/shard_map/decode_rows/ppermute | solution.py:33
  113.2 19.3 %collective-permute-start.25 = (bf16[256,1536]{1,0:T(8,128)(2,1)S(1)}, bf16[256,1536]{1,0:T(8,128)(2,1)S(1)}, u32[]{:S(2)}, u32[]{:S(2)}) collective-permute-start(bf16[256,1536]{1,0:T(8,128)(2,1)S(1)} %get-tuple-element.79.refs_2_), channel_id=1, source_target_pairs={{0,8},{4,12},{8,0},{12,4},{16,24},{20,28},{24,16},{28,20},{1,9},{5... | collective-permute-start | bytes 2359304 | tf_op jit(solution)/shard_map/reduce_z/ppermute | solution.py:33
  133.2 19.3 %collective-permute-start.26 = (bf16[256,768]{1,0:T(8,128)(2,1)S(1)}, bf16[256,768]{1,0:T(8,128)(2,1)S(1)}, u32[]{:S(2)}, u32[]{:S(2)}) collective-permute-start(bf16[256,768]{1,0:T(8,128)(2,1)S(1)} %get-tuple-element.81._), channel_id=1, source_target_pairs={{0,16},{4,20},{8,24},{12,28},{16,0},{20,4},{24,8},{28,12},{1,17},{... | collective-permute-start | bytes 1179656 | tf_op jit(solution)/shard_map/reduce_z/ppermute | solution.py:33
  133.6 19.7 %collective-permute-start.27 = (bf16[256,384]{1,0:T(8,128)(2,1)S(1)}, bf16[256,384]{1,0:T(8,128)(2,1)S(1)}, u32[]{:S(2)}, u32[]{:S(2)}) collective-permute-start(bf16[256,384]{1,0:T(8,128)(2,1)S(1)} %copy-done.16), channel_id=1, source_target_pairs={{0,4},{4,0},{8,12},{12,8},{16,20},{20,16},{24,28},{28,24},{1,5},{5... | collective-permute-start | bytes 589832 | tf_op jit(solution)/shard_map/keys/ppermute | solution.py:33
  144.0 68.4 %copy-start.28 = (f32[1792]{0:T(1024)S(1)}, f32[1792]{0:T(1024)}, u32[]{:S(2)}) copy-start(f32[1792]{0:T(1024)} %param.25) | copy-start | bytes 21508
  144.0 73.7 %copy-start.7 = (bf16[98,1792]{1,0:T(8,128)(2,1)S(1)}, bf16[98,1792]{1,0:T(8,128)(2,1)}, u32[]{:S(2)}) copy-start(bf16[98,1792]{1,0:T(8,128)(2,1)} %x_ref.3) | copy-start | bytes 1053700
  153.1 1.5 collective-permute-start.28
  156.2 10.7 %collective-permute-start.30 = (bf16[272,384]{1,0:T(8,128)(2,1)S(1)}, bf16[272,384]{1,0:T(8,128)(2,1)S(1)}, u32[]{:S(2)}, u32[]{:S(2)}) collective-permute-start(bf16[272,384]{1,0:T(8,128)(2,1)S(1)} %prompt_attention.1.refs_0_), channel_id=1, source_target_pairs={{0,16},{4,20},{8,24},{12,28},{16,0},{20,4},{24,8},{28,12},{1,17},{... | collective-permute-start | bytes 626696 | tf_op jit(solution)/shard_map/gather_attended/ppermute | solution.py:33
  157.7 11.4 %collective-permute-start.29 = (bf16[272,384]{1,0:T(8,128)(2,1)S(1)}, bf16[272,384]{1,0:T(8,128)(2,1)S(1)}, u32[]{:S(2)}, u32[]{:S(2)}) collective-permute-start(bf16[272,384]{1,0:T(8,128)(2,1)S(1)} %prompt_attention.1.refs_0_), channel_id=1, source_target_pairs={{0,8},{4,12},{8,0},{12,4},{16,24},{20,28},{24,16},{28,20},{1,9},{5... | collective-permute-start | bytes 626696 | tf_op jit(solution)/shard_map/gather_attended/ppermute | solution.py:33
  166.9 7.0 %collective-permute-start.31 = (bf16[272,384]{1,0:T(8,128)(2,1)S(1)}, bf16[272,384]{1,0:T(8,128)(2,1)S(1)}, u32[]{:S(2)}, u32[]{:S(2)}) collective-permute-start(bf16[272,384]{1,0:T(8,128)(2,1)S(1)} %collective-permute-done.30.refs_2_), channel_id=1, source_target_pairs={{0,8},{4,12},{8,0},{12,4},{16,24},{20,28},{24,16},{28,20},{1,9},{5... | collective-permute-start | bytes 626696 | tf_op jit(solution)/shard_map/gather_attended/ppermute | solution.py:33
  166.9 7.0 %collective-permute-start.32 = (bf16[272,384]{1,0:T(8,128)(2,1)S(1)}, bf16[272,384]{1,0:T(8,128)(2,1)S(1)}, u32[]{:S(2)}, u32[]{:S(2)}) collective-permute-start(bf16[272,384]{1,0:T(8,128)(2,1)S(1)} %prompt_attention.1.refs_0_), channel_id=1, source_target_pairs={{0,4},{4,0},{8,12},{12,8},{16,20},{20,16},{24,28},{28,24},{1,5},{5... | collective-permute-start | bytes 626696 | tf_op jit(solution)/shard_map/gather_attended/ppermute | solution.py:33
  166.9 7.1 %collective-permute-start.34 = (bf16[272,384]{1,0:T(8,128)(2,1)S(1)}, bf16[272,384]{1,0:T(8,128)(2,1)S(1)}, u32[]{:S(2)}, u32[]{:S(2)}) collective-permute-start(bf16[272,384]{1,0:T(8,128)(2,1)S(1)} %collective-permute-done.30.refs_2_), channel_id=1, source_target_pairs={{0,4},{4,0},{8,12},{12,8},{16,20},{20,16},{24,28},{28,24},{1,5},{5... | collective-permute-start | bytes 626696 | tf_op jit(solution)/shard_map/gather_attended/ppermute | solution.py:33
  169.1 4.8 %collective-permute-start.33 = (bf16[272,384]{1,0:T(8,128)(2,1)S(1)}, bf16[272,384]{1,0:T(8,128)(2,1)S(1)}, u32[]{:S(2)}, u32[]{:S(2)}) collective-permute-start(bf16[272,384]{1,0:T(8,128)(2,1)S(1)} %collective-permute-done.29.refs_1_), channel_id=1, source_target_pairs={{0,4},{4,0},{8,12},{12,8},{16,20},{20,16},{24,28},{28,24},{1,5},{5... | collective-permute-start | bytes 626696 | tf_op jit(solution)/shard_map/gather_attended/ppermute | solution.py:33
  173.9 1.5 collective-permute-start.35
  179.1 9.1 %collective-permute-start.36 = (bf16[144,896]{1,0:T(8,128)(2,1)S(1)}, bf16[144,896]{1,0:T(8,128)(2,1)S(1)}, u32[]{:S(2)}, u32[]{:S(2)}) collective-permute-start(bf16[144,896]{1,0:T(8,128)(2,1)S(1)} %get-tuple-element.88), channel_id=1, source_target_pairs={{0,1},{1,0},{2,3},{3,2},{4,5},{5,4},{6,7},{7,6},{8,9},{9,8},{10,11... | collective-permute-start | bytes 774152 | tf_op jit(solution)/shard_map/sum_mp/ppermute | solution.py:37
  180.7 13.5 %collective-permute-start.37 = (bf16[144,896]{1,0:T(8,128)(2,1)S(1)}, bf16[144,896]{1,0:T(8,128)(2,1)S(1)}, u32[]{:S(2)}, u32[]{:S(2)}) collective-permute-start(bf16[144,896]{1,0:T(8,128)(2,1)S(1)} %get-tuple-element.89), channel_id=1, source_target_pairs={{0,2},{1,3},{2,0},{3,1},{4,6},{5,7},{6,4},{7,5},{8,10},{9,11},{10,... | collective-permute-start | bytes 774152 | tf_op jit(solution)/shard_map/sum_mp/ppermute | solution.py:37
  182.2 12.0 %collective-permute-start.38 = (bf16[144,896]{1,0:T(8,128)(2,1)S(1)}, bf16[144,896]{1,0:T(8,128)(2,1)S(1)}, u32[]{:S(2)}, u32[]{:S(2)}) collective-permute-start(bf16[144,896]{1,0:T(8,128)(2,1)S(1)} %get-tuple-element.90), channel_id=1, source_target_pairs={{0,3},{1,2},{2,1},{3,0},{4,7},{5,6},{6,5},{7,4},{8,11},{9,10},{10,... | collective-permute-start | bytes 774152 | tf_op jit(solution)/shard_map/sum_mp/ppermute | solution.py:37
  195.2 5.6 %collective-permute-start.39 = (bf16[64,896]{1,0:T(8,128)(2,1)S(1)}, bf16[64,896]{1,0:T(8,128)(2,1)S(1)}, u32[]{:S(2)}, u32[]{:S(2)}) collective-permute-start(bf16[64,896]{1,0:T(8,128)(2,1)S(1)} %get-tuple-element.92), channel_id=1, source_target_pairs={{0,8},{4,12},{8,0},{12,4},{16,24},{20,28},{24,16},{28,20},{1,9},{5... | collective-permute-start | bytes 344072 | tf_op jit(solution)/shard_map/return_z/ppermute | solution.py:33
  195.5 11.0 %collective-permute-start.40 = (bf16[64,896]{1,0:T(8,128)(2,1)S(1)}, bf16[64,896]{1,0:T(8,128)(2,1)S(1)}, u32[]{:S(2)}, u32[]{:S(2)}) collective-permute-start(bf16[64,896]{1,0:T(8,128)(2,1)S(1)} %get-tuple-element.93), channel_id=1, source_target_pairs={{0,16},{4,20},{8,24},{12,28},{16,0},{20,4},{24,8},{28,12},{1,17},{... | collective-permute-start | bytes 344072 | tf_op jit(solution)/shard_map/return_z/ppermute | solution.py:33
  197.7 8.9 %collective-permute-start.41 = (bf16[64,896]{1,0:T(8,128)(2,1)S(1)}, bf16[64,896]{1,0:T(8,128)(2,1)S(1)}, u32[]{:S(2)}, u32[]{:S(2)}) collective-permute-start(bf16[64,896]{1,0:T(8,128)(2,1)S(1)} %get-tuple-element.94), channel_id=1, source_target_pairs={{0,24},{4,28},{8,16},{12,20},{16,8},{20,12},{24,0},{28,4},{1,25},{... | collective-permute-start | bytes 344072 | tf_op jit(solution)/shard_map/return_z/ppermute | solution.py:33
  206.6 1.6 collective-permute-start.42
  208.8 5.3 %collective-permute-start.43 = (bf16[32,1792]{1,0:T(8,128)(2,1)S(1)}, bf16[32,1792]{1,0:T(8,128)(2,1)S(1)}, u32[]{:S(2)}, u32[]{:S(2)}) collective-permute-start(bf16[32,1792]{1,0:T(8,128)(2,1)S(1)} %get-tuple-element.96), channel_id=1, source_target_pairs={{0,1},{1,0},{2,3},{3,2},{4,5},{5,4},{6,7},{7,6},{8,9},{9,8},{10,11... | collective-permute-start | bytes 344072 | tf_op jit(solution)/shard_map/return_plane/ppermute | solution.py:37
  210.3 7.4 %collective-permute-start.44 = (bf16[32,1792]{1,0:T(8,128)(2,1)S(1)}, bf16[32,1792]{1,0:T(8,128)(2,1)S(1)}, u32[]{:S(2)}, u32[]{:S(2)}) collective-permute-start(bf16[32,1792]{1,0:T(8,128)(2,1)S(1)} %get-tuple-element.97), channel_id=1, source_target_pairs={{0,2},{1,3},{2,0},{3,1},{4,6},{5,7},{6,4},{7,5},{8,10},{9,11},{10,... | collective-permute-start | bytes 344072 | tf_op jit(solution)/shard_map/return_plane/ppermute | solution.py:37
  210.8 6.8 %collective-permute-start.45 = (bf16[32,1792]{1,0:T(8,128)(2,1)S(1)}, bf16[32,1792]{1,0:T(8,128)(2,1)S(1)}, u32[]{:S(2)}, u32[]{:S(2)}) collective-permute-start(bf16[32,1792]{1,0:T(8,128)(2,1)S(1)} %get-tuple-element.98), channel_id=1, source_target_pairs={{0,3},{1,2},{2,1},{3,0},{4,7},{5,6},{6,5},{7,4},{8,11},{9,10},{10,... | collective-permute-start | bytes 344072 | tf_op jit(solution)/shard_map/return_plane/ppermute | solution.py:37
  (27 other events, 292.6 us)

commit v4 on v3

--- a/solution.py
+++ b/solution.py
@@ -40,11 +40,6 @@
 def gather_z(x):
     far, near = swap_req(x, 4), swap_req(x, 2)
     return [x, near, far, swap_req(far, 2)]
-
-
-def gather_mp(x):
-    one, two = swap_mp(x, 1), swap_mp(x, 2)
-    return [x, one, two, swap_mp(one, 2)]
 
 
 def limit(mib):
@@ -347,7 +342,7 @@
     )(scalars, tables, down, down_other, *pieces, *stats, affine)
 
 
-def expand_kernel(s_ref, t_ref, low_ref, low_other_ref, base_ref, up_ref, _, o_ref, keep_ref, send_ref, *, count):
+def expand_kernel(s_ref, t_ref, low_ref, low_other_ref, base_ref, key_ref, up_ref, _, o_ref, keep_ref, send_ref, *, count):
     m, r, core = s_ref[4], s_ref[5], s_ref[6]
     found = sources(s_ref, t_ref)
     width = count * ADAPTER_RANK
@@ -368,28 +363,29 @@
         total = total + lax.dot_general(hit, low, (((1,), (1,)), ((), ())), preferred_element_type=F32)
     feats = up_ref.shape[3]
     half = keep_ref.shape[0]
-    keep_ref[...] = base_ref[:half, :]
-    send_ref[...] = base_ref[half:, :]
+    keep_ref[:, feats : 2 * feats] = key_ref[:half, :]
+    send_ref[:, feats : 2 * feats] = key_ref[half:, :]
     for t, first in ((0, 0), (1, 2 * feats)):
         rows = total[:, t * width : (t + 1) * width].astype(BF)
         o_ref[t] = rows
         up = up_ref[:, t].reshape(-1, feats)
         term = jnp.dot(rows[NM * CHUNK :, :], up, preferred_element_type=F32)
-        keep_ref[:, first : first + feats] += term[:half]
-        send_ref[:, first : first + feats] += term[half:]
-
-
-def expand_rows(scalars, tables, low, low_other, base, up, count, after):
-    half = jax.ShapeDtypeStruct((base.shape[0] // 2, base.shape[1]), F32)
+        term = term + base_ref[:, t * feats : (t + 1) * feats]
+        keep_ref[:, first : first + feats] = term[:half]
+        send_ref[:, first : first + feats] = term[half:]
+
+
+def expand_rows(scalars, tables, low, low_other, base, keys, up, count, after):
+    half = jax.ShapeDtypeStruct((keys.shape[0] // 2, 3 * keys.shape[1]), F32)
     return pl.pallas_call(
         functools.partial(expand_kernel, count=count),
         out_shape=[jax.ShapeDtypeStruct((2, PACKED, count * ADAPTER_RANK), BF), half, half],
-        in_specs=[SMEM] * 2 + [VMEM] * 4 + [ANY],
+        in_specs=[SMEM] * 2 + [VMEM] * 5 + [ANY],
         out_specs=[VMEM] * 3,
         compiler_params=limit(32),
         cost_estimate=SMALL,
         name="expand_rows",
-    )(scalars, tables, low, low_other, base, up, after)
+    )(scalars, tables, low, low_other, base, keys, up, after)
 
 
 def emit_sums(y, own_ref, other_ref):
@@ -398,7 +394,7 @@
     other_ref[...] = y[half : 2 * half].astype(BF)
 
 
-def first_project_kernel(s_ref, c0, c1, c2, c3, w_ref, _, own_ref, other_ref, x):
+def first_project_kernel(s_ref, c0, c1, c2, c3, w_ref, _, own_ref, other_ref, dec_ref, x):
     z, m, core = s_ref[3], s_ref[4], s_ref[6]
 
     @pl.when(pl.program_id(0) == 0)
@@ -413,7 +409,9 @@
         rows = jnp.concatenate([chunk[CHUNK:, :] for chunk in chunks], axis=0)
         x[NM * CHUNK :, :] = jnp.dot((want == at).astype(BF), rows, preferred_element_type=F32).astype(BF)
 
-    emit_sums(jnp.dot(x[: NM * CHUNK, :], w_ref[0], preferred_element_type=F32), own_ref, other_ref)
+    y = jnp.dot(x[...], w_ref[0], preferred_element_type=F32)
+    emit_sums(y, own_ref, other_ref)
+    dec_ref[...] = y[NM * CHUNK :]
 
 
 def project_rows(scalars, chunks, weight, part, after):
@@ -424,9 +422,10 @@
     out_shape = [
         jax.ShapeDtypeStruct((half, feats), BF),
         jax.ShapeDtypeStruct((half, feats), BF),
+        jax.ShapeDtypeStruct((PACKED - NM * CHUNK, feats), F32),
         jax.ShapeDtypeStruct((PACKED, depth), BF),
     ]
-    out_specs = [pl.BlockSpec((v.shape[0], tile), lambda j: (0, j)) for v in out_shape[:2]]
+    out_specs = [pl.BlockSpec((v.shape[0], tile), lambda j: (0, j)) for v in out_shape[:3]]
     out_specs.append(pl.BlockSpec((PACKED, depth), lambda j: (0, 0)))
     return pl.pallas_call(
         first_project_kernel,
@@ -517,15 +516,15 @@
 
 
 def decode_base(rows, weight, after):
-    parts, depth, feats = weight.shape
+    _, depth, feats = weight.shape
     count = PACKED - NM * CHUNK
     return pl.pallas_call(
         decode_base_kernel,
-        grid=(parts,),
-        out_shape=jax.ShapeDtypeStruct((count, parts * feats), F32),
+        grid=(2,),
+        out_shape=jax.ShapeDtypeStruct((count, 2 * feats), F32),
         in_specs=[
             pl.BlockSpec((count, depth), lambda p: (NM * CHUNK // count, 0)),
-            pl.BlockSpec((1, depth, feats), lambda p: (p, 0, 0)),
+            pl.BlockSpec((1, depth, feats), lambda p: (2 * p, 0, 0)),
             ANY,
         ],
         out_specs=pl.BlockSpec((count, feats), lambda p: (0, p)),
@@ -691,19 +690,42 @@
     )(lengths, q, k, v, cache, after)
 
 
+def out_term(z, k, own, other, w_ref):
+    width = own.shape[1]
+    half = own.shape[0] - DECODE_ROWS
+    block = place_of(jnp.bitwise_xor(z, k))
+    w = w_ref[pl.ds(pl.multiple_of(block * width, width), width), :]
+    rows = jnp.concatenate([own[:half, :], other[:half, :]], axis=0)
+    return jnp.dot(rows, w, preferred_element_type=F32)
+
+
+def out_first_kernel(place_ref, *refs):
+    own, other, w_ref, o_ref = refs[:3], refs[3:6], refs[6], refs[7]
+    total = None
+    for k in range(NZ - 1):
+        term = out_term(place_ref[3], k, own[k], other[k], w_ref)
+        total = term if total is None else total + term
+    o_ref[...] = total
+
+
+def out_first(scalars, own, other, weight):
+    return pl.pallas_call(
+        out_first_kernel,
+        out_shape=jax.ShapeDtypeStruct((NM * CHUNK, weight.shape[1]), F32),
+        in_specs=[SMEM] + [VMEM] * 7,
+        out_specs=VMEM,
+        compiler_params=limit(40),
+        cost_estimate=SMALL,
+        name="out_first",
+    )(scalars, *own[:3], *other[:3], weight)
+
+
 def out_kernel(place_ref, *refs):
-    own, other, w_ref, outs, mixed = refs[:4], refs[4:8], refs[8], refs[9:13], refs[13]
+    own, other, first_ref, w_ref, outs, mixed = refs[:4], refs[4:8], refs[8], refs[9], refs[10:14], refs[14]
     z, m, core = place_ref[3], place_ref[4], place_ref[6]
     width = own[0].shape[1]
     half = own[0].shape[0] - DECODE_ROWS
-    total = None
-    for k in range(NZ):
-        block = place_of(jnp.bitwise_xor(z, k))
-        w = w_ref[pl.ds(pl.multiple_of(block * width, width), width), :]
-        rows = jnp.concatenate([own[k][:half, :], other[k][:half, :]], axis=0)
-        term = jnp.dot(rows, w, preferred_element_type=F32)
-        total = term if total is None else total + term
-    mixed[...] = total.astype(BF)
+    mixed[...] = (first_ref[...] + out_term(z, NZ - 1, own[-1], other[-1], w_ref)).astype(BF)
     tails = jnp.concatenate([v[half:, :] for v in own + other], axis=0)
     count = 2 * NZ * DEC
     n, at = iota((count, tails.shape[0]), 0), iota((count, tails.shape[0]), 1)
@@ -724,18 +746,18 @@
         out[CHUNK:, :] = jnp.dot(pick, decode, preferred_element_type=F32).astype(BF)
 
 
-def out_project(scalars, own, other, weight):
+def out_project(scalars, own, other, first, weight):
     feats = weight.shape[1]
     return pl.pallas_call(
         out_kernel,
         out_shape=[jax.ShapeDtypeStruct((CHUNK + DCH, feats), BF)] * NM,
-        in_specs=[SMEM] + [VMEM] * 9,
+        in_specs=[SMEM] + [VMEM] * 10,
         out_specs=[VMEM] * NM,
         scratch_shapes=[pltpu.VMEM((NM * CHUNK, feats), BF)],
         compiler_params=limit(40),
         cost_estimate=SMALL,
         name="out_project",
-    )(scalars, *own, *other, weight)
+    )(scalars, *own, *other, first, weight)
 
 
 def unpack_kernel(s_ref, t_ref, c0, c1, c2, c3, *outs):
@@ -885,13 +907,13 @@
     with jax.named_scope("pack"):
         chunk = pack_rows(scalars, tables, mine, theirs)
     with jax.named_scope("gather_chunks"):
-        chunks = gather_mp(chunk)
+        chunks = [chunk] + [swap_mp(chunk, k) for k in range(1, NM)]
 
     with jax.named_scope("low_rank"):
-        down_other = swap_req(copy_rows(down, chunk), 1)
+        down_other = swap_req(copy_rows(down, mine), 1)
         part = low_rank_rows(scalars, tables, down, down_other, pieces, spread, affine)
     with jax.named_scope("keys"):
-        own_k, other_k, x_rows = project_rows(scalars, chunks, query_key_value_weight, 1, part)
+        own_k, other_k, dec_k, x_rows = project_rows(scalars, chunks, query_key_value_weight, 1, part)
         core_k = swap_req(other_k, 1)
     with jax.named_scope("decode_rows"):
         base = decode_base(x_rows, query_key_value_weight, other_k)
@@ -904,7 +926,7 @@
         code_col, code_row = packed_codes(scalars, tables, send_k)
         low_rank = add_rows(two, swap_mp(two, 2), code_row, BF)
         expanded, dec, dec_sent = expand_rows(
-            scalars, tables, low_rank, swap_req(low_rank, 1), base, adapter_up_weight, own_adapters, base
+            scalars, tables, low_rank, swap_req(low_rank, 1), base, dec_k, adapter_up_weight, own_adapters, base
         )
     with jax.named_scope("decode_rows"):
         dec_chip = add_rows(dec, swap_req(dec_sent, 1), expanded)
@@ -919,13 +941,13 @@
     with jax.named_scope("keys"):
         (keys,) = finish(scalars, keep_k, got_k, query_key_value_bias, (1,), dec_pair)
         keys_other = swap_req(keys, 1)
+    with jax.named_scope("decode_rows"):
+        dec = decode_finish(dec_pair, swap_req(dec_pair[2:], 4), query_key_value_bias, keys)
     with jax.named_scope("queries"):
-        own_q, other_q = project_adapted(x_rows, query_key_value_weight, 0, expanded, adapter_up_weight, keys)
+        own_q, other_q = project_adapted(x_rows, query_key_value_weight, 0, expanded, adapter_up_weight, dec[0])
         core_q = swap_req(other_q, 1)
-    with jax.named_scope("decode_rows"):
-        dec = decode_finish(dec_pair, swap_req(dec_pair[2:], 4), query_key_value_bias, own_q)
     with jax.named_scope("reduce_z"):
-        send, keep = halve(scalars, [own_v, own_q], [core_v, core_q], 0, dec[0])
+        send, keep = halve(scalars, [own_v, own_q], [core_v, core_q], 0, core_q)
         got = swap_req(send, 2)
     with jax.named_scope("reduce_z"):
         send, keep = halve(scalars, [keep], [got], 1, send, groups=2)
@@ -951,7 +973,8 @@
         own = gather_z(attended)
         other = [swap_req(v, 1) for v in own]
     with jax.named_scope("out_project"):
-        mixed = out_project(scalars, own, other, output_weight)
+        first = out_first(scalars, own, other, output_weight)
+        mixed = out_project(scalars, own, other, first, output_weight)
     with jax.named_scope("sum_mp"):
         shares = [mixed[0]] + [swap_mp(mixed[k], k) for k in range(1, NM)]
     with jax.named_scope("return_z"):

time: 220 us -> 213 us (0.968)
  starting transfers between devices: 42.4 us -> 47.8 us
  local copies, waits for them, and re-layouts: 13.5 us -> 8.14 us
  Pallas kernels: 56.4 us -> 52 us
    ppermute x32, starting transfers between devices: 25.1 us -> 30.5 us  [swap_req(): return lax.ppermute(x, 'req', [(i, i ^ bits) for i in range(2 * NZ)])]
    unnamed x63 -> x59, local copies, waits for them, and re-layouts: 12.5 us -> 7.22 us
    pallas_call x1, Pallas kernels: 10.4 us -> 6.78 us  [decode_attention(): pl.pallas_call(decode_kernel, grid_spec=pltpu.PrefetchScalarGridSpec(num_...]
    pallas_call x1 -> x2, Pallas kernels: 5.27 us -> 6.08 us  [the longest x1 3.82 us: decode_base(): pl.pallas_call(decode_base_kernel, grid=(2,), out_shape=jax.ShapeDtypeStr...]
  transfers between devices with their start and end apart: 46 -> 46, of which waited for: 29 -> 31; matrix products, arithmetic and copies ran while one was open for 1% -> 1% of each run, Pallas kernels for 17% -> 17%
where the time goes in v4:
time: 213 us
  waiting for transfers between devices  103 us (48%)
  Pallas kernels  52 us (24%)
  starting transfers between devices  47.8 us (22%)
  local copies, waits for them, and re-layouts  8.14 us (4%)
    ppermute x32, waiting for transfers between devices, swap_req(): return lax.ppermute(x, 'req', [(i, i ^ bits) for i in range(2 * NZ)])  79.6 us
    ppermute x32, starting transfers between devices, swap_req(): return lax.ppermute(x, 'req', [(i, i ^ bits) for i in range(2 * NZ)])  30.5 us
    ppermute x14, waiting for transfers between devices, swap_mp(): return lax.ppermute(x, 'mp', [(i, i ^ bits) for i in range(NM)])  23 us
    ppermute x14, starting transfers between devices, swap_mp(): return lax.ppermute(x, 'mp', [(i, i ^ bits) for i in range(NM)])  17.3 us
    pallas_call x2, Pallas kernels, project_adapted(): pl.pallas_call(adapted_kernel, grid=(2,), out_shape=out_shape, in_specs=[...  9.92 us
    unnamed x59, local copies, waits for them, and re-layouts  7.22 us
    pallas_call x1, Pallas kernels, decode_attention(): pl.pallas_call(decode_kernel, grid_spec=pltpu.PrefetchScalarGridSpec(num_...  6.78 us
    pallas_call x1, Pallas kernels, project_rows(): pl.pallas_call(first_project_kernel, grid=(feats // tile,), out_shape=out...  4.94 us
  transfers between devices with their start and end apart: 46, of which 31 were waited for; matrix products, arithmetic and copies ran while one was open for 1% of the time, Pallas kernels for 17%

profile of v4, /device:TPU:0, one launch (start us, length us, event | category | flops | bytes accessed | tf_op | source)
XLA Modules:
  0.0 212.7 jit_solution(16852774444824774979)
XLA Ops:
  0.0 4.0 %collective-permute-start.4 = (bf16[98,1792]{1,0:T(8,128)(2,1)}, bf16[98,1792]{1,0:T(8,128)(2,1)S(1)}, u32[]{:S(2)}, u32[]{:S(2)}) collective-permute-start(bf16[98,1792]{1,0:T(8,128)(2,1)} %x_ref.3), channel_id=1, source_target_pairs={{0,16},{4,20},{8,24},{12,28},{16,0},{20,4},{24,8},{28,12},{1,17},{... | collective-permute-start | bytes 1053704 | tf_op jit(solution)/shard_map/gather_home/ppermute | solution.py:33
  4.8 1.6 collective-permute-start.3
  8.6 1.6 collective-permute-start
  14.0 2.5 %collective-permute-done.1.b2 = bf16[32,1792]{1,0:T(8,128)(2,1)S(1)} collective-permute-done((bf16[32,1792]{1,0:T(8,128)(2,1)S(1)}, bf16[32,1792]{1,0:T(8,128)(2,1)S(1)}, u32[]{:S(2)}, u32[]{:S(2)}) %collective-permute-start.1) | collective-permute-done | bytes 114720 | tf_op jit(solution)/shard_map/deal/ppermute | solution.py:37
  17.4 3.6 %collective-permute-done.4.__.x2 = bf16[98,1792]{1,0:T(8,128)(2,1)S(1)} collective-permute-done((bf16[98,1792]{1,0:T(8,128)(2,1)}, bf16[98,1792]{1,0:T(8,128)(2,1)S(1)}, u32[]{:S(2)}, u32[]{:S(2)}) %collective-permute-start.4) | collective-permute-done | bytes 351264 | tf_op jit(solution)/shard_map/gather_home/ppermute | solution.py:33
  23.8 2.4 %collective-permute-start.6 = (bf16[32,1792]{1,0:T(8,128)(2,1)S(1)}, bf16[32,1792]{1,0:T(8,128)(2,1)S(1)}, u32[]{:S(2)}, u32[]{:S(2)}) collective-permute-start(bf16[32,1792]{1,0:T(8,128)(2,1)S(1)} %get-tuple-element.59), channel_id=1, source_target_pairs={{0,16},{4,20},{8,24},{12,28},{16,0},{20,4},{24,8},{28,12},{1,17},{... | collective-permute-start | bytes 344072 | tf_op jit(solution)/shard_map/spread_z/ppermute | solution.py:33
  27.5 1.9 collective-permute-done.5.b1.t1
  29.3 6.1 %collective-permute-done.6.b2.t2 = bf16[32,1792]{1,0:T(8,128)(2,1)S(1)} collective-permute-done((bf16[32,1792]{1,0:T(8,128)(2,1)S(1)}, bf16[32,1792]{1,0:T(8,128)(2,1)S(1)}, u32[]{:S(2)}, u32[]{:S(2)}) %collective-permute-start.6) | collective-permute-done | bytes 114720 | tf_op jit(solution)/shard_map/spread_z/ppermute | solution.py:33
  36.7 1.8 collective-permute-start.13
  40.0 1.6 collective-permute-start.10
  43.5 3.8 %collective-permute-done.13.x3 = bf16[98,1792]{1,0:T(8,128)(2,1)S(1)} collective-permute-done((bf16[98,1792]{1,0:T(8,128)(2,1)S(1)}, bf16[98,1792]{1,0:T(8,128)(2,1)S(1)}, u32[]{:S(2)}, u32[]{:S(2)}) %collective-permute-start.13) | collective-permute-done | bytes 351264 | tf_op jit(solution)/shard_map/gather_home/ppermute | solution.py:33
  47.4 4.0 %low_rank_rows.1._.a_ref = f32[32,512]{1,0:T(8,128)S(1)} custom-call(s32[7]{0:T(128)S(1)} %concatenate.12.s_ref.place_ref, s32[8,8]{1,0:T(8,128)S(1)} %maximum_convert_fusion.t_ref.table_ref, bf16[256,1792]{1,0:T(8,128)(2,1)S(1)} %bitcast.26, bf16[256,1792]{1,0:T(8,128)(2,1)S(1)} %collective-permute-done.12.db_ref, bf16[98,1792]{1,0:T(8,128)(2,1)S(1)} %copy-done.4, ...), custom_call_target="tpu_custom_call" | custom-call | flops 1 | bytes 1 | tf_op jit(solution)/shard_map/low_rank/low_rank_rows/pallas_call | solution.py:334
  52.0 1.8 collective-permute-done.10.c2
  55.8 4.9 %project_keys.1 = (bf16[256,1536]{1,0:T(8,128)(2,1)}, bf16[256,1536]{1,0:T(8,128)(2,1)}, f32[16,1536]{1,0:T(8,128)}, bf16[528,896]{1,0:T(8,128)(2,1)}) custom-call(s32[7]{0:T(128)} %copy-done.16, bf16[144,896]{1,0:T(8,128)(2,1)} %copy-done.10, bf16[144,896]{1,0:T(8,128)(2,1)} %copy-done.25, bf16[144,896]{1,0:T(8,128)(2,1)} %copy-done.23, ...), custom_call_target="tpu_custom_call" | custom-call | flops 1 | bytes 1 | tf_op jit(solution)/shard_map/keys/project_keys/pallas_call | solution.py:430
  60.8 1.6 collective-permute-start.14
  62.3 3.8 %decode_base.1._.base_ref = f32[16,3072]{1,0:T(8,128)} custom-call(bf16[528,896]{1,0:T(8,128)(2,1)} %get-tuple-element.63.x_ref, bf16[3,896,1536]{2,1,0:T(8,128)(2,1)} %w_ref.7, bf16[256,1536]{1,0:T(8,128)(2,1)} %get-tuple-element.64._), custom_call_target="tpu_custom_call" | custom-call | flops 1 | bytes 1 | tf_op jit(solution)/shard_map/decode_rows/decode_base/pallas_call | solution.py:521
  67.9 1.9 collective-permute-start.18
  69.8 1.5 collective-permute-start.15
  71.3 2.4 %packed_codes.1 = (s32[512,1]{1,0:T(8,128)S(1)}, s32[1,512]{1,0:T(1,128)S(1)}) custom-call(s32[7]{0:T(128)S(1)} %copy-done.17, s32[8,8]{1,0:T(8,128)S(1)} %maximum_convert_fusion.t_ref.table_ref, bf16[256,768]{1,0:T(8,128)(2,1)S(1)} %get-tuple-element.66._), custom_call_target="tpu_custom_call" | custom-call | flops 1 | bytes 1 | tf_op jit(solution)/shard_map/low_rank/packed_codes/pallas_call | solution.py:294
  76.3 2.6 %expand_rows.1 = (bf16[2,528,128]{2,1,0:T(8,128)(2,1)S(1)}, f32[8,4608]{1,0:T(8,128)S(1)}, f32[8,4608]{1,0:T(8,128)S(1)}) custom-call(s32[7]{0:T(128)S(1)} %copy-done.17, s32[8,8]{1,0:T(8,128)S(1)} %maximum_convert_fusion.t_ref.table_ref, bf16[32,512]{1,0:T(8,128)(2,1)S(1)} %add_rows.5.low_ref, bf16[32,512]{1,0:T(8,128)(2,1)S(1)} %collective-permute-done.17.low_other_ref, ...), custom_call_target="tpu_custom_call" | custom-call | flops 1 | bytes 1 | tf_op jit(solution)/shard_map/low_rank/expand_rows/pallas_call | solution.py:380
  81.0 1.7 collective-permute-start.22
  84.1 4.9 %project_adapted.2 = (bf16[256,1536]{1,0:T(8,128)(2,1)}, bf16[256,1536]{1,0:T(8,128)(2,1)}) custom-call(bf16[528,896]{1,0:T(8,128)(2,1)} %get-tuple-element.63.x_ref, bf16[3,896,1536]{2,1,0:T(8,128)(2,1)} %w_ref.7, bf16[2,528,128]{2,1,0:T(8,128)(2,1)} %copy-done.9, bf16[8,2,16,1536]{3,2,1,0:T(8,128)(2,1)} %u_ref.3, bf16[256,384]{1,0:T(8,128)(2,1)} %copy-done.18), custom_call_target="tpu_custom_call" | custom-call | flops 1 | bytes 1 | tf_op jit(solution)/shard_map/values/project_adapted/pallas_call | solution.py:458
  90.3 1.9 collective-permute-start.21
  93.5 1.7 collective-permute-done.21.b_ref
  95.8 5.0 %project_adapted.3 = (bf16[256,1536]{1,0:T(8,128)(2,1)}, bf16[256,1536]{1,0:T(8,128)(2,1)}) custom-call(bf16[528,896]{1,0:T(8,128)(2,1)} %get-tuple-element.63.x_ref, bf16[3,896,1536]{2,1,0:T(8,128)(2,1)} %w_ref.7, bf16[2,528,128]{2,1,0:T(8,128)(2,1)} %copy-done.9, bf16[8,2,16,1536]{3,2,1,0:T(8,128)(2,1)} %u_ref.3, bf16[2,1,1536]{2,1,0:T(2,128)(2,1)} %copy-done.20), custom_call_target="tpu_custom_call" | custom-call | flops 1 | bytes 1 | tf_op jit(solution)/shard_map/queries/project_adapted/pallas_call | solution.py:458
  100.8 2.5 %collective-permute-done.24.refs_3_.refs_4_ = bf16[256,1536]{1,0:T(8,128)(2,1)S(1)} collective-permute-done((bf16[256,1536]{1,0:T(8,128)(2,1)}, bf16[256,1536]{1,0:T(8,128)(2,1)S(1)}, u32[]{:S(2)}, u32[]{:S(2)}) %collective-permute-start.24) | collective-permute-done | bytes 786464 | tf_op jit(solution)/shard_map/queries/ppermute | solution.py:33
  105.4 1.7 collective-permute-start.25
  107.0 18.0 %collective-permute-done.25.refs_1_ = bf16[256,1536]{1,0:T(8,128)(2,1)S(1)} collective-permute-done((bf16[256,1536]{1,0:T(8,128)(2,1)S(1)}, bf16[256,1536]{1,0:T(8,128)(2,1)S(1)}, u32[]{:S(2)}, u32[]{:S(2)}) %collective-permute-start.25) | collective-permute-done | bytes 786464 | tf_op jit(solution)/shard_map/reduce_z/ppermute | solution.py:33
  125.7 1.9 collective-permute-start.26
  127.6 6.8 %decode_attention.1 = bf16[2,1,1536]{2,1,0:T(2,128)(2,1)S(1)} custom-call(s32[2]{0:T(128)S(1)} %copy-done.22, bf16[2,1,1536]{2,1,0:T(2,128)(2,1)S(1)} %copy-done.21, bf16[2,1,1536]{2,1,0:T(2,128)(2,1)S(1)} %get-tuple-element.84.k_ref, bf16[2,1,1536]{2,1,0:T(2,128)(2,1)S(1)} %get-tuple-element.85.v_ref, bf16[2,2048,2,1536]{3,2,1,0:T(2,128)(2,1)} %c_ref.1, ...), custom_call_target="tpu_custom_call" | custom-call | flops 1 | bytes 1 | tf_op jit(solution)/shard_map/decode_attention/decode_attention/pallas_call | solution.py:671
  134.4 11.0 %collective-permute-done.26.got_ref = bf16[256,768]{1,0:T(8,128)(2,1)S(1)} collective-permute-done((bf16[256,768]{1,0:T(8,128)(2,1)S(1)}, bf16[256,768]{1,0:T(8,128)(2,1)S(1)}, u32[]{:S(2)}, u32[]{:S(2)}) %collective-permute-start.26) | collective-permute-done | bytes 393248 | tf_op jit(solution)/shard_map/reduce_z/ppermute | solution.py:33
  147.6 1.5 prompt_attention.1.refs_0_
  149.2 2.2 %collective-permute-start.29 = (bf16[272,384]{1,0:T(8,128)(2,1)S(1)}, bf16[272,384]{1,0:T(8,128)(2,1)S(1)}, u32[]{:S(2)}, u32[]{:S(2)}) collective-permute-start(bf16[272,384]{1,0:T(8,128)(2,1)S(1)} %prompt_attention.1.refs_0_), channel_id=1, source_target_pairs={{0,8},{4,12},{8,0},{12,4},{16,24},{20,28},{24,16},{28,20},{1,9},{5... | collective-permute-start | bytes 626696 | tf_op jit(solution)/shard_map/gather_attended/ppermute | solution.py:33
  151.5 9.5 %collective-permute-done.30.refs_2_ = bf16[272,384]{1,0:T(8,128)(2,1)S(1)} collective-permute-done((bf16[272,384]{1,0:T(8,128)(2,1)S(1)}, bf16[272,384]{1,0:T(8,128)(2,1)S(1)}, u32[]{:S(2)}, u32[]{:S(2)}) %collective-permute-start.30) | collective-permute-done | bytes 208928 | tf_op jit(solution)/shard_map/gather_attended/ppermute | solution.py:33
  161.6 6.4 %collective-permute-done.31.refs_3_ = bf16[272,384]{1,0:T(8,128)(2,1)S(1)} collective-permute-done((bf16[272,384]{1,0:T(8,128)(2,1)S(1)}, bf16[272,384]{1,0:T(8,128)(2,1)S(1)}, u32[]{:S(2)}, u32[]{:S(2)}) %collective-permute-start.31) | collective-permute-done | bytes 208928 | tf_op jit(solution)/shard_map/gather_attended/ppermute | solution.py:33
  168.0 2.3 %out_first.1.refs_8_ = f32[512,896]{1,0:T(8,128)S(1)} custom-call(s32[7]{0:T(128)S(1)} %copy-done.17, bf16[272,384]{1,0:T(8,128)(2,1)S(1)} %prompt_attention.1.refs_0_, bf16[272,384]{1,0:T(8,128)(2,1)S(1)} %collective-permute-done.29.refs_1_, bf16[272,384]{1,0:T(8,128)(2,1)S(1)} %collective-permute-done.30.refs_2_, ...), custom_call_target="tpu_custom_call" | custom-call | flops 1 | bytes 1 | tf_op jit(solution)/shard_map/out_project/out_first/pallas_call | solution.py:712
  170.3 2.1 out_project.1
  173.1 1.5 collective-permute-start.37
  176.0 5.5 %collective-permute-done.36.c1 = bf16[144,896]{1,0:T(8,128)(2,1)S(1)} collective-permute-done((bf16[144,896]{1,0:T(8,128)(2,1)S(1)}, bf16[144,896]{1,0:T(8,128)(2,1)S(1)}, u32[]{:S(2)}, u32[]{:S(2)}) %collective-permute-start.36) | collective-permute-done | bytes 258080 | tf_op jit(solution)/shard_map/sum_mp/ppermute | solution.py:37
  181.5 4.5 %collective-permute-done.37.c2 = bf16[144,896]{1,0:T(8,128)(2,1)S(1)} collective-permute-done((bf16[144,896]{1,0:T(8,128)(2,1)S(1)}, bf16[144,896]{1,0:T(8,128)(2,1)S(1)}, u32[]{:S(2)}, u32[]{:S(2)}) %collective-permute-start.37) | collective-permute-done | bytes 258080 | tf_op jit(solution)/shard_map/sum_mp/ppermute | solution.py:37
  186.0 1.6 collective-permute-done.38.c3
  188.9 2.4 %collective-permute-start.40 = (bf16[64,896]{1,0:T(8,128)(2,1)S(1)}, bf16[64,896]{1,0:T(8,128)(2,1)S(1)}, u32[]{:S(2)}, u32[]{:S(2)}) collective-permute-start(bf16[64,896]{1,0:T(8,128)(2,1)S(1)} %get-tuple-element.95), channel_id=1, source_target_pairs={{0,16},{4,20},{8,24},{12,28},{16,0},{20,4},{24,8},{28,12},{1,17},{... | collective-permute-start | bytes 344072 | tf_op jit(solution)/shard_map/return_z/ppermute | solution.py:33
  191.3 1.7 collective-permute-start.41
  193.0 1.9 collective-permute-done.39.a1
  194.9 5.6 %collective-permute-done.40.a2 = bf16[64,896]{1,0:T(8,128)(2,1)S(1)} collective-permute-done((bf16[64,896]{1,0:T(8,128)(2,1)S(1)}, bf16[64,896]{1,0:T(8,128)(2,1)S(1)}, u32[]{:S(2)}, u32[]{:S(2)}) %collective-permute-start.40) | collective-permute-done | bytes 114720 | tf_op jit(solution)/shard_map/return_z/ppermute | solution.py:33
  206.4 2.5 %collective-permute-done.43.b1 = bf16[32,1792]{1,0:T(8,128)(2,1)S(1)} collective-permute-done((bf16[32,1792]{1,0:T(8,128)(2,1)S(1)}, bf16[32,1792]{1,0:T(8,128)(2,1)S(1)}, u32[]{:S(2)}, u32[]{:S(2)}) %collective-permute-start.43) | collective-permute-done | bytes 114720 | tf_op jit(solution)/shard_map/return_plane/ppermute | solution.py:37
  208.9 2.0 collective-permute-done.44.b2
  210.9 1.8 add_home.1
  (150 shorter events, 44.8 us)
Async XLA Ops:
  0.0 21.0 %collective-permute-start.4 = (bf16[98,1792]{1,0:T(8,128)(2,1)}, bf16[98,1792]{1,0:T(8,128)(2,1)S(1)}, u32[]{:S(2)}, u32[]{:S(2)}) collective-permute-start(bf16[98,1792]{1,0:T(8,128)(2,1)} %x_ref.3), channel_id=1, source_target_pairs={{0,16},{4,20},{8,24},{12,28},{16,0},{20,4},{24,8},{28,12},{1,17},{... | collective-permute-start | bytes 1053704 | tf_op jit(solution)/shard_map/gather_home/ppermute | solution.py:33
  4.8 46.6 %copy-start.16 = (s32[7]{0:T(128)}, s32[7]{0:T(128)S(1)}, u32[]{:S(2)}) copy-start(s32[7]{0:T(128)S(1)} %concatenate.12.s_ref.place_ref) | copy-start | bytes 88
  4.8 17.2 %collective-permute-start.3 = (bf16[98,1792]{1,0:T(8,128)(2,1)}, bf16[98,1792]{1,0:T(8,128)(2,1)S(1)}, u32[]{:S(2)}, u32[]{:S(2)}) collective-permute-start(bf16[98,1792]{1,0:T(8,128)(2,1)} %x_ref.3), channel_id=1, source_target_pairs={{0,8},{4,12},{8,0},{12,4},{16,24},{20,28},{24,16},{28,20},{1,9},{5... | collective-permute-start | bytes 1053704 | tf_op jit(solution)/shard_map/gather_home/ppermute | solution.py:33
  7.4 40.0 %copy-start.4 = (bf16[98,1792]{1,0:T(8,128)(2,1)S(1)}, bf16[98,1792]{1,0:T(8,128)(2,1)}, u32[]{:S(2)}) copy-start(bf16[98,1792]{1,0:T(8,128)(2,1)} %x_ref.3) | copy-start | bytes 1053700
  8.6 5.4 %collective-permute-start = (bf16[32,1792]{1,0:T(8,128)(2,1)S(1)}, bf16[32,1792]{1,0:T(8,128)(2,1)S(1)}, u32[]{:S(2)}, u32[]{:S(2)}) collective-permute-start(bf16[32,1792]{1,0:T(8,128)(2,1)S(1)} %get-tuple-element.54), channel_id=1, source_target_pairs={{0,1},{1,0},{2,3},{3,2},{4,5},{5,4},{6,7},{7,6},{8,9},{9,8},{10,11... | collective-permute-start | bytes 344072 | tf_op jit(solution)/shard_map/deal/ppermute | solution.py:37
  10.1 6.4 %collective-permute-start.1 = (bf16[32,1792]{1,0:T(8,128)(2,1)S(1)}, bf16[32,1792]{1,0:T(8,128)(2,1)S(1)}, u32[]{:S(2)}, u32[]{:S(2)}) collective-permute-start(bf16[32,1792]{1,0:T(8,128)(2,1)S(1)} %get-tuple-element.55), channel_id=1, source_target_pairs={{0,2},{1,3},{2,0},{3,1},{4,6},{5,7},{6,4},{7,5},{8,10},{9,11},{10,... | collective-permute-start | bytes 344072 | tf_op jit(solution)/shard_map/deal/ppermute | solution.py:37
  11.7 5.7 %collective-permute-start.2 = (bf16[32,1792]{1,0:T(8,128)(2,1)S(1)}, bf16[32,1792]{1,0:T(8,128)(2,1)S(1)}, u32[]{:S(2)}, u32[]{:S(2)}) collective-permute-start(bf16[32,1792]{1,0:T(8,128)(2,1)S(1)} %get-tuple-element.56), channel_id=1, source_target_pairs={{0,3},{1,2},{2,1},{3,0},{4,7},{5,6},{6,5},{7,4},{8,11},{9,10},{10,... | collective-permute-start | bytes 344072 | tf_op jit(solution)/shard_map/deal/ppermute | solution.py:37
  23.0 6.3 %collective-permute-start.5 = (bf16[32,1792]{1,0:T(8,128)(2,1)S(1)}, bf16[32,1792]{1,0:T(8,128)(2,1)S(1)}, u32[]{:S(2)}, u32[]{:S(2)}) collective-permute-start(bf16[32,1792]{1,0:T(8,128)(2,1)S(1)} %get-tuple-element.58), channel_id=1, source_target_pairs={{0,8},{4,12},{8,0},{12,4},{16,24},{20,28},{24,16},{28,20},{1,9},{5... | collective-permute-start | bytes 344072 | tf_op jit(solution)/shard_map/spread_z/ppermute | solution.py:33
  23.8 11.6 %collective-permute-start.6 = (bf16[32,1792]{1,0:T(8,128)(2,1)S(1)}, bf16[32,1792]{1,0:T(8,128)(2,1)S(1)}, u32[]{:S(2)}, u32[]{:S(2)}) collective-permute-start(bf16[32,1792]{1,0:T(8,128)(2,1)S(1)} %get-tuple-element.59), channel_id=1, source_target_pairs={{0,16},{4,20},{8,24},{12,28},{16,0},{20,4},{24,8},{28,12},{1,17},{... | collective-permute-start | bytes 344072 | tf_op jit(solution)/shard_map/spread_z/ppermute | solution.py:33
  26.2 9.2 %collective-permute-start.7 = (bf16[32,1792]{1,0:T(8,128)(2,1)S(1)}, bf16[32,1792]{1,0:T(8,128)(2,1)S(1)}, u32[]{:S(2)}, u32[]{:S(2)}) collective-permute-start(bf16[32,1792]{1,0:T(8,128)(2,1)S(1)} %get-tuple-element.60), channel_id=1, source_target_pairs={{0,24},{4,28},{8,16},{12,20},{16,8},{20,12},{24,0},{28,4},{1,25},{... | collective-permute-start | bytes 344072 | tf_op jit(solution)/shard_map/spread_z/ppermute | solution.py:33
  36.1 11.3 %collective-permute-start.12 = (bf16[256,1792]{1,0:T(8,128)(2,1)S(1)}, bf16[256,1792]{1,0:T(8,128)(2,1)S(1)}, u32[]{:S(2)}, u32[]{:S(2)}) collective-permute-start(bf16[256,1792]{1,0:T(8,128)(2,1)S(1)} %copy_rows.1), channel_id=1, source_target_pairs={{0,4},{4,0},{8,12},{12,8},{16,20},{20,16},{24,28},{28,24},{1,5},{5... | collective-permute-start | bytes 2752520 | tf_op jit(solution)/shard_map/low_rank/ppermute | solution.py:33
  36.2 2.8 %collective-permute-start.8 = (bf16[128,896]{1,0:T(8,128)(2,1)S(1)}, bf16[128,896]{1,0:T(8,128)(2,1)S(1)}, u32[]{:S(2)}, u32[]{:S(2)}) collective-permute-start(bf16[128,896]{1,0:T(8,128)(2,1)S(1)} %get-tuple-element.62), channel_id=1, source_target_pairs={{0,4},{4,0},{8,12},{12,8},{16,20},{20,16},{24,28},{28,24},{1,5},{5... | collective-permute-start | bytes 688136 | tf_op jit(solution)/shard_map/spread_z/ppermute | solution.py:33
  36.7 10.7 %collective-permute-start.13 = (bf16[98,1792]{1,0:T(8,128)(2,1)S(1)}, bf16[98,1792]{1,0:T(8,128)(2,1)S(1)}, u32[]{:S(2)}, u32[]{:S(2)}) collective-permute-start(bf16[98,1792]{1,0:T(8,128)(2,1)S(1)} %collective-permute-done.4.__.x2), channel_id=1, source_target_pairs={{0,8},{4,12},{8,0},{12,4},{16,24},{20,28},{24,16},{28,20},{1,9},{5... | collective-permute-start | bytes 1053704 | tf_op jit(solution)/shard_map/gather_home/ppermute | solution.py:33
  40.0 13.9 %collective-permute-start.10 = (bf16[144,896]{1,0:T(8,128)(2,1)S(1)}, bf16[144,896]{1,0:T(8,128)(2,1)S(1)}, u32[]{:S(2)}, u32[]{:S(2)}) collective-permute-start(bf16[144,896]{1,0:T(8,128)(2,1)S(1)} %pack_rows.1.c0), channel_id=1, source_target_pairs={{0,2},{1,3},{2,0},{3,1},{4,6},{5,7},{6,4},{7,5},{8,10},{9,11},{10,... | collective-permute-start | bytes 774152 | tf_op jit(solution)/shard_map/gather_chunks/ppermute | solution.py:37
  41.6 12.3 %collective-permute-start.11 = (bf16[144,896]{1,0:T(8,128)(2,1)S(1)}, bf16[144,896]{1,0:T(8,128)(2,1)S(1)}, u32[]{:S(2)}, u32[]{:S(2)}) collective-permute-start(bf16[144,896]{1,0:T(8,128)(2,1)S(1)} %pack_rows.1.c0), channel_id=1, source_target_pairs={{0,3},{1,2},{2,1},{3,0},{4,7},{5,6},{6,5},{7,4},{8,11},{9,10},{10,... | collective-permute-start | bytes 774152 | tf_op jit(solution)/shard_map/gather_chunks/ppermute | solution.py:37
  43.0 12.1 %collective-permute-start.9 = (bf16[144,896]{1,0:T(8,128)(2,1)S(1)}, bf16[144,896]{1,0:T(8,128)(2,1)S(1)}, u32[]{:S(2)}, u32[]{:S(2)}) collective-permute-start(bf16[144,896]{1,0:T(8,128)(2,1)S(1)} %pack_rows.1.c0), channel_id=1, source_target_pairs={{0,1},{1,0},{2,3},{3,2},{4,5},{5,4},{6,7},{7,6},{8,9},{9,8},{10,11... | collective-permute-start | bytes 774152 | tf_op jit(solution)/shard_map/gather_chunks/ppermute | solution.py:37
  60.7 6.4 %collective-permute-start.16 = (bf16[256,1536]{1,0:T(8,128)(2,1)}, bf16[256,1536]{1,0:T(8,128)(2,1)S(1)}, u32[]{:S(2)}, u32[]{:S(2)}) collective-permute-start(bf16[256,1536]{1,0:T(8,128)(2,1)} %get-tuple-element.64._), channel_id=1, source_target_pairs={{0,4},{4,0},{8,12},{12,8},{16,20},{20,16},{24,28},{28,24},{1,5},{5... | collective-permute-start | bytes 2359304 | tf_op jit(solution)/shard_map/keys/ppermute | solution.py:33
  60.8 5.4 %collective-permute-start.14 = (f32[32,512]{1,0:T(8,128)S(1)}, f32[32,512]{1,0:T(8,128)S(1)}, u32[]{:S(2)}, u32[]{:S(2)}) collective-permute-start(f32[32,512]{1,0:T(8,128)S(1)} %copy-done.14), channel_id=1, source_target_pairs={{0,1},{1,0},{2,3},{3,2},{4,5},{5,4},{6,7},{7,6},{8,9},{9,8},{10,11... | collective-permute-start | bytes 196616 | tf_op jit(solution)/shard_map/low_rank/ppermute | solution.py:37
  67.9 12.4 %collective-permute-start.18 = (bf16[256,768]{1,0:T(8,128)(2,1)S(1)}, bf16[256,768]{1,0:T(8,128)(2,1)S(1)}, u32[]{:S(2)}, u32[]{:S(2)}) collective-permute-start(bf16[256,768]{1,0:T(8,128)(2,1)S(1)} %get-tuple-element.66._), channel_id=1, source_target_pairs={{0,8},{4,12},{8,0},{12,4},{16,24},{20,28},{24,16},{28,20},{1,9},{5... | collective-permute-start | bytes 1179656 | tf_op jit(solution)/shard_map/keys/ppermute | solution.py:33
  69.8 4.3 %collective-permute-start.15 = (f32[32,512]{1,0:T(8,128)S(1)}, f32[32,512]{1,0:T(8,128)S(1)}, u32[]{:S(2)}, u32[]{:S(2)}) collective-permute-start(f32[32,512]{1,0:T(8,128)S(1)} %add_rows.4.refs_2_.a_ref), channel_id=1, source_target_pairs={{0,2},{1,3},{2,0},{3,1},{4,6},{5,7},{6,4},{7,5},{8,10},{9,11},{10,... | collective-permute-start | bytes 196616 | tf_op jit(solution)/shard_map/low_rank/ppermute | solution.py:37
  74.1 1.3 collective-permute-start.17
  78.9 1.4 collective-permute-start.19
  81.0 11.9 %collective-permute-start.22 = (bf16[256,384]{1,0:T(8,128)(2,1)S(1)}, bf16[256,384]{1,0:T(8,128)(2,1)S(1)}, u32[]{:S(2)}, u32[]{:S(2)}) collective-permute-start(bf16[256,384]{1,0:T(8,128)(2,1)S(1)} %get-tuple-element.73._), channel_id=1, source_target_pairs={{0,16},{4,20},{8,24},{12,28},{16,0},{20,4},{24,8},{28,12},{1,17},{... | collective-permute-start | bytes 589832 | tf_op jit(solution)/shard_map/keys/ppermute | solution.py:33
  82.7 6.4 %collective-permute-start.20 = (f32[4,4608]{1,0:T(4,128)S(1)}, f32[4,4608]{1,0:T(4,128)S(1)}, u32[]{:S(2)}, u32[]{:S(2)}) collective-permute-start(f32[4,4608]{1,0:T(4,128)S(1)} %slice.38), channel_id=1, source_target_pairs={{0,8},{4,12},{8,0},{12,4},{16,24},{20,28},{24,16},{28,20},{1,9},{5... | collective-permute-start | bytes 221192 | tf_op jit(solution)/shard_map/decode_rows/ppermute | solution.py:33
  90.3 4.9 %collective-permute-start.21 = (f32[2,4608]{1,0:T(2,128)S(1)}, f32[2,4608]{1,0:T(2,128)S(1)}, u32[]{:S(2)}, u32[]{:S(2)}) collective-permute-start(f32[2,4608]{1,0:T(2,128)S(1)} %slice.39), channel_id=1, source_target_pairs={{0,16},{4,20},{8,24},{12,28},{16,0},{20,4},{24,8},{28,12},{1,17},{... | collective-permute-start | bytes 110600 | tf_op jit(solution)/shard_map/decode_rows/ppermute | solution.py:33
  92.1 8.7 %collective-permute-start.23 = (bf16[256,1536]{1,0:T(8,128)(2,1)}, bf16[256,1536]{1,0:T(8,128)(2,1)S(1)}, u32[]{:S(2)}, u32[]{:S(2)}) collective-permute-start(bf16[256,1536]{1,0:T(8,128)(2,1)} %get-tuple-element.78), channel_id=1, source_target_pairs={{0,4},{4,0},{8,12},{12,8},{16,20},{20,16},{24,28},{28,24},{1,5},{5... | collective-permute-start | bytes 2359304 | tf_op jit(solution)/shard_map/values/ppermute | solution.py:33
  100.8 2.5 %collective-permute-start.24 = (bf16[256,1536]{1,0:T(8,128)(2,1)}, bf16[256,1536]{1,0:T(8,128)(2,1)S(1)}, u32[]{:S(2)}, u32[]{:S(2)}) collective-permute-start(bf16[256,1536]{1,0:T(8,128)(2,1)} %get-tuple-element.79), channel_id=1, source_target_pairs={{0,4},{4,0},{8,12},{12,8},{16,20},{20,16},{24,28},{28,24},{1,5},{5... | collective-permute-start | bytes 2359304 | tf_op jit(solution)/shard_map/queries/ppermute | solution.py:33
  105.4 19.6 %collective-permute-start.25 = (bf16[256,1536]{1,0:T(8,128)(2,1)S(1)}, bf16[256,1536]{1,0:T(8,128)(2,1)S(1)}, u32[]{:S(2)}, u32[]{:S(2)}) collective-permute-start(bf16[256,1536]{1,0:T(8,128)(2,1)S(1)} %get-tuple-element.81.refs_2_), channel_id=1, source_target_pairs={{0,8},{4,12},{8,0},{12,4},{16,24},{20,28},{24,16},{28,20},{1,9},{5... | collective-permute-start | bytes 2359304 | tf_op jit(solution)/shard_map/reduce_z/ppermute | solution.py:33
  125.7 19.7 %collective-permute-start.26 = (bf16[256,768]{1,0:T(8,128)(2,1)S(1)}, bf16[256,768]{1,0:T(8,128)(2,1)S(1)}, u32[]{:S(2)}, u32[]{:S(2)}) collective-permute-start(bf16[256,768]{1,0:T(8,128)(2,1)S(1)} %get-tuple-element.83._), channel_id=1, source_target_pairs={{0,16},{4,20},{8,24},{12,28},{16,0},{20,4},{24,8},{28,12},{1,17},{... | collective-permute-start | bytes 1179656 | tf_op jit(solution)/shard_map/reduce_z/ppermute | solution.py:33
  127.6 18.6 %collective-permute-start.27 = (bf16[256,384]{1,0:T(8,128)(2,1)S(1)}, bf16[256,384]{1,0:T(8,128)(2,1)S(1)}, u32[]{:S(2)}, u32[]{:S(2)}) collective-permute-start(bf16[256,384]{1,0:T(8,128)(2,1)S(1)} %finish_sums.2._.ka_ref), channel_id=1, source_target_pairs={{0,4},{4,0},{8,12},{12,8},{16,20},{20,16},{24,28},{28,24},{1,5},{5... | collective-permute-start | bytes 589832 | tf_op jit(solution)/shard_map/keys/ppermute | solution.py:33
  146.1 1.5 collective-permute-start.28
  149.1 11.8 %collective-permute-start.30 = (bf16[272,384]{1,0:T(8,128)(2,1)S(1)}, bf16[272,384]{1,0:T(8,128)(2,1)S(1)}, u32[]{:S(2)}, u32[]{:S(2)}) collective-permute-start(bf16[272,384]{1,0:T(8,128)(2,1)S(1)} %prompt_attention.1.refs_0_), channel_id=1, source_target_pairs={{0,16},{4,20},{8,24},{12,28},{16,0},{20,4},{24,8},{28,12},{1,17},{... | collective-permute-start | bytes 626696 | tf_op jit(solution)/shard_map/gather_attended/ppermute | solution.py:33
  149.2 11.9 %collective-permute-start.29 = (bf16[272,384]{1,0:T(8,128)(2,1)S(1)}, bf16[272,384]{1,0:T(8,128)(2,1)S(1)}, u32[]{:S(2)}, u32[]{:S(2)}) collective-permute-start(bf16[272,384]{1,0:T(8,128)(2,1)S(1)} %prompt_attention.1.refs_0_), channel_id=1, source_target_pairs={{0,8},{4,12},{8,0},{12,4},{16,24},{20,28},{24,16},{28,20},{1,9},{5... | collective-permute-start | bytes 626696 | tf_op jit(solution)/shard_map/gather_attended/ppermute | solution.py:33
  160.9 7.0 %collective-permute-start.31 = (bf16[272,384]{1,0:T(8,128)(2,1)S(1)}, bf16[272,384]{1,0:T(8,128)(2,1)S(1)}, u32[]{:S(2)}, u32[]{:S(2)}) collective-permute-start(bf16[272,384]{1,0:T(8,128)(2,1)S(1)} %collective-permute-done.30.refs_2_), channel_id=1, source_target_pairs={{0,8},{4,12},{8,0},{12,4},{16,24},{20,28},{24,16},{28,20},{1,9},{5... | collective-permute-start | bytes 626696 | tf_op jit(solution)/shard_map/gather_attended/ppermute | solution.py:33
  160.9 7.0 %collective-permute-start.32 = (bf16[272,384]{1,0:T(8,128)(2,1)S(1)}, bf16[272,384]{1,0:T(8,128)(2,1)S(1)}, u32[]{:S(2)}, u32[]{:S(2)}) collective-permute-start(bf16[272,384]{1,0:T(8,128)(2,1)S(1)} %prompt_attention.1.refs_0_), channel_id=1, source_target_pairs={{0,4},{4,0},{8,12},{12,8},{16,20},{20,16},{24,28},{28,24},{1,5},{5... | collective-permute-start | bytes 626696 | tf_op jit(solution)/shard_map/gather_attended/ppermute | solution.py:33
  161.1 6.9 %collective-permute-start.33 = (bf16[272,384]{1,0:T(8,128)(2,1)S(1)}, bf16[272,384]{1,0:T(8,128)(2,1)S(1)}, u32[]{:S(2)}, u32[]{:S(2)}) collective-permute-start(bf16[272,384]{1,0:T(8,128)(2,1)S(1)} %collective-permute-done.29.refs_1_), channel_id=1, source_target_pairs={{0,4},{4,0},{8,12},{12,8},{16,20},{20,16},{24,28},{28,24},{1,5},{5... | collective-permute-start | bytes 626696 | tf_op jit(solution)/shard_map/gather_attended/ppermute | solution.py:33
  161.5 6.5 %collective-permute-start.34 = (bf16[272,384]{1,0:T(8,128)(2,1)S(1)}, bf16[272,384]{1,0:T(8,128)(2,1)S(1)}, u32[]{:S(2)}, u32[]{:S(2)}) collective-permute-start(bf16[272,384]{1,0:T(8,128)(2,1)S(1)} %collective-permute-done.30.refs_2_), channel_id=1, source_target_pairs={{0,4},{4,0},{8,12},{12,8},{16,20},{20,16},{24,28},{28,24},{1,5},{5... | collective-permute-start | bytes 626696 | tf_op jit(solution)/shard_map/gather_attended/ppermute | solution.py:33
  168.0 2.3 %collective-permute-start.35 = (bf16[272,384]{1,0:T(8,128)(2,1)S(1)}, bf16[272,384]{1,0:T(8,128)(2,1)S(1)}, u32[]{:S(2)}, u32[]{:S(2)}) collective-permute-start(bf16[272,384]{1,0:T(8,128)(2,1)S(1)} %collective-permute-done.31.refs_3_), channel_id=1, source_target_pairs={{0,4},{4,0},{8,12},{12,8},{16,20},{20,16},{24,28},{28,24},{1,5},{5... | collective-permute-start | bytes 626696 | tf_op jit(solution)/shard_map/gather_attended/ppermute | solution.py:33
  172.4 9.1 %collective-permute-start.36 = (bf16[144,896]{1,0:T(8,128)(2,1)S(1)}, bf16[144,896]{1,0:T(8,128)(2,1)S(1)}, u32[]{:S(2)}, u32[]{:S(2)}) collective-permute-start(bf16[144,896]{1,0:T(8,128)(2,1)S(1)} %get-tuple-element.90), channel_id=1, source_target_pairs={{0,1},{1,0},{2,3},{3,2},{4,5},{5,4},{6,7},{7,6},{8,9},{9,8},{10,11... | collective-permute-start | bytes 774152 | tf_op jit(solution)/shard_map/sum_mp/ppermute | solution.py:37
  173.1 12.9 %collective-permute-start.37 = (bf16[144,896]{1,0:T(8,128)(2,1)S(1)}, bf16[144,896]{1,0:T(8,128)(2,1)S(1)}, u32[]{:S(2)}, u32[]{:S(2)}) collective-permute-start(bf16[144,896]{1,0:T(8,128)(2,1)S(1)} %get-tuple-element.91), channel_id=1, source_target_pairs={{0,2},{1,3},{2,0},{3,1},{4,6},{5,7},{6,4},{7,5},{8,10},{9,11},{10,... | collective-permute-start | bytes 774152 | tf_op jit(solution)/shard_map/sum_mp/ppermute | solution.py:37
  174.6 13.0 %collective-permute-start.38 = (bf16[144,896]{1,0:T(8,128)(2,1)S(1)}, bf16[144,896]{1,0:T(8,128)(2,1)S(1)}, u32[]{:S(2)}, u32[]{:S(2)}) collective-permute-start(bf16[144,896]{1,0:T(8,128)(2,1)S(1)} %get-tuple-element.92), channel_id=1, source_target_pairs={{0,3},{1,2},{2,1},{3,0},{4,7},{5,6},{6,5},{7,4},{8,11},{9,10},{10,... | collective-permute-start | bytes 774152 | tf_op jit(solution)/shard_map/sum_mp/ppermute | solution.py:37
  188.6 6.4 %collective-permute-start.39 = (bf16[64,896]{1,0:T(8,128)(2,1)S(1)}, bf16[64,896]{1,0:T(8,128)(2,1)S(1)}, u32[]{:S(2)}, u32[]{:S(2)}) collective-permute-start(bf16[64,896]{1,0:T(8,128)(2,1)S(1)} %get-tuple-element.94), channel_id=1, source_target_pairs={{0,8},{4,12},{8,0},{12,4},{16,24},{20,28},{24,16},{28,20},{1,9},{5... | collective-permute-start | bytes 344072 | tf_op jit(solution)/shard_map/return_z/ppermute | solution.py:33
  188.9 11.6 %collective-permute-start.40 = (bf16[64,896]{1,0:T(8,128)(2,1)S(1)}, bf16[64,896]{1,0:T(8,128)(2,1)S(1)}, u32[]{:S(2)}, u32[]{:S(2)}) collective-permute-start(bf16[64,896]{1,0:T(8,128)(2,1)S(1)} %get-tuple-element.95), channel_id=1, source_target_pairs={{0,16},{4,20},{8,24},{12,28},{16,0},{20,4},{24,8},{28,12},{1,17},{... | collective-permute-start | bytes 344072 | tf_op jit(solution)/shard_map/return_z/ppermute | solution.py:33
  191.3 9.2 %collective-permute-start.41 = (bf16[64,896]{1,0:T(8,128)(2,1)S(1)}, bf16[64,896]{1,0:T(8,128)(2,1)S(1)}, u32[]{:S(2)}, u32[]{:S(2)}) collective-permute-start(bf16[64,896]{1,0:T(8,128)(2,1)S(1)} %get-tuple-element.96), channel_id=1, source_target_pairs={{0,24},{4,28},{8,16},{12,20},{16,8},{20,12},{24,0},{28,4},{1,25},{... | collective-permute-start | bytes 344072 | tf_op jit(solution)/shard_map/return_z/ppermute | solution.py:33
  200.6 1.6 collective-permute-start.42
  202.8 6.1 %collective-permute-start.43 = (bf16[32,1792]{1,0:T(8,128)(2,1)S(1)}, bf16[32,1792]{1,0:T(8,128)(2,1)S(1)}, u32[]{:S(2)}, u32[]{:S(2)}) collective-permute-start(bf16[32,1792]{1,0:T(8,128)(2,1)S(1)} %get-tuple-element.98), channel_id=1, source_target_pairs={{0,1},{1,0},{2,3},{3,2},{4,5},{5,4},{6,7},{7,6},{8,9},{9,8},{10,11... | collective-permute-start | bytes 344072 | tf_op jit(solution)/shard_map/return_plane/ppermute | solution.py:37
  203.5 7.4 %collective-permute-start.44 = (bf16[32,1792]{1,0:T(8,128)(2,1)S(1)}, bf16[32,1792]{1,0:T(8,128)(2,1)S(1)}, u32[]{:S(2)}, u32[]{:S(2)}) collective-permute-start(bf16[32,1792]{1,0:T(8,128)(2,1)S(1)} %get-tuple-element.99), channel_id=1, source_target_pairs={{0,2},{1,3},{2,0},{3,1},{4,6},{5,7},{6,4},{7,5},{8,10},{9,11},{10,... | collective-permute-start | bytes 344072 | tf_op jit(solution)/shard_map/return_plane/ppermute | solution.py:37
  204.9 6.0 %collective-permute-start.45 = (bf16[32,1792]{1,0:T(8,128)(2,1)S(1)}, bf16[32,1792]{1,0:T(8,128)(2,1)S(1)}, u32[]{:S(2)}, u32[]{:S(2)}) collective-permute-start(bf16[32,1792]{1,0:T(8,128)(2,1)S(1)} %get-tuple-element.100), channel_id=1, source_target_pairs={{0,3},{1,2},{2,1},{3,0},{4,7},{5,6},{6,5},{7,4},{8,11},{9,10},{10,... | collective-permute-start | bytes 344072 | tf_op jit(solution)/shard_map/return_plane/ppermute | solution.py:37
  (25 other events, 241.7 us)

commit v5 on v4

--- a/solution.py
+++ b/solution.py
@@ -152,7 +152,7 @@
         out_shape=[jax.ShapeDtypeStruct((BLK, tokens.shape[1]), BF)] * NM,
         in_specs=[SMEM, VMEM],
         out_specs=[VMEM] * NM,
-        compiler_params=limit(24),
+        compiler_params=limit(16),
         cost_estimate=SMALL,
         name="deal_rows",
     )(scalars, tokens)
@@ -201,7 +201,7 @@
         in_specs=[SMEM] + [VMEM] * 6 + [ANY] * 2,
         out_specs=[VMEM] * NZ,
         scratch_shapes=[pltpu.VMEM((NM,) + blocks[0].shape, F32)],
-        compiler_params=limit(32),
+        compiler_params=limit(16),
         cost_estimate=SMALL,
         name="norm_rows",
     )(scalars, *blocks, affine, table, near, far)
@@ -336,7 +336,7 @@
         out_shape=jax.ShapeDtypeStruct((2 * ADAPTER_RANK, NZ * LANES), F32),
         in_specs=[SMEM] * 2 + [VMEM] * 11,
         out_specs=VMEM,
-        compiler_params=limit(32),
+        compiler_params=limit(16),
         cost_estimate=SMALL,
         name="low_rank_rows",
     )(scalars, tables, down, down_other, *pieces, *stats, affine)
@@ -382,7 +382,7 @@
         out_shape=[jax.ShapeDtypeStruct((2, PACKED, count * ADAPTER_RANK), BF), half, half],
         in_specs=[SMEM] * 2 + [VMEM] * 5 + [ANY],
         out_specs=[VMEM] * 3,
-        compiler_params=limit(32),
+        compiler_params=limit(16),
         cost_estimate=SMALL,
         name="expand_rows",
     )(scalars, tables, low, low_other, base, keys, up, after)
@@ -433,7 +433,7 @@
         out_shape=out_shape,
         in_specs=[SMEM] + whole + [pl.BlockSpec((1, depth, tile), lambda j: (part, 0, j)), ANY],
         out_specs=out_specs,
-        compiler_params=limit(56),
+        compiler_params=limit(16),
         cost_estimate=SMALL,
         name="project_keys",
     )(scalars, *chunks, weight, after)
@@ -467,7 +467,7 @@
             ANY,
         ],
         out_specs=[pl.BlockSpec((v.shape[0], tile), lambda j: (0, j)) for v in out_shape],
-        compiler_params=limit(56),
+        compiler_params=limit(16),
         cost_estimate=SMALL,
         name="project_adapted",
     )(rows, weight, expanded, up, after)
@@ -528,7 +528,7 @@
             ANY,
         ],
         out_specs=pl.BlockSpec((count, feats), lambda p: (0, p)),
-        compiler_params=limit(56),
+        compiler_params=limit(16),
         cost_estimate=SMALL,
         name="decode_base",
     )(rows, weight, after)
@@ -561,7 +561,7 @@
         out_shape=[jax.ShapeDtypeStruct((rows, feats), BF), jax.ShapeDtypeStruct((rows, feats), F32)],
         in_specs=[SMEM] + [VMEM] * (2 * len(totals)) + [ANY],
         out_specs=[VMEM, VMEM],
-        compiler_params=limit(24),
+        compiler_params=limit(16),
         cost_estimate=SMALL,
         name="halve_sums",
     )(scalars, *totals, *gots, after)
@@ -618,7 +618,7 @@
         out_shape=jax.ShapeDtypeStruct((q.shape[0] + DECODE_ROWS, q.shape[1]), BF),
         in_specs=[VMEM] * 8,
         out_specs=VMEM,
-        compiler_params=limit(32),
+        compiler_params=limit(16),
         cost_estimate=SMALL,
         name="prompt_attention",
     )(q, ka, kb, va, vb, code_rows, code_cols, dec)
@@ -684,7 +684,7 @@
             ],
         ),
         out_shape=jax.ShapeDtypeStruct((count, 1, feats), BF),
-        compiler_params=limit(32),
+        compiler_params=limit(44),
         cost_estimate=SMALL,
         name="decode_attention",
     )(lengths, q, k, v, cache, after)
@@ -714,7 +714,7 @@
         out_shape=jax.ShapeDtypeStruct((NM * CHUNK, weight.shape[1]), F32),
         in_specs=[SMEM] + [VMEM] * 7,
         out_specs=VMEM,
-        compiler_params=limit(40),
+        compiler_params=limit(16),
         cost_estimate=SMALL,
         name="out_first",
     )(scalars, *own[:3], *other[:3], weight)
@@ -754,7 +754,7 @@
         in_specs=[SMEM] + [VMEM] * 10,
         out_specs=[VMEM] * NM,
         scratch_shapes=[pltpu.VMEM((NM * CHUNK, feats), BF)],
-        compiler_params=limit(40),
+        compiler_params=limit(16),
         cost_estimate=SMALL,
         name="out_project",
     )(scalars, *own, *other, first, weight)
@@ -836,7 +836,7 @@
         out_shape=jax.ShapeDtypeStruct(tokens.shape, BF),
         in_specs=[SMEM] + [VMEM] * 6,
         out_specs=VMEM,
-        compiler_params=limit(24),
+        compiler_params=limit(16),
         cost_estimate=SMALL,
         name="add_home",
     )(scalars, tokens, bias, *blocks)
@@ -912,45 +912,46 @@
     with jax.named_scope("low_rank"):
         down_other = swap_req(copy_rows(down, mine), 1)
         part = low_rank_rows(scalars, tables, down, down_other, pieces, spread, affine)
+        two = add_rows(part, swap_mp(part, 1), part)
     with jax.named_scope("keys"):
-        own_k, other_k, dec_k, x_rows = project_rows(scalars, chunks, query_key_value_weight, 1, part)
+        own_k, other_k, dec_k, x_rows = project_rows(scalars, chunks, query_key_value_weight, 1, two)
         core_k = swap_req(other_k, 1)
     with jax.named_scope("decode_rows"):
         base = decode_base(x_rows, query_key_value_weight, other_k)
     with jax.named_scope("low_rank"):
-        two = add_rows(part, swap_mp(part, 1), base)
+        low_rank = add_rows(two, swap_mp(two, 2), base, BF)
     with jax.named_scope("keys"):
-        send_k, keep_k = halve(scalars, [own_k], [core_k], 0, two)
+        send_k, keep_k = halve(scalars, [own_k], [core_k], 0, low_rank)
         got_k = swap_req(send_k, 2)
     with jax.named_scope("low_rank"):
-        code_col, code_row = packed_codes(scalars, tables, send_k)
-        low_rank = add_rows(two, swap_mp(two, 2), code_row, BF)
         expanded, dec, dec_sent = expand_rows(
-            scalars, tables, low_rank, swap_req(low_rank, 1), base, dec_k, adapter_up_weight, own_adapters, base
+            scalars, tables, low_rank, swap_req(low_rank, 1), base, dec_k, adapter_up_weight, own_adapters, send_k
         )
     with jax.named_scope("decode_rows"):
         dec_chip = add_rows(dec, swap_req(dec_sent, 1), expanded)
-    with jax.named_scope("keys"):
-        send_k, keep_k = halve(scalars, [keep_k], [got_k], 1, dec_chip)
-        got_k = swap_req(send_k, 4)
     with jax.named_scope("values"):
-        own_v, other_v = project_adapted(x_rows, query_key_value_weight, 2, expanded, adapter_up_weight, send_k)
+        own_v, other_v = project_adapted(x_rows, query_key_value_weight, 2, expanded, adapter_up_weight, dec_chip)
         core_v = swap_req(other_v, 1)
     with jax.named_scope("decode_rows"):
         dec_pair = add_rows(dec_chip, swap_req(dec_chip[4:], 2), own_v)
     with jax.named_scope("keys"):
-        (keys,) = finish(scalars, keep_k, got_k, query_key_value_bias, (1,), dec_pair)
-        keys_other = swap_req(keys, 1)
+        send_k, keep_k = halve(scalars, [keep_k], [got_k], 1, dec_pair)
+        got_k = swap_req(send_k, 4)
     with jax.named_scope("decode_rows"):
-        dec = decode_finish(dec_pair, swap_req(dec_pair[2:], 4), query_key_value_bias, keys)
+        dec = decode_finish(dec_pair, swap_req(dec_pair[2:], 4), query_key_value_bias, send_k)
     with jax.named_scope("queries"):
         own_q, other_q = project_adapted(x_rows, query_key_value_weight, 0, expanded, adapter_up_weight, dec[0])
         core_q = swap_req(other_q, 1)
     with jax.named_scope("reduce_z"):
         send, keep = halve(scalars, [own_v, own_q], [core_v, core_q], 0, core_q)
         got = swap_req(send, 2)
+    with jax.named_scope("codes"):
+        code_col, code_row = packed_codes(scalars, tables, send)
+    with jax.named_scope("keys"):
+        (keys,) = finish(scalars, keep_k, got_k, query_key_value_bias, (1,), code_row)
+        keys_other = swap_req(keys, 1)
     with jax.named_scope("reduce_z"):
-        send, keep = halve(scalars, [keep], [got], 1, send, groups=2)
+        send, keep = halve(scalars, [keep], [got], 1, keys, groups=2)
         got = swap_req(send, 4)
     with jax.named_scope("decode_attention"):
         dec_out = decode_attention(cache_length_list, *dec, cache, send)

time: 213 us -> 203 us (0.953)
  Pallas kernels: 52 us -> 43.8 us
  local copies, waits for them, and re-layouts: 8.14 us -> 3.01 us
    unnamed x59 -> x25, local copies, waits for them, and re-layouts: 7.22 us -> 2.09 us
    pallas_call x2, Pallas kernels: 9.92 us -> 5.41 us  [project_adapted(): pl.pallas_call(adapted_kernel, grid=(2,), out_shape=out_shape, in_specs=[...]
    pallas_call x1, Pallas kernels: 3.82 us -> 0.95 us  [decode_base(): pl.pallas_call(decode_base_kernel, grid=(2,), out_shape=jax.ShapeDtypeStr...]
    ppermute x14, waiting for transfers between devices: 23 us -> 25.5 us  [swap_mp(): return lax.ppermute(x, 'mp', [(i, i ^ bits) for i in range(NM)])]
  transfers between devices with their start and end apart: 46 -> 46, of which waited for: 31 -> 30; matrix products, arithmetic and copies ran while one was open for 1% -> 1% of each run, Pallas kernels for 17% -> 15%
where the time goes in v5:
time: 203 us; the launch traced here: 202 us
  waiting for transfers between devices  104 us (51%)
  starting transfers between devices  49.6 us (24%)
  Pallas kernels  43.8 us (22%)
  local copies, waits for them, and re-layouts  3.01 us (1%)
    ppermute x32, waiting for transfers between devices, swap_req(): return lax.ppermute(x, 'req', [(i, i ^ bits) for i in range(2 * NZ)])  78.4 us
    ppermute x32, starting transfers between devices, swap_req(): return lax.ppermute(x, 'req', [(i, i ^ bits) for i in range(2 * NZ)])  32.3 us
    ppermute x14, waiting for transfers between devices, swap_mp(): return lax.ppermute(x, 'mp', [(i, i ^ bits) for i in range(NM)])  25.5 us
    ppermute x14, starting transfers between devices, swap_mp(): return lax.ppermute(x, 'mp', [(i, i ^ bits) for i in range(NM)])  17.3 us
    pallas_call x1, Pallas kernels, decode_attention(): pl.pallas_call(decode_kernel, grid_spec=pltpu.PrefetchScalarGridSpec(num_...  7.78 us
    pallas_call x2, Pallas kernels, project_adapted(): pl.pallas_call(adapted_kernel, grid=(2,), out_shape=out_shape, in_specs=[...  5.41 us
  transfers between devices with their start and end apart: 46, of which 30 were waited for; matrix products, arithmetic and copies ran while one was open for 1% of the time, Pallas kernels for 15%

profile of v5, /device:TPU:0, one launch (start us, length us, event | category | flops | bytes accessed | tf_op | source)
XLA Modules:
  0.0 202.4 jit_solution(2167635864518488581)
XLA Ops:
  0.0 4.0 %collective-permute-start.4 = (bf16[98,1792]{1,0:T(8,128)(2,1)}, bf16[98,1792]{1,0:T(8,128)(2,1)S(1)}, u32[]{:S(2)}, u32[]{:S(2)}) collective-permute-start(bf16[98,1792]{1,0:T(8,128)(2,1)} %x_ref.3), channel_id=1, source_target_pairs={{0,16},{4,20},{8,24},{12,28},{16,0},{20,4},{24,8},{28,12},{1,17},{... | collective-permute-start | bytes 1053704 | tf_op jit(solution)/shard_map/gather_home/ppermute | solution.py:33
  4.8 1.6 collective-permute-start.3
  8.6 1.6 collective-permute-start
  14.0 2.5 %collective-permute-done.1.b2 = bf16[32,1792]{1,0:T(8,128)(2,1)S(1)} collective-permute-done((bf16[32,1792]{1,0:T(8,128)(2,1)S(1)}, bf16[32,1792]{1,0:T(8,128)(2,1)S(1)}, u32[]{:S(2)}, u32[]{:S(2)}) %collective-permute-start.1) | collective-permute-done | bytes 114720 | tf_op jit(solution)/shard_map/deal/ppermute | solution.py:37
  17.4 3.6 %collective-permute-done.4.__.x2 = bf16[98,1792]{1,0:T(8,128)(2,1)S(1)} collective-permute-done((bf16[98,1792]{1,0:T(8,128)(2,1)}, bf16[98,1792]{1,0:T(8,128)(2,1)S(1)}, u32[]{:S(2)}, u32[]{:S(2)}) %collective-permute-start.4) | collective-permute-done | bytes 351264 | tf_op jit(solution)/shard_map/gather_home/ppermute | solution.py:33
  23.8 2.4 %collective-permute-start.6 = (bf16[32,1792]{1,0:T(8,128)(2,1)S(1)}, bf16[32,1792]{1,0:T(8,128)(2,1)S(1)}, u32[]{:S(2)}, u32[]{:S(2)}) collective-permute-start(bf16[32,1792]{1,0:T(8,128)(2,1)S(1)} %get-tuple-element.59), channel_id=1, source_target_pairs={{0,16},{4,20},{8,24},{12,28},{16,0},{20,4},{24,8},{28,12},{1,17},{... | collective-permute-start | bytes 344072 | tf_op jit(solution)/shard_map/spread_z/ppermute | solution.py:33
  27.5 1.9 collective-permute-done.5.b1.t1
  29.3 6.1 %collective-permute-done.6.b2.t2 = bf16[32,1792]{1,0:T(8,128)(2,1)S(1)} collective-permute-done((bf16[32,1792]{1,0:T(8,128)(2,1)S(1)}, bf16[32,1792]{1,0:T(8,128)(2,1)S(1)}, u32[]{:S(2)}, u32[]{:S(2)}) %collective-permute-start.6) | collective-permute-done | bytes 114720 | tf_op jit(solution)/shard_map/spread_z/ppermute | solution.py:33
  36.7 1.8 collective-permute-start.13
  40.0 1.6 collective-permute-start.10
  43.5 3.8 %collective-permute-done.13.x3 = bf16[98,1792]{1,0:T(8,128)(2,1)S(1)} collective-permute-done((bf16[98,1792]{1,0:T(8,128)(2,1)S(1)}, bf16[98,1792]{1,0:T(8,128)(2,1)S(1)}, u32[]{:S(2)}, u32[]{:S(2)}) %collective-permute-start.13) | collective-permute-done | bytes 351264 | tf_op jit(solution)/shard_map/gather_home/ppermute | solution.py:33
  48.4 4.0 %low_rank_rows.1.a_ref._ = f32[32,512]{1,0:T(8,128)S(1)} custom-call(s32[7]{0:T(128)S(1)} %concatenate.12.s_ref.place_ref, s32[8,8]{1,0:T(8,128)S(1)} %maximum_convert_fusion.t_ref.table_ref, bf16[256,1792]{1,0:T(8,128)(2,1)S(1)} %bitcast.26, bf16[256,1792]{1,0:T(8,128)(2,1)S(1)} %collective-permute-done.12.db_ref, bf16[98,1792]{1,0:T(8,128)(2,1)S(1)} %copy-done.5, ...), custom_call_target="tpu_custom_call" | custom-call | flops 1 | bytes 1 | tf_op jit(solution)/shard_map/low_rank/low_rank_rows/pallas_call | solution.py:334
  52.4 1.5 collective-permute-start.14
  53.9 2.8 %collective-permute-done.14.b_ref = f32[32,512]{1,0:T(8,128)S(1)} collective-permute-done((f32[32,512]{1,0:T(8,128)S(1)}, f32[32,512]{1,0:T(8,128)S(1)}, u32[]{:S(2)}, u32[]{:S(2)}) %collective-permute-start.14) | collective-permute-done | bytes 65568 | tf_op jit(solution)/shard_map/low_rank/ppermute | solution.py:37
  56.7 3.1 %project_keys.1 = (bf16[256,1536]{1,0:T(8,128)(2,1)S(1)}, bf16[256,1536]{1,0:T(8,128)(2,1)S(1)}, f32[16,1536]{1,0:T(8,128)S(1)}, bf16[528,896]{1,0:T(8,128)(2,1)S(1)}) custom-call(s32[7]{0:T(128)S(1)} %concatenate.12.s_ref.place_ref, bf16[144,896]{1,0:T(8,128)(2,1)S(1)} %pack_rows.1.c0, bf16[144,896]{1,0:T(8,128)(2,1)S(1)} %collective-permute-done.9.c1, ...), custom_call_target="tpu_custom_call" | custom-call | flops 1 | bytes 1 | tf_op jit(solution)/shard_map/keys/project_keys/pallas_call | solution.py:430
  60.0 1.6 collective-permute-start.15
  62.5 2.0 collective-permute-done.15.b_ref
  65.2 1.8 collective-permute-start.21
  68.2 2.6 %expand_rows.1 = (bf16[2,528,128]{2,1,0:T(8,128)(2,1)S(1)}, f32[8,4608]{1,0:T(8,128)S(1)}, f32[8,4608]{1,0:T(8,128)S(1)}) custom-call(s32[7]{0:T(128)S(1)} %concatenate.12.s_ref.place_ref, s32[8,8]{1,0:T(8,128)S(1)} %maximum_convert_fusion.t_ref.table_ref, bf16[32,512]{1,0:T(8,128)(2,1)S(1)} %add_rows.5.refs_2_.low_ref, ...), custom_call_target="tpu_custom_call" | custom-call | flops 1 | bytes 1 | tf_op jit(solution)/shard_map/low_rank/expand_rows/pallas_call | solution.py:380
  72.7 2.7 %project_adapted.2 = (bf16[256,1536]{1,0:T(8,128)(2,1)S(1)}, bf16[256,1536]{1,0:T(8,128)(2,1)S(1)}) custom-call(bf16[528,896]{1,0:T(8,128)(2,1)S(1)} %get-tuple-element.63.x_ref, bf16[3,896,1536]{2,1,0:T(8,128)(2,1)S(1)} %copy-done, bf16[2,528,128]{2,1,0:T(8,128)(2,1)S(1)} %get-tuple-element.68._.e_ref, bf16[8,2,16,1536]{3,2,1,0:T(8,128)(2,1)S(1)} %copy-done.2, ...), custom_call_target="tpu_custom_call" | custom-call | flops 1 | bytes 1 | tf_op jit(solution)/shard_map/values/project_adapted/pallas_call | solution.py:458
  75.4 2.2 %collective-permute-done.19.b_ref = f32[4,4608]{1,0:T(4,128)S(1)} collective-permute-done((f32[4,4608]{1,0:T(4,128)S(1)}, f32[4,4608]{1,0:T(4,128)S(1)}, u32[]{:S(2)}, u32[]{:S(2)}) %collective-permute-start.19) | collective-permute-done | bytes 73760 | tf_op jit(solution)/shard_map/decode_rows/ppermute | solution.py:33
  77.6 2.8 %collective-permute-start.20 = (f32[2,4608]{1,0:T(2,128)S(1)}, f32[2,4608]{1,0:T(2,128)S(1)}, u32[]{:S(2)}, u32[]{:S(2)}) collective-permute-start(f32[2,4608]{1,0:T(2,128)S(1)} %slice.39), channel_id=1, source_target_pairs={{0,16},{4,20},{8,24},{12,28},{16,0},{20,4},{24,8},{28,12},{1,17},{... | collective-permute-start | bytes 110600 | tf_op jit(solution)/shard_map/decode_rows/ppermute | solution.py:33
  82.6 2.7 %project_adapted.3 = (bf16[256,1536]{1,0:T(8,128)(2,1)S(1)}, bf16[256,1536]{1,0:T(8,128)(2,1)S(1)}) custom-call(bf16[528,896]{1,0:T(8,128)(2,1)S(1)} %get-tuple-element.63.x_ref, bf16[3,896,1536]{2,1,0:T(8,128)(2,1)S(1)} %copy-done, bf16[2,528,128]{2,1,0:T(8,128)(2,1)S(1)} %get-tuple-element.68._.e_ref, bf16[8,2,16,1536]{3,2,1,0:T(8,128)(2,1)S(1)} %copy-done.2, ...), custom_call_target="tpu_custom_call" | custom-call | flops 1 | bytes 1 | tf_op jit(solution)/shard_map/queries/project_adapted/pallas_call | solution.py:458
  85.4 2.3 %collective-permute-done.23.refs_3_.refs_4_ = bf16[256,1536]{1,0:T(8,128)(2,1)S(1)} collective-permute-done((bf16[256,1536]{1,0:T(8,128)(2,1)S(1)}, bf16[256,1536]{1,0:T(8,128)(2,1)S(1)}, u32[]{:S(2)}, u32[]{:S(2)}) %collective-permute-start.23) | collective-permute-done | bytes 786464 | tf_op jit(solution)/shard_map/queries/ppermute | solution.py:33
  88.6 1.8 collective-permute-start.24
  91.7 2.4 %packed_codes.1 = (s32[512,1]{1,0:T(8,128)S(1)}, s32[1,512]{1,0:T(1,128)S(1)}) custom-call(s32[7]{0:T(128)S(1)} %concatenate.12.s_ref.place_ref, s32[8,8]{1,0:T(8,128)S(1)} %maximum_convert_fusion.t_ref.table_ref, bf16[256,1536]{1,0:T(8,128)(2,1)S(1)} %get-tuple-element.79._), custom_call_target="tpu_custom_call" | custom-call | flops 1 | bytes 1 | tf_op jit(solution)/shard_map/codes/packed_codes/pallas_call | solution.py:294
  94.1 17.6 %collective-permute-done.25.got_ref = bf16[256,384]{1,0:T(8,128)(2,1)S(1)} collective-permute-done((bf16[256,384]{1,0:T(8,128)(2,1)S(1)}, bf16[256,384]{1,0:T(8,128)(2,1)S(1)}, u32[]{:S(2)}, u32[]{:S(2)}) %collective-permute-start.25) | collective-permute-done | bytes 196640 | tf_op jit(solution)/shard_map/keys/ppermute | solution.py:33
  113.2 3.3 %collective-permute-start.26 = (bf16[256,768]{1,0:T(8,128)(2,1)S(1)}, bf16[256,768]{1,0:T(8,128)(2,1)S(1)}, u32[]{:S(2)}, u32[]{:S(2)}) collective-permute-start(bf16[256,768]{1,0:T(8,128)(2,1)S(1)} %get-tuple-element.83._), channel_id=1, source_target_pairs={{0,16},{4,20},{8,24},{12,28},{16,0},{20,4},{24,8},{28,12},{1,17},{... | collective-permute-start | bytes 1179656 | tf_op jit(solution)/shard_map/reduce_z/ppermute | solution.py:33
  116.5 7.8 %decode_attention.1 = bf16[2,1,1536]{2,1,0:T(2,128)(2,1)S(1)} custom-call(s32[2]{0:T(128)S(1)} %copy-done.8, bf16[2,1,1536]{2,1,0:T(2,128)(2,1)S(1)} %get-tuple-element.74._.q_ref, bf16[2,1,1536]{2,1,0:T(2,128)(2,1)S(1)} %get-tuple-element.84.k_ref, bf16[2,1,1536]{2,1,0:T(2,128)(2,1)S(1)} %get-tuple-element.85.v_ref, bf16[2,2048,2,1536]{3,2,1,0:T(2,128)(2,1)} %c_ref.1, ...), custom_call_target="tpu_custom_call" | custom-call | flops 1 | bytes 1 | tf_op jit(solution)/shard_map/decode_attention/decode_attention/pallas_call | solution.py:671
  124.3 9.2 %collective-permute-done.26.got_ref = bf16[256,768]{1,0:T(8,128)(2,1)S(1)} collective-permute-done((bf16[256,768]{1,0:T(8,128)(2,1)S(1)}, bf16[256,768]{1,0:T(8,128)(2,1)S(1)}, u32[]{:S(2)}, u32[]{:S(2)}) %collective-permute-start.26) | collective-permute-done | bytes 393248 | tf_op jit(solution)/shard_map/reduce_z/ppermute | solution.py:33
  135.6 1.5 prompt_attention.1.refs_0_
  137.9 2.3 %collective-permute-start.29 = (bf16[272,384]{1,0:T(8,128)(2,1)S(1)}, bf16[272,384]{1,0:T(8,128)(2,1)S(1)}, u32[]{:S(2)}, u32[]{:S(2)}) collective-permute-start(bf16[272,384]{1,0:T(8,128)(2,1)S(1)} %prompt_attention.1.refs_0_), channel_id=1, source_target_pairs={{0,8},{4,12},{8,0},{12,4},{16,24},{20,28},{24,16},{28,20},{1,9},{5... | collective-permute-start | bytes 626696 | tf_op jit(solution)/shard_map/gather_attended/ppermute | solution.py:33
  140.2 9.5 %collective-permute-done.30.refs_2_ = bf16[272,384]{1,0:T(8,128)(2,1)S(1)} collective-permute-done((bf16[272,384]{1,0:T(8,128)(2,1)S(1)}, bf16[272,384]{1,0:T(8,128)(2,1)S(1)}, u32[]{:S(2)}, u32[]{:S(2)}) %collective-permute-start.30) | collective-permute-done | bytes 208928 | tf_op jit(solution)/shard_map/gather_attended/ppermute | solution.py:33
  150.4 6.4 %collective-permute-done.31.refs_3_ = bf16[272,384]{1,0:T(8,128)(2,1)S(1)} collective-permute-done((bf16[272,384]{1,0:T(8,128)(2,1)S(1)}, bf16[272,384]{1,0:T(8,128)(2,1)S(1)}, u32[]{:S(2)}, u32[]{:S(2)}) %collective-permute-start.31) | collective-permute-done | bytes 208928 | tf_op jit(solution)/shard_map/gather_attended/ppermute | solution.py:33
  156.8 2.2 %out_first.1.refs_8_ = f32[512,896]{1,0:T(8,128)S(1)} custom-call(s32[7]{0:T(128)S(1)} %concatenate.12.s_ref.place_ref, bf16[272,384]{1,0:T(8,128)(2,1)S(1)} %prompt_attention.1.refs_0_, bf16[272,384]{1,0:T(8,128)(2,1)S(1)} %collective-permute-done.29.refs_1_, bf16[272,384]{1,0:T(8,128)(2,1)S(1)} %collective-permute-done.30.refs_2_, ...), custom_call_target="tpu_custom_call" | custom-call | flops 1 | bytes 1 | tf_op jit(solution)/shard_map/out_project/out_first/pallas_call | solution.py:712
  159.1 2.1 %out_project.1 = (bf16[144,896]{1,0:T(8,128)(2,1)S(1)}, bf16[144,896]{1,0:T(8,128)(2,1)S(1)}, bf16[144,896]{1,0:T(8,128)(2,1)S(1)}, bf16[144,896]{1,0:T(8,128)(2,1)S(1)}) custom-call(s32[7]{0:T(128)S(1)} %concatenate.12.s_ref.place_ref, bf16[272,384]{1,0:T(8,128)(2,1)S(1)} %prompt_attention.1.refs_0_, bf16[272,384]{1,0:T(8,128)(2,1)S(1)} %collective-permute-done.29.refs_1_, ...), custom_call_target="tpu_custom_call" | custom-call | flops 1 | bytes 1 | tf_op jit(solution)/shard_map/out_project/out_project/pallas_call | solution.py:751
  161.2 1.5 collective-permute-start.36
  162.7 1.5 collective-permute-start.37
  164.8 5.5 %collective-permute-done.36.c1 = bf16[144,896]{1,0:T(8,128)(2,1)S(1)} collective-permute-done((bf16[144,896]{1,0:T(8,128)(2,1)S(1)}, bf16[144,896]{1,0:T(8,128)(2,1)S(1)}, u32[]{:S(2)}, u32[]{:S(2)}) %collective-permute-start.36) | collective-permute-done | bytes 258080 | tf_op jit(solution)/shard_map/sum_mp/ppermute | solution.py:37
  170.3 6.3 %collective-permute-done.37.c2 = bf16[144,896]{1,0:T(8,128)(2,1)S(1)} collective-permute-done((bf16[144,896]{1,0:T(8,128)(2,1)S(1)}, bf16[144,896]{1,0:T(8,128)(2,1)S(1)}, u32[]{:S(2)}, u32[]{:S(2)}) %collective-permute-start.37) | collective-permute-done | bytes 258080 | tf_op jit(solution)/shard_map/sum_mp/ppermute | solution.py:37
  177.9 2.3 %collective-permute-start.40 = (bf16[64,896]{1,0:T(8,128)(2,1)S(1)}, bf16[64,896]{1,0:T(8,128)(2,1)S(1)}, u32[]{:S(2)}, u32[]{:S(2)}) collective-permute-start(bf16[64,896]{1,0:T(8,128)(2,1)S(1)} %get-tuple-element.95), channel_id=1, source_target_pairs={{0,16},{4,20},{8,24},{12,28},{16,0},{20,4},{24,8},{28,12},{1,17},{... | collective-permute-start | bytes 344072 | tf_op jit(solution)/shard_map/return_z/ppermute | solution.py:33
  180.2 1.8 collective-permute-start.41
  182.1 1.7 collective-permute-done.39.a1
  183.7 5.7 %collective-permute-done.40.a2 = bf16[64,896]{1,0:T(8,128)(2,1)S(1)} collective-permute-done((bf16[64,896]{1,0:T(8,128)(2,1)S(1)}, bf16[64,896]{1,0:T(8,128)(2,1)S(1)}, u32[]{:S(2)}, u32[]{:S(2)}) %collective-permute-start.40) | collective-permute-done | bytes 114720 | tf_op jit(solution)/shard_map/return_z/ppermute | solution.py:33
  191.6 1.5 collective-permute-start.43
  195.2 1.7 collective-permute-done.43.b1
  196.9 3.6 %collective-permute-done.44.b2 = bf16[32,1792]{1,0:T(8,128)(2,1)S(1)} collective-permute-done((bf16[32,1792]{1,0:T(8,128)(2,1)S(1)}, bf16[32,1792]{1,0:T(8,128)(2,1)S(1)}, u32[]{:S(2)}, u32[]{:S(2)}) %collective-permute-start.44) | collective-permute-done | bytes 114720 | tf_op jit(solution)/shard_map/return_plane/ppermute | solution.py:37
  200.5 1.8 add_home.1
  (116 shorter events, 37.8 us)
Async XLA Ops:
  0.0 21.0 %collective-permute-start.4 = (bf16[98,1792]{1,0:T(8,128)(2,1)}, bf16[98,1792]{1,0:T(8,128)(2,1)S(1)}, u32[]{:S(2)}, u32[]{:S(2)}) collective-permute-start(bf16[98,1792]{1,0:T(8,128)(2,1)} %x_ref.3), channel_id=1, source_target_pairs={{0,16},{4,20},{8,24},{12,28},{16,0},{20,4},{24,8},{28,12},{1,17},{... | collective-permute-start | bytes 1053704 | tf_op jit(solution)/shard_map/gather_home/ppermute | solution.py:33
  4.8 17.2 %collective-permute-start.3 = (bf16[98,1792]{1,0:T(8,128)(2,1)}, bf16[98,1792]{1,0:T(8,128)(2,1)S(1)}, u32[]{:S(2)}, u32[]{:S(2)}) collective-permute-start(bf16[98,1792]{1,0:T(8,128)(2,1)} %x_ref.3), channel_id=1, source_target_pairs={{0,8},{4,12},{8,0},{12,4},{16,24},{20,28},{24,16},{28,20},{1,9},{5... | collective-permute-start | bytes 1053704 | tf_op jit(solution)/shard_map/gather_home/ppermute | solution.py:33
  8.6 5.4 %collective-permute-start = (bf16[32,1792]{1,0:T(8,128)(2,1)S(1)}, bf16[32,1792]{1,0:T(8,128)(2,1)S(1)}, u32[]{:S(2)}, u32[]{:S(2)}) collective-permute-start(bf16[32,1792]{1,0:T(8,128)(2,1)S(1)} %get-tuple-element.54), channel_id=1, source_target_pairs={{0,1},{1,0},{2,3},{3,2},{4,5},{5,4},{6,7},{7,6},{8,9},{9,8},{10,11... | collective-permute-start | bytes 344072 | tf_op jit(solution)/shard_map/deal/ppermute | solution.py:37
  10.1 6.4 %collective-permute-start.1 = (bf16[32,1792]{1,0:T(8,128)(2,1)S(1)}, bf16[32,1792]{1,0:T(8,128)(2,1)S(1)}, u32[]{:S(2)}, u32[]{:S(2)}) collective-permute-start(bf16[32,1792]{1,0:T(8,128)(2,1)S(1)} %get-tuple-element.55), channel_id=1, source_target_pairs={{0,2},{1,3},{2,0},{3,1},{4,6},{5,7},{6,4},{7,5},{8,10},{9,11},{10,... | collective-permute-start | bytes 344072 | tf_op jit(solution)/shard_map/deal/ppermute | solution.py:37
  11.7 5.7 %collective-permute-start.2 = (bf16[32,1792]{1,0:T(8,128)(2,1)S(1)}, bf16[32,1792]{1,0:T(8,128)(2,1)S(1)}, u32[]{:S(2)}, u32[]{:S(2)}) collective-permute-start(bf16[32,1792]{1,0:T(8,128)(2,1)S(1)} %get-tuple-element.56), channel_id=1, source_target_pairs={{0,3},{1,2},{2,1},{3,0},{4,7},{5,6},{6,5},{7,4},{8,11},{9,10},{10,... | collective-permute-start | bytes 344072 | tf_op jit(solution)/shard_map/deal/ppermute | solution.py:37
  23.0 6.3 %collective-permute-start.5 = (bf16[32,1792]{1,0:T(8,128)(2,1)S(1)}, bf16[32,1792]{1,0:T(8,128)(2,1)S(1)}, u32[]{:S(2)}, u32[]{:S(2)}) collective-permute-start(bf16[32,1792]{1,0:T(8,128)(2,1)S(1)} %get-tuple-element.58), channel_id=1, source_target_pairs={{0,8},{4,12},{8,0},{12,4},{16,24},{20,28},{24,16},{28,20},{1,9},{5... | collective-permute-start | bytes 344072 | tf_op jit(solution)/shard_map/spread_z/ppermute | solution.py:33
  23.8 11.6 %collective-permute-start.6 = (bf16[32,1792]{1,0:T(8,128)(2,1)S(1)}, bf16[32,1792]{1,0:T(8,128)(2,1)S(1)}, u32[]{:S(2)}, u32[]{:S(2)}) collective-permute-start(bf16[32,1792]{1,0:T(8,128)(2,1)S(1)} %get-tuple-element.59), channel_id=1, source_target_pairs={{0,16},{4,20},{8,24},{12,28},{16,0},{20,4},{24,8},{28,12},{1,17},{... | collective-permute-start | bytes 344072 | tf_op jit(solution)/shard_map/spread_z/ppermute | solution.py:33
  26.2 9.2 %collective-permute-start.7 = (bf16[32,1792]{1,0:T(8,128)(2,1)S(1)}, bf16[32,1792]{1,0:T(8,128)(2,1)S(1)}, u32[]{:S(2)}, u32[]{:S(2)}) collective-permute-start(bf16[32,1792]{1,0:T(8,128)(2,1)S(1)} %get-tuple-element.60), channel_id=1, source_target_pairs={{0,24},{4,28},{8,16},{12,20},{16,8},{20,12},{24,0},{28,4},{1,25},{... | collective-permute-start | bytes 344072 | tf_op jit(solution)/shard_map/spread_z/ppermute | solution.py:33
  36.1 11.3 %collective-permute-start.12 = (bf16[256,1792]{1,0:T(8,128)(2,1)S(1)}, bf16[256,1792]{1,0:T(8,128)(2,1)S(1)}, u32[]{:S(2)}, u32[]{:S(2)}) collective-permute-start(bf16[256,1792]{1,0:T(8,128)(2,1)S(1)} %copy_rows.1), channel_id=1, source_target_pairs={{0,4},{4,0},{8,12},{12,8},{16,20},{20,16},{24,28},{28,24},{1,5},{5... | collective-permute-start | bytes 2752520 | tf_op jit(solution)/shard_map/low_rank/ppermute | solution.py:33
  36.2 2.8 %collective-permute-start.8 = (bf16[128,896]{1,0:T(8,128)(2,1)S(1)}, bf16[128,896]{1,0:T(8,128)(2,1)S(1)}, u32[]{:S(2)}, u32[]{:S(2)}) collective-permute-start(bf16[128,896]{1,0:T(8,128)(2,1)S(1)} %get-tuple-element.62), channel_id=1, source_target_pairs={{0,4},{4,0},{8,12},{12,8},{16,20},{20,16},{24,28},{28,24},{1,5},{5... | collective-permute-start | bytes 688136 | tf_op jit(solution)/shard_map/spread_z/ppermute | solution.py:33
  36.7 10.7 %collective-permute-start.13 = (bf16[98,1792]{1,0:T(8,128)(2,1)S(1)}, bf16[98,1792]{1,0:T(8,128)(2,1)S(1)}, u32[]{:S(2)}, u32[]{:S(2)}) collective-permute-start(bf16[98,1792]{1,0:T(8,128)(2,1)S(1)} %collective-permute-done.4.__.x2), channel_id=1, source_target_pairs={{0,8},{4,12},{8,0},{12,4},{16,24},{20,28},{24,16},{28,20},{1,9},{5... | collective-permute-start | bytes 1053704 | tf_op jit(solution)/shard_map/gather_home/ppermute | solution.py:33
  40.0 16.7 %collective-permute-start.10 = (bf16[144,896]{1,0:T(8,128)(2,1)S(1)}, bf16[144,896]{1,0:T(8,128)(2,1)S(1)}, u32[]{:S(2)}, u32[]{:S(2)}) collective-permute-start(bf16[144,896]{1,0:T(8,128)(2,1)S(1)} %pack_rows.1.c0), channel_id=1, source_target_pairs={{0,2},{1,3},{2,0},{3,1},{4,6},{5,7},{6,4},{7,5},{8,10},{9,11},{10,... | collective-permute-start | bytes 774152 | tf_op jit(solution)/shard_map/gather_chunks/ppermute | solution.py:37
  41.6 15.1 %collective-permute-start.11 = (bf16[144,896]{1,0:T(8,128)(2,1)S(1)}, bf16[144,896]{1,0:T(8,128)(2,1)S(1)}, u32[]{:S(2)}, u32[]{:S(2)}) collective-permute-start(bf16[144,896]{1,0:T(8,128)(2,1)S(1)} %pack_rows.1.c0), channel_id=1, source_target_pairs={{0,3},{1,2},{2,1},{3,0},{4,7},{5,6},{6,5},{7,4},{8,11},{9,10},{10,... | collective-permute-start | bytes 774152 | tf_op jit(solution)/shard_map/gather_chunks/ppermute | solution.py:37
  43.0 13.7 %collective-permute-start.9 = (bf16[144,896]{1,0:T(8,128)(2,1)S(1)}, bf16[144,896]{1,0:T(8,128)(2,1)S(1)}, u32[]{:S(2)}, u32[]{:S(2)}) collective-permute-start(bf16[144,896]{1,0:T(8,128)(2,1)S(1)} %pack_rows.1.c0), channel_id=1, source_target_pairs={{0,1},{1,0},{2,3},{3,2},{4,5},{5,4},{6,7},{7,6},{8,9},{9,8},{10,11... | collective-permute-start | bytes 774152 | tf_op jit(solution)/shard_map/gather_chunks/ppermute | solution.py:37
  52.4 4.3 %collective-permute-start.14 = (f32[32,512]{1,0:T(8,128)S(1)}, f32[32,512]{1,0:T(8,128)S(1)}, u32[]{:S(2)}, u32[]{:S(2)}) collective-permute-start(f32[32,512]{1,0:T(8,128)S(1)} %low_rank_rows.1.a_ref._), channel_id=1, source_target_pairs={{0,1},{1,0},{2,3},{3,2},{4,5},{5,4},{6,7},{7,6},{8,9},{9,8},{10,11... | collective-permute-start | bytes 196616 | tf_op jit(solution)/shard_map/low_rank/ppermute | solution.py:37
  59.9 4.6 %collective-permute-start.17 = (bf16[256,1536]{1,0:T(8,128)(2,1)S(1)}, bf16[256,1536]{1,0:T(8,128)(2,1)S(1)}, u32[]{:S(2)}, u32[]{:S(2)}) collective-permute-start(bf16[256,1536]{1,0:T(8,128)(2,1)S(1)} %get-tuple-element.64._), channel_id=1, source_target_pairs={{0,4},{4,0},{8,12},{12,8},{16,20},{20,16},{24,28},{28,24},{1,5},{5... | collective-permute-start | bytes 2359304 | tf_op jit(solution)/shard_map/keys/ppermute | solution.py:33
  60.0 4.5 %collective-permute-start.15 = (f32[32,512]{1,0:T(8,128)S(1)}, f32[32,512]{1,0:T(8,128)S(1)}, u32[]{:S(2)}, u32[]{:S(2)}) collective-permute-start(f32[32,512]{1,0:T(8,128)S(1)} %add_rows.4._.a_ref), channel_id=1, source_target_pairs={{0,2},{1,3},{2,0},{3,1},{4,6},{5,7},{6,4},{7,5},{8,10},{9,11},{10,... | collective-permute-start | bytes 196616 | tf_op jit(solution)/shard_map/low_rank/ppermute | solution.py:37
  65.2 15.2 %collective-permute-start.21 = (bf16[256,768]{1,0:T(8,128)(2,1)S(1)}, bf16[256,768]{1,0:T(8,128)(2,1)S(1)}, u32[]{:S(2)}, u32[]{:S(2)}) collective-permute-start(bf16[256,768]{1,0:T(8,128)(2,1)S(1)} %get-tuple-element.67._), channel_id=1, source_target_pairs={{0,8},{4,12},{8,0},{12,4},{16,24},{20,28},{24,16},{28,20},{1,9},{5... | collective-permute-start | bytes 1179656 | tf_op jit(solution)/shard_map/keys/ppermute | solution.py:33
  67.0 1.2 collective-permute-start.16
  70.9 1.4 collective-permute-start.18
  72.3 5.2 %collective-permute-start.19 = (f32[4,4608]{1,0:T(4,128)S(1)}, f32[4,4608]{1,0:T(4,128)S(1)}, u32[]{:S(2)}, u32[]{:S(2)}) collective-permute-start(f32[4,4608]{1,0:T(4,128)S(1)} %slice.38), channel_id=1, source_target_pairs={{0,8},{4,12},{8,0},{12,4},{16,24},{20,28},{24,16},{28,20},{1,9},{5... | collective-permute-start | bytes 221192 | tf_op jit(solution)/shard_map/decode_rows/ppermute | solution.py:33
  77.6 4.9 %collective-permute-start.20 = (f32[2,4608]{1,0:T(2,128)S(1)}, f32[2,4608]{1,0:T(2,128)S(1)}, u32[]{:S(2)}, u32[]{:S(2)}) collective-permute-start(f32[2,4608]{1,0:T(2,128)S(1)} %slice.39), channel_id=1, source_target_pairs={{0,16},{4,20},{8,24},{12,28},{16,0},{20,4},{24,8},{28,12},{1,17},{... | collective-permute-start | bytes 110600 | tf_op jit(solution)/shard_map/decode_rows/ppermute | solution.py:33
  80.4 5.0 %collective-permute-start.22 = (bf16[256,1536]{1,0:T(8,128)(2,1)S(1)}, bf16[256,1536]{1,0:T(8,128)(2,1)S(1)}, u32[]{:S(2)}, u32[]{:S(2)}) collective-permute-start(bf16[256,1536]{1,0:T(8,128)(2,1)S(1)} %get-tuple-element.76), channel_id=1, source_target_pairs={{0,4},{4,0},{8,12},{12,8},{16,20},{20,16},{24,28},{28,24},{1,5},{5... | collective-permute-start | bytes 2359304 | tf_op jit(solution)/shard_map/values/ppermute | solution.py:33
  85.3 2.4 %collective-permute-start.23 = (bf16[256,1536]{1,0:T(8,128)(2,1)S(1)}, bf16[256,1536]{1,0:T(8,128)(2,1)S(1)}, u32[]{:S(2)}, u32[]{:S(2)}) collective-permute-start(bf16[256,1536]{1,0:T(8,128)(2,1)S(1)} %get-tuple-element.77), channel_id=1, source_target_pairs={{0,4},{4,0},{8,12},{12,8},{16,20},{20,16},{24,28},{28,24},{1,5},{5... | collective-permute-start | bytes 2359304 | tf_op jit(solution)/shard_map/queries/ppermute | solution.py:33
  88.6 23.9 %collective-permute-start.24 = (bf16[256,1536]{1,0:T(8,128)(2,1)S(1)}, bf16[256,1536]{1,0:T(8,128)(2,1)S(1)}, u32[]{:S(2)}, u32[]{:S(2)}) collective-permute-start(bf16[256,1536]{1,0:T(8,128)(2,1)S(1)} %get-tuple-element.79._), channel_id=1, source_target_pairs={{0,8},{4,12},{8,0},{12,4},{16,24},{20,28},{24,16},{28,20},{1,9},{5... | collective-permute-start | bytes 2359304 | tf_op jit(solution)/shard_map/reduce_z/ppermute | solution.py:33
  90.4 21.3 %collective-permute-start.25 = (bf16[256,384]{1,0:T(8,128)(2,1)S(1)}, bf16[256,384]{1,0:T(8,128)(2,1)S(1)}, u32[]{:S(2)}, u32[]{:S(2)}) collective-permute-start(bf16[256,384]{1,0:T(8,128)(2,1)S(1)} %get-tuple-element.73._), channel_id=1, source_target_pairs={{0,16},{4,20},{8,24},{12,28},{16,0},{20,4},{24,8},{28,12},{1,17},{... | collective-permute-start | bytes 589832 | tf_op jit(solution)/shard_map/keys/ppermute | solution.py:33
  113.2 20.3 %collective-permute-start.26 = (bf16[256,768]{1,0:T(8,128)(2,1)S(1)}, bf16[256,768]{1,0:T(8,128)(2,1)S(1)}, u32[]{:S(2)}, u32[]{:S(2)}) collective-permute-start(bf16[256,768]{1,0:T(8,128)(2,1)S(1)} %get-tuple-element.83._), channel_id=1, source_target_pairs={{0,16},{4,20},{8,24},{12,28},{16,0},{20,4},{24,8},{28,12},{1,17},{... | collective-permute-start | bytes 1179656 | tf_op jit(solution)/shard_map/reduce_z/ppermute | solution.py:33
  116.5 17.8 %collective-permute-start.27 = (bf16[256,384]{1,0:T(8,128)(2,1)S(1)}, bf16[256,384]{1,0:T(8,128)(2,1)S(1)}, u32[]{:S(2)}, u32[]{:S(2)}) collective-permute-start(bf16[256,384]{1,0:T(8,128)(2,1)S(1)} %finish_sums.2.refs_2_.ka_ref), channel_id=1, source_target_pairs={{0,4},{4,0},{8,12},{12,8},{16,20},{20,16},{24,28},{28,24},{1,5},{5... | collective-permute-start | bytes 589832 | tf_op jit(solution)/shard_map/keys/ppermute | solution.py:33
  134.1 1.5 collective-permute-start.28
  137.2 12.5 %collective-permute-start.30 = (bf16[272,384]{1,0:T(8,128)(2,1)S(1)}, bf16[272,384]{1,0:T(8,128)(2,1)S(1)}, u32[]{:S(2)}, u32[]{:S(2)}) collective-permute-start(bf16[272,384]{1,0:T(8,128)(2,1)S(1)} %prompt_attention.1.refs_0_), channel_id=1, source_target_pairs={{0,16},{4,20},{8,24},{12,28},{16,0},{20,4},{24,8},{28,12},{1,17},{... | collective-permute-start | bytes 626696 | tf_op jit(solution)/shard_map/gather_attended/ppermute | solution.py:33
  137.9 12.0 %collective-permute-start.29 = (bf16[272,384]{1,0:T(8,128)(2,1)S(1)}, bf16[272,384]{1,0:T(8,128)(2,1)S(1)}, u32[]{:S(2)}, u32[]{:S(2)}) collective-permute-start(bf16[272,384]{1,0:T(8,128)(2,1)S(1)} %prompt_attention.1.refs_0_), channel_id=1, source_target_pairs={{0,8},{4,12},{8,0},{12,4},{16,24},{20,28},{24,16},{28,20},{1,9},{5... | collective-permute-start | bytes 626696 | tf_op jit(solution)/shard_map/gather_attended/ppermute | solution.py:33
  149.7 7.0 %collective-permute-start.31 = (bf16[272,384]{1,0:T(8,128)(2,1)S(1)}, bf16[272,384]{1,0:T(8,128)(2,1)S(1)}, u32[]{:S(2)}, u32[]{:S(2)}) collective-permute-start(bf16[272,384]{1,0:T(8,128)(2,1)S(1)} %collective-permute-done.30.refs_2_), channel_id=1, source_target_pairs={{0,8},{4,12},{8,0},{12,4},{16,24},{20,28},{24,16},{28,20},{1,9},{5... | collective-permute-start | bytes 626696 | tf_op jit(solution)/shard_map/gather_attended/ppermute | solution.py:33
  149.7 7.0 %collective-permute-start.32 = (bf16[272,384]{1,0:T(8,128)(2,1)S(1)}, bf16[272,384]{1,0:T(8,128)(2,1)S(1)}, u32[]{:S(2)}, u32[]{:S(2)}) collective-permute-start(bf16[272,384]{1,0:T(8,128)(2,1)S(1)} %prompt_attention.1.refs_0_), channel_id=1, source_target_pairs={{0,4},{4,0},{8,12},{12,8},{16,20},{20,16},{24,28},{28,24},{1,5},{5... | collective-permute-start | bytes 626696 | tf_op jit(solution)/shard_map/gather_attended/ppermute | solution.py:33
  149.9 6.9 %collective-permute-start.33 = (bf16[272,384]{1,0:T(8,128)(2,1)S(1)}, bf16[272,384]{1,0:T(8,128)(2,1)S(1)}, u32[]{:S(2)}, u32[]{:S(2)}) collective-permute-start(bf16[272,384]{1,0:T(8,128)(2,1)S(1)} %collective-permute-done.29.refs_1_), channel_id=1, source_target_pairs={{0,4},{4,0},{8,12},{12,8},{16,20},{20,16},{24,28},{28,24},{1,5},{5... | collective-permute-start | bytes 626696 | tf_op jit(solution)/shard_map/gather_attended/ppermute | solution.py:33
  150.2 6.5 %collective-permute-start.34 = (bf16[272,384]{1,0:T(8,128)(2,1)S(1)}, bf16[272,384]{1,0:T(8,128)(2,1)S(1)}, u32[]{:S(2)}, u32[]{:S(2)}) collective-permute-start(bf16[272,384]{1,0:T(8,128)(2,1)S(1)} %collective-permute-done.30.refs_2_), channel_id=1, source_target_pairs={{0,4},{4,0},{8,12},{12,8},{16,20},{20,16},{24,28},{28,24},{1,5},{5... | collective-permute-start | bytes 626696 | tf_op jit(solution)/shard_map/gather_attended/ppermute | solution.py:33
  156.8 2.3 %collective-permute-start.35 = (bf16[272,384]{1,0:T(8,128)(2,1)S(1)}, bf16[272,384]{1,0:T(8,128)(2,1)S(1)}, u32[]{:S(2)}, u32[]{:S(2)}) collective-permute-start(bf16[272,384]{1,0:T(8,128)(2,1)S(1)} %collective-permute-done.31.refs_3_), channel_id=1, source_target_pairs={{0,4},{4,0},{8,12},{12,8},{16,20},{20,16},{24,28},{28,24},{1,5},{5... | collective-permute-start | bytes 626696 | tf_op jit(solution)/shard_map/gather_attended/ppermute | solution.py:33
  159.1 36.1 %copy-start.9 = (f32[1792]{0:T(1024)S(1)}, f32[1792]{0:T(1024)}, u32[]{:S(2)}) copy-start(f32[1792]{0:T(1024)} %param.25) | copy-start | bytes 21508
  161.2 39.3 %copy-start.6 = (bf16[98,1792]{1,0:T(8,128)(2,1)S(1)}, bf16[98,1792]{1,0:T(8,128)(2,1)}, u32[]{:S(2)}) copy-start(bf16[98,1792]{1,0:T(8,128)(2,1)} %x_ref.3) | copy-start | bytes 1053700
  161.2 9.1 %collective-permute-start.36 = (bf16[144,896]{1,0:T(8,128)(2,1)S(1)}, bf16[144,896]{1,0:T(8,128)(2,1)S(1)}, u32[]{:S(2)}, u32[]{:S(2)}) collective-permute-start(bf16[144,896]{1,0:T(8,128)(2,1)S(1)} %get-tuple-element.90), channel_id=1, source_target_pairs={{0,1},{1,0},{2,3},{3,2},{4,5},{5,4},{6,7},{7,6},{8,9},{9,8},{10,11... | collective-permute-start | bytes 774152 | tf_op jit(solution)/shard_map/sum_mp/ppermute | solution.py:37
  162.7 13.9 %collective-permute-start.37 = (bf16[144,896]{1,0:T(8,128)(2,1)S(1)}, bf16[144,896]{1,0:T(8,128)(2,1)S(1)}, u32[]{:S(2)}, u32[]{:S(2)}) collective-permute-start(bf16[144,896]{1,0:T(8,128)(2,1)S(1)} %get-tuple-element.91), channel_id=1, source_target_pairs={{0,2},{1,3},{2,0},{3,1},{4,6},{5,7},{6,4},{7,5},{8,10},{9,11},{10,... | collective-permute-start | bytes 774152 | tf_op jit(solution)/shard_map/sum_mp/ppermute | solution.py:37
  164.3 12.3 %collective-permute-start.38 = (bf16[144,896]{1,0:T(8,128)(2,1)S(1)}, bf16[144,896]{1,0:T(8,128)(2,1)S(1)}, u32[]{:S(2)}, u32[]{:S(2)}) collective-permute-start(bf16[144,896]{1,0:T(8,128)(2,1)S(1)} %get-tuple-element.92), channel_id=1, source_target_pairs={{0,3},{1,2},{2,1},{3,0},{4,7},{5,6},{6,5},{7,4},{8,11},{9,10},{10,... | collective-permute-start | bytes 774152 | tf_op jit(solution)/shard_map/sum_mp/ppermute | solution.py:37
  177.6 6.1 %collective-permute-start.39 = (bf16[64,896]{1,0:T(8,128)(2,1)S(1)}, bf16[64,896]{1,0:T(8,128)(2,1)S(1)}, u32[]{:S(2)}, u32[]{:S(2)}) collective-permute-start(bf16[64,896]{1,0:T(8,128)(2,1)S(1)} %get-tuple-element.94), channel_id=1, source_target_pairs={{0,8},{4,12},{8,0},{12,4},{16,24},{20,28},{24,16},{28,20},{1,9},{5... | collective-permute-start | bytes 344072 | tf_op jit(solution)/shard_map/return_z/ppermute | solution.py:33
  177.9 11.5 %collective-permute-start.40 = (bf16[64,896]{1,0:T(8,128)(2,1)S(1)}, bf16[64,896]{1,0:T(8,128)(2,1)S(1)}, u32[]{:S(2)}, u32[]{:S(2)}) collective-permute-start(bf16[64,896]{1,0:T(8,128)(2,1)S(1)} %get-tuple-element.95), channel_id=1, source_target_pairs={{0,16},{4,20},{8,24},{12,28},{16,0},{20,4},{24,8},{28,12},{1,17},{... | collective-permute-start | bytes 344072 | tf_op jit(solution)/shard_map/return_z/ppermute | solution.py:33
  180.2 9.2 %collective-permute-start.41 = (bf16[64,896]{1,0:T(8,128)(2,1)S(1)}, bf16[64,896]{1,0:T(8,128)(2,1)S(1)}, u32[]{:S(2)}, u32[]{:S(2)}) collective-permute-start(bf16[64,896]{1,0:T(8,128)(2,1)S(1)} %get-tuple-element.96), channel_id=1, source_target_pairs={{0,24},{4,28},{8,16},{12,20},{16,8},{20,12},{24,0},{28,4},{1,25},{... | collective-permute-start | bytes 344072 | tf_op jit(solution)/shard_map/return_z/ppermute | solution.py:33
  189.5 1.6 collective-permute-start.42
  191.6 5.3 %collective-permute-start.43 = (bf16[32,1792]{1,0:T(8,128)(2,1)S(1)}, bf16[32,1792]{1,0:T(8,128)(2,1)S(1)}, u32[]{:S(2)}, u32[]{:S(2)}) collective-permute-start(bf16[32,1792]{1,0:T(8,128)(2,1)S(1)} %get-tuple-element.98), channel_id=1, source_target_pairs={{0,1},{1,0},{2,3},{3,2},{4,5},{5,4},{6,7},{7,6},{8,9},{9,8},{10,11... | collective-permute-start | bytes 344072 | tf_op jit(solution)/shard_map/return_plane/ppermute | solution.py:37
  193.2 7.4 %collective-permute-start.44 = (bf16[32,1792]{1,0:T(8,128)(2,1)S(1)}, bf16[32,1792]{1,0:T(8,128)(2,1)S(1)}, u32[]{:S(2)}, u32[]{:S(2)}) collective-permute-start(bf16[32,1792]{1,0:T(8,128)(2,1)S(1)} %get-tuple-element.99), channel_id=1, source_target_pairs={{0,2},{1,3},{2,0},{3,1},{4,6},{5,7},{6,4},{7,5},{8,10},{9,11},{10,... | collective-permute-start | bytes 344072 | tf_op jit(solution)/shard_map/return_plane/ppermute | solution.py:37
  193.7 6.8 %collective-permute-start.45 = (bf16[32,1792]{1,0:T(8,128)(2,1)S(1)}, bf16[32,1792]{1,0:T(8,128)(2,1)S(1)}, u32[]{:S(2)}, u32[]{:S(2)}) collective-permute-start(bf16[32,1792]{1,0:T(8,128)(2,1)S(1)} %get-tuple-element.100), channel_id=1, source_target_pairs={{0,3},{1,2},{2,1},{3,0},{4,7},{5,6},{6,5},{7,4},{8,11},{9,10},{10,... | collective-permute-start | bytes 344072 | tf_op jit(solution)/shard_map/return_plane/ppermute | solution.py:37
  (8 other events, 150.1 us)

commit v6 on v5

--- a/solution.py
+++ b/solution.py
@@ -152,7 +152,7 @@
         out_shape=[jax.ShapeDtypeStruct((BLK, tokens.shape[1]), BF)] * NM,
         in_specs=[SMEM, VMEM],
         out_specs=[VMEM] * NM,
-        compiler_params=limit(16),
+        compiler_params=limit(12),
         cost_estimate=SMALL,
         name="deal_rows",
     )(scalars, tokens)
@@ -201,7 +201,7 @@
         in_specs=[SMEM] + [VMEM] * 6 + [ANY] * 2,
         out_specs=[VMEM] * NZ,
         scratch_shapes=[pltpu.VMEM((NM,) + blocks[0].shape, F32)],
-        compiler_params=limit(16),
+        compiler_params=limit(12),
         cost_estimate=SMALL,
         name="norm_rows",
     )(scalars, *blocks, affine, table, near, far)
@@ -223,7 +223,7 @@
         out_shape=[out, out],
         in_specs=[SMEM] + [VMEM] * NZ,
         out_specs=[VMEM] * 2,
-        compiler_params=limit(16),
+        compiler_params=limit(12),
         cost_estimate=SMALL,
         name="split_cores",
     )(scalars, *blocks)
@@ -248,7 +248,7 @@
         out_shape=jax.ShapeDtypeStruct((CHUNK + DCH, mine.shape[1]), BF),
         in_specs=[SMEM] * 2 + [VMEM] * 2,
         out_specs=VMEM,
-        compiler_params=limit(16),
+        compiler_params=limit(12),
         cost_estimate=SMALL,
         name="pack_rows",
     )(scalars, tables, mine, theirs)
@@ -264,7 +264,7 @@
         out_shape=jax.ShapeDtypeStruct(x.shape, x.dtype),
         in_specs=[VMEM, ANY],
         out_specs=VMEM,
-        compiler_params=limit(16),
+        compiler_params=limit(12),
         cost_estimate=SMALL,
         name="copy_rows",
     )(x, after)
@@ -296,7 +296,7 @@
         out_shape=[jax.ShapeDtypeStruct((n, 1), jnp.int32), jax.ShapeDtypeStruct((1, n), jnp.int32)],
         in_specs=[SMEM] * 2 + [ANY],
         out_specs=[VMEM] * 2,
-        compiler_params=limit(16),
+        compiler_params=limit(12),
         cost_estimate=SMALL,
         name="packed_codes",
     )(scalars, tables, after)
@@ -336,7 +336,7 @@
         out_shape=jax.ShapeDtypeStruct((2 * ADAPTER_RANK, NZ * LANES), F32),
         in_specs=[SMEM] * 2 + [VMEM] * 11,
         out_specs=VMEM,
-        compiler_params=limit(16),
+        compiler_params=limit(12),
         cost_estimate=SMALL,
         name="low_rank_rows",
     )(scalars, tables, down, down_other, *pieces, *stats, affine)
@@ -382,7 +382,7 @@
         out_shape=[jax.ShapeDtypeStruct((2, PACKED, count * ADAPTER_RANK), BF), half, half],
         in_specs=[SMEM] * 2 + [VMEM] * 5 + [ANY],
         out_specs=[VMEM] * 3,
-        compiler_params=limit(16),
+        compiler_params=limit(12),
         cost_estimate=SMALL,
         name="expand_rows",
     )(scalars, tables, low, low_other, base, keys, up, after)
@@ -433,7 +433,7 @@
         out_shape=out_shape,
         in_specs=[SMEM] + whole + [pl.BlockSpec((1, depth, tile), lambda j: (part, 0, j)), ANY],
         out_specs=out_specs,
-        compiler_params=limit(16),
+        compiler_params=limit(12),
         cost_estimate=SMALL,
         name="project_keys",
     )(scalars, *chunks, weight, after)
@@ -467,7 +467,7 @@
             ANY,
         ],
         out_specs=[pl.BlockSpec((v.shape[0], tile), lambda j: (0, j)) for v in out_shape],
-        compiler_params=limit(16),
+        compiler_params=limit(12),
         cost_estimate=SMALL,
         name="project_adapted",
     )(rows, weight, expanded, up, after)
@@ -483,7 +483,7 @@
         out_shape=jax.ShapeDtypeStruct(b.shape, dtype),
         in_specs=[VMEM] * 2 + [ANY],
         out_specs=VMEM,
-        compiler_params=limit(16),
+        compiler_params=limit(12),
         cost_estimate=SMALL,
         name="add_rows",
     )(a, b, after)
@@ -505,7 +505,7 @@
         out_shape=[out] * 3,
         in_specs=[VMEM] * 3 + [ANY],
         out_specs=[VMEM] * 3,
-        compiler_params=limit(16),
+        compiler_params=limit(12),
         cost_estimate=SMALL,
         name="decode_finish",
     )(a, b, bias, after)
@@ -528,7 +528,7 @@
             ANY,
         ],
         out_specs=pl.BlockSpec((count, feats), lambda p: (0, p)),
-        compiler_params=limit(16),
+        compiler_params=limit(12),
         cost_estimate=SMALL,
         name="decode_base",
     )(rows, weight, after)
@@ -561,7 +561,7 @@
         out_shape=[jax.ShapeDtypeStruct((rows, feats), BF), jax.ShapeDtypeStruct((rows, feats), F32)],
         in_specs=[SMEM] + [VMEM] * (2 * len(totals)) + [ANY],
         out_specs=[VMEM, VMEM],
-        compiler_params=limit(16),
+        compiler_params=limit(12),
         cost_estimate=SMALL,
         name="halve_sums",
     )(scalars, *totals, *gots, after)
@@ -583,7 +583,7 @@
         out_shape=[jax.ShapeDtypeStruct((rows, feats // len(parts)), BF)] * len(parts),
         in_specs=[SMEM, VMEM, VMEM, VMEM, ANY],
         out_specs=[VMEM] * len(parts),
-        compiler_params=limit(16),
+        compiler_params=limit(12),
         cost_estimate=SMALL,
         name="finish_sums",
     )(scalars, total, got, bias, after)
@@ -618,7 +618,7 @@
         out_shape=jax.ShapeDtypeStruct((q.shape[0] + DECODE_ROWS, q.shape[1]), BF),
         in_specs=[VMEM] * 8,
         out_specs=VMEM,
-        compiler_params=limit(16),
+        compiler_params=limit(12),
         cost_estimate=SMALL,
         name="prompt_attention",
     )(q, ka, kb, va, vb, code_rows, code_cols, dec)
@@ -664,7 +664,7 @@
         o_ref[0] = jnp.sum(jnp.where(diag, o, 0.0), axis=0, keepdims=True).astype(BF)
 
 
-def decode_attention(lengths, q, k, v, cache, after, span=256):
+def decode_attention(lengths, q, k, v, cache, after, span=512):
     count, positions, _, feats = cache.shape
     row = pl.BlockSpec((1, 1, feats), lambda d, t, n: (d, 0, 0))
     heads = 16
@@ -714,7 +714,7 @@
         out_shape=jax.ShapeDtypeStruct((NM * CHUNK, weight.shape[1]), F32),
         in_specs=[SMEM] + [VMEM] * 7,
         out_specs=VMEM,
-        compiler_params=limit(16),
+        compiler_params=limit(12),
         cost_estimate=SMALL,
         name="out_first",
     )(scalars, *own[:3], *other[:3], weight)
@@ -754,7 +754,7 @@
         in_specs=[SMEM] + [VMEM] * 10,
         out_specs=[VMEM] * NM,
         scratch_shapes=[pltpu.VMEM((NM * CHUNK, feats), BF)],
-        compiler_params=limit(16),
+        compiler_params=limit(12),
         cost_estimate=SMALL,
         name="out_project",
     )(scalars, *own, *other, first, weight)
@@ -779,7 +779,7 @@
         out_shape=[jax.ShapeDtypeStruct((2 * BLK, feats), BF)] * NZ,
         in_specs=[SMEM] * 2 + [VMEM] * 4,
         out_specs=[VMEM] * NZ,
-        compiler_params=limit(16),
+        compiler_params=limit(12),
         cost_estimate=SMALL,
         name="unpack_rows",
     )(scalars, tables, *chunks)
@@ -805,7 +805,7 @@
         in_specs=[SMEM] + [VMEM] * 5,
         out_specs=[VMEM] * NM,
         scratch_shapes=[pltpu.VMEM((NZ,) + shape, BF)],
-        compiler_params=limit(16),
+        compiler_params=limit(12),
         cost_estimate=SMALL,
         name="join_halves",
     )(scalars, *parts, other)
@@ -836,7 +836,7 @@
         out_shape=jax.ShapeDtypeStruct(tokens.shape, BF),
         in_specs=[SMEM] + [VMEM] * 6,
         out_specs=VMEM,
-        compiler_params=limit(16),
+        compiler_params=limit(12),
         cost_estimate=SMALL,
         name="add_home",
     )(scalars, tokens, bias, *blocks)

time: 203 us -> 203 us (level)
  waiting for transfers between devices: 104 us -> 99.9 us
  Pallas kernels: 43.8 us -> 47.8 us
    pallas_call x1, Pallas kernels: 7.78 us -> 11.8 us  [decode_attention(): pl.pallas_call(decode_kernel, grid_spec=pltpu.PrefetchScalarGridSpec(num_...]
    ppermute x32, waiting for transfers between devices: 78.4 us -> 74.4 us  [swap_req(): return lax.ppermute(x, 'req', [(i, i ^ bits) for i in range(2 * NZ)])]
  transfers between devices with their start and end apart: 46 -> 46, of which waited for: 30 -> 30; matrix products, arithmetic and copies ran while one was open for 1% -> 1% of each run, Pallas kernels for 15% -> 17%
where the time goes in v6:
time: 203 us; the launch traced here: 202 us
  waiting for transfers between devices  99.9 us (49%)
  starting transfers between devices  49.6 us (24%)
  Pallas kernels  47.8 us (24%)
  local copies, waits for them, and re-layouts  3.01 us (1%)
    ppermute x32, waiting for transfers between devices, swap_req(): return lax.ppermute(x, 'req', [(i, i ^ bits) for i in range(2 * NZ)])  74.4 us
    ppermute x32, starting transfers between devices, swap_req(): return lax.ppermute(x, 'req', [(i, i ^ bits) for i in range(2 * NZ)])  32.3 us
    ppermute x14, waiting for transfers between devices, swap_mp(): return lax.ppermute(x, 'mp', [(i, i ^ bits) for i in range(NM)])  25.5 us
    ppermute x14, starting transfers between devices, swap_mp(): return lax.ppermute(x, 'mp', [(i, i ^ bits) for i in range(NM)])  17.3 us
    pallas_call x1, Pallas kernels, decode_attention(): pl.pallas_call(decode_kernel, grid_spec=pltpu.PrefetchScalarGridSpec(num_...  11.8 us
    pallas_call x2, Pallas kernels, project_adapted(): pl.pallas_call(adapted_kernel, grid=(2,), out_shape=out_shape, in_specs=[...  5.41 us
  transfers between devices with their start and end apart: 46, of which 30 were waited for; matrix products, arithmetic and copies ran while one was open for 1% of the time, Pallas kernels for 17%

profile of v6, /device:TPU:0, one launch (start us, length us, event | category | flops | bytes accessed | tf_op | source)
XLA Modules:
  0.0 202.4 jit_solution(7515781041639838575)
XLA Ops:
  0.0 4.0 %collective-permute-start.4 = (bf16[98,1792]{1,0:T(8,128)(2,1)}, bf16[98,1792]{1,0:T(8,128)(2,1)S(1)}, u32[]{:S(2)}, u32[]{:S(2)}) collective-permute-start(bf16[98,1792]{1,0:T(8,128)(2,1)} %x_ref.3), channel_id=1, source_target_pairs={{0,16},{4,20},{8,24},{12,28},{16,0},{20,4},{24,8},{28,12},{1,17},{... | collective-permute-start | bytes 1053704 | tf_op jit(solution)/shard_map/gather_home/ppermute | solution.py:33
  4.8 1.6 collective-permute-start.3
  8.6 1.6 collective-permute-start
  14.0 2.5 %collective-permute-done.1.b2 = bf16[32,1792]{1,0:T(8,128)(2,1)S(1)} collective-permute-done((bf16[32,1792]{1,0:T(8,128)(2,1)S(1)}, bf16[32,1792]{1,0:T(8,128)(2,1)S(1)}, u32[]{:S(2)}, u32[]{:S(2)}) %collective-permute-start.1) | collective-permute-done | bytes 114720 | tf_op jit(solution)/shard_map/deal/ppermute | solution.py:37
  17.4 3.6 %collective-permute-done.4.__.x2 = bf16[98,1792]{1,0:T(8,128)(2,1)S(1)} collective-permute-done((bf16[98,1792]{1,0:T(8,128)(2,1)}, bf16[98,1792]{1,0:T(8,128)(2,1)S(1)}, u32[]{:S(2)}, u32[]{:S(2)}) %collective-permute-start.4) | collective-permute-done | bytes 351264 | tf_op jit(solution)/shard_map/gather_home/ppermute | solution.py:33
  23.8 2.4 %collective-permute-start.6 = (bf16[32,1792]{1,0:T(8,128)(2,1)S(1)}, bf16[32,1792]{1,0:T(8,128)(2,1)S(1)}, u32[]{:S(2)}, u32[]{:S(2)}) collective-permute-start(bf16[32,1792]{1,0:T(8,128)(2,1)S(1)} %get-tuple-element.59), channel_id=1, source_target_pairs={{0,16},{4,20},{8,24},{12,28},{16,0},{20,4},{24,8},{28,12},{1,17},{... | collective-permute-start | bytes 344072 | tf_op jit(solution)/shard_map/spread_z/ppermute | solution.py:33
  27.5 1.9 collective-permute-done.5.b1.t1
  29.3 6.1 %collective-permute-done.6.b2.t2 = bf16[32,1792]{1,0:T(8,128)(2,1)S(1)} collective-permute-done((bf16[32,1792]{1,0:T(8,128)(2,1)S(1)}, bf16[32,1792]{1,0:T(8,128)(2,1)S(1)}, u32[]{:S(2)}, u32[]{:S(2)}) %collective-permute-start.6) | collective-permute-done | bytes 114720 | tf_op jit(solution)/shard_map/spread_z/ppermute | solution.py:33
  36.7 1.8 collective-permute-start.13
  40.0 1.6 collective-permute-start.10
  43.5 3.8 %collective-permute-done.13.x3 = bf16[98,1792]{1,0:T(8,128)(2,1)S(1)} collective-permute-done((bf16[98,1792]{1,0:T(8,128)(2,1)S(1)}, bf16[98,1792]{1,0:T(8,128)(2,1)S(1)}, u32[]{:S(2)}, u32[]{:S(2)}) %collective-permute-start.13) | collective-permute-done | bytes 351264 | tf_op jit(solution)/shard_map/gather_home/ppermute | solution.py:33
  48.4 4.0 %low_rank_rows.1.a_ref._ = f32[32,512]{1,0:T(8,128)S(1)} custom-call(s32[7]{0:T(128)S(1)} %concatenate.12.s_ref.place_ref, s32[8,8]{1,0:T(8,128)S(1)} %maximum_convert_fusion.t_ref.table_ref, bf16[256,1792]{1,0:T(8,128)(2,1)S(1)} %bitcast.26, bf16[256,1792]{1,0:T(8,128)(2,1)S(1)} %collective-permute-done.12.db_ref, bf16[98,1792]{1,0:T(8,128)(2,1)S(1)} %copy-done.5, ...), custom_call_target="tpu_custom_call" | custom-call | flops 1 | bytes 1 | tf_op jit(solution)/shard_map/low_rank/low_rank_rows/pallas_call | solution.py:334
  52.4 1.5 collective-permute-start.14
  53.9 2.8 %collective-permute-done.14.b_ref = f32[32,512]{1,0:T(8,128)S(1)} collective-permute-done((f32[32,512]{1,0:T(8,128)S(1)}, f32[32,512]{1,0:T(8,128)S(1)}, u32[]{:S(2)}, u32[]{:S(2)}) %collective-permute-start.14) | collective-permute-done | bytes 65568 | tf_op jit(solution)/shard_map/low_rank/ppermute | solution.py:37
  56.7 3.1 %project_keys.1 = (bf16[256,1536]{1,0:T(8,128)(2,1)S(1)}, bf16[256,1536]{1,0:T(8,128)(2,1)S(1)}, f32[16,1536]{1,0:T(8,128)S(1)}, bf16[528,896]{1,0:T(8,128)(2,1)S(1)}) custom-call(s32[7]{0:T(128)S(1)} %concatenate.12.s_ref.place_ref, bf16[144,896]{1,0:T(8,128)(2,1)S(1)} %pack_rows.1.c0, bf16[144,896]{1,0:T(8,128)(2,1)S(1)} %collective-permute-done.9.c1, ...), custom_call_target="tpu_custom_call" | custom-call | flops 1 | bytes 1 | tf_op jit(solution)/shard_map/keys/project_keys/pallas_call | solution.py:430
  60.0 1.6 collective-permute-start.15
  62.5 2.0 collective-permute-done.15.b_ref
  65.2 1.8 collective-permute-start.21
  68.2 2.6 %expand_rows.1 = (bf16[2,528,128]{2,1,0:T(8,128)(2,1)S(1)}, f32[8,4608]{1,0:T(8,128)S(1)}, f32[8,4608]{1,0:T(8,128)S(1)}) custom-call(s32[7]{0:T(128)S(1)} %concatenate.12.s_ref.place_ref, s32[8,8]{1,0:T(8,128)S(1)} %maximum_convert_fusion.t_ref.table_ref, bf16[32,512]{1,0:T(8,128)(2,1)S(1)} %add_rows.5.refs_2_.low_ref, ...), custom_call_target="tpu_custom_call" | custom-call | flops 1 | bytes 1 | tf_op jit(solution)/shard_map/low_rank/expand_rows/pallas_call | solution.py:380
  72.7 2.7 %project_adapted.2 = (bf16[256,1536]{1,0:T(8,128)(2,1)S(1)}, bf16[256,1536]{1,0:T(8,128)(2,1)S(1)}) custom-call(bf16[528,896]{1,0:T(8,128)(2,1)S(1)} %get-tuple-element.63.x_ref, bf16[3,896,1536]{2,1,0:T(8,128)(2,1)S(1)} %copy-done, bf16[2,528,128]{2,1,0:T(8,128)(2,1)S(1)} %get-tuple-element.68._.e_ref, bf16[8,2,16,1536]{3,2,1,0:T(8,128)(2,1)S(1)} %copy-done.2, ...), custom_call_target="tpu_custom_call" | custom-call | flops 1 | bytes 1 | tf_op jit(solution)/shard_map/values/project_adapted/pallas_call | solution.py:458
  75.4 2.2 %collective-permute-done.19.b_ref = f32[4,4608]{1,0:T(4,128)S(1)} collective-permute-done((f32[4,4608]{1,0:T(4,128)S(1)}, f32[4,4608]{1,0:T(4,128)S(1)}, u32[]{:S(2)}, u32[]{:S(2)}) %collective-permute-start.19) | collective-permute-done | bytes 73760 | tf_op jit(solution)/shard_map/decode_rows/ppermute | solution.py:33
  77.6 2.8 %collective-permute-start.20 = (f32[2,4608]{1,0:T(2,128)S(1)}, f32[2,4608]{1,0:T(2,128)S(1)}, u32[]{:S(2)}, u32[]{:S(2)}) collective-permute-start(f32[2,4608]{1,0:T(2,128)S(1)} %slice.39), channel_id=1, source_target_pairs={{0,16},{4,20},{8,24},{12,28},{16,0},{20,4},{24,8},{28,12},{1,17},{... | collective-permute-start | bytes 110600 | tf_op jit(solution)/shard_map/decode_rows/ppermute | solution.py:33
  82.6 2.7 %project_adapted.3 = (bf16[256,1536]{1,0:T(8,128)(2,1)S(1)}, bf16[256,1536]{1,0:T(8,128)(2,1)S(1)}) custom-call(bf16[528,896]{1,0:T(8,128)(2,1)S(1)} %get-tuple-element.63.x_ref, bf16[3,896,1536]{2,1,0:T(8,128)(2,1)S(1)} %copy-done, bf16[2,528,128]{2,1,0:T(8,128)(2,1)S(1)} %get-tuple-element.68._.e_ref, bf16[8,2,16,1536]{3,2,1,0:T(8,128)(2,1)S(1)} %copy-done.2, ...), custom_call_target="tpu_custom_call" | custom-call | flops 1 | bytes 1 | tf_op jit(solution)/shard_map/queries/project_adapted/pallas_call | solution.py:458
  85.4 2.3 %collective-permute-done.23.refs_3_.refs_4_ = bf16[256,1536]{1,0:T(8,128)(2,1)S(1)} collective-permute-done((bf16[256,1536]{1,0:T(8,128)(2,1)S(1)}, bf16[256,1536]{1,0:T(8,128)(2,1)S(1)}, u32[]{:S(2)}, u32[]{:S(2)}) %collective-permute-start.23) | collective-permute-done | bytes 786464 | tf_op jit(solution)/shard_map/queries/ppermute | solution.py:33
  88.6 1.8 collective-permute-start.24
  91.7 2.4 %packed_codes.1 = (s32[512,1]{1,0:T(8,128)S(1)}, s32[1,512]{1,0:T(1,128)S(1)}) custom-call(s32[7]{0:T(128)S(1)} %concatenate.12.s_ref.place_ref, s32[8,8]{1,0:T(8,128)S(1)} %maximum_convert_fusion.t_ref.table_ref, bf16[256,1536]{1,0:T(8,128)(2,1)S(1)} %get-tuple-element.79._), custom_call_target="tpu_custom_call" | custom-call | flops 1 | bytes 1 | tf_op jit(solution)/shard_map/codes/packed_codes/pallas_call | solution.py:294
  94.1 17.6 %collective-permute-done.25.got_ref = bf16[256,384]{1,0:T(8,128)(2,1)S(1)} collective-permute-done((bf16[256,384]{1,0:T(8,128)(2,1)S(1)}, bf16[256,384]{1,0:T(8,128)(2,1)S(1)}, u32[]{:S(2)}, u32[]{:S(2)}) %collective-permute-start.25) | collective-permute-done | bytes 196640 | tf_op jit(solution)/shard_map/keys/ppermute | solution.py:33
  113.2 3.3 %collective-permute-start.26 = (bf16[256,768]{1,0:T(8,128)(2,1)S(1)}, bf16[256,768]{1,0:T(8,128)(2,1)S(1)}, u32[]{:S(2)}, u32[]{:S(2)}) collective-permute-start(bf16[256,768]{1,0:T(8,128)(2,1)S(1)} %get-tuple-element.83._), channel_id=1, source_target_pairs={{0,16},{4,20},{8,24},{12,28},{16,0},{20,4},{24,8},{28,12},{1,17},{... | collective-permute-start | bytes 1179656 | tf_op jit(solution)/shard_map/reduce_z/ppermute | solution.py:33
  116.5 11.8 %decode_attention.1 = bf16[2,1,1536]{2,1,0:T(2,128)(2,1)S(1)} custom-call(s32[2]{0:T(128)S(1)} %copy-done.8, bf16[2,1,1536]{2,1,0:T(2,128)(2,1)S(1)} %get-tuple-element.74._.q_ref, bf16[2,1,1536]{2,1,0:T(2,128)(2,1)S(1)} %get-tuple-element.84.k_ref, bf16[2,1,1536]{2,1,0:T(2,128)(2,1)S(1)} %get-tuple-element.85.v_ref, bf16[2,2048,2,1536]{3,2,1,0:T(2,128)(2,1)} %c_ref.1, ...), custom_call_target="tpu_custom_call" | custom-call | flops 1 | bytes 1 | tf_op jit(solution)/shard_map/decode_attention/decode_attention/pallas_call | solution.py:671
  128.3 5.2 %collective-permute-done.26.got_ref = bf16[256,768]{1,0:T(8,128)(2,1)S(1)} collective-permute-done((bf16[256,768]{1,0:T(8,128)(2,1)S(1)}, bf16[256,768]{1,0:T(8,128)(2,1)S(1)}, u32[]{:S(2)}, u32[]{:S(2)}) %collective-permute-start.26) | collective-permute-done | bytes 393248 | tf_op jit(solution)/shard_map/reduce_z/ppermute | solution.py:33
  135.6 1.5 prompt_attention.1.refs_0_
  137.2 3.0 %collective-permute-start.29 = (bf16[272,384]{1,0:T(8,128)(2,1)S(1)}, bf16[272,384]{1,0:T(8,128)(2,1)S(1)}, u32[]{:S(2)}, u32[]{:S(2)}) collective-permute-start(bf16[272,384]{1,0:T(8,128)(2,1)S(1)} %prompt_attention.1.refs_0_), channel_id=1, source_target_pairs={{0,8},{4,12},{8,0},{12,4},{16,24},{20,28},{24,16},{28,20},{1,9},{5... | collective-permute-start | bytes 626696 | tf_op jit(solution)/shard_map/gather_attended/ppermute | solution.py:33
  140.2 9.5 %collective-permute-done.30.refs_2_ = bf16[272,384]{1,0:T(8,128)(2,1)S(1)} collective-permute-done((bf16[272,384]{1,0:T(8,128)(2,1)S(1)}, bf16[272,384]{1,0:T(8,128)(2,1)S(1)}, u32[]{:S(2)}, u32[]{:S(2)}) %collective-permute-start.30) | collective-permute-done | bytes 208928 | tf_op jit(solution)/shard_map/gather_attended/ppermute | solution.py:33
  150.4 6.4 %collective-permute-done.31.refs_3_ = bf16[272,384]{1,0:T(8,128)(2,1)S(1)} collective-permute-done((bf16[272,384]{1,0:T(8,128)(2,1)S(1)}, bf16[272,384]{1,0:T(8,128)(2,1)S(1)}, u32[]{:S(2)}, u32[]{:S(2)}) %collective-permute-start.31) | collective-permute-done | bytes 208928 | tf_op jit(solution)/shard_map/gather_attended/ppermute | solution.py:33
  156.8 2.2 %out_first.1.refs_8_ = f32[512,896]{1,0:T(8,128)S(1)} custom-call(s32[7]{0:T(128)S(1)} %concatenate.12.s_ref.place_ref, bf16[272,384]{1,0:T(8,128)(2,1)S(1)} %prompt_attention.1.refs_0_, bf16[272,384]{1,0:T(8,128)(2,1)S(1)} %collective-permute-done.29.refs_1_, bf16[272,384]{1,0:T(8,128)(2,1)S(1)} %collective-permute-done.30.refs_2_, ...), custom_call_target="tpu_custom_call" | custom-call | flops 1 | bytes 1 | tf_op jit(solution)/shard_map/out_project/out_first/pallas_call | solution.py:712
  159.1 2.1 %out_project.1 = (bf16[144,896]{1,0:T(8,128)(2,1)S(1)}, bf16[144,896]{1,0:T(8,128)(2,1)S(1)}, bf16[144,896]{1,0:T(8,128)(2,1)S(1)}, bf16[144,896]{1,0:T(8,128)(2,1)S(1)}) custom-call(s32[7]{0:T(128)S(1)} %concatenate.12.s_ref.place_ref, bf16[272,384]{1,0:T(8,128)(2,1)S(1)} %prompt_attention.1.refs_0_, bf16[272,384]{1,0:T(8,128)(2,1)S(1)} %collective-permute-done.29.refs_1_, ...), custom_call_target="tpu_custom_call" | custom-call | flops 1 | bytes 1 | tf_op jit(solution)/shard_map/out_project/out_project/pallas_call | solution.py:751
  161.2 1.5 collective-permute-start.36
  162.7 1.5 collective-permute-start.37
  164.8 5.5 %collective-permute-done.36.c1 = bf16[144,896]{1,0:T(8,128)(2,1)S(1)} collective-permute-done((bf16[144,896]{1,0:T(8,128)(2,1)S(1)}, bf16[144,896]{1,0:T(8,128)(2,1)S(1)}, u32[]{:S(2)}, u32[]{:S(2)}) %collective-permute-start.36) | collective-permute-done | bytes 258080 | tf_op jit(solution)/shard_map/sum_mp/ppermute | solution.py:37
  170.3 6.3 %collective-permute-done.37.c2 = bf16[144,896]{1,0:T(8,128)(2,1)S(1)} collective-permute-done((bf16[144,896]{1,0:T(8,128)(2,1)S(1)}, bf16[144,896]{1,0:T(8,128)(2,1)S(1)}, u32[]{:S(2)}, u32[]{:S(2)}) %collective-permute-start.37) | collective-permute-done | bytes 258080 | tf_op jit(solution)/shard_map/sum_mp/ppermute | solution.py:37
  177.9 1.7 collective-permute-start.40
  179.6 2.4 %collective-permute-start.41 = (bf16[64,896]{1,0:T(8,128)(2,1)S(1)}, bf16[64,896]{1,0:T(8,128)(2,1)S(1)}, u32[]{:S(2)}, u32[]{:S(2)}) collective-permute-start(bf16[64,896]{1,0:T(8,128)(2,1)S(1)} %get-tuple-element.96), channel_id=1, source_target_pairs={{0,24},{4,28},{8,16},{12,20},{16,8},{20,12},{24,0},{28,4},{1,25},{... | collective-permute-start | bytes 344072 | tf_op jit(solution)/shard_map/return_z/ppermute | solution.py:33
  182.1 1.8 collective-permute-done.39.a1
  183.9 5.5 %collective-permute-done.40.a2 = bf16[64,896]{1,0:T(8,128)(2,1)S(1)} collective-permute-done((bf16[64,896]{1,0:T(8,128)(2,1)S(1)}, bf16[64,896]{1,0:T(8,128)(2,1)S(1)}, u32[]{:S(2)}, u32[]{:S(2)}) %collective-permute-start.40) | collective-permute-done | bytes 114720 | tf_op jit(solution)/shard_map/return_z/ppermute | solution.py:33
  191.6 1.5 collective-permute-start.43
  195.2 1.7 collective-permute-done.43.b1
  196.9 3.6 %collective-permute-done.44.b2 = bf16[32,1792]{1,0:T(8,128)(2,1)S(1)} collective-permute-done((bf16[32,1792]{1,0:T(8,128)(2,1)S(1)}, bf16[32,1792]{1,0:T(8,128)(2,1)S(1)}, u32[]{:S(2)}, u32[]{:S(2)}) %collective-permute-start.44) | collective-permute-done | bytes 114720 | tf_op jit(solution)/shard_map/return_plane/ppermute | solution.py:37
  200.5 1.8 add_home.1
  (116 shorter events, 37.1 us)
Async XLA Ops:
  0.0 21.0 %collective-permute-start.4 = (bf16[98,1792]{1,0:T(8,128)(2,1)}, bf16[98,1792]{1,0:T(8,128)(2,1)S(1)}, u32[]{:S(2)}, u32[]{:S(2)}) collective-permute-start(bf16[98,1792]{1,0:T(8,128)(2,1)} %x_ref.3), channel_id=1, source_target_pairs={{0,16},{4,20},{8,24},{12,28},{16,0},{20,4},{24,8},{28,12},{1,17},{... | collective-permute-start | bytes 1053704 | tf_op jit(solution)/shard_map/gather_home/ppermute | solution.py:33
  4.8 17.2 %collective-permute-start.3 = (bf16[98,1792]{1,0:T(8,128)(2,1)}, bf16[98,1792]{1,0:T(8,128)(2,1)S(1)}, u32[]{:S(2)}, u32[]{:S(2)}) collective-permute-start(bf16[98,1792]{1,0:T(8,128)(2,1)} %x_ref.3), channel_id=1, source_target_pairs={{0,8},{4,12},{8,0},{12,4},{16,24},{20,28},{24,16},{28,20},{1,9},{5... | collective-permute-start | bytes 1053704 | tf_op jit(solution)/shard_map/gather_home/ppermute | solution.py:33
  8.6 5.4 %collective-permute-start = (bf16[32,1792]{1,0:T(8,128)(2,1)S(1)}, bf16[32,1792]{1,0:T(8,128)(2,1)S(1)}, u32[]{:S(2)}, u32[]{:S(2)}) collective-permute-start(bf16[32,1792]{1,0:T(8,128)(2,1)S(1)} %get-tuple-element.54), channel_id=1, source_target_pairs={{0,1},{1,0},{2,3},{3,2},{4,5},{5,4},{6,7},{7,6},{8,9},{9,8},{10,11... | collective-permute-start | bytes 344072 | tf_op jit(solution)/shard_map/deal/ppermute | solution.py:37
  10.1 6.4 %collective-permute-start.1 = (bf16[32,1792]{1,0:T(8,128)(2,1)S(1)}, bf16[32,1792]{1,0:T(8,128)(2,1)S(1)}, u32[]{:S(2)}, u32[]{:S(2)}) collective-permute-start(bf16[32,1792]{1,0:T(8,128)(2,1)S(1)} %get-tuple-element.55), channel_id=1, source_target_pairs={{0,2},{1,3},{2,0},{3,1},{4,6},{5,7},{6,4},{7,5},{8,10},{9,11},{10,... | collective-permute-start | bytes 344072 | tf_op jit(solution)/shard_map/deal/ppermute | solution.py:37
  11.7 5.7 %collective-permute-start.2 = (bf16[32,1792]{1,0:T(8,128)(2,1)S(1)}, bf16[32,1792]{1,0:T(8,128)(2,1)S(1)}, u32[]{:S(2)}, u32[]{:S(2)}) collective-permute-start(bf16[32,1792]{1,0:T(8,128)(2,1)S(1)} %get-tuple-element.56), channel_id=1, source_target_pairs={{0,3},{1,2},{2,1},{3,0},{4,7},{5,6},{6,5},{7,4},{8,11},{9,10},{10,... | collective-permute-start | bytes 344072 | tf_op jit(solution)/shard_map/deal/ppermute | solution.py:37
  23.0 6.3 %collective-permute-start.5 = (bf16[32,1792]{1,0:T(8,128)(2,1)S(1)}, bf16[32,1792]{1,0:T(8,128)(2,1)S(1)}, u32[]{:S(2)}, u32[]{:S(2)}) collective-permute-start(bf16[32,1792]{1,0:T(8,128)(2,1)S(1)} %get-tuple-element.58), channel_id=1, source_target_pairs={{0,8},{4,12},{8,0},{12,4},{16,24},{20,28},{24,16},{28,20},{1,9},{5... | collective-permute-start | bytes 344072 | tf_op jit(solution)/shard_map/spread_z/ppermute | solution.py:33
  23.8 11.6 %collective-permute-start.6 = (bf16[32,1792]{1,0:T(8,128)(2,1)S(1)}, bf16[32,1792]{1,0:T(8,128)(2,1)S(1)}, u32[]{:S(2)}, u32[]{:S(2)}) collective-permute-start(bf16[32,1792]{1,0:T(8,128)(2,1)S(1)} %get-tuple-element.59), channel_id=1, source_target_pairs={{0,16},{4,20},{8,24},{12,28},{16,0},{20,4},{24,8},{28,12},{1,17},{... | collective-permute-start | bytes 344072 | tf_op jit(solution)/shard_map/spread_z/ppermute | solution.py:33
  26.2 9.2 %collective-permute-start.7 = (bf16[32,1792]{1,0:T(8,128)(2,1)S(1)}, bf16[32,1792]{1,0:T(8,128)(2,1)S(1)}, u32[]{:S(2)}, u32[]{:S(2)}) collective-permute-start(bf16[32,1792]{1,0:T(8,128)(2,1)S(1)} %get-tuple-element.60), channel_id=1, source_target_pairs={{0,24},{4,28},{8,16},{12,20},{16,8},{20,12},{24,0},{28,4},{1,25},{... | collective-permute-start | bytes 344072 | tf_op jit(solution)/shard_map/spread_z/ppermute | solution.py:33
  36.1 11.3 %collective-permute-start.12 = (bf16[256,1792]{1,0:T(8,128)(2,1)S(1)}, bf16[256,1792]{1,0:T(8,128)(2,1)S(1)}, u32[]{:S(2)}, u32[]{:S(2)}) collective-permute-start(bf16[256,1792]{1,0:T(8,128)(2,1)S(1)} %copy_rows.1), channel_id=1, source_target_pairs={{0,4},{4,0},{8,12},{12,8},{16,20},{20,16},{24,28},{28,24},{1,5},{5... | collective-permute-start | bytes 2752520 | tf_op jit(solution)/shard_map/low_rank/ppermute | solution.py:33
  36.2 2.8 %collective-permute-start.8 = (bf16[128,896]{1,0:T(8,128)(2,1)S(1)}, bf16[128,896]{1,0:T(8,128)(2,1)S(1)}, u32[]{:S(2)}, u32[]{:S(2)}) collective-permute-start(bf16[128,896]{1,0:T(8,128)(2,1)S(1)} %get-tuple-element.62), channel_id=1, source_target_pairs={{0,4},{4,0},{8,12},{12,8},{16,20},{20,16},{24,28},{28,24},{1,5},{5... | collective-permute-start | bytes 688136 | tf_op jit(solution)/shard_map/spread_z/ppermute | solution.py:33
  36.7 10.7 %collective-permute-start.13 = (bf16[98,1792]{1,0:T(8,128)(2,1)S(1)}, bf16[98,1792]{1,0:T(8,128)(2,1)S(1)}, u32[]{:S(2)}, u32[]{:S(2)}) collective-permute-start(bf16[98,1792]{1,0:T(8,128)(2,1)S(1)} %collective-permute-done.4.__.x2), channel_id=1, source_target_pairs={{0,8},{4,12},{8,0},{12,4},{16,24},{20,28},{24,16},{28,20},{1,9},{5... | collective-permute-start | bytes 1053704 | tf_op jit(solution)/shard_map/gather_home/ppermute | solution.py:33
  40.0 16.7 %collective-permute-start.10 = (bf16[144,896]{1,0:T(8,128)(2,1)S(1)}, bf16[144,896]{1,0:T(8,128)(2,1)S(1)}, u32[]{:S(2)}, u32[]{:S(2)}) collective-permute-start(bf16[144,896]{1,0:T(8,128)(2,1)S(1)} %pack_rows.1.c0), channel_id=1, source_target_pairs={{0,2},{1,3},{2,0},{3,1},{4,6},{5,7},{6,4},{7,5},{8,10},{9,11},{10,... | collective-permute-start | bytes 774152 | tf_op jit(solution)/shard_map/gather_chunks/ppermute | solution.py:37
  41.6 15.1 %collective-permute-start.11 = (bf16[144,896]{1,0:T(8,128)(2,1)S(1)}, bf16[144,896]{1,0:T(8,128)(2,1)S(1)}, u32[]{:S(2)}, u32[]{:S(2)}) collective-permute-start(bf16[144,896]{1,0:T(8,128)(2,1)S(1)} %pack_rows.1.c0), channel_id=1, source_target_pairs={{0,3},{1,2},{2,1},{3,0},{4,7},{5,6},{6,5},{7,4},{8,11},{9,10},{10,... | collective-permute-start | bytes 774152 | tf_op jit(solution)/shard_map/gather_chunks/ppermute | solution.py:37
  43.0 13.7 %collective-permute-start.9 = (bf16[144,896]{1,0:T(8,128)(2,1)S(1)}, bf16[144,896]{1,0:T(8,128)(2,1)S(1)}, u32[]{:S(2)}, u32[]{:S(2)}) collective-permute-start(bf16[144,896]{1,0:T(8,128)(2,1)S(1)} %pack_rows.1.c0), channel_id=1, source_target_pairs={{0,1},{1,0},{2,3},{3,2},{4,5},{5,4},{6,7},{7,6},{8,9},{9,8},{10,11... | collective-permute-start | bytes 774152 | tf_op jit(solution)/shard_map/gather_chunks/ppermute | solution.py:37
  52.4 4.3 %collective-permute-start.14 = (f32[32,512]{1,0:T(8,128)S(1)}, f32[32,512]{1,0:T(8,128)S(1)}, u32[]{:S(2)}, u32[]{:S(2)}) collective-permute-start(f32[32,512]{1,0:T(8,128)S(1)} %low_rank_rows.1.a_ref._), channel_id=1, source_target_pairs={{0,1},{1,0},{2,3},{3,2},{4,5},{5,4},{6,7},{7,6},{8,9},{9,8},{10,11... | collective-permute-start | bytes 196616 | tf_op jit(solution)/shard_map/low_rank/ppermute | solution.py:37
  59.9 4.6 %collective-permute-start.17 = (bf16[256,1536]{1,0:T(8,128)(2,1)S(1)}, bf16[256,1536]{1,0:T(8,128)(2,1)S(1)}, u32[]{:S(2)}, u32[]{:S(2)}) collective-permute-start(bf16[256,1536]{1,0:T(8,128)(2,1)S(1)} %get-tuple-element.64._), channel_id=1, source_target_pairs={{0,4},{4,0},{8,12},{12,8},{16,20},{20,16},{24,28},{28,24},{1,5},{5... | collective-permute-start | bytes 2359304 | tf_op jit(solution)/shard_map/keys/ppermute | solution.py:33
  60.0 4.5 %collective-permute-start.15 = (f32[32,512]{1,0:T(8,128)S(1)}, f32[32,512]{1,0:T(8,128)S(1)}, u32[]{:S(2)}, u32[]{:S(2)}) collective-permute-start(f32[32,512]{1,0:T(8,128)S(1)} %add_rows.4._.a_ref), channel_id=1, source_target_pairs={{0,2},{1,3},{2,0},{3,1},{4,6},{5,7},{6,4},{7,5},{8,10},{9,11},{10,... | collective-permute-start | bytes 196616 | tf_op jit(solution)/shard_map/low_rank/ppermute | solution.py:37
  65.2 15.2 %collective-permute-start.21 = (bf16[256,768]{1,0:T(8,128)(2,1)S(1)}, bf16[256,768]{1,0:T(8,128)(2,1)S(1)}, u32[]{:S(2)}, u32[]{:S(2)}) collective-permute-start(bf16[256,768]{1,0:T(8,128)(2,1)S(1)} %get-tuple-element.67._), channel_id=1, source_target_pairs={{0,8},{4,12},{8,0},{12,4},{16,24},{20,28},{24,16},{28,20},{1,9},{5... | collective-permute-start | bytes 1179656 | tf_op jit(solution)/shard_map/keys/ppermute | solution.py:33
  67.0 1.2 collective-permute-start.16
  70.9 1.4 collective-permute-start.18
  72.3 5.2 %collective-permute-start.19 = (f32[4,4608]{1,0:T(4,128)S(1)}, f32[4,4608]{1,0:T(4,128)S(1)}, u32[]{:S(2)}, u32[]{:S(2)}) collective-permute-start(f32[4,4608]{1,0:T(4,128)S(1)} %slice.38), channel_id=1, source_target_pairs={{0,8},{4,12},{8,0},{12,4},{16,24},{20,28},{24,16},{28,20},{1,9},{5... | collective-permute-start | bytes 221192 | tf_op jit(solution)/shard_map/decode_rows/ppermute | solution.py:33
  77.6 4.9 %collective-permute-start.20 = (f32[2,4608]{1,0:T(2,128)S(1)}, f32[2,4608]{1,0:T(2,128)S(1)}, u32[]{:S(2)}, u32[]{:S(2)}) collective-permute-start(f32[2,4608]{1,0:T(2,128)S(1)} %slice.39), channel_id=1, source_target_pairs={{0,16},{4,20},{8,24},{12,28},{16,0},{20,4},{24,8},{28,12},{1,17},{... | collective-permute-start | bytes 110600 | tf_op jit(solution)/shard_map/decode_rows/ppermute | solution.py:33
  80.4 5.0 %collective-permute-start.22 = (bf16[256,1536]{1,0:T(8,128)(2,1)S(1)}, bf16[256,1536]{1,0:T(8,128)(2,1)S(1)}, u32[]{:S(2)}, u32[]{:S(2)}) collective-permute-start(bf16[256,1536]{1,0:T(8,128)(2,1)S(1)} %get-tuple-element.76), channel_id=1, source_target_pairs={{0,4},{4,0},{8,12},{12,8},{16,20},{20,16},{24,28},{28,24},{1,5},{5... | collective-permute-start | bytes 2359304 | tf_op jit(solution)/shard_map/values/ppermute | solution.py:33
  85.3 2.4 %collective-permute-start.23 = (bf16[256,1536]{1,0:T(8,128)(2,1)S(1)}, bf16[256,1536]{1,0:T(8,128)(2,1)S(1)}, u32[]{:S(2)}, u32[]{:S(2)}) collective-permute-start(bf16[256,1536]{1,0:T(8,128)(2,1)S(1)} %get-tuple-element.77), channel_id=1, source_target_pairs={{0,4},{4,0},{8,12},{12,8},{16,20},{20,16},{24,28},{28,24},{1,5},{5... | collective-permute-start | bytes 2359304 | tf_op jit(solution)/shard_map/queries/ppermute | solution.py:33
  88.6 23.9 %collective-permute-start.24 = (bf16[256,1536]{1,0:T(8,128)(2,1)S(1)}, bf16[256,1536]{1,0:T(8,128)(2,1)S(1)}, u32[]{:S(2)}, u32[]{:S(2)}) collective-permute-start(bf16[256,1536]{1,0:T(8,128)(2,1)S(1)} %get-tuple-element.79._), channel_id=1, source_target_pairs={{0,8},{4,12},{8,0},{12,4},{16,24},{20,28},{24,16},{28,20},{1,9},{5... | collective-permute-start | bytes 2359304 | tf_op jit(solution)/shard_map/reduce_z/ppermute | solution.py:33
  90.4 21.3 %collective-permute-start.25 = (bf16[256,384]{1,0:T(8,128)(2,1)S(1)}, bf16[256,384]{1,0:T(8,128)(2,1)S(1)}, u32[]{:S(2)}, u32[]{:S(2)}) collective-permute-start(bf16[256,384]{1,0:T(8,128)(2,1)S(1)} %get-tuple-element.73._), channel_id=1, source_target_pairs={{0,16},{4,20},{8,24},{12,28},{16,0},{20,4},{24,8},{28,12},{1,17},{... | collective-permute-start | bytes 589832 | tf_op jit(solution)/shard_map/keys/ppermute | solution.py:33
  113.2 20.3 %collective-permute-start.26 = (bf16[256,768]{1,0:T(8,128)(2,1)S(1)}, bf16[256,768]{1,0:T(8,128)(2,1)S(1)}, u32[]{:S(2)}, u32[]{:S(2)}) collective-permute-start(bf16[256,768]{1,0:T(8,128)(2,1)S(1)} %get-tuple-element.83._), channel_id=1, source_target_pairs={{0,16},{4,20},{8,24},{12,28},{16,0},{20,4},{24,8},{28,12},{1,17},{... | collective-permute-start | bytes 1179656 | tf_op jit(solution)/shard_map/reduce_z/ppermute | solution.py:33
  116.5 17.8 %collective-permute-start.27 = (bf16[256,384]{1,0:T(8,128)(2,1)S(1)}, bf16[256,384]{1,0:T(8,128)(2,1)S(1)}, u32[]{:S(2)}, u32[]{:S(2)}) collective-permute-start(bf16[256,384]{1,0:T(8,128)(2,1)S(1)} %finish_sums.2.refs_2_.ka_ref), channel_id=1, source_target_pairs={{0,4},{4,0},{8,12},{12,8},{16,20},{20,16},{24,28},{28,24},{1,5},{5... | collective-permute-start | bytes 589832 | tf_op jit(solution)/shard_map/keys/ppermute | solution.py:33
  134.1 1.5 collective-permute-start.28
  137.2 12.5 %collective-permute-start.30 = (bf16[272,384]{1,0:T(8,128)(2,1)S(1)}, bf16[272,384]{1,0:T(8,128)(2,1)S(1)}, u32[]{:S(2)}, u32[]{:S(2)}) collective-permute-start(bf16[272,384]{1,0:T(8,128)(2,1)S(1)} %prompt_attention.1.refs_0_), channel_id=1, source_target_pairs={{0,16},{4,20},{8,24},{12,28},{16,0},{20,4},{24,8},{28,12},{1,17},{... | collective-permute-start | bytes 626696 | tf_op jit(solution)/shard_map/gather_attended/ppermute | solution.py:33
  137.2 12.6 %collective-permute-start.29 = (bf16[272,384]{1,0:T(8,128)(2,1)S(1)}, bf16[272,384]{1,0:T(8,128)(2,1)S(1)}, u32[]{:S(2)}, u32[]{:S(2)}) collective-permute-start(bf16[272,384]{1,0:T(8,128)(2,1)S(1)} %prompt_attention.1.refs_0_), channel_id=1, source_target_pairs={{0,8},{4,12},{8,0},{12,4},{16,24},{20,28},{24,16},{28,20},{1,9},{5... | collective-permute-start | bytes 626696 | tf_op jit(solution)/shard_map/gather_attended/ppermute | solution.py:33
  149.7 7.0 %collective-permute-start.31 = (bf16[272,384]{1,0:T(8,128)(2,1)S(1)}, bf16[272,384]{1,0:T(8,128)(2,1)S(1)}, u32[]{:S(2)}, u32[]{:S(2)}) collective-permute-start(bf16[272,384]{1,0:T(8,128)(2,1)S(1)} %collective-permute-done.30.refs_2_), channel_id=1, source_target_pairs={{0,8},{4,12},{8,0},{12,4},{16,24},{20,28},{24,16},{28,20},{1,9},{5... | collective-permute-start | bytes 626696 | tf_op jit(solution)/shard_map/gather_attended/ppermute | solution.py:33
  149.7 7.0 %collective-permute-start.32 = (bf16[272,384]{1,0:T(8,128)(2,1)S(1)}, bf16[272,384]{1,0:T(8,128)(2,1)S(1)}, u32[]{:S(2)}, u32[]{:S(2)}) collective-permute-start(bf16[272,384]{1,0:T(8,128)(2,1)S(1)} %prompt_attention.1.refs_0_), channel_id=1, source_target_pairs={{0,4},{4,0},{8,12},{12,8},{16,20},{20,16},{24,28},{28,24},{1,5},{5... | collective-permute-start | bytes 626696 | tf_op jit(solution)/shard_map/gather_attended/ppermute | solution.py:33
  149.9 6.9 %collective-permute-start.33 = (bf16[272,384]{1,0:T(8,128)(2,1)S(1)}, bf16[272,384]{1,0:T(8,128)(2,1)S(1)}, u32[]{:S(2)}, u32[]{:S(2)}) collective-permute-start(bf16[272,384]{1,0:T(8,128)(2,1)S(1)} %collective-permute-done.29.refs_1_), channel_id=1, source_target_pairs={{0,4},{4,0},{8,12},{12,8},{16,20},{20,16},{24,28},{28,24},{1,5},{5... | collective-permute-start | bytes 626696 | tf_op jit(solution)/shard_map/gather_attended/ppermute | solution.py:33
  150.2 6.5 %collective-permute-start.34 = (bf16[272,384]{1,0:T(8,128)(2,1)S(1)}, bf16[272,384]{1,0:T(8,128)(2,1)S(1)}, u32[]{:S(2)}, u32[]{:S(2)}) collective-permute-start(bf16[272,384]{1,0:T(8,128)(2,1)S(1)} %collective-permute-done.30.refs_2_), channel_id=1, source_target_pairs={{0,4},{4,0},{8,12},{12,8},{16,20},{20,16},{24,28},{28,24},{1,5},{5... | collective-permute-start | bytes 626696 | tf_op jit(solution)/shard_map/gather_attended/ppermute | solution.py:33
  156.8 2.3 %collective-permute-start.35 = (bf16[272,384]{1,0:T(8,128)(2,1)S(1)}, bf16[272,384]{1,0:T(8,128)(2,1)S(1)}, u32[]{:S(2)}, u32[]{:S(2)}) collective-permute-start(bf16[272,384]{1,0:T(8,128)(2,1)S(1)} %collective-permute-done.31.refs_3_), channel_id=1, source_target_pairs={{0,4},{4,0},{8,12},{12,8},{16,20},{20,16},{24,28},{28,24},{1,5},{5... | collective-permute-start | bytes 626696 | tf_op jit(solution)/shard_map/gather_attended/ppermute | solution.py:33
  159.1 36.1 %copy-start.9 = (f32[1792]{0:T(1024)S(1)}, f32[1792]{0:T(1024)}, u32[]{:S(2)}) copy-start(f32[1792]{0:T(1024)} %param.25) | copy-start | bytes 21508
  161.2 39.3 %copy-start.6 = (bf16[98,1792]{1,0:T(8,128)(2,1)S(1)}, bf16[98,1792]{1,0:T(8,128)(2,1)}, u32[]{:S(2)}) copy-start(bf16[98,1792]{1,0:T(8,128)(2,1)} %x_ref.3) | copy-start | bytes 1053700
  161.2 9.1 %collective-permute-start.36 = (bf16[144,896]{1,0:T(8,128)(2,1)S(1)}, bf16[144,896]{1,0:T(8,128)(2,1)S(1)}, u32[]{:S(2)}, u32[]{:S(2)}) collective-permute-start(bf16[144,896]{1,0:T(8,128)(2,1)S(1)} %get-tuple-element.90), channel_id=1, source_target_pairs={{0,1},{1,0},{2,3},{3,2},{4,5},{5,4},{6,7},{7,6},{8,9},{9,8},{10,11... | collective-permute-start | bytes 774152 | tf_op jit(solution)/shard_map/sum_mp/ppermute | solution.py:37
  162.7 13.9 %collective-permute-start.37 = (bf16[144,896]{1,0:T(8,128)(2,1)S(1)}, bf16[144,896]{1,0:T(8,128)(2,1)S(1)}, u32[]{:S(2)}, u32[]{:S(2)}) collective-permute-start(bf16[144,896]{1,0:T(8,128)(2,1)S(1)} %get-tuple-element.91), channel_id=1, source_target_pairs={{0,2},{1,3},{2,0},{3,1},{4,6},{5,7},{6,4},{7,5},{8,10},{9,11},{10,... | collective-permute-start | bytes 774152 | tf_op jit(solution)/shard_map/sum_mp/ppermute | solution.py:37
  164.3 12.3 %collective-permute-start.38 = (bf16[144,896]{1,0:T(8,128)(2,1)S(1)}, bf16[144,896]{1,0:T(8,128)(2,1)S(1)}, u32[]{:S(2)}, u32[]{:S(2)}) collective-permute-start(bf16[144,896]{1,0:T(8,128)(2,1)S(1)} %get-tuple-element.92), channel_id=1, source_target_pairs={{0,3},{1,2},{2,1},{3,0},{4,7},{5,6},{6,5},{7,4},{8,11},{9,10},{10,... | collective-permute-start | bytes 774152 | tf_op jit(solution)/shard_map/sum_mp/ppermute | solution.py:37
  177.6 6.3 %collective-permute-start.39 = (bf16[64,896]{1,0:T(8,128)(2,1)S(1)}, bf16[64,896]{1,0:T(8,128)(2,1)S(1)}, u32[]{:S(2)}, u32[]{:S(2)}) collective-permute-start(bf16[64,896]{1,0:T(8,128)(2,1)S(1)} %get-tuple-element.94), channel_id=1, source_target_pairs={{0,8},{4,12},{8,0},{12,4},{16,24},{20,28},{24,16},{28,20},{1,9},{5... | collective-permute-start | bytes 344072 | tf_op jit(solution)/shard_map/return_z/ppermute | solution.py:33
  177.9 11.5 %collective-permute-start.40 = (bf16[64,896]{1,0:T(8,128)(2,1)S(1)}, bf16[64,896]{1,0:T(8,128)(2,1)S(1)}, u32[]{:S(2)}, u32[]{:S(2)}) collective-permute-start(bf16[64,896]{1,0:T(8,128)(2,1)S(1)} %get-tuple-element.95), channel_id=1, source_target_pairs={{0,16},{4,20},{8,24},{12,28},{16,0},{20,4},{24,8},{28,12},{1,17},{... | collective-permute-start | bytes 344072 | tf_op jit(solution)/shard_map/return_z/ppermute | solution.py:33
  179.6 9.8 %collective-permute-start.41 = (bf16[64,896]{1,0:T(8,128)(2,1)S(1)}, bf16[64,896]{1,0:T(8,128)(2,1)S(1)}, u32[]{:S(2)}, u32[]{:S(2)}) collective-permute-start(bf16[64,896]{1,0:T(8,128)(2,1)S(1)} %get-tuple-element.96), channel_id=1, source_target_pairs={{0,24},{4,28},{8,16},{12,20},{16,8},{20,12},{24,0},{28,4},{1,25},{... | collective-permute-start | bytes 344072 | tf_op jit(solution)/shard_map/return_z/ppermute | solution.py:33
  189.5 1.6 collective-permute-start.42
  191.6 5.3 %collective-permute-start.43 = (bf16[32,1792]{1,0:T(8,128)(2,1)S(1)}, bf16[32,1792]{1,0:T(8,128)(2,1)S(1)}, u32[]{:S(2)}, u32[]{:S(2)}) collective-permute-start(bf16[32,1792]{1,0:T(8,128)(2,1)S(1)} %get-tuple-element.98), channel_id=1, source_target_pairs={{0,1},{1,0},{2,3},{3,2},{4,5},{5,4},{6,7},{7,6},{8,9},{9,8},{10,11... | collective-permute-start | bytes 344072 | tf_op jit(solution)/shard_map/return_plane/ppermute | solution.py:37
  193.2 7.4 %collective-permute-start.44 = (bf16[32,1792]{1,0:T(8,128)(2,1)S(1)}, bf16[32,1792]{1,0:T(8,128)(2,1)S(1)}, u32[]{:S(2)}, u32[]{:S(2)}) collective-permute-start(bf16[32,1792]{1,0:T(8,128)(2,1)S(1)} %get-tuple-element.99), channel_id=1, source_target_pairs={{0,2},{1,3},{2,0},{3,1},{4,6},{5,7},{6,4},{7,5},{8,10},{9,11},{10,... | collective-permute-start | bytes 344072 | tf_op jit(solution)/shard_map/return_plane/ppermute | solution.py:37
  193.7 6.8 %collective-permute-start.45 = (bf16[32,1792]{1,0:T(8,128)(2,1)S(1)}, bf16[32,1792]{1,0:T(8,128)(2,1)S(1)}, u32[]{:S(2)}, u32[]{:S(2)}) collective-permute-start(bf16[32,1792]{1,0:T(8,128)(2,1)S(1)} %get-tuple-element.100), channel_id=1, source_target_pairs={{0,3},{1,2},{2,1},{3,0},{4,7},{5,6},{6,5},{7,4},{8,11},{9,10},{10,... | collective-permute-start | bytes 344072 | tf_op jit(solution)/shard_map/return_plane/ppermute | solution.py:37
  (8 other events, 146.1 us)
